TPU v7x, 32 devices: a whole 2x2x4 slice. The times are simulated.
32 devices in a mesh: path: 8 (over y, x, core), shard: 4 (over z).
Axes of the slice: x: 2, y: 2, z: 4, core: 2. Of those that a mesh axis runs over, the one named last changes fastest.
Arguments:
- path_delta: float32 [8, 2, 512, 1024], P('path', None, 'shard'), may hold values from -500 to 500
- assign: int32 [8, 2], replicated, may hold values from 0 to 15
- params: float32 [32, 4, 128, 1024], P(None, 'shard', 'path'), may hold values from -6 to 6
- momentum: float32 [32, 4, 128, 1024], P(None, 'shard', 'path'), may hold values from -3 to 3
Outputs:
- path_params: float32 [8, 2, 512, 1024], P('path', None, 'shard')
- new_params: float32 [32, 4, 128, 1024], P(None, 'shard', 'path')
- new_momentum: float32 [32, 4, 128, 1024], P(None, 'shard', 'path')
All inputs are finite; a program needn't handle non-finite values.
Results may differ from a plain program's by a relative error of at most 0.00007.
Values sent between devices are 32-bit elements; how exact they have to be, the bound alone decides.
No kernel may reach another device: no remote copies, remote signals or barrier semaphores. Data moves between devices by JAX's collectives and lax.ppermute only.
A program may use at most 128 MiB of HBM per device.

v0:
```python
import jax
import jax.numpy as jnp
from jax import lax
from jax.experimental import pallas as pl
from jax.experimental.pallas import tpu as pltpu
from jax.sharding import PartitionSpec as P

LEVEL_MODULES = 16
LEVELS = 2
MOST_UNROLLED = 16

outer_rate = 0.7
beta_coef = 0.9
moment_coef = outer_rate * beta_coef * beta_coef
grad_coef = outer_rate * (1.0 + beta_coef)

VMEM_LIMIT = 16 * 1024 * 1024

vmem = pl.BlockSpec(memory_space=pltpu.VMEM)
smem = pl.BlockSpec(memory_space=pltpu.SMEM)
anywhere = pl.BlockSpec(memory_space=pl.ANY)


def call(kernel, out_shape, in_specs, out_specs, **more):
    return pl.pallas_call(
        kernel,
        out_shape=out_shape,
        in_specs=in_specs,
        out_specs=out_specs,
        compiler_params=pltpu.CompilerParams(vmem_limit_bytes=VMEM_LIMIT),
        **more,
    )


def mirrored(k, size):
    if size < 8:
        return k
    return (k & ~6) | ((k & 2) << 1) | ((k & 4) >> 1)


def target(here, k, size):
    if isinstance(here, int):
        return here ^ (mirrored(k, size) if here & 1 else k)
    return here ^ jnp.where(here & 1 == 1, mirrored(k, size), k)


def origin(here, k, size):
    if isinstance(here, int):
        return here ^ (mirrored(k, size) if (here ^ k) & 1 else k)
    return here ^ jnp.where((here ^ k) & 1 == 1, mirrored(k, size), k)


def order_of(size):
    return sorted(range(2, size, 2), key=lambda k: (-bin(k).count("1"), k)) + [0]


def move(array, k, size):
    if k == 0:
        return array
    return lax.ppermute(array, "path", [(i, target(i, k, size)) for i in range(size)])


def tiles_of(rows, width):
    return [(slice(row, row + 8), slice(lane, lane + 128)) for row in range(0, rows, 8) for lane in range(0, width, 128)]


def pack_kernel(here_ref, delta_ref, square_ref, keep_ref, give_ref):
    levels, chips, halves, rows, width = delta_ref.shape

    def pack(core):
        totals = [jnp.zeros((8, 128), jnp.float32) for _ in range(4)]
        for level in range(levels):
            for chip in range(chips):
                for t, spot in enumerate(tiles_of(rows, width)):
                    kept = delta_ref[(level, chip, core, *spot)]
                    given = delta_ref[(level, chip, 1 - core, *spot)]
                    keep_ref[(level, chip, *spot)] = kept
                    give_ref[(level, chip, *spot)] = given
                    totals[t % 4] = totals[t % 4] + (kept * kept + given * given)
        total = jnp.sum((totals[0] + totals[1]) + (totals[2] + totals[3]), axis=0, keepdims=True)
        for first in range(0, square_ref.shape[0], 8):
            row = lax.broadcasted_iota(jnp.int32, (8, 128), 0) + first
            square_ref[first : first + 8] = jnp.where(row == here_ref[0], total, 0.0)

    for core in range(halves):
        pl.when(here_ref[0] & 1 == core)(lambda core=core: pack(core))


def merge_kernel(size, here_ref, square_ref, other_ref, keep_ref, gift_ref, plan_ref, square_out, *outs):
    del plan_ref
    here = here_ref[0]
    core = here & 1
    square_out[...] = square_ref[...] + other_ref[...]
    for k, out in zip(order_of(size), outs):
        chip = target(here, k, size) // 2
        for level in range(LEVELS):
            out[core, level] = keep_ref[level, chip]
            out[1 - core, level] = gift_ref[level, chip]


def sum_kernel(*refs):
    total = refs[0][...]
    for ref in refs[1:-1]:
        total = total + ref[...]
    refs[-1][...] = total


def factor_kernel(entries, here_ref, ids_ref, *refs):
    squares, (out_ref, rescale_ref) = refs[:-2], refs[-2:]
    size = ids_ref.shape[0]
    total = squares[0][...]
    for square_ref in squares[1:]:
        total = total + square_ref[...]
    total = jnp.sum(total, axis=1, keepdims=True)
    rescale_ref[...] = jnp.broadcast_to(1.0 / jnp.sqrt(total / entries + 1e-06), rescale_ref.shape)
    sources = [(origin(here_ref[0], k, size) // 2) * 2 + half for k in order_of(size) for half in range(2)]
    for i, path in enumerate(sources):
        rescale = jnp.broadcast_to(rescale_ref[pl.ds(path, 1), :], (8, 128))
        for level in range(LEVELS):
            sharers = jnp.int32(0)
            for other in range(size):
                sharers = sharers + jnp.where(ids_ref[other, level] == ids_ref[path, level], 1, 0)
            out_ref[level, i] = rescale / jnp.full((8, 128), sharers, jnp.int32).astype(jnp.float32)


def plan_kernel(here_ref, ids_ref, plan_ref, module_ref):
    size = ids_ref.shape[0]
    order = order_of(size)
    here = here_ref[0]
    for level in range(LEVELS):
        first = level * LEVEL_MODULES
        for module in range(LEVEL_MODULES):
            module_ref[first + module] = -1
        sources = [ids_ref[(origin(here, k, size) // 2) * 2 + half, level] + first for k in order for half in range(2)]
        for i in reversed(range(size)):
            module_ref[sources[i]] = i
        for i in range(size):
            plan_ref[level, i] = module_ref[sources[i]]
        for j, k in enumerate(order):
            for half in range(2):
                module = ids_ref[(target(here, k, size) // 2) * 2 + half, level] + first
                plan_ref[level, size + 2 * j + half] = module
                plan_ref[level, 2 * size + 2 * j + half] = module_ref[module]


def outgoing_kernel(rounds, plan_ref, factor_ref, decayed_ref, *refs):
    received, outs, grad_ref = refs[:rounds], refs[rounds:-1], refs[-1]
    size = 2 * rounds
    for level in range(LEVELS):
        for i in range(size):
            factor = factor_ref[level, i]
            for spot in tiles_of(*grad_ref.shape[2:]):
                grad_ref[(level, i, *spot)] = received[i // 2][(i % 2, level, *spot)] * factor
        for i in range(1, size):
            leader = plan_ref[level, i]

            @pl.when(leader != i)
            def _():
                grad_ref[level, leader] += grad_ref[level, i]

        for i in range(size):
            decayed = decayed_ref[plan_ref[level, size + i]]
            outs[i // 2][i % 2, level] = decayed - grad_coef * grad_ref[level, plan_ref[level, 2 * size + i]]


def state_kernel(module_ref, grad_ref, decayed_ref, momentum_ref, new_params_ref, new_momentum_ref, token_ref):
    token_ref[...] = jnp.zeros_like(token_ref)
    count = new_params_ref.shape[0]
    first = pl.program_id(0) * count
    level = first // LEVEL_MODULES
    for place in range(count):
        module = first + place
        leader = module_ref[module]
        taken = jnp.where(leader < 0, 0.0, 1.0)
        grad = taken * grad_ref[level, jnp.maximum(leader, 0)]
        new_momentum_ref[place] = beta_coef * momentum_ref[module] + grad
        new_params_ref[place] = decayed_ref[module] - grad_coef * grad


def give_back_kernel(size, here_ref, *refs):
    here = here_ref[0]
    for j, k in enumerate(order_of(size)):
        for level in range(LEVELS):
            refs[-1][level, origin(here, k, size) // 2] = refs[j][1 - (here & 1), level]


def own_rows_kernel(size, here_ref, *refs):
    here = here_ref[0]
    core = here & 1
    out_ref, sems = refs[-2:]
    copies = []
    for j, k in enumerate(order_of(size)):
        chip = origin(here, k, size) // 2
        for level in range(LEVELS):
            copies.append(
                pltpu.make_async_copy(refs[j].at[core, level], out_ref.at[level, chip, core], sems.at[level, j])
            )
    for copy in copies:
        copy.start()
    for copy in copies:
        copy.wait()


def other_rows_kernel(here_ref, back_ref, held_ref, out_ref, sems):
    del held_ref
    core = here_ref[0] & 1
    copies = []
    for level in range(LEVELS):
        for chip in range(back_ref.shape[1]):
            copies.append(
                pltpu.make_async_copy(
                    back_ref.at[level, chip], out_ref.at[level, chip, 1 - core], sems.at[level, chip]
                )
            )
    for copy in copies:
        copy.start()
    for copy in copies:
        copy.wait()


def local(path_delta, assign, params, momentum):
    own_slab = path_delta[0]
    size = assign.shape[0]
    module_count, _, own_rows, width = params.shape
    entries = float(own_slab.size * lax.axis_size("shard"))
    state_in = params.reshape(module_count, own_rows, width)
    moment_in = momentum.reshape(module_count, own_rows, width)
    split_slab = own_slab.reshape(LEVELS, size // 2, 2, own_rows, width)
    here = lax.axis_index("path").astype(jnp.int32).reshape(1)
    order = order_of(size)
    rounds = len(order)
    swap = [(i, i ^ 1) for i in range(size)]
    shape = lambda *dims: jax.ShapeDtypeStruct(dims, jnp.float32)
    squares_shape = shape(-(-size // 8) * 8, 128)
    by_chip = shape(LEVELS, rounds, own_rows, width)
    message = shape(2, LEVELS, own_rows, width)

    squares, keep, give = call(pack_kernel, [squares_shape, by_chip, by_chip], [smem, vmem], [vmem] * 3)(
        here, split_slab
    )
    other = lax.ppermute(squares, "path", swap)
    gift = lax.ppermute(give, "path", swap)
    plan, leaders = call(
        plan_kernel,
        [jax.ShapeDtypeStruct((LEVELS, 3 * size), jnp.int32), jax.ShapeDtypeStruct((module_count,), jnp.int32)],
        [smem, smem],
        [smem] * 2,
    )(here, assign)
    squares, *messages = call(
        lambda *refs: merge_kernel(size, *refs),
        [squares_shape] + [message] * rounds,
        [smem, vmem, vmem, vmem, vmem, anywhere],
        [vmem] * (1 + rounds),
    )(here, squares, other, keep, gift, plan)
    received = [move(messages[j], k, size) for j, k in enumerate(order)]
    squares = call(sum_kernel, squares_shape, [vmem] * rounds, vmem)(*[move(squares, k, size) for k in order])
    squares = lax.psum(squares, "shard")
    factors = call(
        lambda *refs: factor_kernel(entries, *refs),
        shape(LEVELS, size, 8, 128),
        [smem, smem, vmem],
        vmem,
        scratch_shapes=[pltpu.VMEM(squares_shape.shape, jnp.float32)],
    )(here, assign, squares)
    decayed = state_in - moment_coef * moment_in

    *outgoing, grad = call(
        lambda *refs: outgoing_kernel(rounds, *refs),
        [message] * rounds + [shape(LEVELS, size, own_rows, width)],
        [smem] + [vmem] * (2 + rounds),
        [vmem] * (rounds + 1),
    )(plan, factors, decayed, *received)
    returned = [move(outgoing[j], k, size) for j, k in enumerate(order)]
    block = LEVEL_MODULES // 2
    state_block = pl.BlockSpec((block, own_rows, width), lambda i: (i, 0, 0))
    new_state, new_moment, done = call(
        state_kernel,
        [shape(*state_in.shape)] * 2 + [shape(8, 128)],
        [smem, vmem, vmem, vmem],
        [state_block, state_block, vmem],
        grid=(module_count // block,),
    )(leaders, grad, decayed, moment_in)
    back = call(
        lambda *refs: give_back_kernel(size, *refs), by_chip, [smem] + [vmem] * rounds + [anywhere], vmem
    )(here, *returned, done)
    back = lax.ppermute(back, "path", swap)
    sems = [pltpu.SemaphoreType.DMA((LEVELS, rounds))]
    path_params = call(
        lambda *refs: own_rows_kernel(size, *refs),
        shape(*split_slab.shape),
        [smem] + [anywhere] * rounds,
        anywhere,
        scratch_shapes=sems,
    )(here, *returned)
    path_params = call(
        other_rows_kernel,
        shape(*split_slab.shape),
        [smem, anywhere, anywhere],
        anywhere,
        scratch_shapes=sems,
        input_output_aliases={2: 0},
    )(here, back, path_params)
    return (path_params.reshape(path_delta.shape), new_state[:, None], new_moment[:, None])


def local_wide(path_delta, assign, params, momentum):
    own_slab = path_delta[0]
    path_count = assign.shape[0]
    module_count, _, own_rows, width = params.shape
    entries = float(own_slab.size * lax.axis_size("shard"))
    total_sq = lax.psum(jnp.sum(own_slab * own_slab), "shard")
    scaled = own_slab * (1.0 / jnp.sqrt(total_sq / entries + 1e-06))
    received = lax.all_to_all(
        scaled.reshape(LEVELS, path_count, own_rows, width), "path", split_axis=1, concat_axis=1, tiled=True
    )
    flat_ids = (assign + LEVEL_MODULES * jnp.arange(LEVELS, dtype=jnp.int32)[None, :]).T.reshape(-1)
    member = (jnp.arange(module_count, dtype=jnp.int32)[:, None] == flat_ids[None, :]).astype(jnp.float32)
    mean = member / jnp.maximum(jnp.sum(member, axis=1), 1.0)[:, None]
    grad = jnp.einsum(
        "mp,prd->mrd", mean, received.reshape(-1, own_rows, width), precision=lax.Precision.HIGHEST
    )
    new_moment = beta_coef * momentum[:, 0] + grad
    new_state = params[:, 0] - outer_rate * (grad + beta_coef * new_moment)
    outgoing = jnp.take(new_state, flat_ids, axis=0).reshape(LEVELS, path_count, own_rows, width)
    returned = lax.all_to_all(outgoing, "path", split_axis=1, concat_axis=1, tiled=True)
    return (returned.reshape(path_delta.shape), new_state[:, None], new_moment[:, None])


def solution(mesh):
    in_specs = (
        P("path", None, "shard", None),
        P(),
        P(None, "shard", "path", None),
        P(None, "shard", "path", None),
    )
    out_specs = (
        P("path", None, "shard", None),
        P(None, "shard", "path", None),
        P(None, "shard", "path", None),
    )
    chosen = local if 4 <= mesh.shape["path"] <= MOST_UNROLLED else local_wide
    return jax.shard_map(chosen, mesh=mesh, in_specs=in_specs, out_specs=out_specs, check_vma=False)
```

profile of v0, /device:TPU:0, one launch (start us, length us, event | category | flops | bytes accessed | tf_op | source)
XLA Modules:
  0.0 44.6 jit_solution(10038584118209585741)
XLA Ops:
  0.6 0.0 copy-start.1
  0.6 1.2 %copy-done.1 = f32[1,2,128,1024]{3,2,1,0:T(8,128)S(1)} copy-done((f32[1,2,128,1024]{3,2,1,0:T(8,128)S(1)}, f32[1,2,128,1024]{3,2,1,0:T(8,128)}, u32[]{:S(2)}) %copy-start.1) | copy-done | bytes 1048600
  1.9 0.1 shard_map.68
  2.0 0.5 %collective-permute-start.1 = (f32[2,4,16,1024]{3,2,1,0:T(8,128)S(1)}, f32[2,4,16,1024]{3,2,1,0:T(8,128)S(1)}, u32[]{:S(2)}, u32[]{:S(2)}) collective-permute-start(f32[2,4,16,1024]{3,2,1,0:T(8,128)S(1)} %get-tuple-element.24), channel_id=1, source_target_pairs={{0,4},{4,0},{8,12},{12,8},{16,20},{20,16},{24,28},{28,24},{1,5},{5... | collective-permute-start | bytes 1572872 | tf_op jit(solution)/shard_map/ppermute | solution.py:242
  2.5 0.1 collective-permute-start
  2.6 0.8 %copy.8.ids_ref.refs_1_ = s32[8,2]{1,0:T(8,128)S(1)} copy(s32[8,2]{0,1:T(2,128)} %param.5) | data formatting | bytes 128 | tf_op args[1]
  3.3 1.3 %shard_map.67 = (s32[2,24]{1,0:T(2,128)S(1)}, s32[32]{0:T(128)S(1)}) custom-call(s32[1]{0:T(128)} %bitcast.here_ref.refs_0_, s32[8,2]{1,0:T(8,128)S(1)} %copy.8.ids_ref.refs_1_), custom_call_target="tpu_custom_call" | custom-call | tf_op jit(solution)/shard_map/pallas_call | solution.py:243
  4.7 0.0 collective-permute-done.refs_2_
  4.7 0.0 collective-permute-done.1.refs_4_
  4.7 0.9 %shard_map.69 = (f32[8,128]{1,0:T(8,128)S(1)}, f32[2,2,16,1024]{3,2,1,0:T(8,128)}, f32[2,2,16,1024]{3,2,1,0:T(8,128)}, f32[2,2,16,1024]{3,2,1,0:T(8,128)S(1)}, f32[2,2,16,1024]{3,2,1,0:T(8,128)S(1)}) custom-call(s32[1]{0:T(128)} %bitcast.here_ref.refs_0_, f32[8,128]{1,0:T(8,128)S(1)} %get-tuple-element.22.refs_1_, ...), custom_call_target="tpu_custom_call" | custom-call | tf_op jit(solution)/shard_map/pallas_call | solution.py:249
  5.5 3.9 %collective-permute-start.2 = (f32[8,128]{1,0:T(8,128)S(1)}, f32[8,128]{1,0:T(8,128)S(1)}, u32[]{:S(2)}, u32[]{:S(2)}) collective-permute-start(f32[8,128]{1,0:T(8,128)S(1)} %get-tuple-element.25.refs_3_), channel_id=1, source_target_pairs={{0,24},{4,28},{8,16},{12,20},{16,8},{20,12},{24,0},{28,4},{1,25},{... | collective-permute-start | bytes 12296 | tf_op jit(solution)/shard_map/ppermute | solution.py:60
  9.4 0.5 %collective-permute-start.3 = (f32[8,128]{1,0:T(8,128)S(1)}, f32[8,128]{1,0:T(8,128)S(1)}, u32[]{:S(2)}, u32[]{:S(2)}) collective-permute-start(f32[8,128]{1,0:T(8,128)S(1)} %get-tuple-element.25.refs_3_), channel_id=1, source_target_pairs={{0,8},{4,20},{8,0},{12,28},{16,24},{20,4},{24,16},{28,12},{1,9},{5... | collective-permute-start | bytes 12296 | tf_op jit(solution)/shard_map/ppermute | solution.py:60
  10.0 0.0 collective-permute-start.4
  10.0 2.9 %collective-permute-start.5 = (f32[2,2,16,1024]{3,2,1,0:T(8,128)}, f32[2,2,16,1024]{3,2,1,0:T(8,128)S(1)}, u32[]{:S(2)}, u32[]{:S(2)}) collective-permute-start(f32[2,2,16,1024]{3,2,1,0:T(8,128)} %get-tuple-element.26), channel_id=1, source_target_pairs={{0,24},{4,28},{8,16},{12,20},{16,8},{20,12},{24,0},{28,4},{1,25},{... | collective-permute-start | bytes 786440 | tf_op jit(solution)/shard_map/ppermute | solution.py:60
  12.9 0.5 %collective-permute-start.6 = (f32[2,2,16,1024]{3,2,1,0:T(8,128)}, f32[2,2,16,1024]{3,2,1,0:T(8,128)S(1)}, u32[]{:S(2)}, u32[]{:S(2)}) collective-permute-start(f32[2,2,16,1024]{3,2,1,0:T(8,128)} %get-tuple-element.27), channel_id=1, source_target_pairs={{0,8},{4,20},{8,0},{12,28},{16,24},{20,4},{24,16},{28,12},{1,9},{5... | collective-permute-start | bytes 786440 | tf_op jit(solution)/shard_map/ppermute | solution.py:60
  13.5 0.0 collective-permute-done.2.refs_0_
  13.5 0.0 collective-permute-start.7
  13.5 2.7 %bitcast_subtract_fusion.refs_2_.decayed_ref = f32[32,16,1024]{2,1,0:T(8,128)S(1)} fusion(f32[32,1,16,1024]{3,2,1,0:T(8,128)} %param.6, f32[32,1,16,1024]{3,2,1,0:T(8,128)} %param.7), kind=kLoop, calls=%fused_computation | loop fusion | flops 1048576 | bytes 6291456 | tf_op jit(solution)/shard_map/sub | solution.py:265
  16.2 0.0 collective-permute-done.3.refs_1_
  16.2 0.0 collective-permute-done.4.refs_2_
  16.2 12.4 %psum.7.refs_2_ = f32[8,128]{1,0:T(8,128)S(1)} all-reduce(f32[8,128]{1,0:T(8,128)S(1)} %shard_map.70), channel_id=1, replica_groups=mesh['path'=8,'shard'=4] {'shard'}, use_global_device_ids=true, to_apply=%region_0.0 | all-reduce | flops 1024 | bytes 8192 | tf_op jit(solution)/shard_map/psum | solution.py:257
  28.6 0.0 copy-start
  28.6 0.8 %shard_map.71.refs_1_ = f32[2,8,8,128]{3,2,1,0:T(8,128)S(1)} custom-call(s32[1]{0:T(128)} %bitcast.here_ref.refs_0_, s32[8,2]{1,0:T(8,128)S(1)} %copy.8.ids_ref.refs_1_, f32[8,128]{1,0:T(8,128)S(1)} %psum.7.refs_2_), custom_call_target="tpu_custom_call" | custom-call | tf_op jit(solution)/shard_map/pallas_call | solution.py:258
  29.4 0.0 collective-permute-done.5.refs_3_
  29.4 0.0 collective-permute-done.6.refs_4_
  29.5 0.0 collective-permute-done.7.refs_5_
  29.5 0.9 %shard_map.72 = (f32[2,2,16,1024]{3,2,1,0:T(8,128)S(1)}, f32[2,2,16,1024]{3,2,1,0:T(8,128)S(1)}, f32[2,2,16,1024]{3,2,1,0:T(8,128)S(1)}, f32[2,2,16,1024]{3,2,1,0:T(8,128)S(1)}, f32[2,8,16,1024]{3,2,1,0:T(8,128)S(1)}) custom-call(s32[2,24]{1,0:T(2,128)S(1)} %get-tuple-element.21.refs_5_.refs_0_, f32[2,8,8,128]{3,2,1,0:T(8,128)S(1)} %shard_map.71.refs_1_, ...), custom_call_target="tpu_custom_call" | custom-call | tf_op jit(solution)/shard_map/pallas_call | solution.py:267
  30.4 2.5 %collective-permute-start.8 = (f32[2,2,16,1024]{3,2,1,0:T(8,128)S(1)}, f32[2,2,16,1024]{3,2,1,0:T(8,128)S(1)}, u32[]{:S(2)}, u32[]{:S(2)}) collective-permute-start(f32[2,2,16,1024]{3,2,1,0:T(8,128)S(1)} %get-tuple-element.30), channel_id=1, source_target_pairs={{0,24},{4,28},{8,16},{12,20},{16,8},{20,12},{24,0},{28,4},{1,25},{... | collective-permute-start | bytes 786440 | tf_op jit(solution)/shard_map/ppermute | solution.py:60
  32.9 0.5 %collective-permute-start.9 = (f32[2,2,16,1024]{3,2,1,0:T(8,128)S(1)}, f32[2,2,16,1024]{3,2,1,0:T(8,128)S(1)}, u32[]{:S(2)}, u32[]{:S(2)}) collective-permute-start(f32[2,2,16,1024]{3,2,1,0:T(8,128)S(1)} %get-tuple-element.31), channel_id=1, source_target_pairs={{0,8},{4,20},{8,0},{12,28},{16,24},{20,4},{24,16},{28,12},{1,9},{5... | collective-permute-start | bytes 786440 | tf_op jit(solution)/shard_map/ppermute | solution.py:60
  33.5 0.5 %collective-permute-start.10 = (f32[2,2,16,1024]{3,2,1,0:T(8,128)S(1)}, f32[2,2,16,1024]{3,2,1,0:T(8,128)S(1)}, u32[]{:S(2)}, u32[]{:S(2)}) collective-permute-start(f32[2,2,16,1024]{3,2,1,0:T(8,128)S(1)} %get-tuple-element.32), channel_id=1, source_target_pairs={{0,16},{4,12},{8,24},{12,4},{16,0},{20,28},{24,8},{28,20},{1,17},{... | collective-permute-start | bytes 786440 | tf_op jit(solution)/shard_map/ppermute | solution.py:60
  34.0 0.0 copy-done
  34.0 3.1 %shard_map.73 = (f32[32,16,1024]{2,1,0:T(8,128)}, f32[32,16,1024]{2,1,0:T(8,128)}, f32[8,128]{1,0:T(8,128)S(1)}) custom-call(s32[32]{0:T(128)S(1)} %get-tuple-element.34.module_ref, f32[2,8,16,1024]{3,2,1,0:T(8,128)S(1)} %get-tuple-element.35.grad_ref, f32[32,16,1024]{2,1,0:T(8,128)S(1)} %bitcast_subtract_fusion.refs_2_.decayed_ref, f32[32,16,1024]{2,1,0:T(8,128)S(1)} %bitcast.13), custom_call_target="tpu_custom_call" | custom-call | tf_op jit(solution)/shard_map/pallas_call | solution.py:276
  37.0 1.8 %collective-permute-done.8.refs_1_ = f32[2,2,16,1024]{3,2,1,0:T(8,128)S(1)} collective-permute-done((f32[2,2,16,1024]{3,2,1,0:T(8,128)S(1)}, f32[2,2,16,1024]{3,2,1,0:T(8,128)S(1)}, u32[]{:S(2)}, u32[]{:S(2)}) %collective-permute-start.8) | collective-permute-done | bytes 262176 | tf_op jit(solution)/shard_map/ppermute | solution.py:60
  38.9 2.8 %collective-permute-done.9.refs_2_ = f32[2,2,16,1024]{3,2,1,0:T(8,128)S(1)} collective-permute-done((f32[2,2,16,1024]{3,2,1,0:T(8,128)S(1)}, f32[2,2,16,1024]{3,2,1,0:T(8,128)S(1)}, u32[]{:S(2)}, u32[]{:S(2)}) %collective-permute-start.9) | collective-permute-done | bytes 262176 | tf_op jit(solution)/shard_map/ppermute | solution.py:60
  41.7 0.0 collective-permute-done.10.refs_3_
  41.8 0.1 collective-permute-start.11
  41.8 0.9 %shard_map.75.held_ref = f32[2,4,2,16,1024]{4,3,2,1,0:T(8,128)} custom-call(s32[1]{0:T(128)} %bitcast.here_ref.refs_0_, f32[2,2,16,1024]{3,2,1,0:T(8,128)S(1)} %collective-permute-done.8.refs_1_, f32[2,2,16,1024]{3,2,1,0:T(8,128)S(1)} %collective-permute-done.9.refs_2_, f32[2,2,16,1024]{3,2,1,0:T(8,128)S(1)} %collective-permute-done.10.refs_3_, ...), custom_call_target="tpu_custom_call" | custom-call | tf_op jit(solution)/shard_map/pallas_call | solution.py:288
  42.7 1.0 %collective-permute-done.11.back_ref = f32[2,4,16,1024]{3,2,1,0:T(8,128)S(1)} collective-permute-done((f32[2,4,16,1024]{3,2,1,0:T(8,128)S(1)}, f32[2,4,16,1024]{3,2,1,0:T(8,128)S(1)}, u32[]{:S(2)}, u32[]{:S(2)}) %collective-permute-start.11) | collective-permute-done | bytes 524320 | tf_op jit(solution)/shard_map/ppermute | solution.py:286
  43.7 0.8 %shard_map.76 = f32[2,4,2,16,1024]{4,3,2,1,0:T(8,128)} custom-call(s32[1]{0:T(128)} %bitcast.here_ref.refs_0_, f32[2,4,16,1024]{3,2,1,0:T(8,128)S(1)} %collective-permute-done.11.back_ref, f32[2,4,2,16,1024]{4,3,2,1,0:T(8,128)} %shard_map.75.held_ref), custom_call_target="tpu_custom_call", output_to_operand_aliasing={{}: (2, {})} | custom-call | tf_op jit(solution)/shard_map/pallas_call | solution.py:295
  (2 shorter events, 0.0 us)
Async XLA Ops:
  0.6 1.2 %copy-start.1 = (f32[1,2,128,1024]{3,2,1,0:T(8,128)S(1)}, f32[1,2,128,1024]{3,2,1,0:T(8,128)}, u32[]{:S(2)}) copy-start(f32[1,2,128,1024]{3,2,1,0:T(8,128)} %param.4) | copy-start | bytes 3145732
  2.0 2.7 %collective-permute-start.1 = (f32[2,4,16,1024]{3,2,1,0:T(8,128)S(1)}, f32[2,4,16,1024]{3,2,1,0:T(8,128)S(1)}, u32[]{:S(2)}, u32[]{:S(2)}) collective-permute-start(f32[2,4,16,1024]{3,2,1,0:T(8,128)S(1)} %get-tuple-element.24), channel_id=1, source_target_pairs={{0,4},{4,0},{8,12},{12,8},{16,20},{20,16},{24,28},{28,24},{1,5},{5... | collective-permute-start | bytes 1572872 | tf_op jit(solution)/shard_map/ppermute | solution.py:242
  2.5 2.2 %collective-permute-start = (f32[8,128]{1,0:T(8,128)S(1)}, f32[8,128]{1,0:T(8,128)S(1)}, u32[]{:S(2)}, u32[]{:S(2)}) collective-permute-start(f32[8,128]{1,0:T(8,128)S(1)} %get-tuple-element.22.refs_1_), channel_id=1, source_target_pairs={{0,4},{4,0},{8,12},{12,8},{16,20},{20,16},{24,28},{28,24},{1,5},{5... | collective-permute-start | bytes 12296 | tf_op jit(solution)/shard_map/ppermute | solution.py:241
  5.5 7.9 %collective-permute-start.2 = (f32[8,128]{1,0:T(8,128)S(1)}, f32[8,128]{1,0:T(8,128)S(1)}, u32[]{:S(2)}, u32[]{:S(2)}) collective-permute-start(f32[8,128]{1,0:T(8,128)S(1)} %get-tuple-element.25.refs_3_), channel_id=1, source_target_pairs={{0,24},{4,28},{8,16},{12,20},{16,8},{20,12},{24,0},{28,4},{1,25},{... | collective-permute-start | bytes 12296 | tf_op jit(solution)/shard_map/ppermute | solution.py:60
  9.4 6.7 %collective-permute-start.3 = (f32[8,128]{1,0:T(8,128)S(1)}, f32[8,128]{1,0:T(8,128)S(1)}, u32[]{:S(2)}, u32[]{:S(2)}) collective-permute-start(f32[8,128]{1,0:T(8,128)S(1)} %get-tuple-element.25.refs_3_), channel_id=1, source_target_pairs={{0,8},{4,20},{8,0},{12,28},{16,24},{20,4},{24,16},{28,12},{1,9},{5... | collective-permute-start | bytes 12296 | tf_op jit(solution)/shard_map/ppermute | solution.py:60
  10.0 6.2 %collective-permute-start.4 = (f32[8,128]{1,0:T(8,128)S(1)}, f32[8,128]{1,0:T(8,128)S(1)}, u32[]{:S(2)}, u32[]{:S(2)}) collective-permute-start(f32[8,128]{1,0:T(8,128)S(1)} %get-tuple-element.25.refs_3_), channel_id=1, source_target_pairs={{0,16},{4,12},{8,24},{12,4},{16,0},{20,28},{24,8},{28,20},{1,17},{... | collective-permute-start | bytes 12296 | tf_op jit(solution)/shard_map/ppermute | solution.py:60
  10.0 19.4 %collective-permute-start.5 = (f32[2,2,16,1024]{3,2,1,0:T(8,128)}, f32[2,2,16,1024]{3,2,1,0:T(8,128)S(1)}, u32[]{:S(2)}, u32[]{:S(2)}) collective-permute-start(f32[2,2,16,1024]{3,2,1,0:T(8,128)} %get-tuple-element.26), channel_id=1, source_target_pairs={{0,24},{4,28},{8,16},{12,20},{16,8},{20,12},{24,0},{28,4},{1,25},{... | collective-permute-start | bytes 786440 | tf_op jit(solution)/shard_map/ppermute | solution.py:60
  12.9 16.5 %collective-permute-start.6 = (f32[2,2,16,1024]{3,2,1,0:T(8,128)}, f32[2,2,16,1024]{3,2,1,0:T(8,128)S(1)}, u32[]{:S(2)}, u32[]{:S(2)}) collective-permute-start(f32[2,2,16,1024]{3,2,1,0:T(8,128)} %get-tuple-element.27), channel_id=1, source_target_pairs={{0,8},{4,20},{8,0},{12,28},{16,24},{20,4},{24,16},{28,12},{1,9},{5... | collective-permute-start | bytes 786440 | tf_op jit(solution)/shard_map/ppermute | solution.py:60
  13.5 16.0 %collective-permute-start.7 = (f32[2,2,16,1024]{3,2,1,0:T(8,128)S(1)}, f32[2,2,16,1024]{3,2,1,0:T(8,128)S(1)}, u32[]{:S(2)}, u32[]{:S(2)}) collective-permute-start(f32[2,2,16,1024]{3,2,1,0:T(8,128)S(1)} %get-tuple-element.28), channel_id=1, source_target_pairs={{0,16},{4,12},{8,24},{12,4},{16,0},{20,28},{24,8},{28,20},{1,17},{... | collective-permute-start | bytes 786440 | tf_op jit(solution)/shard_map/ppermute | solution.py:60
  28.6 5.3 %copy-start = (f32[32,1,16,1024]{3,2,1,0:T(8,128)S(1)}, f32[32,1,16,1024]{3,2,1,0:T(8,128)}, u32[]{:S(2)}) copy-start(f32[32,1,16,1024]{3,2,1,0:T(8,128)} %param.7) | copy-start | bytes 6291460
  30.4 8.5 %collective-permute-start.8 = (f32[2,2,16,1024]{3,2,1,0:T(8,128)S(1)}, f32[2,2,16,1024]{3,2,1,0:T(8,128)S(1)}, u32[]{:S(2)}, u32[]{:S(2)}) collective-permute-start(f32[2,2,16,1024]{3,2,1,0:T(8,128)S(1)} %get-tuple-element.30), channel_id=1, source_target_pairs={{0,24},{4,28},{8,16},{12,20},{16,8},{20,12},{24,0},{28,4},{1,25},{... | collective-permute-start | bytes 786440 | tf_op jit(solution)/shard_map/ppermute | solution.py:60
  32.9 8.8 %collective-permute-start.9 = (f32[2,2,16,1024]{3,2,1,0:T(8,128)S(1)}, f32[2,2,16,1024]{3,2,1,0:T(8,128)S(1)}, u32[]{:S(2)}, u32[]{:S(2)}) collective-permute-start(f32[2,2,16,1024]{3,2,1,0:T(8,128)S(1)} %get-tuple-element.31), channel_id=1, source_target_pairs={{0,8},{4,20},{8,0},{12,28},{16,24},{20,4},{24,16},{28,12},{1,9},{5... | collective-permute-start | bytes 786440 | tf_op jit(solution)/shard_map/ppermute | solution.py:60
  33.5 8.3 %collective-permute-start.10 = (f32[2,2,16,1024]{3,2,1,0:T(8,128)S(1)}, f32[2,2,16,1024]{3,2,1,0:T(8,128)S(1)}, u32[]{:S(2)}, u32[]{:S(2)}) collective-permute-start(f32[2,2,16,1024]{3,2,1,0:T(8,128)S(1)} %get-tuple-element.32), channel_id=1, source_target_pairs={{0,16},{4,12},{8,24},{12,4},{16,0},{20,28},{24,8},{28,20},{1,17},{... | collective-permute-start | bytes 786440 | tf_op jit(solution)/shard_map/ppermute | solution.py:60
  41.8 2.0 %collective-permute-start.11 = (f32[2,4,16,1024]{3,2,1,0:T(8,128)S(1)}, f32[2,4,16,1024]{3,2,1,0:T(8,128)S(1)}, u32[]{:S(2)}, u32[]{:S(2)}) collective-permute-start(f32[2,4,16,1024]{3,2,1,0:T(8,128)S(1)} %shard_map.74), channel_id=1, source_target_pairs={{0,4},{4,0},{8,12},{12,8},{16,20},{20,16},{24,28},{28,24},{1,5},{5... | collective-permute-start | bytes 1572872 | tf_op jit(solution)/shard_map/ppermute | solution.py:286
where the time goes:
time: 44.8 us; the launch traced here: 44.6 us
  blocking collectives  12.4 us (28%)
  starting transfers between devices  12.1 us (27%)
  Pallas kernels  8.86 us (20%)
  waiting for transfers between devices  5.74 us (13%)
  other arithmetic  2.66 us (6%)
  local copies, waits for them, and re-layouts  1.97 us (4%)
  between operations  0.77 us (2%)
    psum x1, blocking collectives, local(): squares = lax.psum(squares, 'shard')  12.4 us
    ppermute x9, starting transfers between devices, move(): lax.ppermute(array, 'path', [(i, target(i, k, size)) for i in range(size)])  11.5 us
    ppermute x9, waiting for transfers between devices, move(): lax.ppermute(array, 'path', [(i, target(i, k, size)) for i in range(size)])  4.71 us
    pallas_call x1, Pallas kernels, local(): call(state_kernel, [shape(*state_in.shape)] * 2 + [shape(8, 128)], [smem,...  3.06 us
    sub x1, other arithmetic, local(): decayed = state_in - moment_coef * moment_in  2.66 us
    unnamed x5, local copies, waits for them, and re-layouts  1.97 us
    pallas_call x1, Pallas kernels, local(): call(plan_kernel, [jax.ShapeDtypeStruct((LEVELS, 3 * size), jnp.int32), j...  1.32 us
    ppermute x1, waiting for transfers between devices, local(): back = lax.ppermute(back, 'path', swap)  1.03 us
  transfers between devices with their start and end apart: 12, of which 3 were waited for; matrix products, arithmetic and copies ran while one was open for 8% of the time, Pallas kernels for 14%

commit v1 on v0

--- a/solution.py
+++ b/solution.py
@@ -86,11 +86,10 @@
         pl.when(here_ref[0] & 1 == core)(lambda core=core: pack(core))
 
 
-def merge_kernel(size, here_ref, square_ref, other_ref, keep_ref, gift_ref, plan_ref, square_out, *outs):
-    del plan_ref
+def merge_kernel(size, here_ref, keep_ref, gift_ref, token_ref, *outs):
+    del token_ref
     here = here_ref[0]
     core = here & 1
-    square_out[...] = square_ref[...] + other_ref[...]
     for k, out in zip(order_of(size), outs):
         chip = target(here, k, size) // 2
         for level in range(LEVELS):
@@ -105,50 +104,41 @@
     refs[-1][...] = total
 
 
-def factor_kernel(entries, here_ref, ids_ref, *refs):
-    squares, (out_ref, rescale_ref) = refs[:-2], refs[-2:]
-    size = ids_ref.shape[0]
-    total = squares[0][...]
-    for square_ref in squares[1:]:
-        total = total + square_ref[...]
-    total = jnp.sum(total, axis=1, keepdims=True)
-    rescale_ref[...] = jnp.broadcast_to(1.0 / jnp.sqrt(total / entries + 1e-06), rescale_ref.shape)
-    sources = [(origin(here_ref[0], k, size) // 2) * 2 + half for k in order_of(size) for half in range(2)]
-    for i, path in enumerate(sources):
-        rescale = jnp.broadcast_to(rescale_ref[pl.ds(path, 1), :], (8, 128))
-        for level in range(LEVELS):
-            sharers = jnp.int32(0)
-            for other in range(size):
-                sharers = sharers + jnp.where(ids_ref[other, level] == ids_ref[path, level], 1, 0)
-            out_ref[level, i] = rescale / jnp.full((8, 128), sharers, jnp.int32).astype(jnp.float32)
-
-
-def plan_kernel(here_ref, ids_ref, plan_ref, module_ref):
-    size = ids_ref.shape[0]
+def plan_kernel(here_ref, ids_ref, plan_ref, module_ref, token_ref):
+    size = ids_ref.shape[1]
     order = order_of(size)
     here = here_ref[0]
+    token_ref[...] = jnp.zeros_like(token_ref)
+    paths = [(origin(here, k, size) // 2) * 2 + half for k in order for half in range(2)]
+    targets = [(target(here, k, size) // 2) * 2 + half for k in order for half in range(2)]
     for level in range(LEVELS):
         first = level * LEVEL_MODULES
         for module in range(LEVEL_MODULES):
             module_ref[first + module] = -1
-        sources = [ids_ref[(origin(here, k, size) // 2) * 2 + half, level] + first for k in order for half in range(2)]
+        sources = [ids_ref[level, path] + first for path in paths]
         for i in reversed(range(size)):
             module_ref[sources[i]] = i
         for i in range(size):
             plan_ref[level, i] = module_ref[sources[i]]
-        for j, k in enumerate(order):
-            for half in range(2):
-                module = ids_ref[(target(here, k, size) // 2) * 2 + half, level] + first
-                plan_ref[level, size + 2 * j + half] = module
-                plan_ref[level, 2 * size + 2 * j + half] = module_ref[module]
-
-
-def outgoing_kernel(rounds, plan_ref, factor_ref, decayed_ref, *refs):
-    received, outs, grad_ref = refs[:rounds], refs[rounds:-1], refs[-1]
+            sharers = jnp.int32(0)
+            for other in range(size):
+                sharers = sharers + jnp.where(sources[other] == sources[i], 1, 0)
+            plan_ref[level, size + i] = sharers
+            plan_ref[level, 2 * size + i] = paths[i]
+            module = ids_ref[level, targets[i]] + first
+            plan_ref[level, 3 * size + i] = module
+            plan_ref[level, 4 * size + i] = module_ref[module]
+
+
+def outgoing_kernel(rounds, entries, plan_ref, square_ref, decayed_ref, *refs):
+    received, outs, (grad_ref, rescale_ref) = refs[:rounds], refs[rounds:-2], refs[-2:]
     size = 2 * rounds
+    total = jnp.sum(square_ref[...], axis=1, keepdims=True)
+    rescale_ref[...] = jnp.broadcast_to(1.0 / jnp.sqrt(total / entries + 1e-06), rescale_ref.shape)
     for level in range(LEVELS):
         for i in range(size):
-            factor = factor_ref[level, i]
+            rescale = jnp.broadcast_to(rescale_ref[pl.ds(plan_ref[level, 2 * size + i], 1), :], (8, 128))
+            factor = rescale / jnp.full((8, 128), plan_ref[level, size + i], jnp.int32).astype(jnp.float32)
             for spot in tiles_of(*grad_ref.shape[2:]):
                 grad_ref[(level, i, *spot)] = received[i // 2][(i % 2, level, *spot)] * factor
         for i in range(1, size):
@@ -159,8 +149,8 @@
                 grad_ref[level, leader] += grad_ref[level, i]
 
         for i in range(size):
-            decayed = decayed_ref[plan_ref[level, size + i]]
-            outs[i // 2][i % 2, level] = decayed - grad_coef * grad_ref[level, plan_ref[level, 2 * size + i]]
+            decayed = decayed_ref[plan_ref[level, 3 * size + i]]
+            outs[i // 2][i % 2, level] = decayed - grad_coef * grad_ref[level, plan_ref[level, 4 * size + i]]
 
 
 def state_kernel(module_ref, grad_ref, decayed_ref, momentum_ref, new_params_ref, new_momentum_ref, token_ref):
@@ -238,38 +228,36 @@
     squares, keep, give = call(pack_kernel, [squares_shape, by_chip, by_chip], [smem, vmem], [vmem] * 3)(
         here, split_slab
     )
+    gift = lax.ppermute(give, "path", swap)
+    squares = call(sum_kernel, squares_shape, [vmem] * rounds, vmem)(*[move(squares, k, size) for k in order])
+    plan, leaders, planned = call(
+        plan_kernel,
+        [
+            jax.ShapeDtypeStruct((LEVELS, 5 * size), jnp.int32),
+            jax.ShapeDtypeStruct((module_count,), jnp.int32),
+            shape(8, 128),
+        ],
+        [smem, smem],
+        [smem, smem, vmem],
+    )(here, assign.T)
+    messages = call(
+        lambda *refs: merge_kernel(size, *refs),
+        [message] * rounds,
+        [smem, vmem, vmem, anywhere],
+        [vmem] * rounds,
+    )(here, keep, gift, planned)
+    received = [move(messages[j], k, size) for j, k in enumerate(order)]
     other = lax.ppermute(squares, "path", swap)
-    gift = lax.ppermute(give, "path", swap)
-    plan, leaders = call(
-        plan_kernel,
-        [jax.ShapeDtypeStruct((LEVELS, 3 * size), jnp.int32), jax.ShapeDtypeStruct((module_count,), jnp.int32)],
-        [smem, smem],
-        [smem] * 2,
-    )(here, assign)
-    squares, *messages = call(
-        lambda *refs: merge_kernel(size, *refs),
-        [squares_shape] + [message] * rounds,
-        [smem, vmem, vmem, vmem, vmem, anywhere],
-        [vmem] * (1 + rounds),
-    )(here, squares, other, keep, gift, plan)
-    received = [move(messages[j], k, size) for j, k in enumerate(order)]
-    squares = call(sum_kernel, squares_shape, [vmem] * rounds, vmem)(*[move(squares, k, size) for k in order])
-    squares = lax.psum(squares, "shard")
-    factors = call(
-        lambda *refs: factor_kernel(entries, *refs),
-        shape(LEVELS, size, 8, 128),
-        [smem, smem, vmem],
-        vmem,
-        scratch_shapes=[pltpu.VMEM(squares_shape.shape, jnp.float32)],
-    )(here, assign, squares)
+    squares = lax.psum(call(sum_kernel, squares_shape, [vmem] * 2, vmem)(squares, other), "shard")
     decayed = state_in - moment_coef * moment_in
 
     *outgoing, grad = call(
-        lambda *refs: outgoing_kernel(rounds, *refs),
+        lambda *refs: outgoing_kernel(rounds, entries, *refs),
         [message] * rounds + [shape(LEVELS, size, own_rows, width)],
         [smem] + [vmem] * (2 + rounds),
         [vmem] * (rounds + 1),
-    )(plan, factors, decayed, *received)
+        scratch_shapes=[pltpu.VMEM(squares_shape.shape, jnp.float32)],
+    )(plan, squares, decayed, *received)
     returned = [move(outgoing[j], k, size) for j, k in enumerate(order)]
     block = LEVEL_MODULES // 2
     state_block = pl.BlockSpec((block, own_rows, width), lambda i: (i, 0, 0))

time: 44.8 us -> 45.5 us (1.016)
  waiting for transfers between devices: 5.74 us -> 8.48 us
  Pallas kernels: 8.86 us -> 8.21 us
  other arithmetic: 2.66 us -> 2.03 us
    ppermute x9, waiting for transfers between devices: 4.71 us -> 7.45 us  [move(): lax.ppermute(array, 'path', [(i, target(i, k, size)) for i in range(size)])]
    pallas_call x4, Pallas kernels: 3.93 us -> 3.28 us  [the longest x1 1.4 us: local(): call(plan_kernel, [jax.ShapeDtypeStruct((LEVELS, 5 * size), jnp.int32), j...]
    sub x1, other arithmetic: 2.66 us -> 2.03 us  [local(): decayed = state_in - moment_coef * moment_in]
    unnamed x5 -> x8, local copies, waits for them, and re-layouts: 1.97 us -> 2.05 us
  transfers between devices with their start and end apart: 12 -> 12, of which waited for: 3 -> 6; matrix products, arithmetic and copies ran while one was open for 8% -> 4% of each run, Pallas kernels for 14% -> 14%
where the time goes in v1:
time: 45.5 us; the launch traced here: 45.3 us
  blocking collectives  12 us (26%)
  starting transfers between devices  11.8 us (26%)
  waiting for transfers between devices  8.48 us (19%)
  Pallas kernels  8.21 us (18%)
  local copies, waits for them, and re-layouts  2.05 us (5%)
  other arithmetic  2.03 us (4%)
  between operations  0.76 us (2%)
    psum x1, blocking collectives, local(): lax.psum(call(sum_kernel, squares_shape, [vmem] * 2, vmem)(squares, other...  12 us
    ppermute x9, starting transfers between devices, move(): lax.ppermute(array, 'path', [(i, target(i, k, size)) for i in range(size)])  11.2 us
    ppermute x9, waiting for transfers between devices, move(): lax.ppermute(array, 'path', [(i, target(i, k, size)) for i in range(size)])  7.45 us
    pallas_call x1, Pallas kernels, local(): call(state_kernel, [shape(*state_in.shape)] * 2 + [shape(8, 128)], [smem,...  3.06 us
    unnamed x8, local copies, waits for them, and re-layouts  2.05 us
    sub x1, other arithmetic, local(): decayed = state_in - moment_coef * moment_in  2.03 us
    pallas_call x1, Pallas kernels, local(): call(plan_kernel, [jax.ShapeDtypeStruct((LEVELS, 5 * size), jnp.int32), j...  1.4 us
    ppermute x1, waiting for transfers between devices, local(): back = lax.ppermute(back, 'path', swap)  1.03 us
  transfers between devices with their start and end apart: 12, of which 6 were waited for; matrix products, arithmetic and copies ran while one was open for 4% of the time, Pallas kernels for 14%

profile of v1, /device:TPU:0, one launch (start us, length us, event | category | flops | bytes accessed | tf_op | source)
XLA Modules:
  0.0 45.3 jit_solution(10565857204421586775)
XLA Ops:
  0.6 0.0 copy-start
  0.6 0.0 copy-start.2
  0.7 1.4 %copy-done.2 = f32[1,2,128,1024]{3,2,1,0:T(8,128)S(1)} copy-done((f32[1,2,128,1024]{3,2,1,0:T(8,128)S(1)}, f32[1,2,128,1024]{3,2,1,0:T(8,128)}, u32[]{:S(2)}) %copy-start.2) | copy-done | bytes 1048600
  2.0 0.1 shard_map.68
  2.1 0.5 %collective-permute-start.4 = (f32[2,4,16,1024]{3,2,1,0:T(8,128)S(1)}, f32[2,4,16,1024]{3,2,1,0:T(8,128)S(1)}, u32[]{:S(2)}, u32[]{:S(2)}) collective-permute-start(f32[2,4,16,1024]{3,2,1,0:T(8,128)S(1)} %get-tuple-element.24), channel_id=1, source_target_pairs={{0,4},{4,0},{8,12},{12,8},{16,20},{20,16},{24,28},{28,24},{1,5},{5... | collective-permute-start | bytes 1572872 | tf_op jit(solution)/shard_map/ppermute | solution.py:231
  2.6 3.5 %collective-permute-start = (f32[8,128]{1,0:T(8,128)S(1)}, f32[8,128]{1,0:T(8,128)S(1)}, u32[]{:S(2)}, u32[]{:S(2)}) collective-permute-start(f32[8,128]{1,0:T(8,128)S(1)} %get-tuple-element.22.refs_3_), channel_id=1, source_target_pairs={{0,24},{4,28},{8,16},{12,20},{16,8},{20,12},{24,0},{28,4},{1,25},{... | collective-permute-start | bytes 12296 | tf_op jit(solution)/shard_map/ppermute | solution.py:60
  6.2 0.5 %collective-permute-start.1 = (f32[8,128]{1,0:T(8,128)S(1)}, f32[8,128]{1,0:T(8,128)S(1)}, u32[]{:S(2)}, u32[]{:S(2)}) collective-permute-start(f32[8,128]{1,0:T(8,128)S(1)} %get-tuple-element.22.refs_3_), channel_id=1, source_target_pairs={{0,8},{4,20},{8,0},{12,28},{16,24},{20,4},{24,16},{28,12},{1,9},{5... | collective-permute-start | bytes 12296 | tf_op jit(solution)/shard_map/ppermute | solution.py:60
  6.7 0.1 collective-permute-start.2
  6.8 0.0 copy-start.3
  6.8 0.7 %copy-done.3 = s32[8,2]{0,1:T(2,128)S(1)} copy-done((s32[8,2]{0,1:T(2,128)S(1)}, s32[8,2]{0,1:T(2,128)}, u32[]{:S(2)}) %copy-start.3) | copy-done | bytes 88
  7.5 1.4 %shard_map.67 = (s32[2,40]{1,0:T(2,128)S(1)}, s32[32]{0:T(128)S(1)}, f32[8,128]{1,0:T(8,128)S(1)}) custom-call(s32[1]{0:T(128)} %bitcast.here_ref.refs_0_, s32[2,8]{1,0:T(2,128)S(1)} %bitcast.16), custom_call_target="tpu_custom_call" | custom-call | tf_op jit(solution)/shard_map/pallas_call | solution.py:233
  8.9 0.0 collective-permute-done.refs_0_
  8.9 0.9 %collective-permute-done.1.refs_1_ = f32[8,128]{1,0:T(8,128)S(1)} collective-permute-done((f32[8,128]{1,0:T(8,128)S(1)}, f32[8,128]{1,0:T(8,128)S(1)}, u32[]{:S(2)}, u32[]{:S(2)}) %collective-permute-start.1) | collective-permute-done | bytes 4128 | tf_op jit(solution)/shard_map/ppermute | solution.py:60
  9.8 0.5 %collective-permute-done.2.refs_2_ = f32[8,128]{1,0:T(8,128)S(1)} collective-permute-done((f32[8,128]{1,0:T(8,128)S(1)}, f32[8,128]{1,0:T(8,128)S(1)}, u32[]{:S(2)}, u32[]{:S(2)}) %collective-permute-start.2) | collective-permute-done | bytes 4128 | tf_op jit(solution)/shard_map/ppermute | solution.py:60
  10.3 0.0 collective-permute-start.3
  10.3 0.0 collective-permute-done.4.refs_2_
  10.3 0.9 %shard_map.71 = (f32[2,2,16,1024]{3,2,1,0:T(8,128)}, f32[2,2,16,1024]{3,2,1,0:T(8,128)}, f32[2,2,16,1024]{3,2,1,0:T(8,128)S(1)}, f32[2,2,16,1024]{3,2,1,0:T(8,128)S(1)}) custom-call(s32[1]{0:T(128)} %bitcast.here_ref.refs_0_, f32[2,4,16,1024]{3,2,1,0:T(8,128)S(1)} %get-tuple-element.23.refs_1_, f32[2,4,16,1024]{3,2,1,0:T(8,128)S(1)} %collective-permute-done.4.refs_2_, ...), custom_call_target="tpu_custom_call" | custom-call | tf_op jit(solution)/shard_map/pallas_call | solution.py:243
  11.2 1.6 %collective-permute-start.5 = (f32[2,2,16,1024]{3,2,1,0:T(8,128)}, f32[2,2,16,1024]{3,2,1,0:T(8,128)S(1)}, u32[]{:S(2)}, u32[]{:S(2)}) collective-permute-start(f32[2,2,16,1024]{3,2,1,0:T(8,128)} %get-tuple-element.26), channel_id=1, source_target_pairs={{0,24},{4,28},{8,16},{12,20},{16,8},{20,12},{24,0},{28,4},{1,25},{... | collective-permute-start | bytes 786440 | tf_op jit(solution)/shard_map/ppermute | solution.py:60
  12.8 0.5 %collective-permute-start.6 = (f32[2,2,16,1024]{3,2,1,0:T(8,128)}, f32[2,2,16,1024]{3,2,1,0:T(8,128)S(1)}, u32[]{:S(2)}, u32[]{:S(2)}) collective-permute-start(f32[2,2,16,1024]{3,2,1,0:T(8,128)} %get-tuple-element.27), channel_id=1, source_target_pairs={{0,8},{4,20},{8,0},{12,28},{16,24},{20,4},{24,16},{28,12},{1,9},{5... | collective-permute-start | bytes 786440 | tf_op jit(solution)/shard_map/ppermute | solution.py:60
  13.3 1.4 %collective-permute-start.7 = (f32[2,2,16,1024]{3,2,1,0:T(8,128)S(1)}, f32[2,2,16,1024]{3,2,1,0:T(8,128)S(1)}, u32[]{:S(2)}, u32[]{:S(2)}) collective-permute-start(f32[2,2,16,1024]{3,2,1,0:T(8,128)S(1)} %get-tuple-element.28), channel_id=1, source_target_pairs={{0,16},{4,12},{8,24},{12,4},{16,0},{20,28},{24,8},{28,20},{1,17},{... | collective-permute-start | bytes 786440 | tf_op jit(solution)/shard_map/ppermute | solution.py:60
  14.7 0.0 copy-done
  14.7 2.0 %bitcast_subtract_fusion.refs_2_.decayed_ref = f32[32,16,1024]{2,1,0:T(8,128)S(1)} fusion(f32[32,1,16,1024]{3,2,1,0:T(8,128)} %param.6, f32[32,1,16,1024]{3,2,1,0:T(8,128)S(1)} %copy-done), kind=kLoop, calls=%fused_computation | loop fusion | flops 1048576 | bytes 6291456 | tf_op jit(solution)/shard_map/sub | solution.py:252
  16.7 0.0 collective-permute-done.3.refs_1_
  16.8 12.0 %psum.7.refs_1_ = f32[8,128]{1,0:T(8,128)S(1)} all-reduce(f32[8,128]{1,0:T(8,128)S(1)} %shard_map.70), channel_id=1, replica_groups=mesh['path'=8,'shard'=4] {'shard'}, use_global_device_ids=true, to_apply=%region_0.0 | all-reduce | flops 1024 | bytes 8192 | tf_op jit(solution)/shard_map/psum | solution.py:251
  28.8 0.0 copy-start.1
  28.8 0.0 collective-permute-done.5.refs_3_
  28.8 0.0 collective-permute-done.6.refs_4_
  28.8 0.0 collective-permute-done.7.refs_5_
  28.8 1.0 %shard_map.72 = (f32[2,2,16,1024]{3,2,1,0:T(8,128)S(1)}, f32[2,2,16,1024]{3,2,1,0:T(8,128)S(1)}, f32[2,2,16,1024]{3,2,1,0:T(8,128)S(1)}, f32[2,2,16,1024]{3,2,1,0:T(8,128)S(1)}, f32[2,8,16,1024]{3,2,1,0:T(8,128)S(1)}) custom-call(s32[2,40]{1,0:T(2,128)S(1)} %get-tuple-element.21.refs_0_, f32[8,128]{1,0:T(8,128)S(1)} %psum.7.refs_1_, ...), custom_call_target="tpu_custom_call" | custom-call | tf_op jit(solution)/shard_map/pallas_call | solution.py:254
  29.8 1.6 %collective-permute-start.8 = (f32[2,2,16,1024]{3,2,1,0:T(8,128)S(1)}, f32[2,2,16,1024]{3,2,1,0:T(8,128)S(1)}, u32[]{:S(2)}, u32[]{:S(2)}) collective-permute-start(f32[2,2,16,1024]{3,2,1,0:T(8,128)S(1)} %get-tuple-element.30), channel_id=1, source_target_pairs={{0,24},{4,28},{8,16},{12,20},{16,8},{20,12},{24,0},{28,4},{1,25},{... | collective-permute-start | bytes 786440 | tf_op jit(solution)/shard_map/ppermute | solution.py:60
  31.4 0.5 %collective-permute-start.9 = (f32[2,2,16,1024]{3,2,1,0:T(8,128)S(1)}, f32[2,2,16,1024]{3,2,1,0:T(8,128)S(1)}, u32[]{:S(2)}, u32[]{:S(2)}) collective-permute-start(f32[2,2,16,1024]{3,2,1,0:T(8,128)S(1)} %get-tuple-element.31), channel_id=1, source_target_pairs={{0,8},{4,20},{8,0},{12,28},{16,24},{20,4},{24,16},{28,12},{1,9},{5... | collective-permute-start | bytes 786440 | tf_op jit(solution)/shard_map/ppermute | solution.py:60
  32.0 1.4 %collective-permute-start.10 = (f32[2,2,16,1024]{3,2,1,0:T(8,128)S(1)}, f32[2,2,16,1024]{3,2,1,0:T(8,128)S(1)}, u32[]{:S(2)}, u32[]{:S(2)}) collective-permute-start(f32[2,2,16,1024]{3,2,1,0:T(8,128)S(1)} %get-tuple-element.32), channel_id=1, source_target_pairs={{0,16},{4,12},{8,24},{12,4},{16,0},{20,28},{24,8},{28,20},{1,17},{... | collective-permute-start | bytes 786440 | tf_op jit(solution)/shard_map/ppermute | solution.py:60
  33.4 0.0 copy-done.1
  33.4 3.1 %shard_map.73 = (f32[32,16,1024]{2,1,0:T(8,128)}, f32[32,16,1024]{2,1,0:T(8,128)}, f32[8,128]{1,0:T(8,128)S(1)}) custom-call(s32[32]{0:T(128)S(1)} %get-tuple-element.34.module_ref, f32[2,8,16,1024]{3,2,1,0:T(8,128)S(1)} %get-tuple-element.35.grad_ref, f32[32,16,1024]{2,1,0:T(8,128)S(1)} %bitcast_subtract_fusion.refs_2_.decayed_ref, f32[32,16,1024]{2,1,0:T(8,128)S(1)} %bitcast.14), custom_call_target="tpu_custom_call" | custom-call | tf_op jit(solution)/shard_map/pallas_call | solution.py:264
  36.4 3.3 %collective-permute-done.8.refs_1_ = f32[2,2,16,1024]{3,2,1,0:T(8,128)S(1)} collective-permute-done((f32[2,2,16,1024]{3,2,1,0:T(8,128)S(1)}, f32[2,2,16,1024]{3,2,1,0:T(8,128)S(1)}, u32[]{:S(2)}, u32[]{:S(2)}) %collective-permute-start.8) | collective-permute-done | bytes 262176 | tf_op jit(solution)/shard_map/ppermute | solution.py:60
  39.7 1.9 %collective-permute-done.9.refs_2_ = f32[2,2,16,1024]{3,2,1,0:T(8,128)S(1)} collective-permute-done((f32[2,2,16,1024]{3,2,1,0:T(8,128)S(1)}, f32[2,2,16,1024]{3,2,1,0:T(8,128)S(1)}, u32[]{:S(2)}, u32[]{:S(2)}) %collective-permute-start.9) | collective-permute-done | bytes 262176 | tf_op jit(solution)/shard_map/ppermute | solution.py:60
  41.7 0.8 %collective-permute-done.10.refs_3_ = f32[2,2,16,1024]{3,2,1,0:T(8,128)S(1)} collective-permute-done((f32[2,2,16,1024]{3,2,1,0:T(8,128)S(1)}, f32[2,2,16,1024]{3,2,1,0:T(8,128)S(1)}, u32[]{:S(2)}, u32[]{:S(2)}) %collective-permute-start.10) | collective-permute-done | bytes 262176 | tf_op jit(solution)/shard_map/ppermute | solution.py:60
  42.5 0.1 collective-permute-start.11
  42.6 0.9 %shard_map.75.held_ref = f32[2,4,2,16,1024]{4,3,2,1,0:T(8,128)} custom-call(s32[1]{0:T(128)} %bitcast.here_ref.refs_0_, f32[2,2,16,1024]{3,2,1,0:T(8,128)S(1)} %collective-permute-done.8.refs_1_, f32[2,2,16,1024]{3,2,1,0:T(8,128)S(1)} %collective-permute-done.9.refs_2_, f32[2,2,16,1024]{3,2,1,0:T(8,128)S(1)} %collective-permute-done.10.refs_3_, ...), custom_call_target="tpu_custom_call" | custom-call | tf_op jit(solution)/shard_map/pallas_call | solution.py:276
  43.4 1.0 %collective-permute-done.11.back_ref = f32[2,4,16,1024]{3,2,1,0:T(8,128)S(1)} collective-permute-done((f32[2,4,16,1024]{3,2,1,0:T(8,128)S(1)}, f32[2,4,16,1024]{3,2,1,0:T(8,128)S(1)}, u32[]{:S(2)}, u32[]{:S(2)}) %collective-permute-start.11) | collective-permute-done | bytes 524320 | tf_op jit(solution)/shard_map/ppermute | solution.py:274
  44.5 0.8 %shard_map.76 = f32[2,4,2,16,1024]{4,3,2,1,0:T(8,128)} custom-call(s32[1]{0:T(128)} %bitcast.here_ref.refs_0_, f32[2,4,16,1024]{3,2,1,0:T(8,128)S(1)} %collective-permute-done.11.back_ref, f32[2,4,2,16,1024]{4,3,2,1,0:T(8,128)} %shard_map.75.held_ref), custom_call_target="tpu_custom_call", output_to_operand_aliasing={{}: (2, {})} | custom-call | tf_op jit(solution)/shard_map/pallas_call | solution.py:283
  (3 shorter events, 0.1 us)
Async XLA Ops:
  0.6 14.1 %copy-start = (f32[32,1,16,1024]{3,2,1,0:T(8,128)S(1)}, f32[32,1,16,1024]{3,2,1,0:T(8,128)}, u32[]{:S(2)}) copy-start(f32[32,1,16,1024]{3,2,1,0:T(8,128)} %param.7) | copy-start | bytes 6291460
  0.6 1.4 %copy-start.2 = (f32[1,2,128,1024]{3,2,1,0:T(8,128)S(1)}, f32[1,2,128,1024]{3,2,1,0:T(8,128)}, u32[]{:S(2)}) copy-start(f32[1,2,128,1024]{3,2,1,0:T(8,128)} %param.4) | copy-start | bytes 3145732
  2.1 8.2 %collective-permute-start.4 = (f32[2,4,16,1024]{3,2,1,0:T(8,128)S(1)}, f32[2,4,16,1024]{3,2,1,0:T(8,128)S(1)}, u32[]{:S(2)}, u32[]{:S(2)}) collective-permute-start(f32[2,4,16,1024]{3,2,1,0:T(8,128)S(1)} %get-tuple-element.24), channel_id=1, source_target_pairs={{0,4},{4,0},{8,12},{12,8},{16,20},{20,16},{24,28},{28,24},{1,5},{5... | collective-permute-start | bytes 1572872 | tf_op jit(solution)/shard_map/ppermute | solution.py:231
  2.6 6.3 %collective-permute-start = (f32[8,128]{1,0:T(8,128)S(1)}, f32[8,128]{1,0:T(8,128)S(1)}, u32[]{:S(2)}, u32[]{:S(2)}) collective-permute-start(f32[8,128]{1,0:T(8,128)S(1)} %get-tuple-element.22.refs_3_), channel_id=1, source_target_pairs={{0,24},{4,28},{8,16},{12,20},{16,8},{20,12},{24,0},{28,4},{1,25},{... | collective-permute-start | bytes 12296 | tf_op jit(solution)/shard_map/ppermute | solution.py:60
  6.2 3.6 %collective-permute-start.1 = (f32[8,128]{1,0:T(8,128)S(1)}, f32[8,128]{1,0:T(8,128)S(1)}, u32[]{:S(2)}, u32[]{:S(2)}) collective-permute-start(f32[8,128]{1,0:T(8,128)S(1)} %get-tuple-element.22.refs_3_), channel_id=1, source_target_pairs={{0,8},{4,20},{8,0},{12,28},{16,24},{20,4},{24,16},{28,12},{1,9},{5... | collective-permute-start | bytes 12296 | tf_op jit(solution)/shard_map/ppermute | solution.py:60
  6.7 3.6 %collective-permute-start.2 = (f32[8,128]{1,0:T(8,128)S(1)}, f32[8,128]{1,0:T(8,128)S(1)}, u32[]{:S(2)}, u32[]{:S(2)}) collective-permute-start(f32[8,128]{1,0:T(8,128)S(1)} %get-tuple-element.22.refs_3_), channel_id=1, source_target_pairs={{0,16},{4,12},{8,24},{12,4},{16,0},{20,28},{24,8},{28,20},{1,17},{... | collective-permute-start | bytes 12296 | tf_op jit(solution)/shard_map/ppermute | solution.py:60
  6.8 0.7 %copy-start.3 = (s32[8,2]{0,1:T(2,128)S(1)}, s32[8,2]{0,1:T(2,128)}, u32[]{:S(2)}) copy-start(s32[8,2]{0,1:T(2,128)} %param.5) | copy-start | bytes 196
  10.3 6.4 %collective-permute-start.3 = (f32[8,128]{1,0:T(8,128)S(1)}, f32[8,128]{1,0:T(8,128)S(1)}, u32[]{:S(2)}, u32[]{:S(2)}) collective-permute-start(f32[8,128]{1,0:T(8,128)S(1)} %shard_map.69.refs_0_), channel_id=1, source_target_pairs={{0,4},{4,0},{8,12},{12,8},{16,20},{20,16},{24,28},{28,24},{1,5},{5... | collective-permute-start | bytes 12296 | tf_op jit(solution)/shard_map/ppermute | solution.py:250
  11.2 17.6 %collective-permute-start.5 = (f32[2,2,16,1024]{3,2,1,0:T(8,128)}, f32[2,2,16,1024]{3,2,1,0:T(8,128)S(1)}, u32[]{:S(2)}, u32[]{:S(2)}) collective-permute-start(f32[2,2,16,1024]{3,2,1,0:T(8,128)} %get-tuple-element.26), channel_id=1, source_target_pairs={{0,24},{4,28},{8,16},{12,20},{16,8},{20,12},{24,0},{28,4},{1,25},{... | collective-permute-start | bytes 786440 | tf_op jit(solution)/shard_map/ppermute | solution.py:60
  12.8 16.0 %collective-permute-start.6 = (f32[2,2,16,1024]{3,2,1,0:T(8,128)}, f32[2,2,16,1024]{3,2,1,0:T(8,128)S(1)}, u32[]{:S(2)}, u32[]{:S(2)}) collective-permute-start(f32[2,2,16,1024]{3,2,1,0:T(8,128)} %get-tuple-element.27), channel_id=1, source_target_pairs={{0,8},{4,20},{8,0},{12,28},{16,24},{20,4},{24,16},{28,12},{1,9},{5... | collective-permute-start | bytes 786440 | tf_op jit(solution)/shard_map/ppermute | solution.py:60
  13.3 15.5 %collective-permute-start.7 = (f32[2,2,16,1024]{3,2,1,0:T(8,128)S(1)}, f32[2,2,16,1024]{3,2,1,0:T(8,128)S(1)}, u32[]{:S(2)}, u32[]{:S(2)}) collective-permute-start(f32[2,2,16,1024]{3,2,1,0:T(8,128)S(1)} %get-tuple-element.28), channel_id=1, source_target_pairs={{0,16},{4,12},{8,24},{12,4},{16,0},{20,28},{24,8},{28,20},{1,17},{... | collective-permute-start | bytes 786440 | tf_op jit(solution)/shard_map/ppermute | solution.py:60
  28.8 4.6 %copy-start.1 = (f32[32,1,16,1024]{3,2,1,0:T(8,128)S(1)}, f32[32,1,16,1024]{3,2,1,0:T(8,128)}, u32[]{:S(2)}) copy-start(f32[32,1,16,1024]{3,2,1,0:T(8,128)} %param.7) | copy-start | bytes 6291460
  29.8 9.9 %collective-permute-start.8 = (f32[2,2,16,1024]{3,2,1,0:T(8,128)S(1)}, f32[2,2,16,1024]{3,2,1,0:T(8,128)S(1)}, u32[]{:S(2)}, u32[]{:S(2)}) collective-permute-start(f32[2,2,16,1024]{3,2,1,0:T(8,128)S(1)} %get-tuple-element.30), channel_id=1, source_target_pairs={{0,24},{4,28},{8,16},{12,20},{16,8},{20,12},{24,0},{28,4},{1,25},{... | collective-permute-start | bytes 786440 | tf_op jit(solution)/shard_map/ppermute | solution.py:60
  31.4 10.2 %collective-permute-start.9 = (f32[2,2,16,1024]{3,2,1,0:T(8,128)S(1)}, f32[2,2,16,1024]{3,2,1,0:T(8,128)S(1)}, u32[]{:S(2)}, u32[]{:S(2)}) collective-permute-start(f32[2,2,16,1024]{3,2,1,0:T(8,128)S(1)} %get-tuple-element.31), channel_id=1, source_target_pairs={{0,8},{4,20},{8,0},{12,28},{16,24},{20,4},{24,16},{28,12},{1,9},{5... | collective-permute-start | bytes 786440 | tf_op jit(solution)/shard_map/ppermute | solution.py:60
  32.0 10.5 %collective-permute-start.10 = (f32[2,2,16,1024]{3,2,1,0:T(8,128)S(1)}, f32[2,2,16,1024]{3,2,1,0:T(8,128)S(1)}, u32[]{:S(2)}, u32[]{:S(2)}) collective-permute-start(f32[2,2,16,1024]{3,2,1,0:T(8,128)S(1)} %get-tuple-element.32), channel_id=1, source_target_pairs={{0,16},{4,12},{8,24},{12,4},{16,0},{20,28},{24,8},{28,20},{1,17},{... | collective-permute-start | bytes 786440 | tf_op jit(solution)/shard_map/ppermute | solution.py:60
  42.5 2.0 %collective-permute-start.11 = (f32[2,4,16,1024]{3,2,1,0:T(8,128)S(1)}, f32[2,4,16,1024]{3,2,1,0:T(8,128)S(1)}, u32[]{:S(2)}, u32[]{:S(2)}) collective-permute-start(f32[2,4,16,1024]{3,2,1,0:T(8,128)S(1)} %shard_map.74), channel_id=1, source_target_pairs={{0,4},{4,0},{8,12},{12,8},{16,20},{20,16},{24,28},{28,24},{1,5},{5... | collective-permute-start | bytes 1572872 | tf_op jit(solution)/shard_map/ppermute | solution.py:274

commit v2 on v1

--- a/solution.py
+++ b/solution.py
@@ -86,15 +86,24 @@
         pl.when(here_ref[0] & 1 == core)(lambda core=core: pack(core))
 
 
-def merge_kernel(size, here_ref, keep_ref, gift_ref, token_ref, *outs):
-    del token_ref
+def scale_kernel(entries, here_ref, plan_ref, square_ref, other_ref, keep_ref, gift_ref, *refs):
+    outs, rescale_ref = refs[:-1], refs[-1]
     here = here_ref[0]
     core = here & 1
-    for k, out in zip(order_of(size), outs):
-        chip = target(here, k, size) // 2
+    rounds = len(outs) // LEVELS
+    size = 2 * rounds
+    total = jnp.sum(square_ref[...] + other_ref[...], axis=1, keepdims=True)
+    rescale_ref[...] = jnp.broadcast_to(1.0 / jnp.sqrt(total / entries + 1e-06), rescale_ref.shape)
+    for half, (rows_ref, source) in enumerate(((keep_ref, core), (gift_ref, 1 - core))):
+        rescale = jnp.broadcast_to(rescale_ref[pl.ds((here // 2) * 2 + source, 1), :], (8, 128))
         for level in range(LEVELS):
-            out[core, level] = keep_ref[level, chip]
-            out[1 - core, level] = gift_ref[level, chip]
+            sharers = plan_ref[level, 2 * size - 2 + source]
+            factor = rescale / jnp.full((8, 128), sharers, jnp.int32).astype(jnp.float32)
+            for j, k in enumerate(order_of(size)):
+                out = outs[level * rounds + j]
+                chip = target(here, k, size) // 2
+                for spot in tiles_of(*out.shape[1:]):
+                    out[(source, *spot)] = rows_ref[(level, chip, *spot)] * factor
 
 
 def sum_kernel(*refs):
@@ -130,76 +139,74 @@
             plan_ref[level, 4 * size + i] = module_ref[module]
 
 
-def outgoing_kernel(rounds, entries, plan_ref, square_ref, decayed_ref, *refs):
-    received, outs, (grad_ref, rescale_ref) = refs[:rounds], refs[rounds:-2], refs[-2:]
+def outgoing_kernel(level, rounds, plan_ref, decayed_ref, *refs):
+    received, outs, grad_ref = refs[:rounds], refs[rounds:-1], refs[-1]
     size = 2 * rounds
-    total = jnp.sum(square_ref[...], axis=1, keepdims=True)
-    rescale_ref[...] = jnp.broadcast_to(1.0 / jnp.sqrt(total / entries + 1e-06), rescale_ref.shape)
-    for level in range(LEVELS):
-        for i in range(size):
-            rescale = jnp.broadcast_to(rescale_ref[pl.ds(plan_ref[level, 2 * size + i], 1), :], (8, 128))
-            factor = rescale / jnp.full((8, 128), plan_ref[level, size + i], jnp.int32).astype(jnp.float32)
-            for spot in tiles_of(*grad_ref.shape[2:]):
-                grad_ref[(level, i, *spot)] = received[i // 2][(i % 2, level, *spot)] * factor
-        for i in range(1, size):
-            leader = plan_ref[level, i]
-
-            @pl.when(leader != i)
-            def _():
-                grad_ref[level, leader] += grad_ref[level, i]
-
-        for i in range(size):
-            decayed = decayed_ref[plan_ref[level, 3 * size + i]]
-            outs[i // 2][i % 2, level] = decayed - grad_coef * grad_ref[level, plan_ref[level, 4 * size + i]]
-
-
-def state_kernel(module_ref, grad_ref, decayed_ref, momentum_ref, new_params_ref, new_momentum_ref, token_ref):
+    for i in range(size):
+        grad_ref[i] = received[i // 2][i % 2]
+    for i in range(1, size):
+        leader = plan_ref[level, i]
+
+        @pl.when(leader != i)
+        def _():
+            grad_ref[leader] += grad_ref[i]
+
+    for i in range(size):
+        decayed = decayed_ref[plan_ref[level, 3 * size + i]]
+        outs[i // 2][i % 2] = decayed - grad_coef * grad_ref[plan_ref[level, 4 * size + i]]
+
+
+def state_kernel(module_ref, *refs):
+    grads, (decayed_ref, momentum_ref, new_params_ref, new_momentum_ref, token_ref) = refs[:LEVELS], refs[LEVELS:]
     token_ref[...] = jnp.zeros_like(token_ref)
     count = new_params_ref.shape[0]
     first = pl.program_id(0) * count
-    level = first // LEVEL_MODULES
-    for place in range(count):
-        module = first + place
-        leader = module_ref[module]
-        taken = jnp.where(leader < 0, 0.0, 1.0)
-        grad = taken * grad_ref[level, jnp.maximum(leader, 0)]
-        new_momentum_ref[place] = beta_coef * momentum_ref[module] + grad
-        new_params_ref[place] = decayed_ref[module] - grad_coef * grad
+
+    def update(grad_ref):
+        for place in range(count):
+            module = first + place
+            leader = module_ref[module]
+            taken = jnp.where(leader < 0, 0.0, 1.0)
+            grad = taken * grad_ref[jnp.maximum(leader, 0)]
+            new_momentum_ref[place] = beta_coef * momentum_ref[module] + grad
+            new_params_ref[place] = decayed_ref[module] - grad_coef * grad
+
+    for level, grad_ref in enumerate(grads):
+        pl.when(first // LEVEL_MODULES == level)(lambda grad_ref=grad_ref: update(grad_ref))
 
 
 def give_back_kernel(size, here_ref, *refs):
     here = here_ref[0]
     for j, k in enumerate(order_of(size)):
-        for level in range(LEVELS):
-            refs[-1][level, origin(here, k, size) // 2] = refs[j][1 - (here & 1), level]
+        refs[-1][origin(here, k, size) // 2] = refs[j][1 - (here & 1)]
 
 
 def own_rows_kernel(size, here_ref, *refs):
+    order = order_of(size)
     here = here_ref[0]
     core = here & 1
     out_ref, sems = refs[-2:]
     copies = []
-    for j, k in enumerate(order_of(size)):
-        chip = origin(here, k, size) // 2
-        for level in range(LEVELS):
-            copies.append(
-                pltpu.make_async_copy(refs[j].at[core, level], out_ref.at[level, chip, core], sems.at[level, j])
-            )
+    for level in range(LEVELS):
+        for j, k in enumerate(order):
+            chip = origin(here, k, size) // 2
+            block = refs[level * len(order) + j]
+            copies.append(pltpu.make_async_copy(block.at[core], out_ref.at[level, chip, core], sems.at[level, j]))
     for copy in copies:
         copy.start()
     for copy in copies:
         copy.wait()
 
 
-def other_rows_kernel(here_ref, back_ref, held_ref, out_ref, sems):
-    del held_ref
+def other_rows_kernel(here_ref, *refs):
+    out_ref, sems = refs[-2:]
     core = here_ref[0] & 1
     copies = []
     for level in range(LEVELS):
-        for chip in range(back_ref.shape[1]):
+        for chip in range(refs[level].shape[0]):
             copies.append(
                 pltpu.make_async_copy(
-                    back_ref.at[level, chip], out_ref.at[level, chip, 1 - core], sems.at[level, chip]
+                    refs[level].at[chip], out_ref.at[level, chip, 1 - core], sems.at[level, chip]
                 )
             )
     for copy in copies:
@@ -212,7 +219,8 @@
     own_slab = path_delta[0]
     size = assign.shape[0]
     module_count, _, own_rows, width = params.shape
-    entries = float(own_slab.size * lax.axis_size("shard"))
+    shards = lax.axis_size("shard")
+    entries = float(own_slab.size * shards)
     state_in = params.reshape(module_count, own_rows, width)
     moment_in = momentum.reshape(module_count, own_rows, width)
     split_slab = own_slab.reshape(LEVELS, size // 2, 2, own_rows, width)
@@ -223,13 +231,17 @@
     shape = lambda *dims: jax.ShapeDtypeStruct(dims, jnp.float32)
     squares_shape = shape(-(-size // 8) * 8, 128)
     by_chip = shape(LEVELS, rounds, own_rows, width)
-    message = shape(2, LEVELS, own_rows, width)
+    message = shape(2, own_rows, width)
 
     squares, keep, give = call(pack_kernel, [squares_shape, by_chip, by_chip], [smem, vmem], [vmem] * 3)(
         here, split_slab
     )
     gift = lax.ppermute(give, "path", swap)
-    squares = call(sum_kernel, squares_shape, [vmem] * rounds, vmem)(*[move(squares, k, size) for k in order])
+    tiles = [squares] + [
+        lax.ppermute(squares, "shard", [(i, i ^ step) for i in range(shards)]) for step in range(shards - 1, 0, -1)
+    ]
+    squares = call(sum_kernel, squares_shape, [vmem] * shards, vmem)(*tiles)
+    other = lax.ppermute(squares, "path", swap)
     plan, leaders, planned = call(
         plan_kernel,
         [
@@ -241,53 +253,62 @@
         [smem, smem, vmem],
     )(here, assign.T)
     messages = call(
-        lambda *refs: merge_kernel(size, *refs),
-        [message] * rounds,
-        [smem, vmem, vmem, anywhere],
-        [vmem] * rounds,
-    )(here, keep, gift, planned)
-    received = [move(messages[j], k, size) for j, k in enumerate(order)]
-    other = lax.ppermute(squares, "path", swap)
-    squares = lax.psum(call(sum_kernel, squares_shape, [vmem] * 2, vmem)(squares, other), "shard")
+        lambda *refs: scale_kernel(entries, *refs),
+        [message] * (LEVELS * rounds),
+        [smem, smem, vmem, vmem, vmem, vmem],
+        [vmem] * (LEVELS * rounds),
+        scratch_shapes=[pltpu.VMEM(squares_shape.shape, jnp.float32)],
+    )(here, plan, squares, other, keep, gift)
     decayed = state_in - moment_coef * moment_in
 
-    *outgoing, grad = call(
-        lambda *refs: outgoing_kernel(rounds, entries, *refs),
-        [message] * rounds + [shape(LEVELS, size, own_rows, width)],
-        [smem] + [vmem] * (2 + rounds),
-        [vmem] * (rounds + 1),
-        scratch_shapes=[pltpu.VMEM(squares_shape.shape, jnp.float32)],
-    )(plan, squares, decayed, *received)
-    returned = [move(outgoing[j], k, size) for j, k in enumerate(order)]
+    returned, grads = [], []
+    for level in range(LEVELS):
+        received = [move(messages[level * rounds + j], k, size) for j, k in enumerate(order)]
+        *outgoing, grad = call(
+            lambda *refs, level=level: outgoing_kernel(level, rounds, *refs),
+            [message] * rounds + [shape(size, own_rows, width)],
+            [smem] + [vmem] * (1 + rounds),
+            [vmem] * (rounds + 1),
+        )(plan, decayed, *received)
+        returned.append([move(outgoing[j], k, size) for j, k in enumerate(order)])
+        grads.append(grad)
+
     block = LEVEL_MODULES // 2
     state_block = pl.BlockSpec((block, own_rows, width), lambda i: (i, 0, 0))
     new_state, new_moment, done = call(
         state_kernel,
         [shape(*state_in.shape)] * 2 + [shape(8, 128)],
-        [smem, vmem, vmem, vmem],
+        [smem] + [vmem] * (LEVELS + 2),
         [state_block, state_block, vmem],
         grid=(module_count // block,),
-    )(leaders, grad, decayed, moment_in)
-    back = call(
-        lambda *refs: give_back_kernel(size, *refs), by_chip, [smem] + [vmem] * rounds + [anywhere], vmem
-    )(here, *returned, done)
-    back = lax.ppermute(back, "path", swap)
+    )(leaders, *grads, decayed, moment_in)
+
+    backs = []
+    for level in range(LEVELS):
+        before = [done] if level == LEVELS - 1 else []
+        back = call(
+            lambda *refs: give_back_kernel(size, *refs),
+            shape(rounds, own_rows, width),
+            [smem] + [vmem] * rounds + [anywhere] * len(before),
+            vmem,
+        )(here, *returned[level], *before)
+        backs.append(lax.ppermute(back, "path", swap))
     sems = [pltpu.SemaphoreType.DMA((LEVELS, rounds))]
     path_params = call(
         lambda *refs: own_rows_kernel(size, *refs),
         shape(*split_slab.shape),
-        [smem] + [anywhere] * rounds,
+        [smem] + [anywhere] * (LEVELS * rounds),
         anywhere,
         scratch_shapes=sems,
-    )(here, *returned)
+    )(here, *returned[0], *returned[1])
     path_params = call(
         other_rows_kernel,
         shape(*split_slab.shape),
-        [smem, anywhere, anywhere],
+        [smem] + [anywhere] * (LEVELS + 1),
         anywhere,
         scratch_shapes=sems,
-        input_output_aliases={2: 0},
-    )(here, back, path_params)
+        input_output_aliases={LEVELS + 1: 0},
+    )(here, *backs, path_params)
     return (path_params.reshape(path_delta.shape), new_state[:, None], new_moment[:, None])
 
 

time: 45.5 us -> 44.1 us (0.969)
  blocking collectives: 12 us -> 0 us
  starting transfers between devices: 11.8 us -> 23 us
  waiting for transfers between devices: 8.48 us -> 7.55 us
    psum x1 -> x0, blocking collectives: 12 us -> none  [local(): lax.psum(call(sum_kernel, squares_shape, [vmem] * 2, vmem)(squares, other...]
    ppermute x9 -> x12, starting transfers between devices: 11.2 us -> 17 us  [move(): lax.ppermute(array, 'path', [(i, target(i, k, size)) for i in range(size)])]
    ppermute x1 -> x5, starting transfers between devices: 0.07 us -> 5.47 us  [the longest x3 5.33 us: local(): lax.ppermute(squares, 'shard', [(i, i ^ step) for i in range(shards)])]
    ppermute x9 -> x12, waiting for transfers between devices: 7.45 us -> 3.03 us  [move(): lax.ppermute(array, 'path', [(i, target(i, k, size)) for i in range(size)])]
    ppermute x1 -> x5, waiting for transfers between devices: 1.03 us -> 4.51 us  [the longest x3 3.87 us: local(): lax.ppermute(squares, 'shard', [(i, i ^ step) for i in range(shards)])]
    pallas_call x7 -> x8, Pallas kernels: 5.83 us -> 6.16 us  [the longest x1 3.11 us: local(): call(state_kernel, [shape(*state_in.shape)] * 2 + [shape(8, 128)], [smem]...]
    unnamed x8 -> x6, local copies, waits for them, and re-layouts: 2.05 us -> 2.04 us
  transfers between devices with their start and end apart: 12 -> 19, of which waited for: 6 -> 7; matrix products, arithmetic and copies ran while one was open for 4% -> 5% of each run, Pallas kernels for 14% -> 16%
where the time goes in v2:
time: 44.1 us; the launch traced here: 44 us
  starting transfers between devices  23 us (52%)
  Pallas kernels  8.54 us (19%)
  waiting for transfers between devices  7.55 us (17%)
  local copies, waits for them, and re-layouts  2.04 us (5%)
  other arithmetic  2.03 us (5%)
  between operations  0.8 us (2%)
    ppermute x12, starting transfers between devices, move(): lax.ppermute(array, 'path', [(i, target(i, k, size)) for i in range(size)])  17 us
    ppermute x3, starting transfers between devices, local(): lax.ppermute(squares, 'shard', [(i, i ^ step) for i in range(shards)])  5.33 us
    ppermute x3, waiting for transfers between devices, local(): lax.ppermute(squares, 'shard', [(i, i ^ step) for i in range(shards)])  3.87 us
    pallas_call x1, Pallas kernels, local(): call(state_kernel, [shape(*state_in.shape)] * 2 + [shape(8, 128)], [smem]...  3.11 us
    ppermute x12, waiting for transfers between devices, move(): lax.ppermute(array, 'path', [(i, target(i, k, size)) for i in range(size)])  3.03 us
    unnamed x6, local copies, waits for them, and re-layouts  2.04 us
    sub x1, other arithmetic, local(): decayed = state_in - moment_coef * moment_in  2.03 us
    pallas_call x2, Pallas kernels, local(): call(lambda *refs, level=level: outgoing_kernel(level, rounds, *refs), [m...  1.43 us
  transfers between devices with their start and end apart: 19, of which 7 were waited for; matrix products, arithmetic and copies ran while one was open for 5% of the time, Pallas kernels for 16%

profile of v2, /device:TPU:0, one launch (start us, length us, event | category | flops | bytes accessed | tf_op | source)
XLA Modules:
  0.0 44.0 jit_solution(10804363614751818458)
XLA Ops:
  0.7 1.4 %copy-done.1 = f32[1,2,128,1024]{3,2,1,0:T(8,128)S(1)} copy-done((f32[1,2,128,1024]{3,2,1,0:T(8,128)S(1)}, f32[1,2,128,1024]{3,2,1,0:T(8,128)}, u32[]{:S(2)}) %copy-start.1) | copy-done | bytes 1048600
  2.0 0.1 shard_map.68
  2.1 0.5 %collective-permute-start.4 = (f32[2,4,16,1024]{3,2,1,0:T(8,128)S(1)}, f32[2,4,16,1024]{3,2,1,0:T(8,128)S(1)}, u32[]{:S(2)}, u32[]{:S(2)}) collective-permute-start(f32[2,4,16,1024]{3,2,1,0:T(8,128)S(1)} %get-tuple-element.32), channel_id=1, source_target_pairs={{0,4},{4,0},{8,12},{12,8},{16,20},{20,16},{24,28},{28,24},{1,5},{5... | collective-permute-start | bytes 1572872 | tf_op jit(solution)/shard_map/ppermute | solution.py:239
  2.6 4.7 %collective-permute-start = (f32[8,128]{1,0:T(8,128)S(1)}, f32[8,128]{1,0:T(8,128)S(1)}, u32[]{:S(2)}, u32[]{:S(2)}) collective-permute-start(f32[8,128]{1,0:T(8,128)S(1)} %get-tuple-element.30.refs_0_), channel_id=1, source_target_pairs={{0,3},{1,2},{2,1},{3,0},{4,7},{5,6},{6,5},{7,4},{8,11},{9,10},{10,... | collective-permute-start | bytes 12296 | tf_op jit(solution)/shard_map/ppermute | solution.py:241
  7.3 0.0 collective-permute-start.1
  7.3 0.6 %collective-permute-start.2 = (f32[8,128]{1,0:T(8,128)S(1)}, f32[8,128]{1,0:T(8,128)S(1)}, u32[]{:S(2)}, u32[]{:S(2)}) collective-permute-start(f32[8,128]{1,0:T(8,128)S(1)} %get-tuple-element.30.refs_0_), channel_id=1, source_target_pairs={{0,1},{1,0},{2,3},{3,2},{4,5},{5,4},{6,7},{7,6},{8,9},{9,8},{10,11... | collective-permute-start | bytes 12296 | tf_op jit(solution)/shard_map/ppermute | solution.py:241
  8.0 0.9 %collective-permute-done.refs_1_ = f32[8,128]{1,0:T(8,128)S(1)} collective-permute-done((f32[8,128]{1,0:T(8,128)S(1)}, f32[8,128]{1,0:T(8,128)S(1)}, u32[]{:S(2)}, u32[]{:S(2)}) %collective-permute-start) | collective-permute-done | bytes 4128 | tf_op jit(solution)/shard_map/ppermute | solution.py:241
  8.9 2.9 %collective-permute-done.1.refs_2_ = f32[8,128]{1,0:T(8,128)S(1)} collective-permute-done((f32[8,128]{1,0:T(8,128)S(1)}, f32[8,128]{1,0:T(8,128)S(1)}, u32[]{:S(2)}, u32[]{:S(2)}) %collective-permute-start.1) | collective-permute-done | bytes 4128 | tf_op jit(solution)/shard_map/ppermute | solution.py:241
  11.8 0.0 collective-permute-done.2.refs_3_
  11.8 0.1 collective-permute-start.3
  11.9 0.0 copy-start.2
  11.9 0.7 %copy-done.2 = s32[8,2]{0,1:T(2,128)S(1)} copy-done((s32[8,2]{0,1:T(2,128)S(1)}, s32[8,2]{0,1:T(2,128)}, u32[]{:S(2)}) %copy-start.2) | copy-done | bytes 88
  12.6 1.4 %shard_map.67 = (s32[2,40]{1,0:T(2,128)S(1)}, s32[32]{0:T(128)S(1)}, f32[8,128]{1,0:T(8,128)}) custom-call(s32[1]{0:T(128)} %bitcast.here_ref.refs_0_, s32[2,8]{1,0:T(2,128)S(1)} %bitcast.16), custom_call_target="tpu_custom_call" | custom-call | tf_op jit(solution)/shard_map/pallas_call | solution.py:245
  14.0 0.0 collective-permute-done.3.refs_3_
  14.0 0.0 collective-permute-done.4.refs_5_
  14.0 0.7 %shard_map.70 = (f32[2,16,1024]{2,1,0:T(8,128)S(1)}, f32[2,16,1024]{2,1,0:T(8,128)S(1)}, f32[2,16,1024]{2,1,0:T(8,128)S(1)}, f32[2,16,1024]{2,1,0:T(8,128)S(1)},...) custom-call(s32[1]{0:T(128)} %bitcast.here_ref.refs_0_, ...), custom_call_target="tpu_custom_call" | custom-call | tf_op jit(solution)/shard_map/pallas_call | solution.py:255
  14.8 2.5 %collective-permute-start.5 = (f32[2,16,1024]{2,1,0:T(8,128)S(1)}, f32[2,16,1024]{2,1,0:T(8,128)S(1)}, u32[]{:S(2)}, u32[]{:S(2)}) collective-permute-start(f32[2,16,1024]{2,1,0:T(8,128)S(1)} %get-tuple-element.33), channel_id=1, source_target_pairs={{0,24},{4,28},{8,16},{12,20},{16,8},{20,12},{24,0},{28,4},{1,25},{... | collective-permute-start | bytes 393224 | tf_op jit(solution)/shard_map/ppermute | solution.py:60
  17.3 0.5 %collective-permute-start.6 = (f32[2,16,1024]{2,1,0:T(8,128)S(1)}, f32[2,16,1024]{2,1,0:T(8,128)S(1)}, u32[]{:S(2)}, u32[]{:S(2)}) collective-permute-start(f32[2,16,1024]{2,1,0:T(8,128)S(1)} %get-tuple-element.34), channel_id=1, source_target_pairs={{0,8},{4,20},{8,0},{12,28},{16,24},{20,4},{24,16},{28,12},{1,9},{5... | collective-permute-start | bytes 393224 | tf_op jit(solution)/shard_map/ppermute | solution.py:60
  17.8 0.5 %collective-permute-start.7 = (f32[2,16,1024]{2,1,0:T(8,128)S(1)}, f32[2,16,1024]{2,1,0:T(8,128)S(1)}, u32[]{:S(2)}, u32[]{:S(2)}) collective-permute-start(f32[2,16,1024]{2,1,0:T(8,128)S(1)} %get-tuple-element.35), channel_id=1, source_target_pairs={{0,16},{4,12},{8,24},{12,4},{16,0},{20,28},{24,8},{28,20},{1,17},{... | collective-permute-start | bytes 393224 | tf_op jit(solution)/shard_map/ppermute | solution.py:60
  18.3 2.4 %collective-permute-start.12 = (f32[2,16,1024]{2,1,0:T(8,128)S(1)}, f32[2,16,1024]{2,1,0:T(8,128)S(1)}, u32[]{:S(2)}, u32[]{:S(2)}) collective-permute-start(f32[2,16,1024]{2,1,0:T(8,128)S(1)} %get-tuple-element.41), channel_id=1, source_target_pairs={{0,24},{4,28},{8,16},{12,20},{16,8},{20,12},{24,0},{28,4},{1,25},{... | collective-permute-start | bytes 393224 | tf_op jit(solution)/shard_map/ppermute | solution.py:60
  20.8 0.5 %collective-permute-start.13 = (f32[2,16,1024]{2,1,0:T(8,128)S(1)}, f32[2,16,1024]{2,1,0:T(8,128)S(1)}, u32[]{:S(2)}, u32[]{:S(2)}) collective-permute-start(f32[2,16,1024]{2,1,0:T(8,128)S(1)} %get-tuple-element.42), channel_id=1, source_target_pairs={{0,8},{4,20},{8,0},{12,28},{16,24},{20,4},{24,16},{28,12},{1,9},{5... | collective-permute-start | bytes 393224 | tf_op jit(solution)/shard_map/ppermute | solution.py:60
  21.3 0.6 %collective-permute-done.5.refs_2_ = f32[2,16,1024]{2,1,0:T(8,128)S(1)} collective-permute-done((f32[2,16,1024]{2,1,0:T(8,128)S(1)}, f32[2,16,1024]{2,1,0:T(8,128)S(1)}, u32[]{:S(2)}, u32[]{:S(2)}) %collective-permute-start.5) | collective-permute-done | bytes 131104 | tf_op jit(solution)/shard_map/ppermute | solution.py:60
  21.9 1.7 %collective-permute-start.14 = (f32[2,16,1024]{2,1,0:T(8,128)S(1)}, f32[2,16,1024]{2,1,0:T(8,128)S(1)}, u32[]{:S(2)}, u32[]{:S(2)}) collective-permute-start(f32[2,16,1024]{2,1,0:T(8,128)S(1)} %get-tuple-element.43), channel_id=1, source_target_pairs={{0,16},{4,12},{8,24},{12,4},{16,0},{20,28},{24,8},{28,20},{1,17},{... | collective-permute-start | bytes 393224 | tf_op jit(solution)/shard_map/ppermute | solution.py:60
  23.6 2.0 %bitcast_subtract_fusion.refs_1_.refs_2_ = f32[32,16,1024]{2,1,0:T(8,128)S(1)} fusion(f32[32,1,16,1024]{3,2,1,0:T(8,128)} %param.6, f32[32,1,16,1024]{3,2,1,0:T(8,128)S(1)} %copy-done), kind=kLoop, calls=%fused_computation | loop fusion | flops 1048576 | bytes 6291456 | tf_op jit(solution)/shard_map/sub | solution.py:262
  25.6 0.0 collective-permute-done.6.refs_3_
  25.6 0.0 collective-permute-done.7.refs_4_
  25.6 0.7 %shard_map.71 = (f32[2,16,1024]{2,1,0:T(8,128)S(1)}, f32[2,16,1024]{2,1,0:T(8,128)S(1)}, f32[2,16,1024]{2,1,0:T(8,128)S(1)}, f32[2,16,1024]{2,1,0:T(8,128)S(1)}, f32[8,16,1024]{2,1,0:T(8,128)S(1)}) custom-call(s32[2,40]{1,0:T(2,128)S(1)} %get-tuple-element.29.refs_1_.refs_0_, f32[32,16,1024]{2,1,0:T(8,128)S(1)} %bitcast_subtract_fusion.refs_1_.refs_2_, ...), custom_call_target="tpu_custom_call" | custom-call | tf_op jit(solution)/shard_map/pallas_call | solution.py:267
  26.4 3.9 %collective-permute-start.8 = (f32[2,16,1024]{2,1,0:T(8,128)S(1)}, f32[2,16,1024]{2,1,0:T(8,128)S(1)}, u32[]{:S(2)}, u32[]{:S(2)}) collective-permute-start(f32[2,16,1024]{2,1,0:T(8,128)S(1)} %get-tuple-element.37), channel_id=1, source_target_pairs={{0,24},{4,28},{8,16},{12,20},{16,8},{20,12},{24,0},{28,4},{1,25},{... | collective-permute-start | bytes 393224 | tf_op jit(solution)/shard_map/ppermute | solution.py:60
  30.3 0.0 collective-permute-start.9
  30.3 0.0 collective-permute-done.12.refs_2_
  30.3 0.6 %collective-permute-start.10 = (f32[2,16,1024]{2,1,0:T(8,128)S(1)}, f32[2,16,1024]{2,1,0:T(8,128)S(1)}, u32[]{:S(2)}, u32[]{:S(2)}) collective-permute-start(f32[2,16,1024]{2,1,0:T(8,128)S(1)} %get-tuple-element.39), channel_id=1, source_target_pairs={{0,16},{4,12},{8,24},{12,4},{16,0},{20,28},{24,8},{28,20},{1,17},{... | collective-permute-start | bytes 393224 | tf_op jit(solution)/shard_map/ppermute | solution.py:60
  31.0 0.0 collective-permute-done.13.refs_3_
  31.0 0.7 %collective-permute-done.14.refs_4_ = f32[2,16,1024]{2,1,0:T(8,128)S(1)} collective-permute-done((f32[2,16,1024]{2,1,0:T(8,128)S(1)}, f32[2,16,1024]{2,1,0:T(8,128)S(1)}, u32[]{:S(2)}, u32[]{:S(2)}) %collective-permute-start.14) | collective-permute-done | bytes 131104 | tf_op jit(solution)/shard_map/ppermute | solution.py:60
  31.6 0.7 %shard_map.73 = (f32[2,16,1024]{2,1,0:T(8,128)S(1)}, f32[2,16,1024]{2,1,0:T(8,128)S(1)}, f32[2,16,1024]{2,1,0:T(8,128)S(1)}, f32[2,16,1024]{2,1,0:T(8,128)S(1)}, f32[8,16,1024]{2,1,0:T(8,128)S(1)}) custom-call(s32[2,40]{1,0:T(2,128)S(1)} %get-tuple-element.29.refs_1_.refs_0_, f32[32,16,1024]{2,1,0:T(8,128)S(1)} %bitcast_subtract_fusion.refs_1_.refs_2_, ...), custom_call_target="tpu_custom_call" | custom-call | tf_op jit(solution)/shard_map/pallas_call | solution.py:267
  32.3 2.3 %collective-permute-start.15 = (f32[2,16,1024]{2,1,0:T(8,128)S(1)}, f32[2,16,1024]{2,1,0:T(8,128)S(1)}, u32[]{:S(2)}, u32[]{:S(2)}) collective-permute-start(f32[2,16,1024]{2,1,0:T(8,128)S(1)} %get-tuple-element.45), channel_id=1, source_target_pairs={{0,24},{4,28},{8,16},{12,20},{16,8},{20,12},{24,0},{28,4},{1,25},{... | collective-permute-start | bytes 393224 | tf_op jit(solution)/shard_map/ppermute | solution.py:60
  34.6 1.9 %collective-permute-start.16 = (f32[2,16,1024]{2,1,0:T(8,128)S(1)}, f32[2,16,1024]{2,1,0:T(8,128)S(1)}, u32[]{:S(2)}, u32[]{:S(2)}) collective-permute-start(f32[2,16,1024]{2,1,0:T(8,128)S(1)} %get-tuple-element.46), channel_id=1, source_target_pairs={{0,8},{4,20},{8,0},{12,28},{16,24},{20,4},{24,16},{28,12},{1,9},{5... | collective-permute-start | bytes 393224 | tf_op jit(solution)/shard_map/ppermute | solution.py:60
  36.5 0.0 collective-permute-done.8.refs_1_
  36.5 0.0 collective-permute-start.17
  36.5 3.1 %shard_map.74 = (f32[32,16,1024]{2,1,0:T(8,128)}, f32[32,16,1024]{2,1,0:T(8,128)}, f32[8,128]{1,0:T(8,128)S(1)}) custom-call(s32[32]{0:T(128)S(1)} %get-tuple-element.49.module_ref, f32[8,16,1024]{2,1,0:T(8,128)S(1)} %get-tuple-element.50.refs_0_, f32[8,16,1024]{2,1,0:T(8,128)S(1)} %get-tuple-element.51.refs_1_, ...), custom_call_target="tpu_custom_call" | custom-call | tf_op jit(solution)/shard_map/pallas_call | solution.py:278
  39.6 0.0 collective-permute-done.9.refs_2_
  39.6 0.0 collective-permute-done.10.refs_3_
  39.7 0.1 collective-permute-start.11
  39.8 0.1 collective-permute-done.15.refs_1_.refs_5_
  39.9 1.6 %collective-permute-done.16.refs_2_.refs_6_ = f32[2,16,1024]{2,1,0:T(8,128)S(1)} collective-permute-done((f32[2,16,1024]{2,1,0:T(8,128)S(1)}, f32[2,16,1024]{2,1,0:T(8,128)S(1)}, u32[]{:S(2)}, u32[]{:S(2)}) %collective-permute-start.16) | collective-permute-done | bytes 131104 | tf_op jit(solution)/shard_map/ppermute | solution.py:60
  41.5 0.1 collective-permute-start.18
  41.6 0.9 %shard_map.76.refs_2_ = f32[2,4,2,16,1024]{4,3,2,1,0:T(8,128)} custom-call(s32[1]{0:T(128)} %bitcast.here_ref.refs_0_, f32[2,16,1024]{2,1,0:T(8,128)S(1)} %collective-permute-done.8.refs_1_, f32[2,16,1024]{2,1,0:T(8,128)S(1)} %collective-permute-done.9.refs_2_, f32[2,16,1024]{2,1,0:T(8,128)S(1)} %collective-permute-done.10.refs_3_, ...), custom_call_target="tpu_custom_call" | custom-call | tf_op jit(solution)/shard_map/pallas_call | solution.py:297
  42.5 0.6 %collective-permute-done.18.refs_1_ = f32[4,16,1024]{2,1,0:T(8,128)S(1)} collective-permute-done((f32[4,16,1024]{2,1,0:T(8,128)S(1)}, f32[4,16,1024]{2,1,0:T(8,128)S(1)}, u32[]{:S(2)}, u32[]{:S(2)}) %collective-permute-start.18) | collective-permute-done | bytes 262176 | tf_op jit(solution)/shard_map/ppermute | solution.py:295
  43.1 0.8 %shard_map.77 = f32[2,4,2,16,1024]{4,3,2,1,0:T(8,128)} custom-call(s32[1]{0:T(128)} %bitcast.here_ref.refs_0_, f32[4,16,1024]{2,1,0:T(8,128)S(1)} %collective-permute-done.11.refs_0_, f32[4,16,1024]{2,1,0:T(8,128)S(1)} %collective-permute-done.18.refs_1_, f32[2,4,2,16,1024]{4,3,2,1,0:T(8,128)} %shard_map.76.refs_2_), custom_call_target="tpu_custom_call", output_to_operand_aliasing={{}: (3, {})} | custom-call | tf_op jit(solution)/shard_map/pallas_call | solution.py:304
  (8 shorter events, 0.1 us)
Async XLA Ops:
  0.6 23.0 %copy-start = (f32[32,1,16,1024]{3,2,1,0:T(8,128)S(1)}, f32[32,1,16,1024]{3,2,1,0:T(8,128)}, u32[]{:S(2)}) copy-start(f32[32,1,16,1024]{3,2,1,0:T(8,128)} %param.7) | copy-start | bytes 6291460
  0.6 1.4 %copy-start.1 = (f32[1,2,128,1024]{3,2,1,0:T(8,128)S(1)}, f32[1,2,128,1024]{3,2,1,0:T(8,128)}, u32[]{:S(2)}) copy-start(f32[1,2,128,1024]{3,2,1,0:T(8,128)} %param.4) | copy-start | bytes 3145732
  2.1 11.9 %collective-permute-start.4 = (f32[2,4,16,1024]{3,2,1,0:T(8,128)S(1)}, f32[2,4,16,1024]{3,2,1,0:T(8,128)S(1)}, u32[]{:S(2)}, u32[]{:S(2)}) collective-permute-start(f32[2,4,16,1024]{3,2,1,0:T(8,128)S(1)} %get-tuple-element.32), channel_id=1, source_target_pairs={{0,4},{4,0},{8,12},{12,8},{16,20},{20,16},{24,28},{28,24},{1,5},{5... | collective-permute-start | bytes 1572872 | tf_op jit(solution)/shard_map/ppermute | solution.py:239
  2.6 6.3 %collective-permute-start = (f32[8,128]{1,0:T(8,128)S(1)}, f32[8,128]{1,0:T(8,128)S(1)}, u32[]{:S(2)}, u32[]{:S(2)}) collective-permute-start(f32[8,128]{1,0:T(8,128)S(1)} %get-tuple-element.30.refs_0_), channel_id=1, source_target_pairs={{0,3},{1,2},{2,1},{3,0},{4,7},{5,6},{6,5},{7,4},{8,11},{9,10},{10,... | collective-permute-start | bytes 12296 | tf_op jit(solution)/shard_map/ppermute | solution.py:241
  7.3 4.5 %collective-permute-start.1 = (f32[8,128]{1,0:T(8,128)S(1)}, f32[8,128]{1,0:T(8,128)S(1)}, u32[]{:S(2)}, u32[]{:S(2)}) collective-permute-start(f32[8,128]{1,0:T(8,128)S(1)} %get-tuple-element.30.refs_0_), channel_id=1, source_target_pairs={{0,2},{1,3},{2,0},{3,1},{4,6},{5,7},{6,4},{7,5},{8,10},{9,11},{10,... | collective-permute-start | bytes 12296 | tf_op jit(solution)/shard_map/ppermute | solution.py:241
  7.3 4.5 %collective-permute-start.2 = (f32[8,128]{1,0:T(8,128)S(1)}, f32[8,128]{1,0:T(8,128)S(1)}, u32[]{:S(2)}, u32[]{:S(2)}) collective-permute-start(f32[8,128]{1,0:T(8,128)S(1)} %get-tuple-element.30.refs_0_), channel_id=1, source_target_pairs={{0,1},{1,0},{2,3},{3,2},{4,5},{5,4},{6,7},{7,6},{8,9},{9,8},{10,11... | collective-permute-start | bytes 12296 | tf_op jit(solution)/shard_map/ppermute | solution.py:241
  11.8 2.2 %collective-permute-start.3 = (f32[8,128]{1,0:T(8,128)S(1)}, f32[8,128]{1,0:T(8,128)S(1)}, u32[]{:S(2)}, u32[]{:S(2)}) collective-permute-start(f32[8,128]{1,0:T(8,128)S(1)} %shard_map.69.refs_2_), channel_id=1, source_target_pairs={{0,4},{4,0},{8,12},{12,8},{16,20},{20,16},{24,28},{28,24},{1,5},{5... | collective-permute-start | bytes 12296 | tf_op jit(solution)/shard_map/ppermute | solution.py:244
  11.9 0.7 %copy-start.2 = (s32[8,2]{0,1:T(2,128)S(1)}, s32[8,2]{0,1:T(2,128)}, u32[]{:S(2)}) copy-start(s32[8,2]{0,1:T(2,128)} %param.5) | copy-start | bytes 196
  14.8 7.2 %collective-permute-start.5 = (f32[2,16,1024]{2,1,0:T(8,128)S(1)}, f32[2,16,1024]{2,1,0:T(8,128)S(1)}, u32[]{:S(2)}, u32[]{:S(2)}) collective-permute-start(f32[2,16,1024]{2,1,0:T(8,128)S(1)} %get-tuple-element.33), channel_id=1, source_target_pairs={{0,24},{4,28},{8,16},{12,20},{16,8},{20,12},{24,0},{28,4},{1,25},{... | collective-permute-start | bytes 393224 | tf_op jit(solution)/shard_map/ppermute | solution.py:60
  17.3 8.3 %collective-permute-start.6 = (f32[2,16,1024]{2,1,0:T(8,128)S(1)}, f32[2,16,1024]{2,1,0:T(8,128)S(1)}, u32[]{:S(2)}, u32[]{:S(2)}) collective-permute-start(f32[2,16,1024]{2,1,0:T(8,128)S(1)} %get-tuple-element.34), channel_id=1, source_target_pairs={{0,8},{4,20},{8,0},{12,28},{16,24},{20,4},{24,16},{28,12},{1,9},{5... | collective-permute-start | bytes 393224 | tf_op jit(solution)/shard_map/ppermute | solution.py:60
  17.8 7.8 %collective-permute-start.7 = (f32[2,16,1024]{2,1,0:T(8,128)S(1)}, f32[2,16,1024]{2,1,0:T(8,128)S(1)}, u32[]{:S(2)}, u32[]{:S(2)}) collective-permute-start(f32[2,16,1024]{2,1,0:T(8,128)S(1)} %get-tuple-element.35), channel_id=1, source_target_pairs={{0,16},{4,12},{8,24},{12,4},{16,0},{20,28},{24,8},{28,20},{1,17},{... | collective-permute-start | bytes 393224 | tf_op jit(solution)/shard_map/ppermute | solution.py:60
  18.3 12.0 %collective-permute-start.12 = (f32[2,16,1024]{2,1,0:T(8,128)S(1)}, f32[2,16,1024]{2,1,0:T(8,128)S(1)}, u32[]{:S(2)}, u32[]{:S(2)}) collective-permute-start(f32[2,16,1024]{2,1,0:T(8,128)S(1)} %get-tuple-element.41), channel_id=1, source_target_pairs={{0,24},{4,28},{8,16},{12,20},{16,8},{20,12},{24,0},{28,4},{1,25},{... | collective-permute-start | bytes 393224 | tf_op jit(solution)/shard_map/ppermute | solution.py:60
  20.8 10.2 %collective-permute-start.13 = (f32[2,16,1024]{2,1,0:T(8,128)S(1)}, f32[2,16,1024]{2,1,0:T(8,128)S(1)}, u32[]{:S(2)}, u32[]{:S(2)}) collective-permute-start(f32[2,16,1024]{2,1,0:T(8,128)S(1)} %get-tuple-element.42), channel_id=1, source_target_pairs={{0,8},{4,20},{8,0},{12,28},{16,24},{20,4},{24,16},{28,12},{1,9},{5... | collective-permute-start | bytes 393224 | tf_op jit(solution)/shard_map/ppermute | solution.py:60
  21.9 9.7 %collective-permute-start.14 = (f32[2,16,1024]{2,1,0:T(8,128)S(1)}, f32[2,16,1024]{2,1,0:T(8,128)S(1)}, u32[]{:S(2)}, u32[]{:S(2)}) collective-permute-start(f32[2,16,1024]{2,1,0:T(8,128)S(1)} %get-tuple-element.43), channel_id=1, source_target_pairs={{0,16},{4,12},{8,24},{12,4},{16,0},{20,28},{24,8},{28,20},{1,17},{... | collective-permute-start | bytes 393224 | tf_op jit(solution)/shard_map/ppermute | solution.py:60
  26.4 10.2 %collective-permute-start.8 = (f32[2,16,1024]{2,1,0:T(8,128)S(1)}, f32[2,16,1024]{2,1,0:T(8,128)S(1)}, u32[]{:S(2)}, u32[]{:S(2)}) collective-permute-start(f32[2,16,1024]{2,1,0:T(8,128)S(1)} %get-tuple-element.37), channel_id=1, source_target_pairs={{0,24},{4,28},{8,16},{12,20},{16,8},{20,12},{24,0},{28,4},{1,25},{... | collective-permute-start | bytes 393224 | tf_op jit(solution)/shard_map/ppermute | solution.py:60
  30.3 9.3 %collective-permute-start.9 = (f32[2,16,1024]{2,1,0:T(8,128)S(1)}, f32[2,16,1024]{2,1,0:T(8,128)S(1)}, u32[]{:S(2)}, u32[]{:S(2)}) collective-permute-start(f32[2,16,1024]{2,1,0:T(8,128)S(1)} %get-tuple-element.38), channel_id=1, source_target_pairs={{0,8},{4,20},{8,0},{12,28},{16,24},{20,4},{24,16},{28,12},{1,9},{5... | collective-permute-start | bytes 393224 | tf_op jit(solution)/shard_map/ppermute | solution.py:60
  30.3 9.3 %collective-permute-start.10 = (f32[2,16,1024]{2,1,0:T(8,128)S(1)}, f32[2,16,1024]{2,1,0:T(8,128)S(1)}, u32[]{:S(2)}, u32[]{:S(2)}) collective-permute-start(f32[2,16,1024]{2,1,0:T(8,128)S(1)} %get-tuple-element.39), channel_id=1, source_target_pairs={{0,16},{4,12},{8,24},{12,4},{16,0},{20,28},{24,8},{28,20},{1,17},{... | collective-permute-start | bytes 393224 | tf_op jit(solution)/shard_map/ppermute | solution.py:60
  32.3 7.5 %collective-permute-start.15 = (f32[2,16,1024]{2,1,0:T(8,128)S(1)}, f32[2,16,1024]{2,1,0:T(8,128)S(1)}, u32[]{:S(2)}, u32[]{:S(2)}) collective-permute-start(f32[2,16,1024]{2,1,0:T(8,128)S(1)} %get-tuple-element.45), channel_id=1, source_target_pairs={{0,24},{4,28},{8,16},{12,20},{16,8},{20,12},{24,0},{28,4},{1,25},{... | collective-permute-start | bytes 393224 | tf_op jit(solution)/shard_map/ppermute | solution.py:60
  34.6 6.9 %collective-permute-start.16 = (f32[2,16,1024]{2,1,0:T(8,128)S(1)}, f32[2,16,1024]{2,1,0:T(8,128)S(1)}, u32[]{:S(2)}, u32[]{:S(2)}) collective-permute-start(f32[2,16,1024]{2,1,0:T(8,128)S(1)} %get-tuple-element.46), channel_id=1, source_target_pairs={{0,8},{4,20},{8,0},{12,28},{16,24},{20,4},{24,16},{28,12},{1,9},{5... | collective-permute-start | bytes 393224 | tf_op jit(solution)/shard_map/ppermute | solution.py:60
  36.5 5.0 %collective-permute-start.17 = (f32[2,16,1024]{2,1,0:T(8,128)S(1)}, f32[2,16,1024]{2,1,0:T(8,128)S(1)}, u32[]{:S(2)}, u32[]{:S(2)}) collective-permute-start(f32[2,16,1024]{2,1,0:T(8,128)S(1)} %get-tuple-element.47), channel_id=1, source_target_pairs={{0,16},{4,12},{8,24},{12,4},{16,0},{20,28},{24,8},{28,20},{1,17},{... | collective-permute-start | bytes 393224 | tf_op jit(solution)/shard_map/ppermute | solution.py:60
  39.7 2.8 %collective-permute-start.11 = (f32[4,16,1024]{2,1,0:T(8,128)S(1)}, f32[4,16,1024]{2,1,0:T(8,128)S(1)}, u32[]{:S(2)}, u32[]{:S(2)}) collective-permute-start(f32[4,16,1024]{2,1,0:T(8,128)S(1)} %shard_map.72), channel_id=1, source_target_pairs={{0,4},{4,0},{8,12},{12,8},{16,20},{20,16},{24,28},{28,24},{1,5},{5... | collective-permute-start | bytes 786440 | tf_op jit(solution)/shard_map/ppermute | solution.py:295
  41.5 1.6 %collective-permute-start.18 = (f32[4,16,1024]{2,1,0:T(8,128)S(1)}, f32[4,16,1024]{2,1,0:T(8,128)S(1)}, u32[]{:S(2)}, u32[]{:S(2)}) collective-permute-start(f32[4,16,1024]{2,1,0:T(8,128)S(1)} %shard_map.75), channel_id=1, source_target_pairs={{0,4},{4,0},{8,12},{12,8},{16,20},{20,16},{24,28},{28,24},{1,5},{5... | collective-permute-start | bytes 786440 | tf_op jit(solution)/shard_map/ppermute | solution.py:295

commit v3 on v2

--- a/solution.py
+++ b/solution.py
@@ -7,7 +7,7 @@
 
 LEVEL_MODULES = 16
 LEVELS = 2
-MOST_UNROLLED = 16
+MOST_UNROLLED = 8
 
 outer_rate = 0.7
 beta_coef = 0.9
@@ -64,51 +64,41 @@
     return [(slice(row, row + 8), slice(lane, lane + 128)) for row in range(0, rows, 8) for lane in range(0, width, 128)]
 
 
-def pack_kernel(here_ref, delta_ref, square_ref, keep_ref, give_ref):
-    levels, chips, halves, rows, width = delta_ref.shape
-
-    def pack(core):
-        totals = [jnp.zeros((8, 128), jnp.float32) for _ in range(4)]
-        for level in range(levels):
-            for chip in range(chips):
-                for t, spot in enumerate(tiles_of(rows, width)):
-                    kept = delta_ref[(level, chip, core, *spot)]
-                    given = delta_ref[(level, chip, 1 - core, *spot)]
-                    keep_ref[(level, chip, *spot)] = kept
-                    give_ref[(level, chip, *spot)] = given
-                    totals[t % 4] = totals[t % 4] + (kept * kept + given * given)
-        total = jnp.sum((totals[0] + totals[1]) + (totals[2] + totals[3]), axis=0, keepdims=True)
-        for first in range(0, square_ref.shape[0], 8):
-            row = lax.broadcasted_iota(jnp.int32, (8, 128), 0) + first
-            square_ref[first : first + 8] = jnp.where(row == here_ref[0], total, 0.0)
-
-    for core in range(halves):
-        pl.when(here_ref[0] & 1 == core)(lambda core=core: pack(core))
-
-
-def scale_kernel(entries, here_ref, plan_ref, square_ref, other_ref, keep_ref, gift_ref, *refs):
-    outs, rescale_ref = refs[:-1], refs[-1]
-    here = here_ref[0]
-    core = here & 1
-    rounds = len(outs) // LEVELS
-    size = 2 * rounds
-    total = jnp.sum(square_ref[...] + other_ref[...], axis=1, keepdims=True)
-    rescale_ref[...] = jnp.broadcast_to(1.0 / jnp.sqrt(total / entries + 1e-06), rescale_ref.shape)
-    for half, (rows_ref, source) in enumerate(((keep_ref, core), (gift_ref, 1 - core))):
-        rescale = jnp.broadcast_to(rescale_ref[pl.ds((here // 2) * 2 + source, 1), :], (8, 128))
-        for level in range(LEVELS):
-            sharers = plan_ref[level, 2 * size - 2 + source]
-            factor = rescale / jnp.full((8, 128), sharers, jnp.int32).astype(jnp.float32)
-            for j, k in enumerate(order_of(size)):
-                out = outs[level * rounds + j]
-                chip = target(here, k, size) // 2
-                for spot in tiles_of(*out.shape[1:]):
-                    out[(source, *spot)] = rows_ref[(level, chip, *spot)] * factor
-
-
-def sum_kernel(*refs):
+def pack_kernel(size, here_ref, delta_ref, square_ref, *outs):
+    order = order_of(size)
+    totals = [jnp.zeros((8, 128), jnp.float32) for _ in range(4)]
+    for level in range(LEVELS):
+        for j, k in enumerate(order):
+            out = outs[level * len(order) + j]
+            chip = target(here_ref[0], k, size) // 2
+            for half in range(2):
+                for t, spot in enumerate(tiles_of(*out.shape[1:])):
+                    block = delta_ref[(level, chip, half, *spot)]
+                    out[(half, *spot)] = block
+                    totals[t % 4] = totals[t % 4] + block * block
+    square_ref[...] = (totals[0] + totals[1]) + (totals[2] + totals[3])
+
+
+def scale_kernel(entries, here_ref, plan_ref, square_ref, *refs):
+    count = len(refs) // 2
+    rounds = count // LEVELS
+    give_ref = refs[-1]
+    core = here_ref[0] & 1
+    total = jnp.broadcast_to(jnp.sum(square_ref[...], keepdims=True), (8, 128))
+    rescale = 1.0 / jnp.sqrt(total / entries + 1e-06)
+    for level in range(LEVELS):
+        sharers = plan_ref[level, 2 * rounds + rounds - 1]
+        factor = rescale / jnp.full((8, 128), sharers, jnp.int32).astype(jnp.float32)
+        for j in range(level * rounds, (level + 1) * rounds):
+            for half in range(2):
+                for spot in tiles_of(*refs[j].shape[1:]):
+                    refs[count + j][(half, *spot)] = refs[j][(half, *spot)] * factor
+        give_ref[level] = refs[count + (level + 1) * rounds - 1][1 - core]
+
+
+def sum_kernel(count, *refs):
     total = refs[0][...]
-    for ref in refs[1:-1]:
+    for ref in refs[1:count]:
         total = total + ref[...]
     refs[-1][...] = total
 
@@ -118,7 +108,7 @@
     order = order_of(size)
     here = here_ref[0]
     token_ref[...] = jnp.zeros_like(token_ref)
-    paths = [(origin(here, k, size) // 2) * 2 + half for k in order for half in range(2)]
+    paths = [origin(core, k, size) for core in (here, here ^ 1) for k in order]
     targets = [(target(here, k, size) // 2) * 2 + half for k in order for half in range(2)]
     for level in range(LEVELS):
         first = level * LEVEL_MODULES
@@ -139,11 +129,23 @@
             plan_ref[level, 4 * size + i] = module_ref[module]
 
 
-def outgoing_kernel(level, rounds, plan_ref, decayed_ref, *refs):
-    received, outs, grad_ref = refs[:rounds], refs[rounds:-1], refs[-1]
+def give_kernel(here_ref, *refs):
+    outs = refs[-2:]
+    for j, block in enumerate(refs[:-2]):
+        for part, out in enumerate(outs):
+            out[j] = block[1 - (here_ref[0] & 1), part * out.shape[1] : (part + 1) * out.shape[1]]
+
+
+def outgoing_kernel(level, rounds, here_ref, plan_ref, decayed_ref, own_ref, *refs):
+    received, parts, outs, grad_ref = refs[:rounds], refs[rounds : rounds + 2], refs[rounds + 2 : -1], refs[-1]
     size = 2 * rounds
-    for i in range(size):
-        grad_ref[i] = received[i // 2][i % 2]
+    core = here_ref[0] & 1
+    for j in range(rounds):
+        grad_ref[j] = received[j][core]
+    for j in range(rounds - 1):
+        for part, ref in enumerate(parts):
+            grad_ref[rounds + j, part * ref.shape[1] : (part + 1) * ref.shape[1]] = ref[j]
+    grad_ref[size - 1] = own_ref[level]
     for i in range(1, size):
         leader = plan_ref[level, i]
 
@@ -229,19 +231,15 @@
     rounds = len(order)
     swap = [(i, i ^ 1) for i in range(size)]
     shape = lambda *dims: jax.ShapeDtypeStruct(dims, jnp.float32)
-    squares_shape = shape(-(-size // 8) * 8, 128)
-    by_chip = shape(LEVELS, rounds, own_rows, width)
+    squares_shape = shape(8, 128)
     message = shape(2, own_rows, width)
 
-    squares, keep, give = call(pack_kernel, [squares_shape, by_chip, by_chip], [smem, vmem], [vmem] * 3)(
-        here, split_slab
-    )
-    gift = lax.ppermute(give, "path", swap)
-    tiles = [squares] + [
-        lax.ppermute(squares, "shard", [(i, i ^ step) for i in range(shards)]) for step in range(shards - 1, 0, -1)
-    ]
-    squares = call(sum_kernel, squares_shape, [vmem] * shards, vmem)(*tiles)
-    other = lax.ppermute(squares, "path", swap)
+    squares, *raw = call(
+        lambda *refs: pack_kernel(size, *refs),
+        [squares_shape] + [message] * (LEVELS * rounds),
+        [smem, vmem],
+        [vmem] * (1 + LEVELS * rounds),
+    )(here, split_slab)
     plan, leaders, planned = call(
         plan_kernel,
         [
@@ -252,24 +250,34 @@
         [smem, smem],
         [smem, smem, vmem],
     )(here, assign.T)
-    messages = call(
+    tiles = [squares] + [
+        lax.ppermute(squares, "shard", [(i, i ^ step) for i in range(shards)]) for step in range(shards - 1, 0, -1)
+    ]
+    squares = call(
+        lambda *refs: sum_kernel(shards, *refs), squares_shape, [vmem] * shards + [anywhere], vmem
+    )(*tiles, planned)
+    *messages, give = call(
         lambda *refs: scale_kernel(entries, *refs),
-        [message] * (LEVELS * rounds),
-        [smem, smem, vmem, vmem, vmem, vmem],
-        [vmem] * (LEVELS * rounds),
-        scratch_shapes=[pltpu.VMEM(squares_shape.shape, jnp.float32)],
-    )(here, plan, squares, other, keep, gift)
+        [message] * (LEVELS * rounds) + [shape(LEVELS, own_rows, width)],
+        [smem, smem] + [vmem] * (1 + LEVELS * rounds),
+        [vmem] * (LEVELS * rounds + 1),
+    )(here, plan, squares, *raw)
+    own = lax.ppermute(give, "path", swap)
     decayed = state_in - moment_coef * moment_in
 
     returned, grads = [], []
     for level in range(LEVELS):
         received = [move(messages[level * rounds + j], k, size) for j, k in enumerate(order)]
+        parts = call(
+            give_kernel, [shape(rounds - 1, own_rows // 2, width)] * 2, [smem] + [vmem] * (rounds - 1), [vmem] * 2
+        )(here, *received[:-1])
+        parts = [lax.ppermute(part, "path", swap) for part in parts]
         *outgoing, grad = call(
             lambda *refs, level=level: outgoing_kernel(level, rounds, *refs),
             [message] * rounds + [shape(size, own_rows, width)],
-            [smem] + [vmem] * (1 + rounds),
+            [smem, smem] + [vmem] * (4 + rounds),
             [vmem] * (rounds + 1),
-        )(plan, decayed, *received)
+        )(here, plan, decayed, own, *received, *parts)
         returned.append([move(outgoing[j], k, size) for j, k in enumerate(order)])
         grads.append(grad)
 

time: 44.1 us -> 44.6 us (1.011)
  starting transfers between devices: 23 us -> 23.6 us
    ppermute x3, waiting for transfers between devices: 3.87 us -> 1.76 us  [local(): lax.ppermute(squares, 'shard', [(i, i ^ step) for i in range(shards)])]
    ppermute x12, waiting for transfers between devices: 3.03 us -> 4.59 us  [move(): lax.ppermute(array, 'path', [(i, target(i, k, size)) for i in range(size)])]
    ppermute x2 -> x5, starting transfers between devices: 0.58 us -> 1.13 us  [the longest x4 1.13 us: local(): parts = [lax.ppermute(part, 'path', swap) for part in parts]]
  transfers between devices with their start and end apart: 19 -> 22, of which waited for: 7 -> 8; matrix products, arithmetic and copies ran while one was open for 5% -> 5% of each run, Pallas kernels for 16% -> 15%
where the time goes in v3:
time: 44.6 us; the launch traced here: 44.4 us
  starting transfers between devices  23.6 us (53%)
  Pallas kernels  8.61 us (19%)
  waiting for transfers between devices  7.35 us (16%)
  local copies, waits for them, and re-layouts  2.05 us (5%)
  other arithmetic  2.03 us (5%)
  between operations  0.82 us (2%)
    ppermute x12, starting transfers between devices, move(): lax.ppermute(array, 'path', [(i, target(i, k, size)) for i in range(size)])  16.5 us
    ppermute x3, starting transfers between devices, local(): lax.ppermute(squares, 'shard', [(i, i ^ step) for i in range(shards)])  5.76 us
    ppermute x12, waiting for transfers between devices, move(): lax.ppermute(array, 'path', [(i, target(i, k, size)) for i in range(size)])  4.59 us
    pallas_call x1, Pallas kernels, local(): call(state_kernel, [shape(*state_in.shape)] * 2 + [shape(8, 128)], [smem]...  3.09 us
    unnamed x6, local copies, waits for them, and re-layouts  2.05 us
    sub x1, other arithmetic, local(): decayed = state_in - moment_coef * moment_in  2.03 us
    ppermute x3, waiting for transfers between devices, local(): lax.ppermute(squares, 'shard', [(i, i ^ step) for i in range(shards)])  1.76 us
    pallas_call x2, Pallas kernels, local(): call(lambda *refs, level=level: outgoing_kernel(level, rounds, *refs), [m...  1.43 us
  transfers between devices with their start and end apart: 22, of which 8 were waited for; matrix products, arithmetic and copies ran while one was open for 5% of the time, Pallas kernels for 15%

profile of v3, /device:TPU:0, one launch (start us, length us, event | category | flops | bytes accessed | tf_op | source)
XLA Modules:
  0.0 44.4 jit_solution(15243535646690384089)
XLA Ops:
  0.7 1.4 %copy-done.1 = f32[1,2,128,1024]{3,2,1,0:T(8,128)S(1)} copy-done((f32[1,2,128,1024]{3,2,1,0:T(8,128)S(1)}, f32[1,2,128,1024]{3,2,1,0:T(8,128)}, u32[]{:S(2)}) %copy-start.1) | copy-done | bytes 1048600
  2.0 0.1 shard_map.68
  2.1 5.1 %collective-permute-start = (f32[8,128]{1,0:T(8,128)S(1)}, f32[8,128]{1,0:T(8,128)S(1)}, u32[]{:S(2)}, u32[]{:S(2)}) collective-permute-start(f32[8,128]{1,0:T(8,128)S(1)} %get-tuple-element.42.refs_0_), channel_id=1, source_target_pairs={{0,3},{1,2},{2,1},{3,0},{4,7},{5,6},{6,5},{7,4},{8,11},{9,10},{10,... | collective-permute-start | bytes 12296 | tf_op jit(solution)/shard_map/ppermute | solution.py:254
  7.2 0.0 collective-permute-start.1
  7.2 0.6 %collective-permute-start.2 = (f32[8,128]{1,0:T(8,128)S(1)}, f32[8,128]{1,0:T(8,128)S(1)}, u32[]{:S(2)}, u32[]{:S(2)}) collective-permute-start(f32[8,128]{1,0:T(8,128)S(1)} %get-tuple-element.42.refs_0_), channel_id=1, source_target_pairs={{0,1},{1,0},{2,3},{3,2},{4,5},{5,4},{6,7},{7,6},{8,9},{9,8},{10,11... | collective-permute-start | bytes 12296 | tf_op jit(solution)/shard_map/ppermute | solution.py:254
  7.9 0.7 %copy-done.2 = s32[8,2]{0,1:T(2,128)S(1)} copy-done((s32[8,2]{0,1:T(2,128)S(1)}, s32[8,2]{0,1:T(2,128)}, u32[]{:S(2)}) %copy-start.2) | copy-done | bytes 88
  8.6 1.4 %shard_map.67 = (s32[2,40]{1,0:T(2,128)S(1)}, s32[32]{0:T(128)S(1)}, f32[8,128]{1,0:T(8,128)S(1)}) custom-call(s32[1]{0:T(128)} %bitcast.here_ref.refs_0_, s32[2,8]{1,0:T(2,128)S(1)} %bitcast.16), custom_call_target="tpu_custom_call" | custom-call | tf_op jit(solution)/shard_map/pallas_call | solution.py:243
  10.0 0.0 collective-permute-done.refs_1_
  10.0 1.8 %collective-permute-done.1.refs_2_ = f32[8,128]{1,0:T(8,128)S(1)} collective-permute-done((f32[8,128]{1,0:T(8,128)S(1)}, f32[8,128]{1,0:T(8,128)S(1)}, u32[]{:S(2)}, u32[]{:S(2)}) %collective-permute-start.1) | collective-permute-done | bytes 4128 | tf_op jit(solution)/shard_map/ppermute | solution.py:254
  11.7 0.0 collective-permute-done.2.refs_3_
  11.8 0.8 %shard_map.70 = (f32[2,16,1024]{2,1,0:T(8,128)S(1)}, f32[2,16,1024]{2,1,0:T(8,128)S(1)}, f32[2,16,1024]{2,1,0:T(8,128)S(1)}, f32[2,16,1024]{2,1,0:T(8,128)S(1)},...) custom-call(s32[1]{0:T(128)} %bitcast.here_ref.refs_0_, ...), custom_call_target="tpu_custom_call" | custom-call | tf_op jit(solution)/shard_map/pallas_call | solution.py:259
  12.5 2.5 %collective-permute-start.4 = (f32[2,16,1024]{2,1,0:T(8,128)S(1)}, f32[2,16,1024]{2,1,0:T(8,128)S(1)}, u32[]{:S(2)}, u32[]{:S(2)}) collective-permute-start(f32[2,16,1024]{2,1,0:T(8,128)S(1)} %get-tuple-element.53), channel_id=1, source_target_pairs={{0,24},{4,28},{8,16},{12,20},{16,8},{20,12},{24,0},{28,4},{1,25},{... | collective-permute-start | bytes 393224 | tf_op jit(solution)/shard_map/ppermute | solution.py:60
  15.0 0.5 %collective-permute-start.5 = (f32[2,16,1024]{2,1,0:T(8,128)S(1)}, f32[2,16,1024]{2,1,0:T(8,128)S(1)}, u32[]{:S(2)}, u32[]{:S(2)}) collective-permute-start(f32[2,16,1024]{2,1,0:T(8,128)S(1)} %get-tuple-element.54), channel_id=1, source_target_pairs={{0,8},{4,20},{8,0},{12,28},{16,24},{20,4},{24,16},{28,12},{1,9},{5... | collective-permute-start | bytes 393224 | tf_op jit(solution)/shard_map/ppermute | solution.py:60
  15.6 0.5 %collective-permute-start.6 = (f32[2,16,1024]{2,1,0:T(8,128)S(1)}, f32[2,16,1024]{2,1,0:T(8,128)S(1)}, u32[]{:S(2)}, u32[]{:S(2)}) collective-permute-start(f32[2,16,1024]{2,1,0:T(8,128)S(1)} %get-tuple-element.55), channel_id=1, source_target_pairs={{0,16},{4,12},{8,24},{12,4},{16,0},{20,28},{24,8},{28,20},{1,17},{... | collective-permute-start | bytes 393224 | tf_op jit(solution)/shard_map/ppermute | solution.py:60
  16.1 0.0 collective-permute-start.3
  16.1 2.4 %collective-permute-start.13 = (f32[2,16,1024]{2,1,0:T(8,128)S(1)}, f32[2,16,1024]{2,1,0:T(8,128)S(1)}, u32[]{:S(2)}, u32[]{:S(2)}) collective-permute-start(f32[2,16,1024]{2,1,0:T(8,128)S(1)} %get-tuple-element.63), channel_id=1, source_target_pairs={{0,24},{4,28},{8,16},{12,20},{16,8},{20,12},{24,0},{28,4},{1,25},{... | collective-permute-start | bytes 393224 | tf_op jit(solution)/shard_map/ppermute | solution.py:60
  18.5 1.3 %collective-permute-done.4.refs_0_.refs_4_ = f32[2,16,1024]{2,1,0:T(8,128)S(1)} collective-permute-done((f32[2,16,1024]{2,1,0:T(8,128)S(1)}, f32[2,16,1024]{2,1,0:T(8,128)S(1)}, u32[]{:S(2)}, u32[]{:S(2)}) %collective-permute-start.4) | collective-permute-done | bytes 131104 | tf_op jit(solution)/shard_map/ppermute | solution.py:60
  19.9 0.4 collective-permute-start.14
  20.3 2.4 %collective-permute-start.15 = (f32[2,16,1024]{2,1,0:T(8,128)S(1)}, f32[2,16,1024]{2,1,0:T(8,128)S(1)}, u32[]{:S(2)}, u32[]{:S(2)}) collective-permute-start(f32[2,16,1024]{2,1,0:T(8,128)S(1)} %get-tuple-element.65), channel_id=1, source_target_pairs={{0,16},{4,12},{8,24},{12,4},{16,0},{20,28},{24,8},{28,20},{1,17},{... | collective-permute-start | bytes 393224 | tf_op jit(solution)/shard_map/ppermute | solution.py:60
  22.7 0.0 collective-permute-done.6.refs_2_.refs_6_
  22.7 0.1 collective-permute-start.7
  22.8 0.0 collective-permute-done.3.refs_3_
  22.8 0.5 %collective-permute-start.8 = (f32[3,8,1024]{2,1,0:T(8,128)S(1)}, f32[3,8,1024]{2,1,0:T(8,128)S(1)}, u32[]{:S(2)}, u32[]{:S(2)}) collective-permute-start(f32[3,8,1024]{2,1,0:T(8,128)S(1)} %get-tuple-element.58), channel_id=1, source_target_pairs={{0,4},{4,0},{8,12},{12,8},{16,20},{20,16},{24,28},{28,24},{1,5},{5... | collective-permute-start | bytes 294920 | tf_op jit(solution)/shard_map/ppermute | solution.py:274
  23.3 2.0 %bitcast_subtract_fusion.refs_2_ = f32[32,16,1024]{2,1,0:T(8,128)S(1)} fusion(f32[32,1,16,1024]{3,2,1,0:T(8,128)} %param.6, f32[32,1,16,1024]{3,2,1,0:T(8,128)S(1)} %copy-done), kind=kLoop, calls=%fused_computation | loop fusion | flops 1048576 | bytes 6291456 | tf_op jit(solution)/shard_map/sub | solution.py:266
  25.4 0.0 collective-permute-done.7.refs_8_
  25.4 0.7 %shard_map.72 = (f32[2,16,1024]{2,1,0:T(8,128)S(1)}, f32[2,16,1024]{2,1,0:T(8,128)S(1)}, f32[2,16,1024]{2,1,0:T(8,128)S(1)}, f32[2,16,1024]{2,1,0:T(8,128)S(1)}, f32[8,16,1024]{2,1,0:T(8,128)S(1)}) custom-call(s32[1]{0:T(128)} %bitcast.here_ref.refs_0_, s32[2,40]{1,0:T(2,128)S(1)} %get-tuple-element.41.refs_1_, ...), custom_call_target="tpu_custom_call" | custom-call | tf_op jit(solution)/shard_map/pallas_call | solution.py:275
  26.1 3.5 %collective-permute-start.9 = (f32[2,16,1024]{2,1,0:T(8,128)S(1)}, f32[2,16,1024]{2,1,0:T(8,128)S(1)}, u32[]{:S(2)}, u32[]{:S(2)}) collective-permute-start(f32[2,16,1024]{2,1,0:T(8,128)S(1)} %get-tuple-element.59), channel_id=1, source_target_pairs={{0,24},{4,28},{8,16},{12,20},{16,8},{20,12},{24,0},{28,4},{1,25},{... | collective-permute-start | bytes 393224 | tf_op jit(solution)/shard_map/ppermute | solution.py:60
  29.6 0.0 collective-permute-done.13.refs_0_.refs_4_
  29.6 0.0 collective-permute-done.14.refs_1_.refs_5_
  29.6 0.0 collective-permute-done.15.refs_2_.refs_6_
  29.6 0.1 collective-permute-start.16
  29.7 0.5 %collective-permute-start.17 = (f32[3,8,1024]{2,1,0:T(8,128)S(1)}, f32[3,8,1024]{2,1,0:T(8,128)S(1)}, u32[]{:S(2)}, u32[]{:S(2)}) collective-permute-start(f32[3,8,1024]{2,1,0:T(8,128)S(1)} %get-tuple-element.68), channel_id=1, source_target_pairs={{0,4},{4,0},{8,12},{12,8},{16,20},{20,16},{24,28},{28,24},{1,5},{5... | collective-permute-start | bytes 294920 | tf_op jit(solution)/shard_map/ppermute | solution.py:274
  30.2 0.6 %collective-permute-start.11 = (f32[2,16,1024]{2,1,0:T(8,128)S(1)}, f32[2,16,1024]{2,1,0:T(8,128)S(1)}, u32[]{:S(2)}, u32[]{:S(2)}) collective-permute-start(f32[2,16,1024]{2,1,0:T(8,128)S(1)} %get-tuple-element.61), channel_id=1, source_target_pairs={{0,16},{4,12},{8,24},{12,4},{16,0},{20,28},{24,8},{28,20},{1,17},{... | collective-permute-start | bytes 393224 | tf_op jit(solution)/shard_map/ppermute | solution.py:60
  30.8 0.2 collective-permute-done.16.refs_8_
  31.0 0.2 collective-permute-done.17.refs_9_
  31.1 0.7 %shard_map.75 = (f32[2,16,1024]{2,1,0:T(8,128)S(1)}, f32[2,16,1024]{2,1,0:T(8,128)S(1)}, f32[2,16,1024]{2,1,0:T(8,128)S(1)}, f32[2,16,1024]{2,1,0:T(8,128)S(1)}, f32[8,16,1024]{2,1,0:T(8,128)S(1)}) custom-call(s32[1]{0:T(128)} %bitcast.here_ref.refs_0_, s32[2,40]{1,0:T(2,128)S(1)} %get-tuple-element.41.refs_1_, ...), custom_call_target="tpu_custom_call" | custom-call | tf_op jit(solution)/shard_map/pallas_call | solution.py:275
  31.9 2.6 %collective-permute-start.18 = (f32[2,16,1024]{2,1,0:T(8,128)S(1)}, f32[2,16,1024]{2,1,0:T(8,128)S(1)}, u32[]{:S(2)}, u32[]{:S(2)}) collective-permute-start(f32[2,16,1024]{2,1,0:T(8,128)S(1)} %get-tuple-element.69), channel_id=1, source_target_pairs={{0,24},{4,28},{8,16},{12,20},{16,8},{20,12},{24,0},{28,4},{1,25},{... | collective-permute-start | bytes 393224 | tf_op jit(solution)/shard_map/ppermute | solution.py:60
  34.5 0.0 collective-permute-start.19
  34.5 1.0 %collective-permute-start.20 = (f32[2,16,1024]{2,1,0:T(8,128)S(1)}, f32[2,16,1024]{2,1,0:T(8,128)S(1)}, u32[]{:S(2)}, u32[]{:S(2)}) collective-permute-start(f32[2,16,1024]{2,1,0:T(8,128)S(1)} %get-tuple-element.71), channel_id=1, source_target_pairs={{0,16},{4,12},{8,24},{12,4},{16,0},{20,28},{24,8},{28,20},{1,17},{... | collective-permute-start | bytes 393224 | tf_op jit(solution)/shard_map/ppermute | solution.py:60
  35.5 3.1 %shard_map.76 = (f32[32,16,1024]{2,1,0:T(8,128)}, f32[32,16,1024]{2,1,0:T(8,128)}, f32[8,128]{1,0:T(8,128)S(1)}) custom-call(s32[32]{0:T(128)S(1)} %get-tuple-element.73.module_ref, f32[8,16,1024]{2,1,0:T(8,128)S(1)} %get-tuple-element.74.refs_0_, f32[8,16,1024]{2,1,0:T(8,128)S(1)} %get-tuple-element.75.refs_1_, ...), custom_call_target="tpu_custom_call" | custom-call | tf_op jit(solution)/shard_map/pallas_call | solution.py:286
  38.6 0.1 collective-permute-start.12
  38.7 0.6 %collective-permute-done.18.refs_1_.refs_5_ = f32[2,16,1024]{2,1,0:T(8,128)S(1)} collective-permute-done((f32[2,16,1024]{2,1,0:T(8,128)S(1)}, f32[2,16,1024]{2,1,0:T(8,128)S(1)}, u32[]{:S(2)}, u32[]{:S(2)}) %collective-permute-start.18) | collective-permute-done | bytes 131104 | tf_op jit(solution)/shard_map/ppermute | solution.py:60
  39.3 2.1 %collective-permute-done.19.refs_2_.refs_6_ = f32[2,16,1024]{2,1,0:T(8,128)S(1)} collective-permute-done((f32[2,16,1024]{2,1,0:T(8,128)S(1)}, f32[2,16,1024]{2,1,0:T(8,128)S(1)}, u32[]{:S(2)}, u32[]{:S(2)}) %collective-permute-start.19) | collective-permute-done | bytes 131104 | tf_op jit(solution)/shard_map/ppermute | solution.py:60
  41.4 0.5 %collective-permute-done.20.refs_3_.refs_7_ = f32[2,16,1024]{2,1,0:T(8,128)S(1)} collective-permute-done((f32[2,16,1024]{2,1,0:T(8,128)S(1)}, f32[2,16,1024]{2,1,0:T(8,128)S(1)}, u32[]{:S(2)}, u32[]{:S(2)}) %collective-permute-start.20) | collective-permute-done | bytes 131104 | tf_op jit(solution)/shard_map/ppermute | solution.py:60
  42.0 0.1 collective-permute-start.21
  42.0 0.9 %shard_map.78.refs_2_ = f32[2,4,2,16,1024]{4,3,2,1,0:T(8,128)} custom-call(s32[1]{0:T(128)} %bitcast.here_ref.refs_0_, f32[2,16,1024]{2,1,0:T(8,128)S(1)} %collective-permute-done.9.refs_1_, f32[2,16,1024]{2,1,0:T(8,128)S(1)} %collective-permute-done.10.refs_2_, f32[2,16,1024]{2,1,0:T(8,128)S(1)} %collective-permute-done.11.refs_3_, ...), custom_call_target="tpu_custom_call" | custom-call | tf_op jit(solution)/shard_map/pallas_call | solution.py:305
  42.9 0.6 %collective-permute-done.21.refs_1_ = f32[4,16,1024]{2,1,0:T(8,128)S(1)} collective-permute-done((f32[4,16,1024]{2,1,0:T(8,128)S(1)}, f32[4,16,1024]{2,1,0:T(8,128)S(1)}, u32[]{:S(2)}, u32[]{:S(2)}) %collective-permute-start.21) | collective-permute-done | bytes 262176 | tf_op jit(solution)/shard_map/ppermute | solution.py:303
  43.6 0.8 %shard_map.79 = f32[2,4,2,16,1024]{4,3,2,1,0:T(8,128)} custom-call(s32[1]{0:T(128)} %bitcast.here_ref.refs_0_, f32[4,16,1024]{2,1,0:T(8,128)S(1)} %collective-permute-done.12.refs_0_, f32[4,16,1024]{2,1,0:T(8,128)S(1)} %collective-permute-done.21.refs_1_, f32[2,4,2,16,1024]{4,3,2,1,0:T(8,128)} %shard_map.78.refs_2_), custom_call_target="tpu_custom_call", output_to_operand_aliasing={{}: (3, {})} | custom-call | tf_op jit(solution)/shard_map/pallas_call | solution.py:312
  (16 shorter events, 0.1 us)
Async XLA Ops:
  0.6 22.7 %copy-start = (f32[32,1,16,1024]{3,2,1,0:T(8,128)S(1)}, f32[32,1,16,1024]{3,2,1,0:T(8,128)}, u32[]{:S(2)}) copy-start(f32[32,1,16,1024]{3,2,1,0:T(8,128)} %param.7) | copy-start | bytes 6291460
  0.6 1.4 %copy-start.1 = (f32[1,2,128,1024]{3,2,1,0:T(8,128)S(1)}, f32[1,2,128,1024]{3,2,1,0:T(8,128)}, u32[]{:S(2)}) copy-start(f32[1,2,128,1024]{3,2,1,0:T(8,128)} %param.4) | copy-start | bytes 3145732
  2.1 7.9 %collective-permute-start = (f32[8,128]{1,0:T(8,128)S(1)}, f32[8,128]{1,0:T(8,128)S(1)}, u32[]{:S(2)}, u32[]{:S(2)}) collective-permute-start(f32[8,128]{1,0:T(8,128)S(1)} %get-tuple-element.42.refs_0_), channel_id=1, source_target_pairs={{0,3},{1,2},{2,1},{3,0},{4,7},{5,6},{6,5},{7,4},{8,11},{9,10},{10,... | collective-permute-start | bytes 12296 | tf_op jit(solution)/shard_map/ppermute | solution.py:254
  7.2 4.5 %collective-permute-start.1 = (f32[8,128]{1,0:T(8,128)S(1)}, f32[8,128]{1,0:T(8,128)S(1)}, u32[]{:S(2)}, u32[]{:S(2)}) collective-permute-start(f32[8,128]{1,0:T(8,128)S(1)} %get-tuple-element.42.refs_0_), channel_id=1, source_target_pairs={{0,2},{1,3},{2,0},{3,1},{4,6},{5,7},{6,4},{7,5},{8,10},{9,11},{10,... | collective-permute-start | bytes 12296 | tf_op jit(solution)/shard_map/ppermute | solution.py:254
  7.2 4.5 %collective-permute-start.2 = (f32[8,128]{1,0:T(8,128)S(1)}, f32[8,128]{1,0:T(8,128)S(1)}, u32[]{:S(2)}, u32[]{:S(2)}) collective-permute-start(f32[8,128]{1,0:T(8,128)S(1)} %get-tuple-element.42.refs_0_), channel_id=1, source_target_pairs={{0,1},{1,0},{2,3},{3,2},{4,5},{5,4},{6,7},{7,6},{8,9},{9,8},{10,11... | collective-permute-start | bytes 12296 | tf_op jit(solution)/shard_map/ppermute | solution.py:254
  7.9 0.7 %copy-start.2 = (s32[8,2]{0,1:T(2,128)S(1)}, s32[8,2]{0,1:T(2,128)}, u32[]{:S(2)}) copy-start(s32[8,2]{0,1:T(2,128)} %param.5) | copy-start | bytes 196
  12.5 7.3 %collective-permute-start.4 = (f32[2,16,1024]{2,1,0:T(8,128)S(1)}, f32[2,16,1024]{2,1,0:T(8,128)S(1)}, u32[]{:S(2)}, u32[]{:S(2)}) collective-permute-start(f32[2,16,1024]{2,1,0:T(8,128)S(1)} %get-tuple-element.53), channel_id=1, source_target_pairs={{0,24},{4,28},{8,16},{12,20},{16,8},{20,12},{24,0},{28,4},{1,25},{... | collective-permute-start | bytes 393224 | tf_op jit(solution)/shard_map/ppermute | solution.py:60
  15.0 5.2 %collective-permute-start.5 = (f32[2,16,1024]{2,1,0:T(8,128)S(1)}, f32[2,16,1024]{2,1,0:T(8,128)S(1)}, u32[]{:S(2)}, u32[]{:S(2)}) collective-permute-start(f32[2,16,1024]{2,1,0:T(8,128)S(1)} %get-tuple-element.54), channel_id=1, source_target_pairs={{0,8},{4,20},{8,0},{12,28},{16,24},{20,4},{24,16},{28,12},{1,9},{5... | collective-permute-start | bytes 393224 | tf_op jit(solution)/shard_map/ppermute | solution.py:60
  15.6 7.1 %collective-permute-start.6 = (f32[2,16,1024]{2,1,0:T(8,128)S(1)}, f32[2,16,1024]{2,1,0:T(8,128)S(1)}, u32[]{:S(2)}, u32[]{:S(2)}) collective-permute-start(f32[2,16,1024]{2,1,0:T(8,128)S(1)} %get-tuple-element.55), channel_id=1, source_target_pairs={{0,16},{4,12},{8,24},{12,4},{16,0},{20,28},{24,8},{28,20},{1,17},{... | collective-permute-start | bytes 393224 | tf_op jit(solution)/shard_map/ppermute | solution.py:60
  16.1 6.7 %collective-permute-start.3 = (f32[2,16,1024]{2,1,0:T(8,128)S(1)}, f32[2,16,1024]{2,1,0:T(8,128)S(1)}, u32[]{:S(2)}, u32[]{:S(2)}) collective-permute-start(f32[2,16,1024]{2,1,0:T(8,128)S(1)} %get-tuple-element.52), channel_id=1, source_target_pairs={{0,4},{4,0},{8,12},{12,8},{16,20},{20,16},{24,28},{28,24},{1,5},{5... | collective-permute-start | bytes 393224 | tf_op jit(solution)/shard_map/ppermute | solution.py:265
  16.1 13.5 %collective-permute-start.13 = (f32[2,16,1024]{2,1,0:T(8,128)S(1)}, f32[2,16,1024]{2,1,0:T(8,128)S(1)}, u32[]{:S(2)}, u32[]{:S(2)}) collective-permute-start(f32[2,16,1024]{2,1,0:T(8,128)S(1)} %get-tuple-element.63), channel_id=1, source_target_pairs={{0,24},{4,28},{8,16},{12,20},{16,8},{20,12},{24,0},{28,4},{1,25},{... | collective-permute-start | bytes 393224 | tf_op jit(solution)/shard_map/ppermute | solution.py:60
  19.9 9.7 %collective-permute-start.14 = (f32[2,16,1024]{2,1,0:T(8,128)S(1)}, f32[2,16,1024]{2,1,0:T(8,128)S(1)}, u32[]{:S(2)}, u32[]{:S(2)}) collective-permute-start(f32[2,16,1024]{2,1,0:T(8,128)S(1)} %get-tuple-element.64), channel_id=1, source_target_pairs={{0,8},{4,20},{8,0},{12,28},{16,24},{20,4},{24,16},{28,12},{1,9},{5... | collective-permute-start | bytes 393224 | tf_op jit(solution)/shard_map/ppermute | solution.py:60
  20.3 9.3 %collective-permute-start.15 = (f32[2,16,1024]{2,1,0:T(8,128)S(1)}, f32[2,16,1024]{2,1,0:T(8,128)S(1)}, u32[]{:S(2)}, u32[]{:S(2)}) collective-permute-start(f32[2,16,1024]{2,1,0:T(8,128)S(1)} %get-tuple-element.65), channel_id=1, source_target_pairs={{0,16},{4,12},{8,24},{12,4},{16,0},{20,28},{24,8},{28,20},{1,17},{... | collective-permute-start | bytes 393224 | tf_op jit(solution)/shard_map/ppermute | solution.py:60
  22.7 2.6 %collective-permute-start.7 = (f32[3,8,1024]{2,1,0:T(8,128)S(1)}, f32[3,8,1024]{2,1,0:T(8,128)S(1)}, u32[]{:S(2)}, u32[]{:S(2)}) collective-permute-start(f32[3,8,1024]{2,1,0:T(8,128)S(1)} %get-tuple-element.57), channel_id=1, source_target_pairs={{0,4},{4,0},{8,12},{12,8},{16,20},{20,16},{24,28},{28,24},{1,5},{5... | collective-permute-start | bytes 294920 | tf_op jit(solution)/shard_map/ppermute | solution.py:274
  22.8 2.5 %collective-permute-start.8 = (f32[3,8,1024]{2,1,0:T(8,128)S(1)}, f32[3,8,1024]{2,1,0:T(8,128)S(1)}, u32[]{:S(2)}, u32[]{:S(2)}) collective-permute-start(f32[3,8,1024]{2,1,0:T(8,128)S(1)} %get-tuple-element.58), channel_id=1, source_target_pairs={{0,4},{4,0},{8,12},{12,8},{16,20},{20,16},{24,28},{28,24},{1,5},{5... | collective-permute-start | bytes 294920 | tf_op jit(solution)/shard_map/ppermute | solution.py:274
  26.1 8.4 %collective-permute-start.9 = (f32[2,16,1024]{2,1,0:T(8,128)S(1)}, f32[2,16,1024]{2,1,0:T(8,128)S(1)}, u32[]{:S(2)}, u32[]{:S(2)}) collective-permute-start(f32[2,16,1024]{2,1,0:T(8,128)S(1)} %get-tuple-element.59), channel_id=1, source_target_pairs={{0,24},{4,28},{8,16},{12,20},{16,8},{20,12},{24,0},{28,4},{1,25},{... | collective-permute-start | bytes 393224 | tf_op jit(solution)/shard_map/ppermute | solution.py:60
  29.6 1.4 %collective-permute-start.16 = (f32[3,8,1024]{2,1,0:T(8,128)S(1)}, f32[3,8,1024]{2,1,0:T(8,128)S(1)}, u32[]{:S(2)}, u32[]{:S(2)}) collective-permute-start(f32[3,8,1024]{2,1,0:T(8,128)S(1)} %get-tuple-element.67), channel_id=1, source_target_pairs={{0,4},{4,0},{8,12},{12,8},{16,20},{20,16},{24,28},{28,24},{1,5},{5... | collective-permute-start | bytes 294920 | tf_op jit(solution)/shard_map/ppermute | solution.py:274
  29.7 1.4 %collective-permute-start.17 = (f32[3,8,1024]{2,1,0:T(8,128)S(1)}, f32[3,8,1024]{2,1,0:T(8,128)S(1)}, u32[]{:S(2)}, u32[]{:S(2)}) collective-permute-start(f32[3,8,1024]{2,1,0:T(8,128)S(1)} %get-tuple-element.68), channel_id=1, source_target_pairs={{0,4},{4,0},{8,12},{12,8},{16,20},{20,16},{24,28},{28,24},{1,5},{5... | collective-permute-start | bytes 294920 | tf_op jit(solution)/shard_map/ppermute | solution.py:274
  30.2 8.4 %collective-permute-start.10 = (f32[2,16,1024]{2,1,0:T(8,128)S(1)}, f32[2,16,1024]{2,1,0:T(8,128)S(1)}, u32[]{:S(2)}, u32[]{:S(2)}) collective-permute-start(f32[2,16,1024]{2,1,0:T(8,128)S(1)} %get-tuple-element.60), channel_id=1, source_target_pairs={{0,8},{4,20},{8,0},{12,28},{16,24},{20,4},{24,16},{28,12},{1,9},{5... | collective-permute-start | bytes 393224 | tf_op jit(solution)/shard_map/ppermute | solution.py:60
  30.2 8.4 %collective-permute-start.11 = (f32[2,16,1024]{2,1,0:T(8,128)S(1)}, f32[2,16,1024]{2,1,0:T(8,128)S(1)}, u32[]{:S(2)}, u32[]{:S(2)}) collective-permute-start(f32[2,16,1024]{2,1,0:T(8,128)S(1)} %get-tuple-element.61), channel_id=1, source_target_pairs={{0,16},{4,12},{8,24},{12,4},{16,0},{20,28},{24,8},{28,20},{1,17},{... | collective-permute-start | bytes 393224 | tf_op jit(solution)/shard_map/ppermute | solution.py:60
  31.9 7.5 %collective-permute-start.18 = (f32[2,16,1024]{2,1,0:T(8,128)S(1)}, f32[2,16,1024]{2,1,0:T(8,128)S(1)}, u32[]{:S(2)}, u32[]{:S(2)}) collective-permute-start(f32[2,16,1024]{2,1,0:T(8,128)S(1)} %get-tuple-element.69), channel_id=1, source_target_pairs={{0,24},{4,28},{8,16},{12,20},{16,8},{20,12},{24,0},{28,4},{1,25},{... | collective-permute-start | bytes 393224 | tf_op jit(solution)/shard_map/ppermute | solution.py:60
  34.5 7.0 %collective-permute-start.19 = (f32[2,16,1024]{2,1,0:T(8,128)S(1)}, f32[2,16,1024]{2,1,0:T(8,128)S(1)}, u32[]{:S(2)}, u32[]{:S(2)}) collective-permute-start(f32[2,16,1024]{2,1,0:T(8,128)S(1)} %get-tuple-element.70), channel_id=1, source_target_pairs={{0,8},{4,20},{8,0},{12,28},{16,24},{20,4},{24,16},{28,12},{1,9},{5... | collective-permute-start | bytes 393224 | tf_op jit(solution)/shard_map/ppermute | solution.py:60
  34.5 7.4 %collective-permute-start.20 = (f32[2,16,1024]{2,1,0:T(8,128)S(1)}, f32[2,16,1024]{2,1,0:T(8,128)S(1)}, u32[]{:S(2)}, u32[]{:S(2)}) collective-permute-start(f32[2,16,1024]{2,1,0:T(8,128)S(1)} %get-tuple-element.71), channel_id=1, source_target_pairs={{0,16},{4,12},{8,24},{12,4},{16,0},{20,28},{24,8},{28,20},{1,17},{... | collective-permute-start | bytes 393224 | tf_op jit(solution)/shard_map/ppermute | solution.py:60
  38.6 4.3 %collective-permute-start.12 = (f32[4,16,1024]{2,1,0:T(8,128)S(1)}, f32[4,16,1024]{2,1,0:T(8,128)S(1)}, u32[]{:S(2)}, u32[]{:S(2)}) collective-permute-start(f32[4,16,1024]{2,1,0:T(8,128)S(1)} %shard_map.73), channel_id=1, source_target_pairs={{0,4},{4,0},{8,12},{12,8},{16,20},{20,16},{24,28},{28,24},{1,5},{5... | collective-permute-start | bytes 786440 | tf_op jit(solution)/shard_map/ppermute | solution.py:303
  42.0 1.6 %collective-permute-start.21 = (f32[4,16,1024]{2,1,0:T(8,128)S(1)}, f32[4,16,1024]{2,1,0:T(8,128)S(1)}, u32[]{:S(2)}, u32[]{:S(2)}) collective-permute-start(f32[4,16,1024]{2,1,0:T(8,128)S(1)} %shard_map.77), channel_id=1, source_target_pairs={{0,4},{4,0},{8,12},{12,8},{16,20},{20,16},{24,28},{28,24},{1,5},{5... | collective-permute-start | bytes 786440 | tf_op jit(solution)/shard_map/ppermute | solution.py:303

commit v4 on v1

--- a/solution.py
+++ b/solution.py
@@ -7,7 +7,7 @@
 
 LEVEL_MODULES = 16
 LEVELS = 2
-MOST_UNROLLED = 16
+MOST_UNROLLED = 8
 
 outer_rate = 0.7
 beta_coef = 0.9
@@ -86,20 +86,34 @@
         pl.when(here_ref[0] & 1 == core)(lambda core=core: pack(core))
 
 
-def merge_kernel(size, here_ref, keep_ref, gift_ref, token_ref, *outs):
-    del token_ref
+def first_merge_kernel(size, here_ref, keep_ref, gift_ref, *outs):
     here = here_ref[0]
     core = here & 1
     for k, out in zip(order_of(size), outs):
         chip = target(here, k, size) // 2
-        for level in range(LEVELS):
-            out[core, level] = keep_ref[level, chip]
-            out[1 - core, level] = gift_ref[level, chip]
-
-
-def sum_kernel(*refs):
+        rows = keep_ref.shape[2]
+        for source, ref in ((core, keep_ref), (1 - core, gift_ref)):
+            out[source, :rows] = ref[0, chip]
+            out[source, rows:] = ref[1, chip, : rows // 2]
+
+
+def second_merge_kernel(size, here_ref, square_ref, other_ref, keep_ref, gift_ref, *outs):
+    here = here_ref[0]
+    core = here & 1
+    squares = square_ref[...] + other_ref[...]
+    _, _, rows, width = keep_ref.shape
+    spots = tiles_of(rows, width)[-(rows * width // 2048) :]
+    for k, out in zip(order_of(size), outs):
+        chip = target(here, k, size) // 2
+        for source, ref in ((core, keep_ref), (1 - core, gift_ref)):
+            for t, spot in enumerate(spots):
+                out[source * len(spots) + t] = ref[(1, chip, *spot)]
+        out[2 * len(spots)] = squares
+
+
+def sum_kernel(count, *refs):
     total = refs[0][...]
-    for ref in refs[1:-1]:
+    for ref in refs[1:count]:
         total = total + ref[...]
     refs[-1][...] = total
 
@@ -130,17 +144,29 @@
             plan_ref[level, 4 * size + i] = module_ref[module]
 
 
-def outgoing_kernel(rounds, entries, plan_ref, square_ref, decayed_ref, *refs):
-    received, outs, (grad_ref, rescale_ref) = refs[:rounds], refs[rounds:-2], refs[-2:]
+def outgoing_kernel(rounds, entries, plan_ref, decayed_ref, *refs):
+    firsts, seconds = refs[:rounds], refs[rounds : 2 * rounds]
+    outs, (grad_ref, rescale_ref) = refs[2 * rounds : -2], refs[-2:]
     size = 2 * rounds
-    total = jnp.sum(square_ref[...], axis=1, keepdims=True)
+    rows, width = grad_ref.shape[2:]
+    spots = tiles_of(rows, width)
+    half = len(spots) // 2
+    squares = seconds[0][2 * half]
+    for second in seconds[1:]:
+        squares = squares + second[2 * half]
+    total = jnp.sum(squares, axis=1, keepdims=True)
     rescale_ref[...] = jnp.broadcast_to(1.0 / jnp.sqrt(total / entries + 1e-06), rescale_ref.shape)
     for level in range(LEVELS):
         for i in range(size):
             rescale = jnp.broadcast_to(rescale_ref[pl.ds(plan_ref[level, 2 * size + i], 1), :], (8, 128))
             factor = rescale / jnp.full((8, 128), plan_ref[level, size + i], jnp.int32).astype(jnp.float32)
-            for spot in tiles_of(*grad_ref.shape[2:]):
-                grad_ref[(level, i, *spot)] = received[i // 2][(i % 2, level, *spot)] * factor
+            for t, spot in enumerate(spots):
+                if level == 0 or t < half:
+                    place = slice(level * rows + spot[0].start, level * rows + spot[0].stop)
+                    block = firsts[i // 2][i % 2, place, spot[1]]
+                else:
+                    block = seconds[i // 2][(i % 2) * half + t - half]
+                grad_ref[(level, i, *spot)] = block * factor
         for i in range(1, size):
             leader = plan_ref[level, i]
 
@@ -212,7 +238,8 @@
     own_slab = path_delta[0]
     size = assign.shape[0]
     module_count, _, own_rows, width = params.shape
-    entries = float(own_slab.size * lax.axis_size("shard"))
+    shards = lax.axis_size("shard")
+    entries = float(own_slab.size * shards)
     state_in = params.reshape(module_count, own_rows, width)
     moment_in = momentum.reshape(module_count, own_rows, width)
     split_slab = own_slab.reshape(LEVELS, size // 2, 2, own_rows, width)
@@ -229,7 +256,17 @@
         here, split_slab
     )
     gift = lax.ppermute(give, "path", swap)
-    squares = call(sum_kernel, squares_shape, [vmem] * rounds, vmem)(*[move(squares, k, size) for k in order])
+    tiles = [squares] + [
+        lax.ppermute(squares, "shard", [(i, i ^ step) for i in range(shards)]) for step in range(shards - 1, 0, -1)
+    ]
+    firsts = call(
+        lambda *refs: first_merge_kernel(size, *refs),
+        [shape(2, own_rows + own_rows // 2, width)] * rounds,
+        [smem, vmem, vmem],
+        [vmem] * rounds,
+    )(here, keep, gift)
+    firsts = [move(firsts[j], k, size) for j, k in enumerate(order)]
+    decayed = state_in - moment_coef * moment_in
     plan, leaders, planned = call(
         plan_kernel,
         [
@@ -240,24 +277,25 @@
         [smem, smem],
         [smem, smem, vmem],
     )(here, assign.T)
-    messages = call(
-        lambda *refs: merge_kernel(size, *refs),
-        [message] * rounds,
-        [smem, vmem, vmem, anywhere],
+    squares = call(
+        lambda *refs: sum_kernel(shards, *refs), squares_shape, [vmem] * shards + [anywhere] * 2, vmem
+    )(*tiles, planned, decayed)
+    other = lax.ppermute(squares, "path", swap)
+    seconds = call(
+        lambda *refs: second_merge_kernel(size, *refs),
+        [shape(own_rows * width // 1024 + 1, 8, 128)] * rounds,
+        [smem] + [vmem] * 4,
         [vmem] * rounds,
-    )(here, keep, gift, planned)
-    received = [move(messages[j], k, size) for j, k in enumerate(order)]
-    other = lax.ppermute(squares, "path", swap)
-    squares = lax.psum(call(sum_kernel, squares_shape, [vmem] * 2, vmem)(squares, other), "shard")
-    decayed = state_in - moment_coef * moment_in
+    )(here, squares, other, keep, gift)
+    seconds = [move(seconds[j], k, size) for j, k in enumerate(order)]
 
     *outgoing, grad = call(
         lambda *refs: outgoing_kernel(rounds, entries, *refs),
         [message] * rounds + [shape(LEVELS, size, own_rows, width)],
-        [smem] + [vmem] * (2 + rounds),
+        [smem] + [vmem] * (1 + 2 * rounds),
         [vmem] * (rounds + 1),
         scratch_shapes=[pltpu.VMEM(squares_shape.shape, jnp.float32)],
-    )(plan, squares, decayed, *received)
+    )(plan, decayed, *firsts, *seconds)
     returned = [move(outgoing[j], k, size) for j, k in enumerate(order)]
     block = LEVEL_MODULES // 2
     state_block = pl.BlockSpec((block, own_rows, width), lambda i: (i, 0, 0))

time: 45.5 us -> 42.9 us (0.943)
  blocking collectives: 12 us -> 0 us
  starting transfers between devices: 11.8 us -> 18 us
  waiting for transfers between devices: 8.48 us -> 13.2 us
  Pallas kernels: 8.21 us -> 7.42 us
  local copies, waits for them, and re-layouts: 2.05 us -> 1.37 us
    psum x1 -> x0, blocking collectives: 12 us -> none  [local(): lax.psum(call(sum_kernel, squares_shape, [vmem] * 2, vmem)(squares, other...]
    ppermute x0 -> x3, starting transfers between devices: none -> 5.33 us  [local(): lax.ppermute(squares, 'shard', [(i, i ^ step) for i in range(shards)])]
    ppermute x9, waiting for transfers between devices: 7.45 us -> 11 us  [move(): lax.ppermute(array, 'path', [(i, target(i, k, size)) for i in range(size)])]
    ppermute x1, waiting for transfers between devices: 0.01 us -> 1.15 us  [local(): other = lax.ppermute(squares, 'path', swap)]
    pallas_call x3, Pallas kernels: 0.88 us -> 0.08 us  [the longest x1 0.05 us: local(): call(lambda *refs: first_merge_kernel(size, *refs), [shape(2, own_rows +...]
    ppermute x9, starting transfers between devices: 11.2 us -> 12 us  [move(): lax.ppermute(array, 'path', [(i, target(i, k, size)) for i in range(size)])]
    unnamed x8 -> x6, local copies, waits for them, and re-layouts: 2.05 us -> 1.37 us
  transfers between devices with their start and end apart: 12 -> 15, of which waited for: 6 -> 7; matrix products, arithmetic and copies ran while one was open for 4% -> 5% of each run, Pallas kernels for 14% -> 13%
where the time goes in v4:
time: 42.9 us; the launch traced here: 42.8 us
  starting transfers between devices  18 us (42%)
  waiting for transfers between devices  13.2 us (31%)
  Pallas kernels  7.42 us (17%)
  other arithmetic  2.03 us (5%)
  local copies, waits for them, and re-layouts  1.37 us (3%)
  between operations  0.77 us (2%)
    ppermute x9, starting transfers between devices, move(): lax.ppermute(array, 'path', [(i, target(i, k, size)) for i in range(size)])  12 us
    ppermute x9, waiting for transfers between devices, move(): lax.ppermute(array, 'path', [(i, target(i, k, size)) for i in range(size)])  11 us
    ppermute x3, starting transfers between devices, local(): lax.ppermute(squares, 'shard', [(i, i ^ step) for i in range(shards)])  5.33 us
    pallas_call x1, Pallas kernels, local(): call(state_kernel, [shape(*state_in.shape)] * 2 + [shape(8, 128)], [smem,...  3.08 us
    sub x1, other arithmetic, local(): decayed = state_in - moment_coef * moment_in  2.03 us
    pallas_call x1, Pallas kernels, local(): call(plan_kernel, [jax.ShapeDtypeStruct((LEVELS, 5 * size), jnp.int32), j...  1.41 us
    unnamed x6, local copies, waits for them, and re-layouts  1.37 us
    ppermute x1, waiting for transfers between devices, local(): other = lax.ppermute(squares, 'path', swap)  1.15 us
  transfers between devices with their start and end apart: 15, of which 7 were waited for; matrix products, arithmetic and copies ran while one was open for 5% of the time, Pallas kernels for 13%

profile of v4, /device:TPU:0, one launch (start us, length us, event | category | flops | bytes accessed | tf_op | source)
XLA Modules:
  0.0 42.8 jit_solution(14713016226112222908)
XLA Ops:
  0.6 0.0 copy-start
  0.6 0.0 copy-start.1
  0.7 1.4 %copy-done.1 = f32[1,2,128,1024]{3,2,1,0:T(8,128)S(1)} copy-done((f32[1,2,128,1024]{3,2,1,0:T(8,128)S(1)}, f32[1,2,128,1024]{3,2,1,0:T(8,128)}, u32[]{:S(2)}) %copy-start.1) | copy-done | bytes 1048600
  2.0 0.1 shard_map.68
  2.1 0.5 %collective-permute-start = (f32[2,4,16,1024]{3,2,1,0:T(8,128)S(1)}, f32[2,4,16,1024]{3,2,1,0:T(8,128)S(1)}, u32[]{:S(2)}, u32[]{:S(2)}) collective-permute-start(f32[2,4,16,1024]{3,2,1,0:T(8,128)S(1)} %get-tuple-element.27), channel_id=1, source_target_pairs={{0,4},{4,0},{8,12},{12,8},{16,20},{20,16},{24,28},{28,24},{1,5},{5... | collective-permute-start | bytes 1572872 | tf_op jit(solution)/shard_map/ppermute | solution.py:258
  2.6 4.7 %collective-permute-start.4 = (f32[8,128]{1,0:T(8,128)S(1)}, f32[8,128]{1,0:T(8,128)S(1)}, u32[]{:S(2)}, u32[]{:S(2)}) collective-permute-start(f32[8,128]{1,0:T(8,128)S(1)} %get-tuple-element.32.refs_0_), channel_id=1, source_target_pairs={{0,3},{1,2},{2,1},{3,0},{4,7},{5,6},{6,5},{7,4},{8,11},{9,10},{10,... | collective-permute-start | bytes 12296 | tf_op jit(solution)/shard_map/ppermute | solution.py:260
  7.3 0.0 collective-permute-start.5
  7.3 0.6 %collective-permute-start.6 = (f32[8,128]{1,0:T(8,128)S(1)}, f32[8,128]{1,0:T(8,128)S(1)}, u32[]{:S(2)}, u32[]{:S(2)}) collective-permute-start(f32[8,128]{1,0:T(8,128)S(1)} %get-tuple-element.32.refs_0_), channel_id=1, source_target_pairs={{0,1},{1,0},{2,3},{3,2},{4,5},{5,4},{6,7},{7,6},{8,9},{9,8},{10,11... | collective-permute-start | bytes 12296 | tf_op jit(solution)/shard_map/ppermute | solution.py:260
  8.0 0.0 collective-permute-done.refs_2_.refs_4_
  8.0 0.1 shard_map.69
  8.0 2.7 %collective-permute-start.1 = (f32[2,24,1024]{2,1,0:T(8,128)S(1)}, f32[2,24,1024]{2,1,0:T(8,128)S(1)}, u32[]{:S(2)}, u32[]{:S(2)}) collective-permute-start(f32[2,24,1024]{2,1,0:T(8,128)S(1)} %get-tuple-element.28), channel_id=1, source_target_pairs={{0,24},{4,28},{8,16},{12,20},{16,8},{20,12},{24,0},{28,4},{1,25},{... | collective-permute-start | bytes 589832 | tf_op jit(solution)/shard_map/ppermute | solution.py:60
  10.7 0.5 %collective-permute-start.2 = (f32[2,24,1024]{2,1,0:T(8,128)S(1)}, f32[2,24,1024]{2,1,0:T(8,128)S(1)}, u32[]{:S(2)}, u32[]{:S(2)}) collective-permute-start(f32[2,24,1024]{2,1,0:T(8,128)S(1)} %get-tuple-element.29), channel_id=1, source_target_pairs={{0,8},{4,20},{8,0},{12,28},{16,24},{20,4},{24,16},{28,12},{1,9},{5... | collective-permute-start | bytes 589832 | tf_op jit(solution)/shard_map/ppermute | solution.py:60
  11.2 0.0 collective-permute-done.4.refs_1_
  11.2 0.0 copy-start.2
  11.2 0.4 collective-permute-start.3
  11.6 0.0 copy-done
  11.6 2.0 %bitcast_subtract_fusion.refs_5_.refs_1_.decayed_ref = f32[32,16,1024]{2,1,0:T(8,128)S(1)} fusion(f32[32,1,16,1024]{3,2,1,0:T(8,128)} %param.6, f32[32,1,16,1024]{3,2,1,0:T(8,128)S(1)} %copy-done), kind=kLoop, calls=%fused_computation | loop fusion | flops 1048576 | bytes 6291456 | tf_op jit(solution)/shard_map/sub | solution.py:269
  13.6 0.0 copy-done.2
  13.6 1.4 %shard_map.67 = (s32[2,40]{1,0:T(2,128)S(1)}, s32[32]{0:T(128)S(1)}, f32[8,128]{1,0:T(8,128)S(1)}) custom-call(s32[1]{0:T(128)} %bitcast.here_ref.refs_0_, s32[2,8]{1,0:T(2,128)S(1)} %bitcast.16), custom_call_target="tpu_custom_call" | custom-call | tf_op jit(solution)/shard_map/pallas_call | solution.py:270
  15.1 0.0 collective-permute-done.5.refs_2_
  15.1 0.0 collective-permute-done.6.refs_3_
  15.1 0.1 collective-permute-start.7
  15.2 1.2 %collective-permute-done.7.refs_2_ = f32[8,128]{1,0:T(8,128)S(1)} collective-permute-done((f32[8,128]{1,0:T(8,128)S(1)}, f32[8,128]{1,0:T(8,128)S(1)}, u32[]{:S(2)}, u32[]{:S(2)}) %collective-permute-start.7) | collective-permute-done | bytes 4128 | tf_op jit(solution)/shard_map/ppermute | solution.py:283
  16.4 2.7 %collective-permute-start.8 = (f32[17,8,128]{2,1,0:T(8,128)S(1)}, f32[17,8,128]{2,1,0:T(8,128)S(1)}, u32[]{:S(2)}, u32[]{:S(2)}) collective-permute-start(f32[17,8,128]{2,1,0:T(8,128)S(1)} %get-tuple-element.34), channel_id=1, source_target_pairs={{0,24},{4,28},{8,16},{12,20},{16,8},{20,12},{24,0},{28,4},{1,25},{... | collective-permute-start | bytes 208904 | tf_op jit(solution)/shard_map/ppermute | solution.py:60
  19.0 0.5 %collective-permute-start.9 = (f32[17,8,128]{2,1,0:T(8,128)S(1)}, f32[17,8,128]{2,1,0:T(8,128)S(1)}, u32[]{:S(2)}, u32[]{:S(2)}) collective-permute-start(f32[17,8,128]{2,1,0:T(8,128)S(1)} %get-tuple-element.35), channel_id=1, source_target_pairs={{0,8},{4,20},{8,0},{12,28},{16,24},{20,4},{24,16},{28,12},{1,9},{5... | collective-permute-start | bytes 208904 | tf_op jit(solution)/shard_map/ppermute | solution.py:60
  19.5 2.1 %collective-permute-done.8.refs_6_ = f32[17,8,128]{2,1,0:T(8,128)S(1)} collective-permute-done((f32[17,8,128]{2,1,0:T(8,128)S(1)}, f32[17,8,128]{2,1,0:T(8,128)S(1)}, u32[]{:S(2)}, u32[]{:S(2)}) %collective-permute-start.8) | collective-permute-done | bytes 69664 | tf_op jit(solution)/shard_map/ppermute | solution.py:60
  21.6 1.7 %collective-permute-start.10 = (f32[17,8,128]{2,1,0:T(8,128)S(1)}, f32[17,8,128]{2,1,0:T(8,128)S(1)}, u32[]{:S(2)}, u32[]{:S(2)}) collective-permute-start(f32[17,8,128]{2,1,0:T(8,128)S(1)} %get-tuple-element.36), channel_id=1, source_target_pairs={{0,16},{4,12},{8,24},{12,4},{16,0},{20,28},{24,8},{28,20},{1,17},{... | collective-permute-start | bytes 208904 | tf_op jit(solution)/shard_map/ppermute | solution.py:60
  23.3 0.1 collective-permute-done.9.refs_7_
  23.4 2.5 %collective-permute-done.10.refs_8_ = f32[17,8,128]{2,1,0:T(8,128)S(1)} collective-permute-done((f32[17,8,128]{2,1,0:T(8,128)S(1)}, f32[17,8,128]{2,1,0:T(8,128)S(1)}, u32[]{:S(2)}, u32[]{:S(2)}) %collective-permute-start.10) | collective-permute-done | bytes 69664 | tf_op jit(solution)/shard_map/ppermute | solution.py:60
  25.9 0.0 collective-permute-done.1.refs_2_
  25.9 0.0 collective-permute-done.2.refs_3_
  26.0 0.0 collective-permute-done.3.refs_4_
  26.0 1.0 %shard_map.72 = (f32[2,2,16,1024]{3,2,1,0:T(8,128)S(1)}, f32[2,2,16,1024]{3,2,1,0:T(8,128)S(1)}, f32[2,2,16,1024]{3,2,1,0:T(8,128)S(1)}, f32[2,2,16,1024]{3,2,1,0:T(8,128)S(1)}, f32[2,8,16,1024]{3,2,1,0:T(8,128)S(1)}) custom-call(s32[2,40]{1,0:T(2,128)S(1)} %get-tuple-element.25.refs_0_, ...), custom_call_target="tpu_custom_call" | custom-call | tf_op jit(solution)/shard_map/pallas_call | solution.py:292
  27.0 2.6 %collective-permute-start.11 = (f32[2,2,16,1024]{3,2,1,0:T(8,128)S(1)}, f32[2,2,16,1024]{3,2,1,0:T(8,128)S(1)}, u32[]{:S(2)}, u32[]{:S(2)}) collective-permute-start(f32[2,2,16,1024]{3,2,1,0:T(8,128)S(1)} %get-tuple-element.38), channel_id=1, source_target_pairs={{0,24},{4,28},{8,16},{12,20},{16,8},{20,12},{24,0},{28,4},{1,25},{... | collective-permute-start | bytes 786440 | tf_op jit(solution)/shard_map/ppermute | solution.py:60
  29.6 0.6 %collective-permute-start.12 = (f32[2,2,16,1024]{3,2,1,0:T(8,128)S(1)}, f32[2,2,16,1024]{3,2,1,0:T(8,128)S(1)}, u32[]{:S(2)}, u32[]{:S(2)}) collective-permute-start(f32[2,2,16,1024]{3,2,1,0:T(8,128)S(1)} %get-tuple-element.39), channel_id=1, source_target_pairs={{0,8},{4,20},{8,0},{12,28},{16,24},{20,4},{24,16},{28,12},{1,9},{5... | collective-permute-start | bytes 786440 | tf_op jit(solution)/shard_map/ppermute | solution.py:60
  30.2 0.3 collective-permute-start.13
  30.5 3.1 %shard_map.73 = (f32[32,16,1024]{2,1,0:T(8,128)}, f32[32,16,1024]{2,1,0:T(8,128)}, f32[8,128]{1,0:T(8,128)S(1)}) custom-call(s32[32]{0:T(128)S(1)} %get-tuple-element.42.module_ref, f32[2,8,16,1024]{3,2,1,0:T(8,128)S(1)} %get-tuple-element.43.grad_ref, f32[32,16,1024]{2,1,0:T(8,128)S(1)} %bitcast_subtract_fusion.refs_5_.refs_1_.decayed_ref, ...), custom_call_target="tpu_custom_call" | custom-call | tf_op jit(solution)/shard_map/pallas_call | solution.py:302
  33.6 3.3 %collective-permute-done.11.refs_1_ = f32[2,2,16,1024]{3,2,1,0:T(8,128)S(1)} collective-permute-done((f32[2,2,16,1024]{3,2,1,0:T(8,128)S(1)}, f32[2,2,16,1024]{3,2,1,0:T(8,128)S(1)}, u32[]{:S(2)}, u32[]{:S(2)}) %collective-permute-start.11) | collective-permute-done | bytes 262176 | tf_op jit(solution)/shard_map/ppermute | solution.py:60
  36.9 3.0 %collective-permute-done.12.refs_2_ = f32[2,2,16,1024]{3,2,1,0:T(8,128)S(1)} collective-permute-done((f32[2,2,16,1024]{3,2,1,0:T(8,128)S(1)}, f32[2,2,16,1024]{3,2,1,0:T(8,128)S(1)}, u32[]{:S(2)}, u32[]{:S(2)}) %collective-permute-start.12) | collective-permute-done | bytes 262176 | tf_op jit(solution)/shard_map/ppermute | solution.py:60
  39.9 0.0 collective-permute-done.13.refs_3_
  39.9 0.1 collective-permute-start.14
  40.0 0.9 %shard_map.75.held_ref = f32[2,4,2,16,1024]{4,3,2,1,0:T(8,128)} custom-call(s32[1]{0:T(128)} %bitcast.here_ref.refs_0_, f32[2,2,16,1024]{3,2,1,0:T(8,128)S(1)} %collective-permute-done.11.refs_1_, f32[2,2,16,1024]{3,2,1,0:T(8,128)S(1)} %collective-permute-done.12.refs_2_, f32[2,2,16,1024]{3,2,1,0:T(8,128)S(1)} %collective-permute-done.13.refs_3_, ...), custom_call_target="tpu_custom_call" | custom-call | tf_op jit(solution)/shard_map/pallas_call | solution.py:314
  40.9 1.0 %collective-permute-done.14.back_ref = f32[2,4,16,1024]{3,2,1,0:T(8,128)S(1)} collective-permute-done((f32[2,4,16,1024]{3,2,1,0:T(8,128)S(1)}, f32[2,4,16,1024]{3,2,1,0:T(8,128)S(1)}, u32[]{:S(2)}, u32[]{:S(2)}) %collective-permute-start.14) | collective-permute-done | bytes 524320 | tf_op jit(solution)/shard_map/ppermute | solution.py:312
  41.9 0.8 %shard_map.76 = f32[2,4,2,16,1024]{4,3,2,1,0:T(8,128)} custom-call(s32[1]{0:T(128)} %bitcast.here_ref.refs_0_, f32[2,4,16,1024]{3,2,1,0:T(8,128)S(1)} %collective-permute-done.14.back_ref, f32[2,4,2,16,1024]{4,3,2,1,0:T(8,128)} %shard_map.75.held_ref), custom_call_target="tpu_custom_call", output_to_operand_aliasing={{}: (2, {})} | custom-call | tf_op jit(solution)/shard_map/pallas_call | solution.py:321
  (3 shorter events, 0.1 us)
Async XLA Ops:
  0.6 11.0 %copy-start = (f32[32,1,16,1024]{3,2,1,0:T(8,128)S(1)}, f32[32,1,16,1024]{3,2,1,0:T(8,128)}, u32[]{:S(2)}) copy-start(f32[32,1,16,1024]{3,2,1,0:T(8,128)} %param.7) | copy-start | bytes 6291460
  0.6 1.4 %copy-start.1 = (f32[1,2,128,1024]{3,2,1,0:T(8,128)S(1)}, f32[1,2,128,1024]{3,2,1,0:T(8,128)}, u32[]{:S(2)}) copy-start(f32[1,2,128,1024]{3,2,1,0:T(8,128)} %param.4) | copy-start | bytes 3145732
  2.1 5.8 %collective-permute-start = (f32[2,4,16,1024]{3,2,1,0:T(8,128)S(1)}, f32[2,4,16,1024]{3,2,1,0:T(8,128)S(1)}, u32[]{:S(2)}, u32[]{:S(2)}) collective-permute-start(f32[2,4,16,1024]{3,2,1,0:T(8,128)S(1)} %get-tuple-element.27), channel_id=1, source_target_pairs={{0,4},{4,0},{8,12},{12,8},{16,20},{20,16},{24,28},{28,24},{1,5},{5... | collective-permute-start | bytes 1572872 | tf_op jit(solution)/shard_map/ppermute | solution.py:258
  2.6 8.6 %collective-permute-start.4 = (f32[8,128]{1,0:T(8,128)S(1)}, f32[8,128]{1,0:T(8,128)S(1)}, u32[]{:S(2)}, u32[]{:S(2)}) collective-permute-start(f32[8,128]{1,0:T(8,128)S(1)} %get-tuple-element.32.refs_0_), channel_id=1, source_target_pairs={{0,3},{1,2},{2,1},{3,0},{4,7},{5,6},{6,5},{7,4},{8,11},{9,10},{10,... | collective-permute-start | bytes 12296 | tf_op jit(solution)/shard_map/ppermute | solution.py:260
  7.3 7.7 %collective-permute-start.5 = (f32[8,128]{1,0:T(8,128)S(1)}, f32[8,128]{1,0:T(8,128)S(1)}, u32[]{:S(2)}, u32[]{:S(2)}) collective-permute-start(f32[8,128]{1,0:T(8,128)S(1)} %get-tuple-element.32.refs_0_), channel_id=1, source_target_pairs={{0,2},{1,3},{2,0},{3,1},{4,6},{5,7},{6,4},{7,5},{8,10},{9,11},{10,... | collective-permute-start | bytes 12296 | tf_op jit(solution)/shard_map/ppermute | solution.py:260
  7.3 7.7 %collective-permute-start.6 = (f32[8,128]{1,0:T(8,128)S(1)}, f32[8,128]{1,0:T(8,128)S(1)}, u32[]{:S(2)}, u32[]{:S(2)}) collective-permute-start(f32[8,128]{1,0:T(8,128)S(1)} %get-tuple-element.32.refs_0_), channel_id=1, source_target_pairs={{0,1},{1,0},{2,3},{3,2},{4,5},{5,4},{6,7},{7,6},{8,9},{9,8},{10,11... | collective-permute-start | bytes 12296 | tf_op jit(solution)/shard_map/ppermute | solution.py:260
  8.0 17.9 %collective-permute-start.1 = (f32[2,24,1024]{2,1,0:T(8,128)S(1)}, f32[2,24,1024]{2,1,0:T(8,128)S(1)}, u32[]{:S(2)}, u32[]{:S(2)}) collective-permute-start(f32[2,24,1024]{2,1,0:T(8,128)S(1)} %get-tuple-element.28), channel_id=1, source_target_pairs={{0,24},{4,28},{8,16},{12,20},{16,8},{20,12},{24,0},{28,4},{1,25},{... | collective-permute-start | bytes 589832 | tf_op jit(solution)/shard_map/ppermute | solution.py:60
  10.7 15.3 %collective-permute-start.2 = (f32[2,24,1024]{2,1,0:T(8,128)S(1)}, f32[2,24,1024]{2,1,0:T(8,128)S(1)}, u32[]{:S(2)}, u32[]{:S(2)}) collective-permute-start(f32[2,24,1024]{2,1,0:T(8,128)S(1)} %get-tuple-element.29), channel_id=1, source_target_pairs={{0,8},{4,20},{8,0},{12,28},{16,24},{20,4},{24,16},{28,12},{1,9},{5... | collective-permute-start | bytes 589832 | tf_op jit(solution)/shard_map/ppermute | solution.py:60
  11.2 2.4 %copy-start.2 = (s32[8,2]{0,1:T(2,128)S(1)}, s32[8,2]{0,1:T(2,128)}, u32[]{:S(2)}) copy-start(s32[8,2]{0,1:T(2,128)} %param.5) | copy-start | bytes 196
  11.2 14.7 %collective-permute-start.3 = (f32[2,24,1024]{2,1,0:T(8,128)S(1)}, f32[2,24,1024]{2,1,0:T(8,128)S(1)}, u32[]{:S(2)}, u32[]{:S(2)}) collective-permute-start(f32[2,24,1024]{2,1,0:T(8,128)S(1)} %get-tuple-element.30), channel_id=1, source_target_pairs={{0,16},{4,12},{8,24},{12,4},{16,0},{20,28},{24,8},{28,20},{1,17},{... | collective-permute-start | bytes 589832 | tf_op jit(solution)/shard_map/ppermute | solution.py:60
  15.1 1.2 %collective-permute-start.7 = (f32[8,128]{1,0:T(8,128)S(1)}, f32[8,128]{1,0:T(8,128)S(1)}, u32[]{:S(2)}, u32[]{:S(2)}) collective-permute-start(f32[8,128]{1,0:T(8,128)S(1)} %shard_map.70.refs_1_), channel_id=1, source_target_pairs={{0,4},{4,0},{8,12},{12,8},{16,20},{20,16},{24,28},{28,24},{1,5},{5... | collective-permute-start | bytes 12296 | tf_op jit(solution)/shard_map/ppermute | solution.py:283
  16.4 5.3 %collective-permute-start.8 = (f32[17,8,128]{2,1,0:T(8,128)S(1)}, f32[17,8,128]{2,1,0:T(8,128)S(1)}, u32[]{:S(2)}, u32[]{:S(2)}) collective-permute-start(f32[17,8,128]{2,1,0:T(8,128)S(1)} %get-tuple-element.34), channel_id=1, source_target_pairs={{0,24},{4,28},{8,16},{12,20},{16,8},{20,12},{24,0},{28,4},{1,25},{... | collective-permute-start | bytes 208904 | tf_op jit(solution)/shard_map/ppermute | solution.py:60
  19.0 4.4 %collective-permute-start.9 = (f32[17,8,128]{2,1,0:T(8,128)S(1)}, f32[17,8,128]{2,1,0:T(8,128)S(1)}, u32[]{:S(2)}, u32[]{:S(2)}) collective-permute-start(f32[17,8,128]{2,1,0:T(8,128)S(1)} %get-tuple-element.35), channel_id=1, source_target_pairs={{0,8},{4,20},{8,0},{12,28},{16,24},{20,4},{24,16},{28,12},{1,9},{5... | collective-permute-start | bytes 208904 | tf_op jit(solution)/shard_map/ppermute | solution.py:60
  21.6 4.3 %collective-permute-start.10 = (f32[17,8,128]{2,1,0:T(8,128)S(1)}, f32[17,8,128]{2,1,0:T(8,128)S(1)}, u32[]{:S(2)}, u32[]{:S(2)}) collective-permute-start(f32[17,8,128]{2,1,0:T(8,128)S(1)} %get-tuple-element.36), channel_id=1, source_target_pairs={{0,16},{4,12},{8,24},{12,4},{16,0},{20,28},{24,8},{28,20},{1,17},{... | collective-permute-start | bytes 208904 | tf_op jit(solution)/shard_map/ppermute | solution.py:60
  27.0 9.9 %collective-permute-start.11 = (f32[2,2,16,1024]{3,2,1,0:T(8,128)S(1)}, f32[2,2,16,1024]{3,2,1,0:T(8,128)S(1)}, u32[]{:S(2)}, u32[]{:S(2)}) collective-permute-start(f32[2,2,16,1024]{3,2,1,0:T(8,128)S(1)} %get-tuple-element.38), channel_id=1, source_target_pairs={{0,24},{4,28},{8,16},{12,20},{16,8},{20,12},{24,0},{28,4},{1,25},{... | collective-permute-start | bytes 786440 | tf_op jit(solution)/shard_map/ppermute | solution.py:60
  29.6 10.3 %collective-permute-start.12 = (f32[2,2,16,1024]{3,2,1,0:T(8,128)S(1)}, f32[2,2,16,1024]{3,2,1,0:T(8,128)S(1)}, u32[]{:S(2)}, u32[]{:S(2)}) collective-permute-start(f32[2,2,16,1024]{3,2,1,0:T(8,128)S(1)} %get-tuple-element.39), channel_id=1, source_target_pairs={{0,8},{4,20},{8,0},{12,28},{16,24},{20,4},{24,16},{28,12},{1,9},{5... | collective-permute-start | bytes 786440 | tf_op jit(solution)/shard_map/ppermute | solution.py:60
  30.2 9.7 %collective-permute-start.13 = (f32[2,2,16,1024]{3,2,1,0:T(8,128)S(1)}, f32[2,2,16,1024]{3,2,1,0:T(8,128)S(1)}, u32[]{:S(2)}, u32[]{:S(2)}) collective-permute-start(f32[2,2,16,1024]{3,2,1,0:T(8,128)S(1)} %get-tuple-element.40), channel_id=1, source_target_pairs={{0,16},{4,12},{8,24},{12,4},{16,0},{20,28},{24,8},{28,20},{1,17},{... | collective-permute-start | bytes 786440 | tf_op jit(solution)/shard_map/ppermute | solution.py:60
  39.9 2.0 %collective-permute-start.14 = (f32[2,4,16,1024]{3,2,1,0:T(8,128)S(1)}, f32[2,4,16,1024]{3,2,1,0:T(8,128)S(1)}, u32[]{:S(2)}, u32[]{:S(2)}) collective-permute-start(f32[2,4,16,1024]{3,2,1,0:T(8,128)S(1)} %shard_map.74), channel_id=1, source_target_pairs={{0,4},{4,0},{8,12},{12,8},{16,20},{20,16},{24,28},{28,24},{1,5},{5... | collective-permute-start | bytes 1572872 | tf_op jit(solution)/shard_map/ppermute | solution.py:312

commit v5 on v4

--- a/solution.py
+++ b/solution.py
@@ -111,18 +111,25 @@
         out[2 * len(spots)] = squares
 
 
-def sum_kernel(count, *refs):
+def sum_kernel(*refs):
     total = refs[0][...]
-    for ref in refs[1:count]:
+    for ref in refs[1:-1]:
         total = total + ref[...]
     refs[-1][...] = total
 
 
-def plan_kernel(here_ref, ids_ref, plan_ref, module_ref, token_ref):
+def decay_kernel(params_ref, momentum_ref, out_ref):
+    def decay(module, carry):
+        out_ref[module] = params_ref[module] - moment_coef * momentum_ref[module]
+        return carry
+
+    lax.fori_loop(0, out_ref.shape[0], decay, 0)
+
+
+def plan_kernel(here_ref, ids_ref, plan_ref, module_ref):
     size = ids_ref.shape[1]
     order = order_of(size)
     here = here_ref[0]
-    token_ref[...] = jnp.zeros_like(token_ref)
     paths = [(origin(here, k, size) // 2) * 2 + half for k in order for half in range(2)]
     targets = [(target(here, k, size) // 2) * 2 + half for k in order for half in range(2)]
     for level in range(LEVELS):
@@ -266,20 +273,17 @@
         [vmem] * rounds,
     )(here, keep, gift)
     firsts = [move(firsts[j], k, size) for j, k in enumerate(order)]
-    decayed = state_in - moment_coef * moment_in
-    plan, leaders, planned = call(
+    decayed = call(decay_kernel, shape(*state_in.shape), [vmem, vmem], vmem)(state_in, moment_in)
+    plan, leaders = call(
         plan_kernel,
         [
             jax.ShapeDtypeStruct((LEVELS, 5 * size), jnp.int32),
             jax.ShapeDtypeStruct((module_count,), jnp.int32),
-            shape(8, 128),
         ],
         [smem, smem],
-        [smem, smem, vmem],
+        [smem, smem],
     )(here, assign.T)
-    squares = call(
-        lambda *refs: sum_kernel(shards, *refs), squares_shape, [vmem] * shards + [anywhere] * 2, vmem
-    )(*tiles, planned, decayed)
+    squares = call(sum_kernel, squares_shape, [vmem] * shards, vmem)(*tiles)
     other = lax.ppermute(squares, "path", swap)
     seconds = call(
         lambda *refs: second_merge_kernel(size, *refs),

time: 42.9 us -> 47.3 us (1.10)
  waiting for transfers between devices: 13.2 us -> 17.8 us
  other arithmetic: 2.03 us -> 0 us
  local copies, waits for them, and re-layouts: 1.37 us -> 2.96 us
    ppermute x3, waiting for transfers between devices: 0.01 us -> 5.18 us  [local(): lax.ppermute(squares, 'shard', [(i, i ^ step) for i in range(shards)])]
    ppermute x9, waiting for transfers between devices: 11 us -> 8.93 us  [move(): lax.ppermute(array, 'path', [(i, target(i, k, size)) for i in range(size)])]
    sub x1 -> x0, other arithmetic: 2.03 us -> none  [local(): decayed = state_in - moment_coef * moment_in]
    unnamed x6 -> x8, local copies, waits for them, and re-layouts: 1.37 us -> 2.96 us
    ppermute x1, waiting for transfers between devices: 0.01 us -> 1.54 us  [local(): gift = lax.ppermute(give, 'path', swap)]
    ppermute x3, starting transfers between devices: 5.33 us -> 4.01 us  [local(): lax.ppermute(squares, 'shard', [(i, i ^ step) for i in range(shards)])]
    ppermute x9, starting transfers between devices: 12 us -> 13.1 us  [move(): lax.ppermute(array, 'path', [(i, target(i, k, size)) for i in range(size)])]
  transfers between devices with their start and end apart: 15 -> 15, of which waited for: 7 -> 9; matrix products, arithmetic and copies ran while one was open for 5% -> 0% of each run, Pallas kernels for 13% -> 12%
where the time goes in v5:
time: 47.3 us; the launch traced here: 47.2 us
  waiting for transfers between devices  17.8 us (38%)
  starting transfers between devices  17.7 us (37%)
  Pallas kernels  7.86 us (17%)
  local copies, waits for them, and re-layouts  2.96 us (6%)
  between operations  0.78 us (2%)
    ppermute x9, starting transfers between devices, move(): lax.ppermute(array, 'path', [(i, target(i, k, size)) for i in range(size)])  13.1 us
    ppermute x9, waiting for transfers between devices, move(): lax.ppermute(array, 'path', [(i, target(i, k, size)) for i in range(size)])  8.93 us
    ppermute x3, waiting for transfers between devices, local(): lax.ppermute(squares, 'shard', [(i, i ^ step) for i in range(shards)])  5.18 us
    ppermute x3, starting transfers between devices, local(): lax.ppermute(squares, 'shard', [(i, i ^ step) for i in range(shards)])  4.01 us
    pallas_call x1, Pallas kernels, local(): call(state_kernel, [shape(*state_in.shape)] * 2 + [shape(8, 128)], [smem,...  3.08 us
    unnamed x8, local copies, waits for them, and re-layouts  2.96 us
    ppermute x1, waiting for transfers between devices, local(): gift = lax.ppermute(give, 'path', swap)  1.54 us
    pallas_call x1, Pallas kernels, local(): call(plan_kernel, [jax.ShapeDtypeStruct((LEVELS, 5 * size), jnp.int32), j...  1.4 us
  transfers between devices with their start and end apart: 15, of which 9 were waited for; matrix products, arithmetic and copies ran while one was open for 0% of the time, Pallas kernels for 12%

profile of v5, /device:TPU:0, one launch (start us, length us, event | category | flops | bytes accessed | tf_op | source)
XLA Modules:
  0.0 47.2 jit_solution(13597456411659604172)
XLA Ops:
  0.6 0.0 copy-start
  0.6 0.0 copy-start.2
  0.7 1.4 %copy-done.2 = f32[1,2,128,1024]{3,2,1,0:T(8,128)S(1)} copy-done((f32[1,2,128,1024]{3,2,1,0:T(8,128)S(1)}, f32[1,2,128,1024]{3,2,1,0:T(8,128)}, u32[]{:S(2)}) %copy-start.2) | copy-done | bytes 1048600
  2.0 0.0 copy-start.3
  2.0 0.1 shard_map.69
  2.1 0.5 %collective-permute-start = (f32[2,4,16,1024]{3,2,1,0:T(8,128)S(1)}, f32[2,4,16,1024]{3,2,1,0:T(8,128)S(1)}, u32[]{:S(2)}, u32[]{:S(2)}) collective-permute-start(f32[2,4,16,1024]{3,2,1,0:T(8,128)S(1)} %get-tuple-element.26), channel_id=1, source_target_pairs={{0,4},{4,0},{8,12},{12,8},{16,20},{20,16},{24,28},{28,24},{1,5},{5... | collective-permute-start | bytes 1572872 | tf_op jit(solution)/shard_map/ppermute | solution.py:265
  2.7 1.5 %collective-permute-done.refs_2_.refs_4_ = f32[2,4,16,1024]{3,2,1,0:T(8,128)S(1)} collective-permute-done((f32[2,4,16,1024]{3,2,1,0:T(8,128)S(1)}, f32[2,4,16,1024]{3,2,1,0:T(8,128)S(1)}, u32[]{:S(2)}, u32[]{:S(2)}) %collective-permute-start) | collective-permute-done | bytes 524320 | tf_op jit(solution)/shard_map/ppermute | solution.py:265
  4.2 0.1 shard_map.70
  4.2 3.9 %collective-permute-start.1 = (f32[2,24,1024]{2,1,0:T(8,128)S(1)}, f32[2,24,1024]{2,1,0:T(8,128)S(1)}, u32[]{:S(2)}, u32[]{:S(2)}) collective-permute-start(f32[2,24,1024]{2,1,0:T(8,128)S(1)} %get-tuple-element.27), channel_id=1, source_target_pairs={{0,24},{4,28},{8,16},{12,20},{16,8},{20,12},{24,0},{28,4},{1,25},{... | collective-permute-start | bytes 589832 | tf_op jit(solution)/shard_map/ppermute | solution.py:60
  8.1 0.5 %collective-permute-start.2 = (f32[2,24,1024]{2,1,0:T(8,128)S(1)}, f32[2,24,1024]{2,1,0:T(8,128)S(1)}, u32[]{:S(2)}, u32[]{:S(2)}) collective-permute-start(f32[2,24,1024]{2,1,0:T(8,128)S(1)} %get-tuple-element.28), channel_id=1, source_target_pairs={{0,8},{4,20},{8,0},{12,28},{16,24},{20,4},{24,16},{28,12},{1,9},{5... | collective-permute-start | bytes 589832 | tf_op jit(solution)/shard_map/ppermute | solution.py:60
  8.7 0.1 collective-permute-start.3
  8.8 4.0 %collective-permute-start.4 = (f32[8,128]{1,0:T(8,128)S(1)}, f32[8,128]{1,0:T(8,128)S(1)}, u32[]{:S(2)}, u32[]{:S(2)}) collective-permute-start(f32[8,128]{1,0:T(8,128)S(1)} %get-tuple-element.31.refs_0_), channel_id=1, source_target_pairs={{0,3},{1,2},{2,1},{3,0},{4,7},{5,6},{6,5},{7,4},{8,11},{9,10},{10,... | collective-permute-start | bytes 12296 | tf_op jit(solution)/shard_map/ppermute | solution.py:267
  12.8 0.0 collective-permute-start.5
  12.8 1.6 %collective-permute-done.4.refs_1_ = f32[8,128]{1,0:T(8,128)S(1)} collective-permute-done((f32[8,128]{1,0:T(8,128)S(1)}, f32[8,128]{1,0:T(8,128)S(1)}, u32[]{:S(2)}, u32[]{:S(2)}) %collective-permute-start.4) | collective-permute-done | bytes 4128 | tf_op jit(solution)/shard_map/ppermute | solution.py:267
  14.4 0.0 collective-permute-start.6
  14.4 2.9 %collective-permute-done.5.refs_2_ = f32[8,128]{1,0:T(8,128)S(1)} collective-permute-done((f32[8,128]{1,0:T(8,128)S(1)}, f32[8,128]{1,0:T(8,128)S(1)}, u32[]{:S(2)}, u32[]{:S(2)}) %collective-permute-start.5) | collective-permute-done | bytes 4128 | tf_op jit(solution)/shard_map/ppermute | solution.py:267
  17.3 0.7 %collective-permute-done.6.refs_3_ = f32[8,128]{1,0:T(8,128)S(1)} collective-permute-done((f32[8,128]{1,0:T(8,128)S(1)}, f32[8,128]{1,0:T(8,128)S(1)}, u32[]{:S(2)}, u32[]{:S(2)}) %collective-permute-start.6) | collective-permute-done | bytes 4128 | tf_op jit(solution)/shard_map/ppermute | solution.py:267
  18.0 0.0 collective-permute-start.7
  18.0 1.2 %collective-permute-done.7.refs_2_ = f32[8,128]{1,0:T(8,128)S(1)} collective-permute-done((f32[8,128]{1,0:T(8,128)S(1)}, f32[8,128]{1,0:T(8,128)S(1)}, u32[]{:S(2)}, u32[]{:S(2)}) %collective-permute-start.7) | collective-permute-done | bytes 4128 | tf_op jit(solution)/shard_map/ppermute | solution.py:287
  19.2 2.7 %collective-permute-start.8 = (f32[17,8,128]{2,1,0:T(8,128)S(1)}, f32[17,8,128]{2,1,0:T(8,128)S(1)}, u32[]{:S(2)}, u32[]{:S(2)}) collective-permute-start(f32[17,8,128]{2,1,0:T(8,128)S(1)} %get-tuple-element.32), channel_id=1, source_target_pairs={{0,24},{4,28},{8,16},{12,20},{16,8},{20,12},{24,0},{28,4},{1,25},{... | collective-permute-start | bytes 208904 | tf_op jit(solution)/shard_map/ppermute | solution.py:60
  21.9 0.5 %collective-permute-start.9 = (f32[17,8,128]{2,1,0:T(8,128)S(1)}, f32[17,8,128]{2,1,0:T(8,128)S(1)}, u32[]{:S(2)}, u32[]{:S(2)}) collective-permute-start(f32[17,8,128]{2,1,0:T(8,128)S(1)} %get-tuple-element.33), channel_id=1, source_target_pairs={{0,8},{4,20},{8,0},{12,28},{16,24},{20,4},{24,16},{28,12},{1,9},{5... | collective-permute-start | bytes 208904 | tf_op jit(solution)/shard_map/ppermute | solution.py:60
  22.4 2.0 %collective-permute-done.8.refs_6_ = f32[17,8,128]{2,1,0:T(8,128)S(1)} collective-permute-done((f32[17,8,128]{2,1,0:T(8,128)S(1)}, f32[17,8,128]{2,1,0:T(8,128)S(1)}, u32[]{:S(2)}, u32[]{:S(2)}) %collective-permute-start.8) | collective-permute-done | bytes 69664 | tf_op jit(solution)/shard_map/ppermute | solution.py:60
  24.5 1.8 %collective-permute-start.10 = (f32[17,8,128]{2,1,0:T(8,128)S(1)}, f32[17,8,128]{2,1,0:T(8,128)S(1)}, u32[]{:S(2)}, u32[]{:S(2)}) collective-permute-start(f32[17,8,128]{2,1,0:T(8,128)S(1)} %get-tuple-element.34), channel_id=1, source_target_pairs={{0,16},{4,12},{8,24},{12,4},{16,0},{20,28},{24,8},{28,20},{1,17},{... | collective-permute-start | bytes 208904 | tf_op jit(solution)/shard_map/ppermute | solution.py:60
  26.2 0.0 copy-done.3
  26.2 1.4 %shard_map.67 = (s32[2,40]{1,0:T(2,128)S(1)}, s32[32]{0:T(128)S(1)}) custom-call(s32[1]{0:T(128)} %bitcast.here_ref.refs_0_, s32[2,8]{1,0:T(2,128)S(1)} %bitcast.16), custom_call_target="tpu_custom_call" | custom-call | tf_op jit(solution)/shard_map/pallas_call | solution.py:277
  27.7 0.0 copy-done
  27.7 0.0 copy-start.1
  27.7 1.6 %copy-done.1 = f32[32,1,16,1024]{3,2,1,0:T(8,128)S(1)} copy-done((f32[32,1,16,1024]{3,2,1,0:T(8,128)S(1)}, f32[32,1,16,1024]{3,2,1,0:T(8,128)}, u32[]{:S(2)}) %copy-start.1) | copy-done | bytes 2097176
  29.3 0.4 shard_map.68.refs_1_.decayed_ref
  29.6 0.0 collective-permute-done.9.refs_7_
  29.7 0.0 collective-permute-done.10.refs_8_
  29.7 0.0 collective-permute-done.1.refs_2_
  29.7 0.0 collective-permute-done.2.refs_3_
  29.7 0.0 collective-permute-done.3.refs_4_
  29.7 1.1 %shard_map.73 = (f32[2,2,16,1024]{3,2,1,0:T(8,128)S(1)}, f32[2,2,16,1024]{3,2,1,0:T(8,128)S(1)}, f32[2,2,16,1024]{3,2,1,0:T(8,128)S(1)}, f32[2,2,16,1024]{3,2,1,0:T(8,128)S(1)}, f32[2,8,16,1024]{3,2,1,0:T(8,128)S(1)}) custom-call(s32[2,40]{1,0:T(2,128)S(1)} %get-tuple-element.24.refs_0_, f32[32,16,1024]{2,1,0:T(8,128)S(1)} %shard_map.68.refs_1_.decayed_ref, ...), custom_call_target="tpu_custom_call" | custom-call | tf_op jit(solution)/shard_map/pallas_call | solution.py:296
  30.8 1.8 %collective-permute-start.11 = (f32[2,2,16,1024]{3,2,1,0:T(8,128)S(1)}, f32[2,2,16,1024]{3,2,1,0:T(8,128)S(1)}, u32[]{:S(2)}, u32[]{:S(2)}) collective-permute-start(f32[2,2,16,1024]{3,2,1,0:T(8,128)S(1)} %get-tuple-element.36), channel_id=1, source_target_pairs={{0,24},{4,28},{8,16},{12,20},{16,8},{20,12},{24,0},{28,4},{1,25},{... | collective-permute-start | bytes 786440 | tf_op jit(solution)/shard_map/ppermute | solution.py:60
  32.5 0.6 %collective-permute-start.12 = (f32[2,2,16,1024]{3,2,1,0:T(8,128)S(1)}, f32[2,2,16,1024]{3,2,1,0:T(8,128)S(1)}, u32[]{:S(2)}, u32[]{:S(2)}) collective-permute-start(f32[2,2,16,1024]{3,2,1,0:T(8,128)S(1)} %get-tuple-element.37), channel_id=1, source_target_pairs={{0,8},{4,20},{8,0},{12,28},{16,24},{20,4},{24,16},{28,12},{1,9},{5... | collective-permute-start | bytes 786440 | tf_op jit(solution)/shard_map/ppermute | solution.py:60
  33.1 1.2 %collective-permute-start.13 = (f32[2,2,16,1024]{3,2,1,0:T(8,128)S(1)}, f32[2,2,16,1024]{3,2,1,0:T(8,128)S(1)}, u32[]{:S(2)}, u32[]{:S(2)}) collective-permute-start(f32[2,2,16,1024]{3,2,1,0:T(8,128)S(1)} %get-tuple-element.38), channel_id=1, source_target_pairs={{0,16},{4,12},{8,24},{12,4},{16,0},{20,28},{24,8},{28,20},{1,17},{... | collective-permute-start | bytes 786440 | tf_op jit(solution)/shard_map/ppermute | solution.py:60
  34.3 3.1 %shard_map.74 = (f32[32,16,1024]{2,1,0:T(8,128)}, f32[32,16,1024]{2,1,0:T(8,128)}, f32[8,128]{1,0:T(8,128)S(1)}) custom-call(s32[32]{0:T(128)S(1)} %get-tuple-element.40.module_ref, f32[2,8,16,1024]{3,2,1,0:T(8,128)S(1)} %get-tuple-element.41.grad_ref, f32[32,16,1024]{2,1,0:T(8,128)S(1)} %shard_map.68.refs_1_.decayed_ref, f32[32,16,1024]{2,1,0:T(8,128)S(1)} %bitcast.13), custom_call_target="tpu_custom_call" | custom-call | tf_op jit(solution)/shard_map/pallas_call | solution.py:306
  37.4 3.6 %collective-permute-done.11.refs_1_ = f32[2,2,16,1024]{3,2,1,0:T(8,128)S(1)} collective-permute-done((f32[2,2,16,1024]{3,2,1,0:T(8,128)S(1)}, f32[2,2,16,1024]{3,2,1,0:T(8,128)S(1)}, u32[]{:S(2)}, u32[]{:S(2)}) %collective-permute-start.11) | collective-permute-done | bytes 262176 | tf_op jit(solution)/shard_map/ppermute | solution.py:60
  41.0 3.3 %collective-permute-done.12.refs_2_ = f32[2,2,16,1024]{3,2,1,0:T(8,128)S(1)} collective-permute-done((f32[2,2,16,1024]{3,2,1,0:T(8,128)S(1)}, f32[2,2,16,1024]{3,2,1,0:T(8,128)S(1)}, u32[]{:S(2)}, u32[]{:S(2)}) %collective-permute-start.12) | collective-permute-done | bytes 262176 | tf_op jit(solution)/shard_map/ppermute | solution.py:60
  44.3 0.0 collective-permute-done.13.refs_3_
  44.3 0.1 collective-permute-start.14
  44.4 0.9 %shard_map.76.held_ref = f32[2,4,2,16,1024]{4,3,2,1,0:T(8,128)} custom-call(s32[1]{0:T(128)} %bitcast.here_ref.refs_0_, f32[2,2,16,1024]{3,2,1,0:T(8,128)S(1)} %collective-permute-done.11.refs_1_, f32[2,2,16,1024]{3,2,1,0:T(8,128)S(1)} %collective-permute-done.12.refs_2_, f32[2,2,16,1024]{3,2,1,0:T(8,128)S(1)} %collective-permute-done.13.refs_3_, ...), custom_call_target="tpu_custom_call" | custom-call | tf_op jit(solution)/shard_map/pallas_call | solution.py:318
  45.3 1.0 %collective-permute-done.14.back_ref = f32[2,4,16,1024]{3,2,1,0:T(8,128)S(1)} collective-permute-done((f32[2,4,16,1024]{3,2,1,0:T(8,128)S(1)}, f32[2,4,16,1024]{3,2,1,0:T(8,128)S(1)}, u32[]{:S(2)}, u32[]{:S(2)}) %collective-permute-start.14) | collective-permute-done | bytes 524320 | tf_op jit(solution)/shard_map/ppermute | solution.py:316
  46.3 0.8 %shard_map.77 = f32[2,4,2,16,1024]{4,3,2,1,0:T(8,128)} custom-call(s32[1]{0:T(128)} %bitcast.here_ref.refs_0_, f32[2,4,16,1024]{3,2,1,0:T(8,128)S(1)} %collective-permute-done.14.back_ref, f32[2,4,2,16,1024]{4,3,2,1,0:T(8,128)} %shard_map.76.held_ref), custom_call_target="tpu_custom_call", output_to_operand_aliasing={{}: (2, {})} | custom-call | tf_op jit(solution)/shard_map/pallas_call | solution.py:325
  (3 shorter events, 0.1 us)
Async XLA Ops:
  0.6 27.0 %copy-start = (f32[32,1,16,1024]{3,2,1,0:T(8,128)S(1)}, f32[32,1,16,1024]{3,2,1,0:T(8,128)}, u32[]{:S(2)}) copy-start(f32[32,1,16,1024]{3,2,1,0:T(8,128)} %param.7) | copy-start | bytes 6291460
  0.6 1.4 %copy-start.2 = (f32[1,2,128,1024]{3,2,1,0:T(8,128)S(1)}, f32[1,2,128,1024]{3,2,1,0:T(8,128)}, u32[]{:S(2)}) copy-start(f32[1,2,128,1024]{3,2,1,0:T(8,128)} %param.4) | copy-start | bytes 3145732
  2.0 24.2 %copy-start.3 = (s32[8,2]{0,1:T(2,128)S(1)}, s32[8,2]{0,1:T(2,128)}, u32[]{:S(2)}) copy-start(s32[8,2]{0,1:T(2,128)} %param.5) | copy-start | bytes 196
  2.1 2.0 %collective-permute-start = (f32[2,4,16,1024]{3,2,1,0:T(8,128)S(1)}, f32[2,4,16,1024]{3,2,1,0:T(8,128)S(1)}, u32[]{:S(2)}, u32[]{:S(2)}) collective-permute-start(f32[2,4,16,1024]{3,2,1,0:T(8,128)S(1)} %get-tuple-element.26), channel_id=1, source_target_pairs={{0,4},{4,0},{8,12},{12,8},{16,20},{20,16},{24,28},{28,24},{1,5},{5... | collective-permute-start | bytes 1572872 | tf_op jit(solution)/shard_map/ppermute | solution.py:265
  4.2 25.4 %collective-permute-start.1 = (f32[2,24,1024]{2,1,0:T(8,128)S(1)}, f32[2,24,1024]{2,1,0:T(8,128)S(1)}, u32[]{:S(2)}, u32[]{:S(2)}) collective-permute-start(f32[2,24,1024]{2,1,0:T(8,128)S(1)} %get-tuple-element.27), channel_id=1, source_target_pairs={{0,24},{4,28},{8,16},{12,20},{16,8},{20,12},{24,0},{28,4},{1,25},{... | collective-permute-start | bytes 589832 | tf_op jit(solution)/shard_map/ppermute | solution.py:60
  8.1 21.6 %collective-permute-start.2 = (f32[2,24,1024]{2,1,0:T(8,128)S(1)}, f32[2,24,1024]{2,1,0:T(8,128)S(1)}, u32[]{:S(2)}, u32[]{:S(2)}) collective-permute-start(f32[2,24,1024]{2,1,0:T(8,128)S(1)} %get-tuple-element.28), channel_id=1, source_target_pairs={{0,8},{4,20},{8,0},{12,28},{16,24},{20,4},{24,16},{28,12},{1,9},{5... | collective-permute-start | bytes 589832 | tf_op jit(solution)/shard_map/ppermute | solution.py:60
  8.7 21.0 %collective-permute-start.3 = (f32[2,24,1024]{2,1,0:T(8,128)S(1)}, f32[2,24,1024]{2,1,0:T(8,128)S(1)}, u32[]{:S(2)}, u32[]{:S(2)}) collective-permute-start(f32[2,24,1024]{2,1,0:T(8,128)S(1)} %get-tuple-element.29), channel_id=1, source_target_pairs={{0,16},{4,12},{8,24},{12,4},{16,0},{20,28},{24,8},{28,20},{1,17},{... | collective-permute-start | bytes 589832 | tf_op jit(solution)/shard_map/ppermute | solution.py:60
  8.8 5.6 %collective-permute-start.4 = (f32[8,128]{1,0:T(8,128)S(1)}, f32[8,128]{1,0:T(8,128)S(1)}, u32[]{:S(2)}, u32[]{:S(2)}) collective-permute-start(f32[8,128]{1,0:T(8,128)S(1)} %get-tuple-element.31.refs_0_), channel_id=1, source_target_pairs={{0,3},{1,2},{2,1},{3,0},{4,7},{5,6},{6,5},{7,4},{8,11},{9,10},{10,... | collective-permute-start | bytes 12296 | tf_op jit(solution)/shard_map/ppermute | solution.py:267
  12.8 4.5 %collective-permute-start.5 = (f32[8,128]{1,0:T(8,128)S(1)}, f32[8,128]{1,0:T(8,128)S(1)}, u32[]{:S(2)}, u32[]{:S(2)}) collective-permute-start(f32[8,128]{1,0:T(8,128)S(1)} %get-tuple-element.31.refs_0_), channel_id=1, source_target_pairs={{0,2},{1,3},{2,0},{3,1},{4,6},{5,7},{6,4},{7,5},{8,10},{9,11},{10,... | collective-permute-start | bytes 12296 | tf_op jit(solution)/shard_map/ppermute | solution.py:267
  14.4 3.6 %collective-permute-start.6 = (f32[8,128]{1,0:T(8,128)S(1)}, f32[8,128]{1,0:T(8,128)S(1)}, u32[]{:S(2)}, u32[]{:S(2)}) collective-permute-start(f32[8,128]{1,0:T(8,128)S(1)} %get-tuple-element.31.refs_0_), channel_id=1, source_target_pairs={{0,1},{1,0},{2,3},{3,2},{4,5},{5,4},{6,7},{7,6},{8,9},{9,8},{10,11... | collective-permute-start | bytes 12296 | tf_op jit(solution)/shard_map/ppermute | solution.py:267
  18.0 1.2 %collective-permute-start.7 = (f32[8,128]{1,0:T(8,128)S(1)}, f32[8,128]{1,0:T(8,128)S(1)}, u32[]{:S(2)}, u32[]{:S(2)}) collective-permute-start(f32[8,128]{1,0:T(8,128)S(1)} %shard_map.71.refs_1_), channel_id=1, source_target_pairs={{0,4},{4,0},{8,12},{12,8},{16,20},{20,16},{24,28},{28,24},{1,5},{5... | collective-permute-start | bytes 12296 | tf_op jit(solution)/shard_map/ppermute | solution.py:287
  19.2 5.3 %collective-permute-start.8 = (f32[17,8,128]{2,1,0:T(8,128)S(1)}, f32[17,8,128]{2,1,0:T(8,128)S(1)}, u32[]{:S(2)}, u32[]{:S(2)}) collective-permute-start(f32[17,8,128]{2,1,0:T(8,128)S(1)} %get-tuple-element.32), channel_id=1, source_target_pairs={{0,24},{4,28},{8,16},{12,20},{16,8},{20,12},{24,0},{28,4},{1,25},{... | collective-permute-start | bytes 208904 | tf_op jit(solution)/shard_map/ppermute | solution.py:60
  21.9 7.8 %collective-permute-start.9 = (f32[17,8,128]{2,1,0:T(8,128)S(1)}, f32[17,8,128]{2,1,0:T(8,128)S(1)}, u32[]{:S(2)}, u32[]{:S(2)}) collective-permute-start(f32[17,8,128]{2,1,0:T(8,128)S(1)} %get-tuple-element.33), channel_id=1, source_target_pairs={{0,8},{4,20},{8,0},{12,28},{16,24},{20,4},{24,16},{28,12},{1,9},{5... | collective-permute-start | bytes 208904 | tf_op jit(solution)/shard_map/ppermute | solution.py:60
  24.5 5.2 %collective-permute-start.10 = (f32[17,8,128]{2,1,0:T(8,128)S(1)}, f32[17,8,128]{2,1,0:T(8,128)S(1)}, u32[]{:S(2)}, u32[]{:S(2)}) collective-permute-start(f32[17,8,128]{2,1,0:T(8,128)S(1)} %get-tuple-element.34), channel_id=1, source_target_pairs={{0,16},{4,12},{8,24},{12,4},{16,0},{20,28},{24,8},{28,20},{1,17},{... | collective-permute-start | bytes 208904 | tf_op jit(solution)/shard_map/ppermute | solution.py:60
  27.7 1.6 %copy-start.1 = (f32[32,1,16,1024]{3,2,1,0:T(8,128)S(1)}, f32[32,1,16,1024]{3,2,1,0:T(8,128)}, u32[]{:S(2)}) copy-start(f32[32,1,16,1024]{3,2,1,0:T(8,128)} %param.6) | copy-start | bytes 6291460
  30.8 10.2 %collective-permute-start.11 = (f32[2,2,16,1024]{3,2,1,0:T(8,128)S(1)}, f32[2,2,16,1024]{3,2,1,0:T(8,128)S(1)}, u32[]{:S(2)}, u32[]{:S(2)}) collective-permute-start(f32[2,2,16,1024]{3,2,1,0:T(8,128)S(1)} %get-tuple-element.36), channel_id=1, source_target_pairs={{0,24},{4,28},{8,16},{12,20},{16,8},{20,12},{24,0},{28,4},{1,25},{... | collective-permute-start | bytes 786440 | tf_op jit(solution)/shard_map/ppermute | solution.py:60
  32.5 11.8 %collective-permute-start.12 = (f32[2,2,16,1024]{3,2,1,0:T(8,128)S(1)}, f32[2,2,16,1024]{3,2,1,0:T(8,128)S(1)}, u32[]{:S(2)}, u32[]{:S(2)}) collective-permute-start(f32[2,2,16,1024]{3,2,1,0:T(8,128)S(1)} %get-tuple-element.37), channel_id=1, source_target_pairs={{0,8},{4,20},{8,0},{12,28},{16,24},{20,4},{24,16},{28,12},{1,9},{5... | collective-permute-start | bytes 786440 | tf_op jit(solution)/shard_map/ppermute | solution.py:60
  33.1 11.2 %collective-permute-start.13 = (f32[2,2,16,1024]{3,2,1,0:T(8,128)S(1)}, f32[2,2,16,1024]{3,2,1,0:T(8,128)S(1)}, u32[]{:S(2)}, u32[]{:S(2)}) collective-permute-start(f32[2,2,16,1024]{3,2,1,0:T(8,128)S(1)} %get-tuple-element.38), channel_id=1, source_target_pairs={{0,16},{4,12},{8,24},{12,4},{16,0},{20,28},{24,8},{28,20},{1,17},{... | collective-permute-start | bytes 786440 | tf_op jit(solution)/shard_map/ppermute | solution.py:60
  44.3 2.0 %collective-permute-start.14 = (f32[2,4,16,1024]{3,2,1,0:T(8,128)S(1)}, f32[2,4,16,1024]{3,2,1,0:T(8,128)S(1)}, u32[]{:S(2)}, u32[]{:S(2)}) collective-permute-start(f32[2,4,16,1024]{3,2,1,0:T(8,128)S(1)} %shard_map.75), channel_id=1, source_target_pairs={{0,4},{4,0},{8,12},{12,8},{16,20},{20,16},{24,28},{28,24},{1,5},{5... | collective-permute-start | bytes 1572872 | tf_op jit(solution)/shard_map/ppermute | solution.py:316

commit v6 on v5

--- a/solution.py
+++ b/solution.py
@@ -111,16 +111,16 @@
         out[2 * len(spots)] = squares
 
 
-def sum_kernel(*refs):
+def sum_kernel(count, *refs):
     total = refs[0][...]
-    for ref in refs[1:-1]:
+    for ref in refs[1:count]:
         total = total + ref[...]
     refs[-1][...] = total
 
 
-def decay_kernel(params_ref, momentum_ref, out_ref):
+def decay_kernel(params_ref, decay_ref, out_ref):
     def decay(module, carry):
-        out_ref[module] = params_ref[module] - moment_coef * momentum_ref[module]
+        out_ref[module] = params_ref[module] - decay_ref[module]
         return carry
 
     lax.fori_loop(0, out_ref.shape[0], decay, 0)
@@ -273,7 +273,8 @@
         [vmem] * rounds,
     )(here, keep, gift)
     firsts = [move(firsts[j], k, size) for j, k in enumerate(order)]
-    decayed = call(decay_kernel, shape(*state_in.shape), [vmem, vmem], vmem)(state_in, moment_in)
+    decay = moment_coef * moment_in
+    decayed = call(decay_kernel, shape(*state_in.shape), [vmem, vmem], vmem)(state_in, decay)
     plan, leaders = call(
         plan_kernel,
         [
@@ -283,7 +284,9 @@
         [smem, smem],
         [smem, smem],
     )(here, assign.T)
-    squares = call(sum_kernel, squares_shape, [vmem] * shards, vmem)(*tiles)
+    squares = call(
+        lambda *refs: sum_kernel(shards, *refs), squares_shape, [vmem] * shards + [anywhere], vmem
+    )(*tiles, decay)
     other = lax.ppermute(squares, "path", swap)
     seconds = call(
         lambda *refs: second_merge_kernel(size, *refs),

time: 47.3 us -> 42 us (0.89)
  waiting for transfers between devices: 17.8 us -> 13.8 us
  local copies, waits for them, and re-layouts: 2.96 us -> 1.38 us
    ppermute x3, waiting for transfers between devices: 5.18 us -> 0.01 us  [local(): lax.ppermute(squares, 'shard', [(i, i ^ step) for i in range(shards)])]
    ppermute x9, waiting for transfers between devices: 8.93 us -> 11.6 us  [move(): lax.ppermute(array, 'path', [(i, target(i, k, size)) for i in range(size)])]
    unnamed x8, local copies, waits for them, and re-layouts: 2.96 us -> 1.38 us
    ppermute x1, waiting for transfers between devices: 1.54 us -> 0.01 us  [local(): gift = lax.ppermute(give, 'path', swap)]
    ppermute x3, starting transfers between devices: 4.01 us -> 5.33 us  [local(): lax.ppermute(squares, 'shard', [(i, i ^ step) for i in range(shards)])]
    ppermute x9, starting transfers between devices: 13.1 us -> 11.8 us  [move(): lax.ppermute(array, 'path', [(i, target(i, k, size)) for i in range(size)])]
  transfers between devices with their start and end apart: 15 -> 15, of which waited for: 9 -> 6; matrix products, arithmetic and copies ran while one was open for 0% -> 1% of each run, Pallas kernels for 12% -> 14%
where the time goes in v6:
time: 42 us; the launch traced here: 41.8 us
  starting transfers between devices  17.8 us (42%)
  waiting for transfers between devices  13.8 us (33%)
  Pallas kernels  7.77 us (18%)
  local copies, waits for them, and re-layouts  1.38 us (3%)
  between operations  0.79 us (2%)
    ppermute x9, starting transfers between devices, move(): lax.ppermute(array, 'path', [(i, target(i, k, size)) for i in range(size)])  11.8 us
    ppermute x9, waiting for transfers between devices, move(): lax.ppermute(array, 'path', [(i, target(i, k, size)) for i in range(size)])  11.6 us
    ppermute x3, starting transfers between devices, local(): lax.ppermute(squares, 'shard', [(i, i ^ step) for i in range(shards)])  5.33 us
    pallas_call x1, Pallas kernels, local(): call(state_kernel, [shape(*state_in.shape)] * 2 + [shape(8, 128)], [smem,...  3.08 us
    pallas_call x1, Pallas kernels, local(): call(plan_kernel, [jax.ShapeDtypeStruct((LEVELS, 5 * size), jnp.int32), j...  1.4 us
    unnamed x8, local copies, waits for them, and re-layouts  1.38 us
    ppermute x1, waiting for transfers between devices, local(): other = lax.ppermute(squares, 'path', swap)  1.15 us
    pallas_call x1, Pallas kernels, local(): call(lambda *refs: outgoing_kernel(rounds, entries, *refs), [message] * r...  1.04 us
  transfers between devices with their start and end apart: 15, of which 6 were waited for; matrix products, arithmetic and copies ran while one was open for 1% of the time, Pallas kernels for 14%

profile of v6, /device:TPU:0, one launch (start us, length us, event | category | flops | bytes accessed | tf_op | source)
XLA Modules:
  0.0 41.8 jit_solution(4394923054143283023)
XLA Ops:
  0.6 0.0 copy-start
  0.6 0.0 copy-start.2
  0.7 1.4 %copy-done.2 = f32[1,2,128,1024]{3,2,1,0:T(8,128)S(1)} copy-done((f32[1,2,128,1024]{3,2,1,0:T(8,128)S(1)}, f32[1,2,128,1024]{3,2,1,0:T(8,128)}, u32[]{:S(2)}) %copy-start.2) | copy-done | bytes 1048600
  2.0 0.1 shard_map.69
  2.1 0.5 %collective-permute-start = (f32[2,4,16,1024]{3,2,1,0:T(8,128)S(1)}, f32[2,4,16,1024]{3,2,1,0:T(8,128)S(1)}, u32[]{:S(2)}, u32[]{:S(2)}) collective-permute-start(f32[2,4,16,1024]{3,2,1,0:T(8,128)S(1)} %get-tuple-element.26), channel_id=1, source_target_pairs={{0,4},{4,0},{8,12},{12,8},{16,20},{20,16},{24,28},{28,24},{1,5},{5... | collective-permute-start | bytes 1572872 | tf_op jit(solution)/shard_map/ppermute | solution.py:265
  2.6 4.7 %collective-permute-start.4 = (f32[8,128]{1,0:T(8,128)S(1)}, f32[8,128]{1,0:T(8,128)S(1)}, u32[]{:S(2)}, u32[]{:S(2)}) collective-permute-start(f32[8,128]{1,0:T(8,128)S(1)} %get-tuple-element.31.refs_0_), channel_id=1, source_target_pairs={{0,3},{1,2},{2,1},{3,0},{4,7},{5,6},{6,5},{7,4},{8,11},{9,10},{10,... | collective-permute-start | bytes 12296 | tf_op jit(solution)/shard_map/ppermute | solution.py:267
  7.3 0.0 collective-permute-start.5
  7.3 0.6 %collective-permute-start.6 = (f32[8,128]{1,0:T(8,128)S(1)}, f32[8,128]{1,0:T(8,128)S(1)}, u32[]{:S(2)}, u32[]{:S(2)}) collective-permute-start(f32[8,128]{1,0:T(8,128)S(1)} %get-tuple-element.31.refs_0_), channel_id=1, source_target_pairs={{0,1},{1,0},{2,3},{3,2},{4,5},{5,4},{6,7},{7,6},{8,9},{9,8},{10,11... | collective-permute-start | bytes 12296 | tf_op jit(solution)/shard_map/ppermute | solution.py:267
  8.0 0.0 collective-permute-done.refs_2_.refs_4_
  8.0 0.1 shard_map.70
  8.0 2.7 %collective-permute-start.1 = (f32[2,24,1024]{2,1,0:T(8,128)S(1)}, f32[2,24,1024]{2,1,0:T(8,128)S(1)}, u32[]{:S(2)}, u32[]{:S(2)}) collective-permute-start(f32[2,24,1024]{2,1,0:T(8,128)S(1)} %get-tuple-element.27), channel_id=1, source_target_pairs={{0,24},{4,28},{8,16},{12,20},{16,8},{20,12},{24,0},{28,4},{1,25},{... | collective-permute-start | bytes 589832 | tf_op jit(solution)/shard_map/ppermute | solution.py:60
  10.7 0.5 %collective-permute-start.2 = (f32[2,24,1024]{2,1,0:T(8,128)S(1)}, f32[2,24,1024]{2,1,0:T(8,128)S(1)}, u32[]{:S(2)}, u32[]{:S(2)}) collective-permute-start(f32[2,24,1024]{2,1,0:T(8,128)S(1)} %get-tuple-element.28), channel_id=1, source_target_pairs={{0,8},{4,20},{8,0},{12,28},{16,24},{20,4},{24,16},{28,12},{1,9},{5... | collective-permute-start | bytes 589832 | tf_op jit(solution)/shard_map/ppermute | solution.py:60
  11.2 0.0 collective-permute-done.4.refs_1_
  11.2 0.4 collective-permute-start.3
  11.6 0.0 copy-done
  11.6 0.3 broadcast_multiply_fusion.decay_ref.refs_4_
  11.9 0.0 copy-start.3
  11.9 0.0 copy-start.1
  11.9 0.0 collective-permute-done.5.refs_2_
  11.9 0.0 collective-permute-done.6.refs_3_
  11.9 0.1 collective-permute-start.7
  12.0 1.2 %collective-permute-done.7.refs_2_ = f32[8,128]{1,0:T(8,128)S(1)} collective-permute-done((f32[8,128]{1,0:T(8,128)S(1)}, f32[8,128]{1,0:T(8,128)S(1)}, u32[]{:S(2)}, u32[]{:S(2)}) %collective-permute-start.7) | collective-permute-done | bytes 4128 | tf_op jit(solution)/shard_map/ppermute | solution.py:290
  13.2 2.7 %collective-permute-start.8 = (f32[17,8,128]{2,1,0:T(8,128)S(1)}, f32[17,8,128]{2,1,0:T(8,128)S(1)}, u32[]{:S(2)}, u32[]{:S(2)}) collective-permute-start(f32[17,8,128]{2,1,0:T(8,128)S(1)} %get-tuple-element.32), channel_id=1, source_target_pairs={{0,24},{4,28},{8,16},{12,20},{16,8},{20,12},{24,0},{28,4},{1,25},{... | collective-permute-start | bytes 208904 | tf_op jit(solution)/shard_map/ppermute | solution.py:60
  15.9 0.5 %collective-permute-start.9 = (f32[17,8,128]{2,1,0:T(8,128)S(1)}, f32[17,8,128]{2,1,0:T(8,128)S(1)}, u32[]{:S(2)}, u32[]{:S(2)}) collective-permute-start(f32[17,8,128]{2,1,0:T(8,128)S(1)} %get-tuple-element.33), channel_id=1, source_target_pairs={{0,8},{4,20},{8,0},{12,28},{16,24},{20,4},{24,16},{28,12},{1,9},{5... | collective-permute-start | bytes 208904 | tf_op jit(solution)/shard_map/ppermute | solution.py:60
  16.4 5.0 %collective-permute-done.8.refs_6_ = f32[17,8,128]{2,1,0:T(8,128)S(1)} collective-permute-done((f32[17,8,128]{2,1,0:T(8,128)S(1)}, f32[17,8,128]{2,1,0:T(8,128)S(1)}, u32[]{:S(2)}, u32[]{:S(2)}) %collective-permute-start.8) | collective-permute-done | bytes 69664 | tf_op jit(solution)/shard_map/ppermute | solution.py:60
  21.4 1.5 %collective-permute-start.10 = (f32[17,8,128]{2,1,0:T(8,128)S(1)}, f32[17,8,128]{2,1,0:T(8,128)S(1)}, u32[]{:S(2)}, u32[]{:S(2)}) collective-permute-start(f32[17,8,128]{2,1,0:T(8,128)S(1)} %get-tuple-element.34), channel_id=1, source_target_pairs={{0,16},{4,12},{8,24},{12,4},{16,0},{20,28},{24,8},{28,20},{1,17},{... | collective-permute-start | bytes 208904 | tf_op jit(solution)/shard_map/ppermute | solution.py:60
  23.0 0.0 copy-done.3
  23.0 1.4 %shard_map.67 = (s32[2,40]{1,0:T(2,128)S(1)}, s32[32]{0:T(128)S(1)}) custom-call(s32[1]{0:T(128)} %bitcast.here_ref.refs_0_, s32[2,8]{1,0:T(2,128)S(1)} %bitcast.16), custom_call_target="tpu_custom_call" | custom-call | tf_op jit(solution)/shard_map/pallas_call | solution.py:278
  24.4 0.0 copy-done.1
  24.4 0.3 shard_map.68.refs_1_.decayed_ref
  24.7 0.0 collective-permute-done.9.refs_7_
  24.7 1.0 %collective-permute-done.10.refs_8_ = f32[17,8,128]{2,1,0:T(8,128)S(1)} collective-permute-done((f32[17,8,128]{2,1,0:T(8,128)S(1)}, f32[17,8,128]{2,1,0:T(8,128)S(1)}, u32[]{:S(2)}, u32[]{:S(2)}) %collective-permute-start.10) | collective-permute-done | bytes 69664 | tf_op jit(solution)/shard_map/ppermute | solution.py:60
  25.7 0.0 collective-permute-done.1.refs_2_
  25.8 0.0 collective-permute-done.2.refs_3_
  25.8 0.0 collective-permute-done.3.refs_4_
  25.8 1.0 %shard_map.73 = (f32[2,2,16,1024]{3,2,1,0:T(8,128)S(1)}, f32[2,2,16,1024]{3,2,1,0:T(8,128)S(1)}, f32[2,2,16,1024]{3,2,1,0:T(8,128)S(1)}, f32[2,2,16,1024]{3,2,1,0:T(8,128)S(1)}, f32[2,8,16,1024]{3,2,1,0:T(8,128)S(1)}) custom-call(s32[2,40]{1,0:T(2,128)S(1)} %get-tuple-element.24.refs_0_, f32[32,16,1024]{2,1,0:T(8,128)S(1)} %shard_map.68.refs_1_.decayed_ref, ...), custom_call_target="tpu_custom_call" | custom-call | tf_op jit(solution)/shard_map/pallas_call | solution.py:299
  26.8 2.4 %collective-permute-start.11 = (f32[2,2,16,1024]{3,2,1,0:T(8,128)S(1)}, f32[2,2,16,1024]{3,2,1,0:T(8,128)S(1)}, u32[]{:S(2)}, u32[]{:S(2)}) collective-permute-start(f32[2,2,16,1024]{3,2,1,0:T(8,128)S(1)} %get-tuple-element.36), channel_id=1, source_target_pairs={{0,24},{4,28},{8,16},{12,20},{16,8},{20,12},{24,0},{28,4},{1,25},{... | collective-permute-start | bytes 786440 | tf_op jit(solution)/shard_map/ppermute | solution.py:60
  29.2 0.6 %collective-permute-start.12 = (f32[2,2,16,1024]{3,2,1,0:T(8,128)S(1)}, f32[2,2,16,1024]{3,2,1,0:T(8,128)S(1)}, u32[]{:S(2)}, u32[]{:S(2)}) collective-permute-start(f32[2,2,16,1024]{3,2,1,0:T(8,128)S(1)} %get-tuple-element.37), channel_id=1, source_target_pairs={{0,8},{4,20},{8,0},{12,28},{16,24},{20,4},{24,16},{28,12},{1,9},{5... | collective-permute-start | bytes 786440 | tf_op jit(solution)/shard_map/ppermute | solution.py:60
  29.9 0.5 %collective-permute-start.13 = (f32[2,2,16,1024]{3,2,1,0:T(8,128)S(1)}, f32[2,2,16,1024]{3,2,1,0:T(8,128)S(1)}, u32[]{:S(2)}, u32[]{:S(2)}) collective-permute-start(f32[2,2,16,1024]{3,2,1,0:T(8,128)S(1)} %get-tuple-element.38), channel_id=1, source_target_pairs={{0,16},{4,12},{8,24},{12,4},{16,0},{20,28},{24,8},{28,20},{1,17},{... | collective-permute-start | bytes 786440 | tf_op jit(solution)/shard_map/ppermute | solution.py:60
  30.4 3.1 %shard_map.74 = (f32[32,16,1024]{2,1,0:T(8,128)}, f32[32,16,1024]{2,1,0:T(8,128)}, f32[8,128]{1,0:T(8,128)S(1)}) custom-call(s32[32]{0:T(128)S(1)} %get-tuple-element.40.module_ref, f32[2,8,16,1024]{3,2,1,0:T(8,128)S(1)} %get-tuple-element.41.grad_ref, f32[32,16,1024]{2,1,0:T(8,128)S(1)} %shard_map.68.refs_1_.decayed_ref, f32[32,16,1024]{2,1,0:T(8,128)S(1)} %bitcast.13), custom_call_target="tpu_custom_call" | custom-call | tf_op jit(solution)/shard_map/pallas_call | solution.py:309
  33.4 2.8 %collective-permute-done.11.refs_1_ = f32[2,2,16,1024]{3,2,1,0:T(8,128)S(1)} collective-permute-done((f32[2,2,16,1024]{3,2,1,0:T(8,128)S(1)}, f32[2,2,16,1024]{3,2,1,0:T(8,128)S(1)}, u32[]{:S(2)}, u32[]{:S(2)}) %collective-permute-start.11) | collective-permute-done | bytes 262176 | tf_op jit(solution)/shard_map/ppermute | solution.py:60
  36.3 2.7 %collective-permute-done.12.refs_2_ = f32[2,2,16,1024]{3,2,1,0:T(8,128)S(1)} collective-permute-done((f32[2,2,16,1024]{3,2,1,0:T(8,128)S(1)}, f32[2,2,16,1024]{3,2,1,0:T(8,128)S(1)}, u32[]{:S(2)}, u32[]{:S(2)}) %collective-permute-start.12) | collective-permute-done | bytes 262176 | tf_op jit(solution)/shard_map/ppermute | solution.py:60
  39.0 0.0 collective-permute-done.13.refs_3_
  39.0 0.1 collective-permute-start.14
  39.1 0.9 %shard_map.76.held_ref = f32[2,4,2,16,1024]{4,3,2,1,0:T(8,128)} custom-call(s32[1]{0:T(128)} %bitcast.here_ref.refs_0_, f32[2,2,16,1024]{3,2,1,0:T(8,128)S(1)} %collective-permute-done.11.refs_1_, f32[2,2,16,1024]{3,2,1,0:T(8,128)S(1)} %collective-permute-done.12.refs_2_, f32[2,2,16,1024]{3,2,1,0:T(8,128)S(1)} %collective-permute-done.13.refs_3_, ...), custom_call_target="tpu_custom_call" | custom-call | tf_op jit(solution)/shard_map/pallas_call | solution.py:321
  40.0 1.0 %collective-permute-done.14.back_ref = f32[2,4,16,1024]{3,2,1,0:T(8,128)S(1)} collective-permute-done((f32[2,4,16,1024]{3,2,1,0:T(8,128)S(1)}, f32[2,4,16,1024]{3,2,1,0:T(8,128)S(1)}, u32[]{:S(2)}, u32[]{:S(2)}) %collective-permute-start.14) | collective-permute-done | bytes 524320 | tf_op jit(solution)/shard_map/ppermute | solution.py:319
  41.0 0.8 %shard_map.77 = f32[2,4,2,16,1024]{4,3,2,1,0:T(8,128)} custom-call(s32[1]{0:T(128)} %bitcast.here_ref.refs_0_, f32[2,4,16,1024]{3,2,1,0:T(8,128)S(1)} %collective-permute-done.14.back_ref, f32[2,4,2,16,1024]{4,3,2,1,0:T(8,128)} %shard_map.76.held_ref), custom_call_target="tpu_custom_call", output_to_operand_aliasing={{}: (2, {})} | custom-call | tf_op jit(solution)/shard_map/pallas_call | solution.py:328
  (3 shorter events, 0.1 us)
Async XLA Ops:
  0.6 11.0 %copy-start = (f32[32,1,16,1024]{3,2,1,0:T(8,128)S(1)}, f32[32,1,16,1024]{3,2,1,0:T(8,128)}, u32[]{:S(2)}) copy-start(f32[32,1,16,1024]{3,2,1,0:T(8,128)} %param.7) | copy-start | bytes 6291460
  0.6 1.4 %copy-start.2 = (f32[1,2,128,1024]{3,2,1,0:T(8,128)S(1)}, f32[1,2,128,1024]{3,2,1,0:T(8,128)}, u32[]{:S(2)}) copy-start(f32[1,2,128,1024]{3,2,1,0:T(8,128)} %param.4) | copy-start | bytes 3145732
  2.1 5.8 %collective-permute-start = (f32[2,4,16,1024]{3,2,1,0:T(8,128)S(1)}, f32[2,4,16,1024]{3,2,1,0:T(8,128)S(1)}, u32[]{:S(2)}, u32[]{:S(2)}) collective-permute-start(f32[2,4,16,1024]{3,2,1,0:T(8,128)S(1)} %get-tuple-element.26), channel_id=1, source_target_pairs={{0,4},{4,0},{8,12},{12,8},{16,20},{20,16},{24,28},{28,24},{1,5},{5... | collective-permute-start | bytes 1572872 | tf_op jit(solution)/shard_map/ppermute | solution.py:265
  2.6 8.6 %collective-permute-start.4 = (f32[8,128]{1,0:T(8,128)S(1)}, f32[8,128]{1,0:T(8,128)S(1)}, u32[]{:S(2)}, u32[]{:S(2)}) collective-permute-start(f32[8,128]{1,0:T(8,128)S(1)} %get-tuple-element.31.refs_0_), channel_id=1, source_target_pairs={{0,3},{1,2},{2,1},{3,0},{4,7},{5,6},{6,5},{7,4},{8,11},{9,10},{10,... | collective-permute-start | bytes 12296 | tf_op jit(solution)/shard_map/ppermute | solution.py:267
  7.3 4.6 %collective-permute-start.5 = (f32[8,128]{1,0:T(8,128)S(1)}, f32[8,128]{1,0:T(8,128)S(1)}, u32[]{:S(2)}, u32[]{:S(2)}) collective-permute-start(f32[8,128]{1,0:T(8,128)S(1)} %get-tuple-element.31.refs_0_), channel_id=1, source_target_pairs={{0,2},{1,3},{2,0},{3,1},{4,6},{5,7},{6,4},{7,5},{8,10},{9,11},{10,... | collective-permute-start | bytes 12296 | tf_op jit(solution)/shard_map/ppermute | solution.py:267
  7.3 4.6 %collective-permute-start.6 = (f32[8,128]{1,0:T(8,128)S(1)}, f32[8,128]{1,0:T(8,128)S(1)}, u32[]{:S(2)}, u32[]{:S(2)}) collective-permute-start(f32[8,128]{1,0:T(8,128)S(1)} %get-tuple-element.31.refs_0_), channel_id=1, source_target_pairs={{0,1},{1,0},{2,3},{3,2},{4,5},{5,4},{6,7},{7,6},{8,9},{9,8},{10,11... | collective-permute-start | bytes 12296 | tf_op jit(solution)/shard_map/ppermute | solution.py:267
  8.0 17.7 %collective-permute-start.1 = (f32[2,24,1024]{2,1,0:T(8,128)S(1)}, f32[2,24,1024]{2,1,0:T(8,128)S(1)}, u32[]{:S(2)}, u32[]{:S(2)}) collective-permute-start(f32[2,24,1024]{2,1,0:T(8,128)S(1)} %get-tuple-element.27), channel_id=1, source_target_pairs={{0,24},{4,28},{8,16},{12,20},{16,8},{20,12},{24,0},{28,4},{1,25},{... | collective-permute-start | bytes 589832 | tf_op jit(solution)/shard_map/ppermute | solution.py:60
  10.7 15.1 %collective-permute-start.2 = (f32[2,24,1024]{2,1,0:T(8,128)S(1)}, f32[2,24,1024]{2,1,0:T(8,128)S(1)}, u32[]{:S(2)}, u32[]{:S(2)}) collective-permute-start(f32[2,24,1024]{2,1,0:T(8,128)S(1)} %get-tuple-element.28), channel_id=1, source_target_pairs={{0,8},{4,20},{8,0},{12,28},{16,24},{20,4},{24,16},{28,12},{1,9},{5... | collective-permute-start | bytes 589832 | tf_op jit(solution)/shard_map/ppermute | solution.py:60
  11.2 14.5 %collective-permute-start.3 = (f32[2,24,1024]{2,1,0:T(8,128)S(1)}, f32[2,24,1024]{2,1,0:T(8,128)S(1)}, u32[]{:S(2)}, u32[]{:S(2)}) collective-permute-start(f32[2,24,1024]{2,1,0:T(8,128)S(1)} %get-tuple-element.29), channel_id=1, source_target_pairs={{0,16},{4,12},{8,24},{12,4},{16,0},{20,28},{24,8},{28,20},{1,17},{... | collective-permute-start | bytes 589832 | tf_op jit(solution)/shard_map/ppermute | solution.py:60
  11.9 11.1 %copy-start.3 = (s32[8,2]{0,1:T(2,128)S(1)}, s32[8,2]{0,1:T(2,128)}, u32[]{:S(2)}) copy-start(s32[8,2]{0,1:T(2,128)} %param.5) | copy-start | bytes 196
  11.9 12.5 %copy-start.1 = (f32[32,1,16,1024]{3,2,1,0:T(8,128)S(1)}, f32[32,1,16,1024]{3,2,1,0:T(8,128)}, u32[]{:S(2)}) copy-start(f32[32,1,16,1024]{3,2,1,0:T(8,128)} %param.6) | copy-start | bytes 6291460
  11.9 1.2 %collective-permute-start.7 = (f32[8,128]{1,0:T(8,128)S(1)}, f32[8,128]{1,0:T(8,128)S(1)}, u32[]{:S(2)}, u32[]{:S(2)}) collective-permute-start(f32[8,128]{1,0:T(8,128)S(1)} %shard_map.71.refs_1_), channel_id=1, source_target_pairs={{0,4},{4,0},{8,12},{12,8},{16,20},{20,16},{24,28},{28,24},{1,5},{5... | collective-permute-start | bytes 12296 | tf_op jit(solution)/shard_map/ppermute | solution.py:290
  13.2 8.2 %collective-permute-start.8 = (f32[17,8,128]{2,1,0:T(8,128)S(1)}, f32[17,8,128]{2,1,0:T(8,128)S(1)}, u32[]{:S(2)}, u32[]{:S(2)}) collective-permute-start(f32[17,8,128]{2,1,0:T(8,128)S(1)} %get-tuple-element.32), channel_id=1, source_target_pairs={{0,24},{4,28},{8,16},{12,20},{16,8},{20,12},{24,0},{28,4},{1,25},{... | collective-permute-start | bytes 208904 | tf_op jit(solution)/shard_map/ppermute | solution.py:60
  15.9 8.9 %collective-permute-start.9 = (f32[17,8,128]{2,1,0:T(8,128)S(1)}, f32[17,8,128]{2,1,0:T(8,128)S(1)}, u32[]{:S(2)}, u32[]{:S(2)}) collective-permute-start(f32[17,8,128]{2,1,0:T(8,128)S(1)} %get-tuple-element.33), channel_id=1, source_target_pairs={{0,8},{4,20},{8,0},{12,28},{16,24},{20,4},{24,16},{28,12},{1,9},{5... | collective-permute-start | bytes 208904 | tf_op jit(solution)/shard_map/ppermute | solution.py:60
  21.4 4.3 %collective-permute-start.10 = (f32[17,8,128]{2,1,0:T(8,128)S(1)}, f32[17,8,128]{2,1,0:T(8,128)S(1)}, u32[]{:S(2)}, u32[]{:S(2)}) collective-permute-start(f32[17,8,128]{2,1,0:T(8,128)S(1)} %get-tuple-element.34), channel_id=1, source_target_pairs={{0,16},{4,12},{8,24},{12,4},{16,0},{20,28},{24,8},{28,20},{1,17},{... | collective-permute-start | bytes 208904 | tf_op jit(solution)/shard_map/ppermute | solution.py:60
  26.8 9.5 %collective-permute-start.11 = (f32[2,2,16,1024]{3,2,1,0:T(8,128)S(1)}, f32[2,2,16,1024]{3,2,1,0:T(8,128)S(1)}, u32[]{:S(2)}, u32[]{:S(2)}) collective-permute-start(f32[2,2,16,1024]{3,2,1,0:T(8,128)S(1)} %get-tuple-element.36), channel_id=1, source_target_pairs={{0,24},{4,28},{8,16},{12,20},{16,8},{20,12},{24,0},{28,4},{1,25},{... | collective-permute-start | bytes 786440 | tf_op jit(solution)/shard_map/ppermute | solution.py:60
  29.2 9.7 %collective-permute-start.12 = (f32[2,2,16,1024]{3,2,1,0:T(8,128)S(1)}, f32[2,2,16,1024]{3,2,1,0:T(8,128)S(1)}, u32[]{:S(2)}, u32[]{:S(2)}) collective-permute-start(f32[2,2,16,1024]{3,2,1,0:T(8,128)S(1)} %get-tuple-element.37), channel_id=1, source_target_pairs={{0,8},{4,20},{8,0},{12,28},{16,24},{20,4},{24,16},{28,12},{1,9},{5... | collective-permute-start | bytes 786440 | tf_op jit(solution)/shard_map/ppermute | solution.py:60
  29.9 9.1 %collective-permute-start.13 = (f32[2,2,16,1024]{3,2,1,0:T(8,128)S(1)}, f32[2,2,16,1024]{3,2,1,0:T(8,128)S(1)}, u32[]{:S(2)}, u32[]{:S(2)}) collective-permute-start(f32[2,2,16,1024]{3,2,1,0:T(8,128)S(1)} %get-tuple-element.38), channel_id=1, source_target_pairs={{0,16},{4,12},{8,24},{12,4},{16,0},{20,28},{24,8},{28,20},{1,17},{... | collective-permute-start | bytes 786440 | tf_op jit(solution)/shard_map/ppermute | solution.py:60
  39.0 2.0 %collective-permute-start.14 = (f32[2,4,16,1024]{3,2,1,0:T(8,128)S(1)}, f32[2,4,16,1024]{3,2,1,0:T(8,128)S(1)}, u32[]{:S(2)}, u32[]{:S(2)}) collective-permute-start(f32[2,4,16,1024]{3,2,1,0:T(8,128)S(1)} %shard_map.75), channel_id=1, source_target_pairs={{0,4},{4,0},{8,12},{12,8},{16,20},{20,16},{24,28},{28,24},{1,5},{5... | collective-permute-start | bytes 1572872 | tf_op jit(solution)/shard_map/ppermute | solution.py:319

commit v7 on v6

--- a/solution.py
+++ b/solution.py
@@ -52,6 +52,10 @@
 
 def order_of(size):
     return sorted(range(2, size, 2), key=lambda k: (-bin(k).count("1"), k)) + [0]
+
+
+def whole_in_first(k):
+    return bin(k).count("1") > 1
 
 
 def move(array, k, size):
@@ -94,7 +98,7 @@
         rows = keep_ref.shape[2]
         for source, ref in ((core, keep_ref), (1 - core, gift_ref)):
             out[source, :rows] = ref[0, chip]
-            out[source, rows:] = ref[1, chip, : rows // 2]
+            out[source, rows:] = ref[1, chip, : out.shape[1] - rows]
 
 
 def second_merge_kernel(size, here_ref, square_ref, other_ref, keep_ref, gift_ref, *outs):
@@ -104,11 +108,13 @@
     _, _, rows, width = keep_ref.shape
     spots = tiles_of(rows, width)[-(rows * width // 2048) :]
     for k, out in zip(order_of(size), outs):
+        out[0] = squares
+        if whole_in_first(k):
+            continue
         chip = target(here, k, size) // 2
         for source, ref in ((core, keep_ref), (1 - core, gift_ref)):
             for t, spot in enumerate(spots):
-                out[source * len(spots) + t] = ref[(1, chip, *spot)]
-        out[2 * len(spots)] = squares
+                out[1 + source * len(spots) + t] = ref[(1, chip, *spot)]
 
 
 def sum_kernel(count, *refs):
@@ -158,9 +164,9 @@
     rows, width = grad_ref.shape[2:]
     spots = tiles_of(rows, width)
     half = len(spots) // 2
-    squares = seconds[0][2 * half]
+    squares = seconds[0][0]
     for second in seconds[1:]:
-        squares = squares + second[2 * half]
+        squares = squares + second[0]
     total = jnp.sum(squares, axis=1, keepdims=True)
     rescale_ref[...] = jnp.broadcast_to(1.0 / jnp.sqrt(total / entries + 1e-06), rescale_ref.shape)
     for level in range(LEVELS):
@@ -168,11 +174,11 @@
             rescale = jnp.broadcast_to(rescale_ref[pl.ds(plan_ref[level, 2 * size + i], 1), :], (8, 128))
             factor = rescale / jnp.full((8, 128), plan_ref[level, size + i], jnp.int32).astype(jnp.float32)
             for t, spot in enumerate(spots):
-                if level == 0 or t < half:
+                if level == 0 or t < half or whole_in_first(order_of(size)[i // 2]):
                     place = slice(level * rows + spot[0].start, level * rows + spot[0].stop)
                     block = firsts[i // 2][i % 2, place, spot[1]]
                 else:
-                    block = seconds[i // 2][(i % 2) * half + t - half]
+                    block = seconds[i // 2][1 + (i % 2) * half + t - half]
                 grad_ref[(level, i, *spot)] = block * factor
         for i in range(1, size):
             leader = plan_ref[level, i]
@@ -268,7 +274,7 @@
     ]
     firsts = call(
         lambda *refs: first_merge_kernel(size, *refs),
-        [shape(2, own_rows + own_rows // 2, width)] * rounds,
+        [shape(2, own_rows + (own_rows if whole_in_first(k) else own_rows // 2), width) for k in order],
         [smem, vmem, vmem],
         [vmem] * rounds,
     )(here, keep, gift)
@@ -290,7 +296,7 @@
     other = lax.ppermute(squares, "path", swap)
     seconds = call(
         lambda *refs: second_merge_kernel(size, *refs),
-        [shape(own_rows * width // 1024 + 1, 8, 128)] * rounds,
+        [shape(1 if whole_in_first(k) else 1 + own_rows * width // 1024, 8, 128) for k in order],
         [smem] + [vmem] * 4,
         [vmem] * rounds,
     )(here, squares, other, keep, gift)

time: 42 us -> 42 us (level)
  no operation moved by 1% of the time
where the time goes in v7:
time: 42 us; the launch traced here: 41.9 us
  starting transfers between devices  17.8 us (42%)
  waiting for transfers between devices  13.8 us (33%)
  Pallas kernels  7.78 us (19%)
  local copies, waits for them, and re-layouts  1.38 us (3%)
  between operations  0.79 us (2%)
    ppermute x9, starting transfers between devices, move(): lax.ppermute(array, 'path', [(i, target(i, k, size)) for i in range(size)])  11.8 us
    ppermute x9, waiting for transfers between devices, move(): lax.ppermute(array, 'path', [(i, target(i, k, size)) for i in range(size)])  11.6 us
    ppermute x3, starting transfers between devices, local(): lax.ppermute(squares, 'shard', [(i, i ^ step) for i in range(shards)])  5.33 us
    pallas_call x1, Pallas kernels, local(): call(state_kernel, [shape(*state_in.shape)] * 2 + [shape(8, 128)], [smem,...  3.08 us
    pallas_call x1, Pallas kernels, local(): call(plan_kernel, [jax.ShapeDtypeStruct((LEVELS, 5 * size), jnp.int32), j...  1.4 us
    unnamed x8, local copies, waits for them, and re-layouts  1.38 us
    ppermute x1, waiting for transfers between devices, local(): other = lax.ppermute(squares, 'path', swap)  1.15 us
    pallas_call x1, Pallas kernels, local(): call(lambda *refs: outgoing_kernel(rounds, entries, *refs), [message] * r...  1.05 us
  transfers between devices with their start and end apart: 15, of which 6 were waited for; matrix products, arithmetic and copies ran while one was open for 1% of the time, Pallas kernels for 14%

profile of v7, /device:TPU:0, one launch (start us, length us, event | category | flops | bytes accessed | tf_op | source)
XLA Modules:
  0.0 41.9 jit_solution(1491638900290244142)
XLA Ops:
  0.6 0.0 copy-start
  0.6 0.0 copy-start.2
  0.7 1.4 %copy-done.2 = f32[1,2,128,1024]{3,2,1,0:T(8,128)S(1)} copy-done((f32[1,2,128,1024]{3,2,1,0:T(8,128)S(1)}, f32[1,2,128,1024]{3,2,1,0:T(8,128)}, u32[]{:S(2)}) %copy-start.2) | copy-done | bytes 1048600
  2.0 0.1 shard_map.69
  2.1 0.5 %collective-permute-start = (f32[2,4,16,1024]{3,2,1,0:T(8,128)S(1)}, f32[2,4,16,1024]{3,2,1,0:T(8,128)S(1)}, u32[]{:S(2)}, u32[]{:S(2)}) collective-permute-start(f32[2,4,16,1024]{3,2,1,0:T(8,128)S(1)} %get-tuple-element.26), channel_id=1, source_target_pairs={{0,4},{4,0},{8,12},{12,8},{16,20},{20,16},{24,28},{28,24},{1,5},{5... | collective-permute-start | bytes 1572872 | tf_op jit(solution)/shard_map/ppermute | solution.py:271
  2.6 4.7 %collective-permute-start.4 = (f32[8,128]{1,0:T(8,128)S(1)}, f32[8,128]{1,0:T(8,128)S(1)}, u32[]{:S(2)}, u32[]{:S(2)}) collective-permute-start(f32[8,128]{1,0:T(8,128)S(1)} %get-tuple-element.31.refs_0_), channel_id=1, source_target_pairs={{0,3},{1,2},{2,1},{3,0},{4,7},{5,6},{6,5},{7,4},{8,11},{9,10},{10,... | collective-permute-start | bytes 12296 | tf_op jit(solution)/shard_map/ppermute | solution.py:273
  7.3 0.0 collective-permute-start.5
  7.3 0.6 %collective-permute-start.6 = (f32[8,128]{1,0:T(8,128)S(1)}, f32[8,128]{1,0:T(8,128)S(1)}, u32[]{:S(2)}, u32[]{:S(2)}) collective-permute-start(f32[8,128]{1,0:T(8,128)S(1)} %get-tuple-element.31.refs_0_), channel_id=1, source_target_pairs={{0,1},{1,0},{2,3},{3,2},{4,5},{5,4},{6,7},{7,6},{8,9},{9,8},{10,11... | collective-permute-start | bytes 12296 | tf_op jit(solution)/shard_map/ppermute | solution.py:273
  8.0 0.0 collective-permute-done.refs_2_.refs_4_
  8.0 0.1 shard_map.70
  8.0 2.7 %collective-permute-start.1 = (f32[2,32,1024]{2,1,0:T(8,128)S(1)}, f32[2,32,1024]{2,1,0:T(8,128)S(1)}, u32[]{:S(2)}, u32[]{:S(2)}) collective-permute-start(f32[2,32,1024]{2,1,0:T(8,128)S(1)} %get-tuple-element.27), channel_id=1, source_target_pairs={{0,24},{4,28},{8,16},{12,20},{16,8},{20,12},{24,0},{28,4},{1,25},{... | collective-permute-start | bytes 786440 | tf_op jit(solution)/shard_map/ppermute | solution.py:64
  10.7 0.5 %collective-permute-start.2 = (f32[2,24,1024]{2,1,0:T(8,128)S(1)}, f32[2,24,1024]{2,1,0:T(8,128)S(1)}, u32[]{:S(2)}, u32[]{:S(2)}) collective-permute-start(f32[2,24,1024]{2,1,0:T(8,128)S(1)} %get-tuple-element.28), channel_id=1, source_target_pairs={{0,8},{4,20},{8,0},{12,28},{16,24},{20,4},{24,16},{28,12},{1,9},{5... | collective-permute-start | bytes 589832 | tf_op jit(solution)/shard_map/ppermute | solution.py:64
  11.2 0.0 collective-permute-done.4.refs_1_
  11.2 0.4 collective-permute-start.3
  11.6 0.0 copy-done
  11.6 0.3 broadcast_multiply_fusion.decay_ref.refs_4_
  11.9 0.0 copy-start.3
  11.9 0.0 copy-start.1
  11.9 0.0 collective-permute-done.5.refs_2_
  11.9 0.0 collective-permute-done.6.refs_3_
  11.9 0.1 collective-permute-start.7
  12.0 1.2 %collective-permute-done.7.refs_2_ = f32[8,128]{1,0:T(8,128)S(1)} collective-permute-done((f32[8,128]{1,0:T(8,128)S(1)}, f32[8,128]{1,0:T(8,128)S(1)}, u32[]{:S(2)}, u32[]{:S(2)}) %collective-permute-start.7) | collective-permute-done | bytes 4128 | tf_op jit(solution)/shard_map/ppermute | solution.py:296
  13.2 2.7 %collective-permute-start.8 = (f32[1,8,128]{2,1,0:T(8,128)S(1)}, f32[1,8,128]{2,1,0:T(8,128)S(1)}, u32[]{:S(2)}, u32[]{:S(2)}) collective-permute-start(f32[1,8,128]{2,1,0:T(8,128)S(1)} %get-tuple-element.32), channel_id=1, source_target_pairs={{0,24},{4,28},{8,16},{12,20},{16,8},{20,12},{24,0},{28,4},{1,25},{... | collective-permute-start | bytes 12296 | tf_op jit(solution)/shard_map/ppermute | solution.py:64
  15.9 0.5 %collective-permute-start.9 = (f32[17,8,128]{2,1,0:T(8,128)S(1)}, f32[17,8,128]{2,1,0:T(8,128)S(1)}, u32[]{:S(2)}, u32[]{:S(2)}) collective-permute-start(f32[17,8,128]{2,1,0:T(8,128)S(1)} %get-tuple-element.33), channel_id=1, source_target_pairs={{0,8},{4,20},{8,0},{12,28},{16,24},{20,4},{24,16},{28,12},{1,9},{5... | collective-permute-start | bytes 208904 | tf_op jit(solution)/shard_map/ppermute | solution.py:64
  16.4 5.1 %collective-permute-done.8.refs_6_ = f32[1,8,128]{2,1,0:T(8,128)S(1)} collective-permute-done((f32[1,8,128]{2,1,0:T(8,128)S(1)}, f32[1,8,128]{2,1,0:T(8,128)S(1)}, u32[]{:S(2)}, u32[]{:S(2)}) %collective-permute-start.8) | collective-permute-done | bytes 4128 | tf_op jit(solution)/shard_map/ppermute | solution.py:64
  21.5 1.5 %collective-permute-start.10 = (f32[17,8,128]{2,1,0:T(8,128)S(1)}, f32[17,8,128]{2,1,0:T(8,128)S(1)}, u32[]{:S(2)}, u32[]{:S(2)}) collective-permute-start(f32[17,8,128]{2,1,0:T(8,128)S(1)} %get-tuple-element.34), channel_id=1, source_target_pairs={{0,16},{4,12},{8,24},{12,4},{16,0},{20,28},{24,8},{28,20},{1,17},{... | collective-permute-start | bytes 208904 | tf_op jit(solution)/shard_map/ppermute | solution.py:64
  23.0 0.0 copy-done.3
  23.0 1.4 %shard_map.67 = (s32[2,40]{1,0:T(2,128)S(1)}, s32[32]{0:T(128)S(1)}) custom-call(s32[1]{0:T(128)} %bitcast.here_ref.refs_0_, s32[2,8]{1,0:T(2,128)S(1)} %bitcast.16), custom_call_target="tpu_custom_call" | custom-call | tf_op jit(solution)/shard_map/pallas_call | solution.py:284
  24.4 0.0 copy-done.1
  24.4 0.3 shard_map.68.refs_1_.decayed_ref
  24.7 0.0 collective-permute-done.9.refs_7_
  24.7 1.0 %collective-permute-done.10.refs_8_ = f32[17,8,128]{2,1,0:T(8,128)S(1)} collective-permute-done((f32[17,8,128]{2,1,0:T(8,128)S(1)}, f32[17,8,128]{2,1,0:T(8,128)S(1)}, u32[]{:S(2)}, u32[]{:S(2)}) %collective-permute-start.10) | collective-permute-done | bytes 69664 | tf_op jit(solution)/shard_map/ppermute | solution.py:64
  25.8 0.0 collective-permute-done.2.refs_3_
  25.8 0.0 collective-permute-done.3.refs_4_
  25.8 0.0 collective-permute-done.1.refs_2_
  25.8 1.0 %shard_map.73 = (f32[2,2,16,1024]{3,2,1,0:T(8,128)S(1)}, f32[2,2,16,1024]{3,2,1,0:T(8,128)S(1)}, f32[2,2,16,1024]{3,2,1,0:T(8,128)S(1)}, f32[2,2,16,1024]{3,2,1,0:T(8,128)S(1)}, f32[2,8,16,1024]{3,2,1,0:T(8,128)S(1)}) custom-call(s32[2,40]{1,0:T(2,128)S(1)} %get-tuple-element.24.refs_0_, f32[32,16,1024]{2,1,0:T(8,128)S(1)} %shard_map.68.refs_1_.decayed_ref, ...), custom_call_target="tpu_custom_call" | custom-call | tf_op jit(solution)/shard_map/pallas_call | solution.py:305
  26.8 2.4 %collective-permute-start.11 = (f32[2,2,16,1024]{3,2,1,0:T(8,128)S(1)}, f32[2,2,16,1024]{3,2,1,0:T(8,128)S(1)}, u32[]{:S(2)}, u32[]{:S(2)}) collective-permute-start(f32[2,2,16,1024]{3,2,1,0:T(8,128)S(1)} %get-tuple-element.36), channel_id=1, source_target_pairs={{0,24},{4,28},{8,16},{12,20},{16,8},{20,12},{24,0},{28,4},{1,25},{... | collective-permute-start | bytes 786440 | tf_op jit(solution)/shard_map/ppermute | solution.py:64
  29.2 0.6 %collective-permute-start.12 = (f32[2,2,16,1024]{3,2,1,0:T(8,128)S(1)}, f32[2,2,16,1024]{3,2,1,0:T(8,128)S(1)}, u32[]{:S(2)}, u32[]{:S(2)}) collective-permute-start(f32[2,2,16,1024]{3,2,1,0:T(8,128)S(1)} %get-tuple-element.37), channel_id=1, source_target_pairs={{0,8},{4,20},{8,0},{12,28},{16,24},{20,4},{24,16},{28,12},{1,9},{5... | collective-permute-start | bytes 786440 | tf_op jit(solution)/shard_map/ppermute | solution.py:64
  29.9 0.5 %collective-permute-start.13 = (f32[2,2,16,1024]{3,2,1,0:T(8,128)S(1)}, f32[2,2,16,1024]{3,2,1,0:T(8,128)S(1)}, u32[]{:S(2)}, u32[]{:S(2)}) collective-permute-start(f32[2,2,16,1024]{3,2,1,0:T(8,128)S(1)} %get-tuple-element.38), channel_id=1, source_target_pairs={{0,16},{4,12},{8,24},{12,4},{16,0},{20,28},{24,8},{28,20},{1,17},{... | collective-permute-start | bytes 786440 | tf_op jit(solution)/shard_map/ppermute | solution.py:64
  30.4 3.1 %shard_map.74 = (f32[32,16,1024]{2,1,0:T(8,128)}, f32[32,16,1024]{2,1,0:T(8,128)}, f32[8,128]{1,0:T(8,128)S(1)}) custom-call(s32[32]{0:T(128)S(1)} %get-tuple-element.40.module_ref, f32[2,8,16,1024]{3,2,1,0:T(8,128)S(1)} %get-tuple-element.41.grad_ref, f32[32,16,1024]{2,1,0:T(8,128)S(1)} %shard_map.68.refs_1_.decayed_ref, f32[32,16,1024]{2,1,0:T(8,128)S(1)} %bitcast.13), custom_call_target="tpu_custom_call" | custom-call | tf_op jit(solution)/shard_map/pallas_call | solution.py:315
  33.5 2.8 %collective-permute-done.11.refs_1_ = f32[2,2,16,1024]{3,2,1,0:T(8,128)S(1)} collective-permute-done((f32[2,2,16,1024]{3,2,1,0:T(8,128)S(1)}, f32[2,2,16,1024]{3,2,1,0:T(8,128)S(1)}, u32[]{:S(2)}, u32[]{:S(2)}) %collective-permute-start.11) | collective-permute-done | bytes 262176 | tf_op jit(solution)/shard_map/ppermute | solution.py:64
  36.3 2.7 %collective-permute-done.12.refs_2_ = f32[2,2,16,1024]{3,2,1,0:T(8,128)S(1)} collective-permute-done((f32[2,2,16,1024]{3,2,1,0:T(8,128)S(1)}, f32[2,2,16,1024]{3,2,1,0:T(8,128)S(1)}, u32[]{:S(2)}, u32[]{:S(2)}) %collective-permute-start.12) | collective-permute-done | bytes 262176 | tf_op jit(solution)/shard_map/ppermute | solution.py:64
  39.0 0.0 collective-permute-done.13.refs_3_
  39.0 0.1 collective-permute-start.14
  39.1 0.9 %shard_map.76.held_ref = f32[2,4,2,16,1024]{4,3,2,1,0:T(8,128)} custom-call(s32[1]{0:T(128)} %bitcast.here_ref.refs_0_, f32[2,2,16,1024]{3,2,1,0:T(8,128)S(1)} %collective-permute-done.11.refs_1_, f32[2,2,16,1024]{3,2,1,0:T(8,128)S(1)} %collective-permute-done.12.refs_2_, f32[2,2,16,1024]{3,2,1,0:T(8,128)S(1)} %collective-permute-done.13.refs_3_, ...), custom_call_target="tpu_custom_call" | custom-call | tf_op jit(solution)/shard_map/pallas_call | solution.py:327
  40.0 1.0 %collective-permute-done.14.back_ref = f32[2,4,16,1024]{3,2,1,0:T(8,128)S(1)} collective-permute-done((f32[2,4,16,1024]{3,2,1,0:T(8,128)S(1)}, f32[2,4,16,1024]{3,2,1,0:T(8,128)S(1)}, u32[]{:S(2)}, u32[]{:S(2)}) %collective-permute-start.14) | collective-permute-done | bytes 524320 | tf_op jit(solution)/shard_map/ppermute | solution.py:325
  41.0 0.8 %shard_map.77 = f32[2,4,2,16,1024]{4,3,2,1,0:T(8,128)} custom-call(s32[1]{0:T(128)} %bitcast.here_ref.refs_0_, f32[2,4,16,1024]{3,2,1,0:T(8,128)S(1)} %collective-permute-done.14.back_ref, f32[2,4,2,16,1024]{4,3,2,1,0:T(8,128)} %shard_map.76.held_ref), custom_call_target="tpu_custom_call", output_to_operand_aliasing={{}: (2, {})} | custom-call | tf_op jit(solution)/shard_map/pallas_call | solution.py:334
  (3 shorter events, 0.1 us)
Async XLA Ops:
  0.6 11.0 %copy-start = (f32[32,1,16,1024]{3,2,1,0:T(8,128)S(1)}, f32[32,1,16,1024]{3,2,1,0:T(8,128)}, u32[]{:S(2)}) copy-start(f32[32,1,16,1024]{3,2,1,0:T(8,128)} %param.7) | copy-start | bytes 6291460
  0.6 1.4 %copy-start.2 = (f32[1,2,128,1024]{3,2,1,0:T(8,128)S(1)}, f32[1,2,128,1024]{3,2,1,0:T(8,128)}, u32[]{:S(2)}) copy-start(f32[1,2,128,1024]{3,2,1,0:T(8,128)} %param.4) | copy-start | bytes 3145732
  2.1 5.8 %collective-permute-start = (f32[2,4,16,1024]{3,2,1,0:T(8,128)S(1)}, f32[2,4,16,1024]{3,2,1,0:T(8,128)S(1)}, u32[]{:S(2)}, u32[]{:S(2)}) collective-permute-start(f32[2,4,16,1024]{3,2,1,0:T(8,128)S(1)} %get-tuple-element.26), channel_id=1, source_target_pairs={{0,4},{4,0},{8,12},{12,8},{16,20},{20,16},{24,28},{28,24},{1,5},{5... | collective-permute-start | bytes 1572872 | tf_op jit(solution)/shard_map/ppermute | solution.py:271
  2.6 8.6 %collective-permute-start.4 = (f32[8,128]{1,0:T(8,128)S(1)}, f32[8,128]{1,0:T(8,128)S(1)}, u32[]{:S(2)}, u32[]{:S(2)}) collective-permute-start(f32[8,128]{1,0:T(8,128)S(1)} %get-tuple-element.31.refs_0_), channel_id=1, source_target_pairs={{0,3},{1,2},{2,1},{3,0},{4,7},{5,6},{6,5},{7,4},{8,11},{9,10},{10,... | collective-permute-start | bytes 12296 | tf_op jit(solution)/shard_map/ppermute | solution.py:273
  7.3 4.6 %collective-permute-start.5 = (f32[8,128]{1,0:T(8,128)S(1)}, f32[8,128]{1,0:T(8,128)S(1)}, u32[]{:S(2)}, u32[]{:S(2)}) collective-permute-start(f32[8,128]{1,0:T(8,128)S(1)} %get-tuple-element.31.refs_0_), channel_id=1, source_target_pairs={{0,2},{1,3},{2,0},{3,1},{4,6},{5,7},{6,4},{7,5},{8,10},{9,11},{10,... | collective-permute-start | bytes 12296 | tf_op jit(solution)/shard_map/ppermute | solution.py:273
  7.3 4.6 %collective-permute-start.6 = (f32[8,128]{1,0:T(8,128)S(1)}, f32[8,128]{1,0:T(8,128)S(1)}, u32[]{:S(2)}, u32[]{:S(2)}) collective-permute-start(f32[8,128]{1,0:T(8,128)S(1)} %get-tuple-element.31.refs_0_), channel_id=1, source_target_pairs={{0,1},{1,0},{2,3},{3,2},{4,5},{5,4},{6,7},{7,6},{8,9},{9,8},{10,11... | collective-permute-start | bytes 12296 | tf_op jit(solution)/shard_map/ppermute | solution.py:273
  8.0 17.7 %collective-permute-start.1 = (f32[2,32,1024]{2,1,0:T(8,128)S(1)}, f32[2,32,1024]{2,1,0:T(8,128)S(1)}, u32[]{:S(2)}, u32[]{:S(2)}) collective-permute-start(f32[2,32,1024]{2,1,0:T(8,128)S(1)} %get-tuple-element.27), channel_id=1, source_target_pairs={{0,24},{4,28},{8,16},{12,20},{16,8},{20,12},{24,0},{28,4},{1,25},{... | collective-permute-start | bytes 786440 | tf_op jit(solution)/shard_map/ppermute | solution.py:64
  10.7 15.1 %collective-permute-start.2 = (f32[2,24,1024]{2,1,0:T(8,128)S(1)}, f32[2,24,1024]{2,1,0:T(8,128)S(1)}, u32[]{:S(2)}, u32[]{:S(2)}) collective-permute-start(f32[2,24,1024]{2,1,0:T(8,128)S(1)} %get-tuple-element.28), channel_id=1, source_target_pairs={{0,8},{4,20},{8,0},{12,28},{16,24},{20,4},{24,16},{28,12},{1,9},{5... | collective-permute-start | bytes 589832 | tf_op jit(solution)/shard_map/ppermute | solution.py:64
  11.2 14.5 %collective-permute-start.3 = (f32[2,24,1024]{2,1,0:T(8,128)S(1)}, f32[2,24,1024]{2,1,0:T(8,128)S(1)}, u32[]{:S(2)}, u32[]{:S(2)}) collective-permute-start(f32[2,24,1024]{2,1,0:T(8,128)S(1)} %get-tuple-element.29), channel_id=1, source_target_pairs={{0,16},{4,12},{8,24},{12,4},{16,0},{20,28},{24,8},{28,20},{1,17},{... | collective-permute-start | bytes 589832 | tf_op jit(solution)/shard_map/ppermute | solution.py:64
  11.9 11.1 %copy-start.3 = (s32[8,2]{0,1:T(2,128)S(1)}, s32[8,2]{0,1:T(2,128)}, u32[]{:S(2)}) copy-start(s32[8,2]{0,1:T(2,128)} %param.5) | copy-start | bytes 196
  11.9 12.5 %copy-start.1 = (f32[32,1,16,1024]{3,2,1,0:T(8,128)S(1)}, f32[32,1,16,1024]{3,2,1,0:T(8,128)}, u32[]{:S(2)}) copy-start(f32[32,1,16,1024]{3,2,1,0:T(8,128)} %param.6) | copy-start | bytes 6291460
  11.9 1.2 %collective-permute-start.7 = (f32[8,128]{1,0:T(8,128)S(1)}, f32[8,128]{1,0:T(8,128)S(1)}, u32[]{:S(2)}, u32[]{:S(2)}) collective-permute-start(f32[8,128]{1,0:T(8,128)S(1)} %shard_map.71.refs_1_), channel_id=1, source_target_pairs={{0,4},{4,0},{8,12},{12,8},{16,20},{20,16},{24,28},{28,24},{1,5},{5... | collective-permute-start | bytes 12296 | tf_op jit(solution)/shard_map/ppermute | solution.py:296
  13.2 8.3 %collective-permute-start.8 = (f32[1,8,128]{2,1,0:T(8,128)S(1)}, f32[1,8,128]{2,1,0:T(8,128)S(1)}, u32[]{:S(2)}, u32[]{:S(2)}) collective-permute-start(f32[1,8,128]{2,1,0:T(8,128)S(1)} %get-tuple-element.32), channel_id=1, source_target_pairs={{0,24},{4,28},{8,16},{12,20},{16,8},{20,12},{24,0},{28,4},{1,25},{... | collective-permute-start | bytes 12296 | tf_op jit(solution)/shard_map/ppermute | solution.py:64
  15.9 8.9 %collective-permute-start.9 = (f32[17,8,128]{2,1,0:T(8,128)S(1)}, f32[17,8,128]{2,1,0:T(8,128)S(1)}, u32[]{:S(2)}, u32[]{:S(2)}) collective-permute-start(f32[17,8,128]{2,1,0:T(8,128)S(1)} %get-tuple-element.33), channel_id=1, source_target_pairs={{0,8},{4,20},{8,0},{12,28},{16,24},{20,4},{24,16},{28,12},{1,9},{5... | collective-permute-start | bytes 208904 | tf_op jit(solution)/shard_map/ppermute | solution.py:64
  21.5 4.3 %collective-permute-start.10 = (f32[17,8,128]{2,1,0:T(8,128)S(1)}, f32[17,8,128]{2,1,0:T(8,128)S(1)}, u32[]{:S(2)}, u32[]{:S(2)}) collective-permute-start(f32[17,8,128]{2,1,0:T(8,128)S(1)} %get-tuple-element.34), channel_id=1, source_target_pairs={{0,16},{4,12},{8,24},{12,4},{16,0},{20,28},{24,8},{28,20},{1,17},{... | collective-permute-start | bytes 208904 | tf_op jit(solution)/shard_map/ppermute | solution.py:64
  26.8 9.5 %collective-permute-start.11 = (f32[2,2,16,1024]{3,2,1,0:T(8,128)S(1)}, f32[2,2,16,1024]{3,2,1,0:T(8,128)S(1)}, u32[]{:S(2)}, u32[]{:S(2)}) collective-permute-start(f32[2,2,16,1024]{3,2,1,0:T(8,128)S(1)} %get-tuple-element.36), channel_id=1, source_target_pairs={{0,24},{4,28},{8,16},{12,20},{16,8},{20,12},{24,0},{28,4},{1,25},{... | collective-permute-start | bytes 786440 | tf_op jit(solution)/shard_map/ppermute | solution.py:64
  29.2 9.7 %collective-permute-start.12 = (f32[2,2,16,1024]{3,2,1,0:T(8,128)S(1)}, f32[2,2,16,1024]{3,2,1,0:T(8,128)S(1)}, u32[]{:S(2)}, u32[]{:S(2)}) collective-permute-start(f32[2,2,16,1024]{3,2,1,0:T(8,128)S(1)} %get-tuple-element.37), channel_id=1, source_target_pairs={{0,8},{4,20},{8,0},{12,28},{16,24},{20,4},{24,16},{28,12},{1,9},{5... | collective-permute-start | bytes 786440 | tf_op jit(solution)/shard_map/ppermute | solution.py:64
  29.9 9.1 %collective-permute-start.13 = (f32[2,2,16,1024]{3,2,1,0:T(8,128)S(1)}, f32[2,2,16,1024]{3,2,1,0:T(8,128)S(1)}, u32[]{:S(2)}, u32[]{:S(2)}) collective-permute-start(f32[2,2,16,1024]{3,2,1,0:T(8,128)S(1)} %get-tuple-element.38), channel_id=1, source_target_pairs={{0,16},{4,12},{8,24},{12,4},{16,0},{20,28},{24,8},{28,20},{1,17},{... | collective-permute-start | bytes 786440 | tf_op jit(solution)/shard_map/ppermute | solution.py:64
  39.0 2.0 %collective-permute-start.14 = (f32[2,4,16,1024]{3,2,1,0:T(8,128)S(1)}, f32[2,4,16,1024]{3,2,1,0:T(8,128)S(1)}, u32[]{:S(2)}, u32[]{:S(2)}) collective-permute-start(f32[2,4,16,1024]{3,2,1,0:T(8,128)S(1)} %shard_map.75), channel_id=1, source_target_pairs={{0,4},{4,0},{8,12},{12,8},{16,20},{20,16},{24,28},{28,24},{1,5},{5... | collective-permute-start | bytes 1572872 | tf_op jit(solution)/shard_map/ppermute | solution.py:325

commit v8 on v7

--- a/solution.py
+++ b/solution.py
@@ -8,6 +8,7 @@
 LEVEL_MODULES = 16
 LEVELS = 2
 MOST_UNROLLED = 8
+EIGHTHS = 3
 
 outer_rate = 0.7
 beta_coef = 0.9
@@ -52,10 +53,6 @@
 
 def order_of(size):
     return sorted(range(2, size, 2), key=lambda k: (-bin(k).count("1"), k)) + [0]
-
-
-def whole_in_first(k):
-    return bin(k).count("1") > 1
 
 
 def move(array, k, size):
@@ -90,28 +87,31 @@
         pl.when(here_ref[0] & 1 == core)(lambda core=core: pack(core))
 
 
+def in_first(count):
+    return count * EIGHTHS // 8
+
+
 def first_merge_kernel(size, here_ref, keep_ref, gift_ref, *outs):
     here = here_ref[0]
     core = here & 1
+    spots = tiles_of(*keep_ref.shape[2:])
+    sent = [(0, spot) for spot in spots] + [(1, spot) for spot in spots[: in_first(len(spots))]]
     for k, out in zip(order_of(size), outs):
         chip = target(here, k, size) // 2
-        rows = keep_ref.shape[2]
         for source, ref in ((core, keep_ref), (1 - core, gift_ref)):
-            out[source, :rows] = ref[0, chip]
-            out[source, rows:] = ref[1, chip, : out.shape[1] - rows]
+            for t, (level, spot) in enumerate(sent):
+                out[source * len(sent) + t] = ref[(level, chip, *spot)]
 
 
 def second_merge_kernel(size, here_ref, square_ref, other_ref, keep_ref, gift_ref, *outs):
     here = here_ref[0]
     core = here & 1
     squares = square_ref[...] + other_ref[...]
-    _, _, rows, width = keep_ref.shape
-    spots = tiles_of(rows, width)[-(rows * width // 2048) :]
+    spots = tiles_of(*keep_ref.shape[2:])
+    spots = spots[in_first(len(spots)) :]
     for k, out in zip(order_of(size), outs):
+        chip = target(here, k, size) // 2
         out[0] = squares
-        if whole_in_first(k):
-            continue
-        chip = target(here, k, size) // 2
         for source, ref in ((core, keep_ref), (1 - core, gift_ref)):
             for t, spot in enumerate(spots):
                 out[1 + source * len(spots) + t] = ref[(1, chip, *spot)]
@@ -163,7 +163,7 @@
     size = 2 * rounds
     rows, width = grad_ref.shape[2:]
     spots = tiles_of(rows, width)
-    half = len(spots) // 2
+    count, early = len(spots), in_first(len(spots))
     squares = seconds[0][0]
     for second in seconds[1:]:
         squares = squares + second[0]
@@ -174,11 +174,10 @@
             rescale = jnp.broadcast_to(rescale_ref[pl.ds(plan_ref[level, 2 * size + i], 1), :], (8, 128))
             factor = rescale / jnp.full((8, 128), plan_ref[level, size + i], jnp.int32).astype(jnp.float32)
             for t, spot in enumerate(spots):
-                if level == 0 or t < half or whole_in_first(order_of(size)[i // 2]):
-                    place = slice(level * rows + spot[0].start, level * rows + spot[0].stop)
-                    block = firsts[i // 2][i % 2, place, spot[1]]
+                if level == 0 or t < early:
+                    block = firsts[i // 2][(i % 2) * (count + early) + level * count + t]
                 else:
-                    block = seconds[i // 2][1 + (i % 2) * half + t - half]
+                    block = seconds[i // 2][1 + (i % 2) * (count - early) + t - early]
                 grad_ref[(level, i, *spot)] = block * factor
         for i in range(1, size):
             leader = plan_ref[level, i]
@@ -264,6 +263,7 @@
     squares_shape = shape(-(-size // 8) * 8, 128)
     by_chip = shape(LEVELS, rounds, own_rows, width)
     message = shape(2, LEVELS, own_rows, width)
+    count = own_rows * width // 1024
 
     squares, keep, give = call(pack_kernel, [squares_shape, by_chip, by_chip], [smem, vmem], [vmem] * 3)(
         here, split_slab
@@ -274,7 +274,7 @@
     ]
     firsts = call(
         lambda *refs: first_merge_kernel(size, *refs),
-        [shape(2, own_rows + (own_rows if whole_in_first(k) else own_rows // 2), width) for k in order],
+        [shape(2 * (count + in_first(count)), 8, 128)] * rounds,
         [smem, vmem, vmem],
         [vmem] * rounds,
     )(here, keep, gift)
@@ -296,7 +296,7 @@
     other = lax.ppermute(squares, "path", swap)
     seconds = call(
         lambda *refs: second_merge_kernel(size, *refs),
-        [shape(1 if whole_in_first(k) else 1 + own_rows * width // 1024, 8, 128) for k in order],
+        [shape(1 + 2 * (count - in_first(count)), 8, 128)] * rounds,
         [smem] + [vmem] * 4,
         [vmem] * rounds,
     )(here, squares, other, keep, gift)

time: 42 us -> 41.8 us (level)
  no operation moved by 1% of the time
where the time goes in v8:
time: 41.8 us; the launch traced here: 41.7 us
  starting transfers between devices  17.8 us (43%)
  waiting for transfers between devices  13.6 us (33%)
  Pallas kernels  7.79 us (19%)
  local copies, waits for them, and re-layouts  1.38 us (3%)
  between operations  0.79 us (2%)
    ppermute x9, starting transfers between devices, move(): lax.ppermute(array, 'path', [(i, target(i, k, size)) for i in range(size)])  11.9 us
    ppermute x9, waiting for transfers between devices, move(): lax.ppermute(array, 'path', [(i, target(i, k, size)) for i in range(size)])  11.4 us
    ppermute x3, starting transfers between devices, local(): lax.ppermute(squares, 'shard', [(i, i ^ step) for i in range(shards)])  5.33 us
    pallas_call x1, Pallas kernels, local(): call(state_kernel, [shape(*state_in.shape)] * 2 + [shape(8, 128)], [smem,...  3.08 us
    pallas_call x1, Pallas kernels, local(): call(plan_kernel, [jax.ShapeDtypeStruct((LEVELS, 5 * size), jnp.int32), j...  1.4 us
    unnamed x8, local copies, waits for them, and re-layouts  1.38 us
    ppermute x1, waiting for transfers between devices, local(): other = lax.ppermute(squares, 'path', swap)  1.15 us
    pallas_call x1, Pallas kernels, local(): call(lambda *refs: outgoing_kernel(rounds, entries, *refs), [message] * r...  1.06 us
  transfers between devices with their start and end apart: 15, of which 6 were waited for; matrix products, arithmetic and copies ran while one was open for 1% of the time, Pallas kernels for 14%

profile of v8, /device:TPU:0, one launch (start us, length us, event | category | flops | bytes accessed | tf_op | source)
XLA Modules:
  0.0 41.7 jit_solution(14184659136018865172)
XLA Ops:
  0.6 0.0 copy-start
  0.6 0.0 copy-start.2
  0.7 1.4 %copy-done.2 = f32[1,2,128,1024]{3,2,1,0:T(8,128)S(1)} copy-done((f32[1,2,128,1024]{3,2,1,0:T(8,128)S(1)}, f32[1,2,128,1024]{3,2,1,0:T(8,128)}, u32[]{:S(2)}) %copy-start.2) | copy-done | bytes 1048600
  2.0 0.1 shard_map.69
  2.1 0.5 %collective-permute-start = (f32[2,4,16,1024]{3,2,1,0:T(8,128)S(1)}, f32[2,4,16,1024]{3,2,1,0:T(8,128)S(1)}, u32[]{:S(2)}, u32[]{:S(2)}) collective-permute-start(f32[2,4,16,1024]{3,2,1,0:T(8,128)S(1)} %get-tuple-element.26), channel_id=1, source_target_pairs={{0,4},{4,0},{8,12},{12,8},{16,20},{20,16},{24,28},{28,24},{1,5},{5... | collective-permute-start | bytes 1572872 | tf_op jit(solution)/shard_map/ppermute | solution.py:271
  2.6 4.7 %collective-permute-start.4 = (f32[8,128]{1,0:T(8,128)S(1)}, f32[8,128]{1,0:T(8,128)S(1)}, u32[]{:S(2)}, u32[]{:S(2)}) collective-permute-start(f32[8,128]{1,0:T(8,128)S(1)} %get-tuple-element.31.refs_0_), channel_id=1, source_target_pairs={{0,3},{1,2},{2,1},{3,0},{4,7},{5,6},{6,5},{7,4},{8,11},{9,10},{10,... | collective-permute-start | bytes 12296 | tf_op jit(solution)/shard_map/ppermute | solution.py:273
  7.3 0.0 collective-permute-start.5
  7.3 0.6 %collective-permute-start.6 = (f32[8,128]{1,0:T(8,128)S(1)}, f32[8,128]{1,0:T(8,128)S(1)}, u32[]{:S(2)}, u32[]{:S(2)}) collective-permute-start(f32[8,128]{1,0:T(8,128)S(1)} %get-tuple-element.31.refs_0_), channel_id=1, source_target_pairs={{0,1},{1,0},{2,3},{3,2},{4,5},{5,4},{6,7},{7,6},{8,9},{9,8},{10,11... | collective-permute-start | bytes 12296 | tf_op jit(solution)/shard_map/ppermute | solution.py:273
  8.0 0.0 collective-permute-done.refs_2_.refs_4_
  8.0 2.7 %collective-permute-start.1 = (f32[44,8,128]{2,1,0:T(8,128)S(1)}, f32[44,8,128]{2,1,0:T(8,128)S(1)}, u32[]{:S(2)}, u32[]{:S(2)}) collective-permute-start(f32[44,8,128]{2,1,0:T(8,128)S(1)} %get-tuple-element.27), channel_id=1, source_target_pairs={{0,24},{4,28},{8,16},{12,20},{16,8},{20,12},{24,0},{28,4},{1,25},{... | collective-permute-start | bytes 540680 | tf_op jit(solution)/shard_map/ppermute | solution.py:61
  10.7 0.5 %collective-permute-start.2 = (f32[44,8,128]{2,1,0:T(8,128)S(1)}, f32[44,8,128]{2,1,0:T(8,128)S(1)}, u32[]{:S(2)}, u32[]{:S(2)}) collective-permute-start(f32[44,8,128]{2,1,0:T(8,128)S(1)} %get-tuple-element.28), channel_id=1, source_target_pairs={{0,8},{4,20},{8,0},{12,28},{16,24},{20,4},{24,16},{28,12},{1,9},{5... | collective-permute-start | bytes 540680 | tf_op jit(solution)/shard_map/ppermute | solution.py:61
  11.2 0.0 collective-permute-done.4.refs_1_
  11.2 0.4 collective-permute-start.3
  11.6 0.0 copy-done
  11.6 0.3 broadcast_multiply_fusion.decay_ref.refs_4_
  11.9 0.0 copy-start.3
  11.9 0.0 copy-start.1
  11.9 0.0 collective-permute-done.5.refs_2_
  11.9 0.0 collective-permute-done.6.refs_3_
  11.9 0.1 collective-permute-start.7
  12.0 1.2 %collective-permute-done.7.refs_2_ = f32[8,128]{1,0:T(8,128)S(1)} collective-permute-done((f32[8,128]{1,0:T(8,128)S(1)}, f32[8,128]{1,0:T(8,128)S(1)}, u32[]{:S(2)}, u32[]{:S(2)}) %collective-permute-start.7) | collective-permute-done | bytes 4128 | tf_op jit(solution)/shard_map/ppermute | solution.py:296
  13.2 2.7 %collective-permute-start.8 = (f32[21,8,128]{2,1,0:T(8,128)S(1)}, f32[21,8,128]{2,1,0:T(8,128)S(1)}, u32[]{:S(2)}, u32[]{:S(2)}) collective-permute-start(f32[21,8,128]{2,1,0:T(8,128)S(1)} %get-tuple-element.32), channel_id=1, source_target_pairs={{0,24},{4,28},{8,16},{12,20},{16,8},{20,12},{24,0},{28,4},{1,25},{... | collective-permute-start | bytes 258056 | tf_op jit(solution)/shard_map/ppermute | solution.py:61
  15.9 0.5 %collective-permute-start.9 = (f32[21,8,128]{2,1,0:T(8,128)S(1)}, f32[21,8,128]{2,1,0:T(8,128)S(1)}, u32[]{:S(2)}, u32[]{:S(2)}) collective-permute-start(f32[21,8,128]{2,1,0:T(8,128)S(1)} %get-tuple-element.33), channel_id=1, source_target_pairs={{0,8},{4,20},{8,0},{12,28},{16,24},{20,4},{24,16},{28,12},{1,9},{5... | collective-permute-start | bytes 258056 | tf_op jit(solution)/shard_map/ppermute | solution.py:61
  16.4 4.7 %collective-permute-done.8.refs_6_ = f32[21,8,128]{2,1,0:T(8,128)S(1)} collective-permute-done((f32[21,8,128]{2,1,0:T(8,128)S(1)}, f32[21,8,128]{2,1,0:T(8,128)S(1)}, u32[]{:S(2)}, u32[]{:S(2)}) %collective-permute-start.8) | collective-permute-done | bytes 86048 | tf_op jit(solution)/shard_map/ppermute | solution.py:61
  21.1 1.6 %collective-permute-start.10 = (f32[21,8,128]{2,1,0:T(8,128)S(1)}, f32[21,8,128]{2,1,0:T(8,128)S(1)}, u32[]{:S(2)}, u32[]{:S(2)}) collective-permute-start(f32[21,8,128]{2,1,0:T(8,128)S(1)} %get-tuple-element.34), channel_id=1, source_target_pairs={{0,16},{4,12},{8,24},{12,4},{16,0},{20,28},{24,8},{28,20},{1,17},{... | collective-permute-start | bytes 258056 | tf_op jit(solution)/shard_map/ppermute | solution.py:61
  22.6 0.0 copy-done.3
  22.6 1.4 %shard_map.67 = (s32[2,40]{1,0:T(2,128)S(1)}, s32[32]{0:T(128)S(1)}) custom-call(s32[1]{0:T(128)} %bitcast.here_ref.refs_0_, s32[2,8]{1,0:T(2,128)S(1)} %bitcast.16), custom_call_target="tpu_custom_call" | custom-call | tf_op jit(solution)/shard_map/pallas_call | solution.py:284
  24.0 0.0 copy-done.1
  24.0 0.3 shard_map.68.refs_1_.decayed_ref
  24.4 0.0 collective-permute-done.9.refs_7_
  24.4 1.2 %collective-permute-done.10.refs_8_ = f32[21,8,128]{2,1,0:T(8,128)S(1)} collective-permute-done((f32[21,8,128]{2,1,0:T(8,128)S(1)}, f32[21,8,128]{2,1,0:T(8,128)S(1)}, u32[]{:S(2)}, u32[]{:S(2)}) %collective-permute-start.10) | collective-permute-done | bytes 86048 | tf_op jit(solution)/shard_map/ppermute | solution.py:61
  25.5 0.0 collective-permute-done.1.refs_2_
  25.5 0.0 collective-permute-done.2.refs_3_
  25.5 0.0 collective-permute-done.3.refs_4_
  25.6 1.1 %shard_map.73 = (f32[2,2,16,1024]{3,2,1,0:T(8,128)S(1)}, f32[2,2,16,1024]{3,2,1,0:T(8,128)S(1)}, f32[2,2,16,1024]{3,2,1,0:T(8,128)S(1)}, f32[2,2,16,1024]{3,2,1,0:T(8,128)S(1)}, f32[2,8,16,1024]{3,2,1,0:T(8,128)S(1)}) custom-call(s32[2,40]{1,0:T(2,128)S(1)} %get-tuple-element.24.refs_0_, f32[32,16,1024]{2,1,0:T(8,128)S(1)} %shard_map.68.refs_1_.decayed_ref, ...), custom_call_target="tpu_custom_call" | custom-call | tf_op jit(solution)/shard_map/pallas_call | solution.py:305
  26.6 2.6 %collective-permute-start.11 = (f32[2,2,16,1024]{3,2,1,0:T(8,128)S(1)}, f32[2,2,16,1024]{3,2,1,0:T(8,128)S(1)}, u32[]{:S(2)}, u32[]{:S(2)}) collective-permute-start(f32[2,2,16,1024]{3,2,1,0:T(8,128)S(1)} %get-tuple-element.36), channel_id=1, source_target_pairs={{0,24},{4,28},{8,16},{12,20},{16,8},{20,12},{24,0},{28,4},{1,25},{... | collective-permute-start | bytes 786440 | tf_op jit(solution)/shard_map/ppermute | solution.py:61
  29.2 0.5 %collective-permute-start.12 = (f32[2,2,16,1024]{3,2,1,0:T(8,128)S(1)}, f32[2,2,16,1024]{3,2,1,0:T(8,128)S(1)}, u32[]{:S(2)}, u32[]{:S(2)}) collective-permute-start(f32[2,2,16,1024]{3,2,1,0:T(8,128)S(1)} %get-tuple-element.37), channel_id=1, source_target_pairs={{0,8},{4,20},{8,0},{12,28},{16,24},{20,4},{24,16},{28,12},{1,9},{5... | collective-permute-start | bytes 786440 | tf_op jit(solution)/shard_map/ppermute | solution.py:61
  29.7 0.5 %collective-permute-start.13 = (f32[2,2,16,1024]{3,2,1,0:T(8,128)S(1)}, f32[2,2,16,1024]{3,2,1,0:T(8,128)S(1)}, u32[]{:S(2)}, u32[]{:S(2)}) collective-permute-start(f32[2,2,16,1024]{3,2,1,0:T(8,128)S(1)} %get-tuple-element.38), channel_id=1, source_target_pairs={{0,16},{4,12},{8,24},{12,4},{16,0},{20,28},{24,8},{28,20},{1,17},{... | collective-permute-start | bytes 786440 | tf_op jit(solution)/shard_map/ppermute | solution.py:61
  30.2 3.1 %shard_map.74 = (f32[32,16,1024]{2,1,0:T(8,128)}, f32[32,16,1024]{2,1,0:T(8,128)}, f32[8,128]{1,0:T(8,128)S(1)}) custom-call(s32[32]{0:T(128)S(1)} %get-tuple-element.40.module_ref, f32[2,8,16,1024]{3,2,1,0:T(8,128)S(1)} %get-tuple-element.41.grad_ref, f32[32,16,1024]{2,1,0:T(8,128)S(1)} %shard_map.68.refs_1_.decayed_ref, f32[32,16,1024]{2,1,0:T(8,128)S(1)} %bitcast.13), custom_call_target="tpu_custom_call" | custom-call | tf_op jit(solution)/shard_map/pallas_call | solution.py:315
  33.3 2.8 %collective-permute-done.11.refs_1_ = f32[2,2,16,1024]{3,2,1,0:T(8,128)S(1)} collective-permute-done((f32[2,2,16,1024]{3,2,1,0:T(8,128)S(1)}, f32[2,2,16,1024]{3,2,1,0:T(8,128)S(1)}, u32[]{:S(2)}, u32[]{:S(2)}) %collective-permute-start.11) | collective-permute-done | bytes 262176 | tf_op jit(solution)/shard_map/ppermute | solution.py:61
  36.1 2.7 %collective-permute-done.12.refs_2_ = f32[2,2,16,1024]{3,2,1,0:T(8,128)S(1)} collective-permute-done((f32[2,2,16,1024]{3,2,1,0:T(8,128)S(1)}, f32[2,2,16,1024]{3,2,1,0:T(8,128)S(1)}, u32[]{:S(2)}, u32[]{:S(2)}) %collective-permute-start.12) | collective-permute-done | bytes 262176 | tf_op jit(solution)/shard_map/ppermute | solution.py:61
  38.8 0.0 collective-permute-done.13.refs_3_
  38.8 0.1 collective-permute-start.14
  38.9 0.9 %shard_map.76.held_ref = f32[2,4,2,16,1024]{4,3,2,1,0:T(8,128)} custom-call(s32[1]{0:T(128)} %bitcast.here_ref.refs_0_, f32[2,2,16,1024]{3,2,1,0:T(8,128)S(1)} %collective-permute-done.11.refs_1_, f32[2,2,16,1024]{3,2,1,0:T(8,128)S(1)} %collective-permute-done.12.refs_2_, f32[2,2,16,1024]{3,2,1,0:T(8,128)S(1)} %collective-permute-done.13.refs_3_, ...), custom_call_target="tpu_custom_call" | custom-call | tf_op jit(solution)/shard_map/pallas_call | solution.py:327
  39.8 1.0 %collective-permute-done.14.back_ref = f32[2,4,16,1024]{3,2,1,0:T(8,128)S(1)} collective-permute-done((f32[2,4,16,1024]{3,2,1,0:T(8,128)S(1)}, f32[2,4,16,1024]{3,2,1,0:T(8,128)S(1)}, u32[]{:S(2)}, u32[]{:S(2)}) %collective-permute-start.14) | collective-permute-done | bytes 524320 | tf_op jit(solution)/shard_map/ppermute | solution.py:325
  40.8 0.8 %shard_map.77 = f32[2,4,2,16,1024]{4,3,2,1,0:T(8,128)} custom-call(s32[1]{0:T(128)} %bitcast.here_ref.refs_0_, f32[2,4,16,1024]{3,2,1,0:T(8,128)S(1)} %collective-permute-done.14.back_ref, f32[2,4,2,16,1024]{4,3,2,1,0:T(8,128)} %shard_map.76.held_ref), custom_call_target="tpu_custom_call", output_to_operand_aliasing={{}: (2, {})} | custom-call | tf_op jit(solution)/shard_map/pallas_call | solution.py:334
  (4 shorter events, 0.1 us)
Async XLA Ops:
  0.6 11.0 %copy-start = (f32[32,1,16,1024]{3,2,1,0:T(8,128)S(1)}, f32[32,1,16,1024]{3,2,1,0:T(8,128)}, u32[]{:S(2)}) copy-start(f32[32,1,16,1024]{3,2,1,0:T(8,128)} %param.7) | copy-start | bytes 6291460
  0.6 1.4 %copy-start.2 = (f32[1,2,128,1024]{3,2,1,0:T(8,128)S(1)}, f32[1,2,128,1024]{3,2,1,0:T(8,128)}, u32[]{:S(2)}) copy-start(f32[1,2,128,1024]{3,2,1,0:T(8,128)} %param.4) | copy-start | bytes 3145732
  2.1 5.8 %collective-permute-start = (f32[2,4,16,1024]{3,2,1,0:T(8,128)S(1)}, f32[2,4,16,1024]{3,2,1,0:T(8,128)S(1)}, u32[]{:S(2)}, u32[]{:S(2)}) collective-permute-start(f32[2,4,16,1024]{3,2,1,0:T(8,128)S(1)} %get-tuple-element.26), channel_id=1, source_target_pairs={{0,4},{4,0},{8,12},{12,8},{16,20},{20,16},{24,28},{28,24},{1,5},{5... | collective-permute-start | bytes 1572872 | tf_op jit(solution)/shard_map/ppermute | solution.py:271
  2.6 8.6 %collective-permute-start.4 = (f32[8,128]{1,0:T(8,128)S(1)}, f32[8,128]{1,0:T(8,128)S(1)}, u32[]{:S(2)}, u32[]{:S(2)}) collective-permute-start(f32[8,128]{1,0:T(8,128)S(1)} %get-tuple-element.31.refs_0_), channel_id=1, source_target_pairs={{0,3},{1,2},{2,1},{3,0},{4,7},{5,6},{6,5},{7,4},{8,11},{9,10},{10,... | collective-permute-start | bytes 12296 | tf_op jit(solution)/shard_map/ppermute | solution.py:273
  7.3 4.6 %collective-permute-start.5 = (f32[8,128]{1,0:T(8,128)S(1)}, f32[8,128]{1,0:T(8,128)S(1)}, u32[]{:S(2)}, u32[]{:S(2)}) collective-permute-start(f32[8,128]{1,0:T(8,128)S(1)} %get-tuple-element.31.refs_0_), channel_id=1, source_target_pairs={{0,2},{1,3},{2,0},{3,1},{4,6},{5,7},{6,4},{7,5},{8,10},{9,11},{10,... | collective-permute-start | bytes 12296 | tf_op jit(solution)/shard_map/ppermute | solution.py:273
  7.3 4.6 %collective-permute-start.6 = (f32[8,128]{1,0:T(8,128)S(1)}, f32[8,128]{1,0:T(8,128)S(1)}, u32[]{:S(2)}, u32[]{:S(2)}) collective-permute-start(f32[8,128]{1,0:T(8,128)S(1)} %get-tuple-element.31.refs_0_), channel_id=1, source_target_pairs={{0,1},{1,0},{2,3},{3,2},{4,5},{5,4},{6,7},{7,6},{8,9},{9,8},{10,11... | collective-permute-start | bytes 12296 | tf_op jit(solution)/shard_map/ppermute | solution.py:273
  8.0 17.5 %collective-permute-start.1 = (f32[44,8,128]{2,1,0:T(8,128)S(1)}, f32[44,8,128]{2,1,0:T(8,128)S(1)}, u32[]{:S(2)}, u32[]{:S(2)}) collective-permute-start(f32[44,8,128]{2,1,0:T(8,128)S(1)} %get-tuple-element.27), channel_id=1, source_target_pairs={{0,24},{4,28},{8,16},{12,20},{16,8},{20,12},{24,0},{28,4},{1,25},{... | collective-permute-start | bytes 540680 | tf_op jit(solution)/shard_map/ppermute | solution.py:61
  10.7 14.9 %collective-permute-start.2 = (f32[44,8,128]{2,1,0:T(8,128)S(1)}, f32[44,8,128]{2,1,0:T(8,128)S(1)}, u32[]{:S(2)}, u32[]{:S(2)}) collective-permute-start(f32[44,8,128]{2,1,0:T(8,128)S(1)} %get-tuple-element.28), channel_id=1, source_target_pairs={{0,8},{4,20},{8,0},{12,28},{16,24},{20,4},{24,16},{28,12},{1,9},{5... | collective-permute-start | bytes 540680 | tf_op jit(solution)/shard_map/ppermute | solution.py:61
  11.2 14.3 %collective-permute-start.3 = (f32[44,8,128]{2,1,0:T(8,128)S(1)}, f32[44,8,128]{2,1,0:T(8,128)S(1)}, u32[]{:S(2)}, u32[]{:S(2)}) collective-permute-start(f32[44,8,128]{2,1,0:T(8,128)S(1)} %get-tuple-element.29), channel_id=1, source_target_pairs={{0,16},{4,12},{8,24},{12,4},{16,0},{20,28},{24,8},{28,20},{1,17},{... | collective-permute-start | bytes 540680 | tf_op jit(solution)/shard_map/ppermute | solution.py:61
  11.9 10.7 %copy-start.3 = (s32[8,2]{0,1:T(2,128)S(1)}, s32[8,2]{0,1:T(2,128)}, u32[]{:S(2)}) copy-start(s32[8,2]{0,1:T(2,128)} %param.5) | copy-start | bytes 196
  11.9 12.1 %copy-start.1 = (f32[32,1,16,1024]{3,2,1,0:T(8,128)S(1)}, f32[32,1,16,1024]{3,2,1,0:T(8,128)}, u32[]{:S(2)}) copy-start(f32[32,1,16,1024]{3,2,1,0:T(8,128)} %param.6) | copy-start | bytes 6291460
  11.9 1.2 %collective-permute-start.7 = (f32[8,128]{1,0:T(8,128)S(1)}, f32[8,128]{1,0:T(8,128)S(1)}, u32[]{:S(2)}, u32[]{:S(2)}) collective-permute-start(f32[8,128]{1,0:T(8,128)S(1)} %shard_map.71.refs_1_), channel_id=1, source_target_pairs={{0,4},{4,0},{8,12},{12,8},{16,20},{20,16},{24,28},{28,24},{1,5},{5... | collective-permute-start | bytes 12296 | tf_op jit(solution)/shard_map/ppermute | solution.py:296
  13.2 7.9 %collective-permute-start.8 = (f32[21,8,128]{2,1,0:T(8,128)S(1)}, f32[21,8,128]{2,1,0:T(8,128)S(1)}, u32[]{:S(2)}, u32[]{:S(2)}) collective-permute-start(f32[21,8,128]{2,1,0:T(8,128)S(1)} %get-tuple-element.32), channel_id=1, source_target_pairs={{0,24},{4,28},{8,16},{12,20},{16,8},{20,12},{24,0},{28,4},{1,25},{... | collective-permute-start | bytes 258056 | tf_op jit(solution)/shard_map/ppermute | solution.py:61
  15.9 8.5 %collective-permute-start.9 = (f32[21,8,128]{2,1,0:T(8,128)S(1)}, f32[21,8,128]{2,1,0:T(8,128)S(1)}, u32[]{:S(2)}, u32[]{:S(2)}) collective-permute-start(f32[21,8,128]{2,1,0:T(8,128)S(1)} %get-tuple-element.33), channel_id=1, source_target_pairs={{0,8},{4,20},{8,0},{12,28},{16,24},{20,4},{24,16},{28,12},{1,9},{5... | collective-permute-start | bytes 258056 | tf_op jit(solution)/shard_map/ppermute | solution.py:61
  21.1 4.5 %collective-permute-start.10 = (f32[21,8,128]{2,1,0:T(8,128)S(1)}, f32[21,8,128]{2,1,0:T(8,128)S(1)}, u32[]{:S(2)}, u32[]{:S(2)}) collective-permute-start(f32[21,8,128]{2,1,0:T(8,128)S(1)} %get-tuple-element.34), channel_id=1, source_target_pairs={{0,16},{4,12},{8,24},{12,4},{16,0},{20,28},{24,8},{28,20},{1,17},{... | collective-permute-start | bytes 258056 | tf_op jit(solution)/shard_map/ppermute | solution.py:61
  26.6 9.5 %collective-permute-start.11 = (f32[2,2,16,1024]{3,2,1,0:T(8,128)S(1)}, f32[2,2,16,1024]{3,2,1,0:T(8,128)S(1)}, u32[]{:S(2)}, u32[]{:S(2)}) collective-permute-start(f32[2,2,16,1024]{3,2,1,0:T(8,128)S(1)} %get-tuple-element.36), channel_id=1, source_target_pairs={{0,24},{4,28},{8,16},{12,20},{16,8},{20,12},{24,0},{28,4},{1,25},{... | collective-permute-start | bytes 786440 | tf_op jit(solution)/shard_map/ppermute | solution.py:61
  29.2 9.6 %collective-permute-start.12 = (f32[2,2,16,1024]{3,2,1,0:T(8,128)S(1)}, f32[2,2,16,1024]{3,2,1,0:T(8,128)S(1)}, u32[]{:S(2)}, u32[]{:S(2)}) collective-permute-start(f32[2,2,16,1024]{3,2,1,0:T(8,128)S(1)} %get-tuple-element.37), channel_id=1, source_target_pairs={{0,8},{4,20},{8,0},{12,28},{16,24},{20,4},{24,16},{28,12},{1,9},{5... | collective-permute-start | bytes 786440 | tf_op jit(solution)/shard_map/ppermute | solution.py:61
  29.7 9.1 %collective-permute-start.13 = (f32[2,2,16,1024]{3,2,1,0:T(8,128)S(1)}, f32[2,2,16,1024]{3,2,1,0:T(8,128)S(1)}, u32[]{:S(2)}, u32[]{:S(2)}) collective-permute-start(f32[2,2,16,1024]{3,2,1,0:T(8,128)S(1)} %get-tuple-element.38), channel_id=1, source_target_pairs={{0,16},{4,12},{8,24},{12,4},{16,0},{20,28},{24,8},{28,20},{1,17},{... | collective-permute-start | bytes 786440 | tf_op jit(solution)/shard_map/ppermute | solution.py:61
  38.8 2.0 %collective-permute-start.14 = (f32[2,4,16,1024]{3,2,1,0:T(8,128)S(1)}, f32[2,4,16,1024]{3,2,1,0:T(8,128)S(1)}, u32[]{:S(2)}, u32[]{:S(2)}) collective-permute-start(f32[2,4,16,1024]{3,2,1,0:T(8,128)S(1)} %shard_map.75), channel_id=1, source_target_pairs={{0,4},{4,0},{8,12},{12,8},{16,20},{20,16},{24,28},{28,24},{1,5},{5... | collective-permute-start | bytes 1572872 | tf_op jit(solution)/shard_map/ppermute | solution.py:325

commit v9 on v8

--- a/solution.py
+++ b/solution.py
@@ -8,7 +8,7 @@
 LEVEL_MODULES = 16
 LEVELS = 2
 MOST_UNROLLED = 8
-EIGHTHS = 3
+EIGHTHS = 5
 
 outer_rate = 0.7
 beta_coef = 0.9
@@ -117,16 +117,13 @@
                 out[1 + source * len(spots) + t] = ref[(1, chip, *spot)]
 
 
-def sum_kernel(count, *refs):
-    total = refs[0][...]
-    for ref in refs[1:count]:
-        total = total + ref[...]
-    refs[-1][...] = total
-
-
-def decay_kernel(params_ref, decay_ref, out_ref):
+def add_kernel(a_ref, b_ref, out_ref):
+    out_ref[...] = a_ref[...] + b_ref[...]
+
+
+def decay_kernel(params_ref, momentum_ref, out_ref):
     def decay(module, carry):
-        out_ref[module] = params_ref[module] - decay_ref[module]
+        out_ref[module] = params_ref[module] - moment_coef * momentum_ref[module]
         return carry
 
     lax.fori_loop(0, out_ref.shape[0], decay, 0)
@@ -269,9 +266,6 @@
         here, split_slab
     )
     gift = lax.ppermute(give, "path", swap)
-    tiles = [squares] + [
-        lax.ppermute(squares, "shard", [(i, i ^ step) for i in range(shards)]) for step in range(shards - 1, 0, -1)
-    ]
     firsts = call(
         lambda *refs: first_merge_kernel(size, *refs),
         [shape(2 * (count + in_first(count)), 8, 128)] * rounds,
@@ -279,8 +273,7 @@
         [vmem] * rounds,
     )(here, keep, gift)
     firsts = [move(firsts[j], k, size) for j, k in enumerate(order)]
-    decay = moment_coef * moment_in
-    decayed = call(decay_kernel, shape(*state_in.shape), [vmem, vmem], vmem)(state_in, decay)
+    decayed = call(decay_kernel, shape(*state_in.shape), [vmem, vmem], vmem)(state_in, moment_in)
     plan, leaders = call(
         plan_kernel,
         [
@@ -290,9 +283,11 @@
         [smem, smem],
         [smem, smem],
     )(here, assign.T)
-    squares = call(
-        lambda *refs: sum_kernel(shards, *refs), squares_shape, [vmem] * shards + [anywhere], vmem
-    )(*tiles, decay)
+    step = shards // 2
+    while step:
+        other = lax.ppermute(squares, "shard", [(i, i ^ step) for i in range(shards)])
+        squares = call(add_kernel, squares_shape, [vmem, vmem], vmem)(squares, other)
+        step //= 2
     other = lax.ppermute(squares, "path", swap)
     seconds = call(
         lambda *refs: second_merge_kernel(size, *refs),

time: 41.8 us -> 46.2 us (1.11)
  waiting for transfers between devices: 13.6 us -> 15.6 us
  local copies, waits for them, and re-layouts: 1.38 us -> 2.96 us
  starting transfers between devices: 17.8 us -> 18.9 us
    ppermute x3 -> x2, waiting for transfers between devices: 0.01 us -> 3.28 us  [local(): lax.ppermute(squares, 'shard', [(i, i ^ step) for i in range(shards)])]
    ppermute x9, waiting for transfers between devices: 11.4 us -> 8.64 us  [move(): lax.ppermute(array, 'path', [(i, target(i, k, size)) for i in range(size)])]
    unnamed x8, local copies, waits for them, and re-layouts: 1.38 us -> 2.96 us
    ppermute x1, waiting for transfers between devices: 0.01 us -> 1.54 us  [local(): gift = lax.ppermute(give, 'path', swap)]
    ppermute x9, starting transfers between devices: 11.9 us -> 13.4 us  [move(): lax.ppermute(array, 'path', [(i, target(i, k, size)) for i in range(size)])]
    ppermute x3 -> x2, starting transfers between devices: 5.33 us -> 4.9 us  [local(): lax.ppermute(squares, 'shard', [(i, i ^ step) for i in range(shards)])]
  transfers between devices with their start and end apart: 15 -> 14, of which waited for: 6 -> 8; matrix products, arithmetic and copies ran while one was open for 1% -> 0% of each run, Pallas kernels for 14% -> 12%
where the time goes in v9:
time: 46.2 us; the launch traced here: 46.1 us
  starting transfers between devices  18.9 us (41%)
  waiting for transfers between devices  15.6 us (34%)
  Pallas kernels  7.85 us (17%)
  local copies, waits for them, and re-layouts  2.96 us (6%)
  between operations  0.77 us (2%)
    ppermute x9, starting transfers between devices, move(): lax.ppermute(array, 'path', [(i, target(i, k, size)) for i in range(size)])  13.4 us
    ppermute x9, waiting for transfers between devices, move(): lax.ppermute(array, 'path', [(i, target(i, k, size)) for i in range(size)])  8.64 us
    ppermute x2, starting transfers between devices, local(): lax.ppermute(squares, 'shard', [(i, i ^ step) for i in range(shards)])  4.9 us
    ppermute x2, waiting for transfers between devices, local(): lax.ppermute(squares, 'shard', [(i, i ^ step) for i in range(shards)])  3.28 us
    pallas_call x1, Pallas kernels, local(): call(state_kernel, [shape(*state_in.shape)] * 2 + [shape(8, 128)], [smem,...  3.08 us
    unnamed x8, local copies, waits for them, and re-layouts  2.96 us
    ppermute x1, waiting for transfers between devices, local(): gift = lax.ppermute(give, 'path', swap)  1.54 us
    pallas_call x1, Pallas kernels, local(): call(plan_kernel, [jax.ShapeDtypeStruct((LEVELS, 5 * size), jnp.int32), j...  1.4 us
  transfers between devices with their start and end apart: 14, of which 8 were waited for; matrix products, arithmetic and copies ran while one was open for 0% of the time, Pallas kernels for 12%

profile of v9, /device:TPU:0, one launch (start us, length us, event | category | flops | bytes accessed | tf_op | source)
XLA Modules:
  0.0 46.1 jit_solution(2070159962389322769)
XLA Ops:
  0.6 0.0 copy-start
  0.6 0.0 copy-start.2
  0.7 1.4 %copy-done.2 = f32[1,2,128,1024]{3,2,1,0:T(8,128)S(1)} copy-done((f32[1,2,128,1024]{3,2,1,0:T(8,128)S(1)}, f32[1,2,128,1024]{3,2,1,0:T(8,128)}, u32[]{:S(2)}) %copy-start.2) | copy-done | bytes 1048600
  2.0 0.0 copy-start.3
  2.0 0.1 shard_map.69
  2.1 0.5 %collective-permute-start = (f32[2,4,16,1024]{3,2,1,0:T(8,128)S(1)}, f32[2,4,16,1024]{3,2,1,0:T(8,128)S(1)}, u32[]{:S(2)}, u32[]{:S(2)}) collective-permute-start(f32[2,4,16,1024]{3,2,1,0:T(8,128)S(1)} %get-tuple-element.26), channel_id=1, source_target_pairs={{0,4},{4,0},{8,12},{12,8},{16,20},{20,16},{24,28},{28,24},{1,5},{5... | collective-permute-start | bytes 1572872 | tf_op jit(solution)/shard_map/ppermute | solution.py:268
  2.7 1.5 %collective-permute-done.refs_2_.refs_4_ = f32[2,4,16,1024]{3,2,1,0:T(8,128)S(1)} collective-permute-done((f32[2,4,16,1024]{3,2,1,0:T(8,128)S(1)}, f32[2,4,16,1024]{3,2,1,0:T(8,128)S(1)}, u32[]{:S(2)}, u32[]{:S(2)}) %collective-permute-start) | collective-permute-done | bytes 524320 | tf_op jit(solution)/shard_map/ppermute | solution.py:268
  4.2 0.1 shard_map.70
  4.2 3.9 %collective-permute-start.1 = (f32[52,8,128]{2,1,0:T(8,128)S(1)}, f32[52,8,128]{2,1,0:T(8,128)S(1)}, u32[]{:S(2)}, u32[]{:S(2)}) collective-permute-start(f32[52,8,128]{2,1,0:T(8,128)S(1)} %get-tuple-element.27), channel_id=1, source_target_pairs={{0,24},{4,28},{8,16},{12,20},{16,8},{20,12},{24,0},{28,4},{1,25},{... | collective-permute-start | bytes 638984 | tf_op jit(solution)/shard_map/ppermute | solution.py:61
  8.1 0.5 %collective-permute-start.2 = (f32[52,8,128]{2,1,0:T(8,128)S(1)}, f32[52,8,128]{2,1,0:T(8,128)S(1)}, u32[]{:S(2)}, u32[]{:S(2)}) collective-permute-start(f32[52,8,128]{2,1,0:T(8,128)S(1)} %get-tuple-element.28), channel_id=1, source_target_pairs={{0,8},{4,20},{8,0},{12,28},{16,24},{20,4},{24,16},{28,12},{1,9},{5... | collective-permute-start | bytes 638984 | tf_op jit(solution)/shard_map/ppermute | solution.py:61
  8.7 0.1 collective-permute-start.3
  8.8 3.0 %collective-permute-start.4 = (f32[8,128]{1,0:T(8,128)S(1)}, f32[8,128]{1,0:T(8,128)S(1)}, u32[]{:S(2)}, u32[]{:S(2)}) collective-permute-start(f32[8,128]{1,0:T(8,128)S(1)} %get-tuple-element.31.a_ref), channel_id=1, source_target_pairs={{0,2},{1,3},{2,0},{3,1},{4,6},{5,7},{6,4},{7,5},{8,10},{9,11},{10,... | collective-permute-start | bytes 12296 | tf_op jit(solution)/shard_map/ppermute | solution.py:288
  11.8 1.6 %collective-permute-done.4.b_ref = f32[8,128]{1,0:T(8,128)S(1)} collective-permute-done((f32[8,128]{1,0:T(8,128)S(1)}, f32[8,128]{1,0:T(8,128)S(1)}, u32[]{:S(2)}, u32[]{:S(2)}) %collective-permute-start.4) | collective-permute-done | bytes 4128 | tf_op jit(solution)/shard_map/ppermute | solution.py:288
  13.4 1.9 %collective-permute-start.5 = (f32[8,128]{1,0:T(8,128)S(1)}, f32[8,128]{1,0:T(8,128)S(1)}, u32[]{:S(2)}, u32[]{:S(2)}) collective-permute-start(f32[8,128]{1,0:T(8,128)S(1)} %shard_map.71.a_ref), channel_id=1, source_target_pairs={{0,1},{1,0},{2,3},{3,2},{4,5},{5,4},{6,7},{7,6},{8,9},{9,8},{10,11... | collective-permute-start | bytes 12296 | tf_op jit(solution)/shard_map/ppermute | solution.py:288
  15.3 1.7 %collective-permute-done.5.b_ref = f32[8,128]{1,0:T(8,128)S(1)} collective-permute-done((f32[8,128]{1,0:T(8,128)S(1)}, f32[8,128]{1,0:T(8,128)S(1)}, u32[]{:S(2)}, u32[]{:S(2)}) %collective-permute-start.5) | collective-permute-done | bytes 4128 | tf_op jit(solution)/shard_map/ppermute | solution.py:288
  17.0 0.0 collective-permute-start.6
  17.0 1.2 %collective-permute-done.6.refs_2_ = f32[8,128]{1,0:T(8,128)S(1)} collective-permute-done((f32[8,128]{1,0:T(8,128)S(1)}, f32[8,128]{1,0:T(8,128)S(1)}, u32[]{:S(2)}, u32[]{:S(2)}) %collective-permute-start.6) | collective-permute-done | bytes 4128 | tf_op jit(solution)/shard_map/ppermute | solution.py:291
  18.2 2.8 %collective-permute-start.7 = (f32[13,8,128]{2,1,0:T(8,128)S(1)}, f32[13,8,128]{2,1,0:T(8,128)S(1)}, u32[]{:S(2)}, u32[]{:S(2)}) collective-permute-start(f32[13,8,128]{2,1,0:T(8,128)S(1)} %get-tuple-element.32), channel_id=1, source_target_pairs={{0,24},{4,28},{8,16},{12,20},{16,8},{20,12},{24,0},{28,4},{1,25},{... | collective-permute-start | bytes 159752 | tf_op jit(solution)/shard_map/ppermute | solution.py:61
  21.0 0.5 %collective-permute-start.8 = (f32[13,8,128]{2,1,0:T(8,128)S(1)}, f32[13,8,128]{2,1,0:T(8,128)S(1)}, u32[]{:S(2)}, u32[]{:S(2)}) collective-permute-start(f32[13,8,128]{2,1,0:T(8,128)S(1)} %get-tuple-element.33), channel_id=1, source_target_pairs={{0,8},{4,20},{8,0},{12,28},{16,24},{20,4},{24,16},{28,12},{1,9},{5... | collective-permute-start | bytes 159752 | tf_op jit(solution)/shard_map/ppermute | solution.py:61
  21.5 1.7 %collective-permute-done.7.refs_6_ = f32[13,8,128]{2,1,0:T(8,128)S(1)} collective-permute-done((f32[13,8,128]{2,1,0:T(8,128)S(1)}, f32[13,8,128]{2,1,0:T(8,128)S(1)}, u32[]{:S(2)}, u32[]{:S(2)}) %collective-permute-start.7) | collective-permute-done | bytes 53280 | tf_op jit(solution)/shard_map/ppermute | solution.py:61
  23.3 1.9 %collective-permute-start.9 = (f32[13,8,128]{2,1,0:T(8,128)S(1)}, f32[13,8,128]{2,1,0:T(8,128)S(1)}, u32[]{:S(2)}, u32[]{:S(2)}) collective-permute-start(f32[13,8,128]{2,1,0:T(8,128)S(1)} %get-tuple-element.34), channel_id=1, source_target_pairs={{0,16},{4,12},{8,24},{12,4},{16,0},{20,28},{24,8},{28,20},{1,17},{... | collective-permute-start | bytes 159752 | tf_op jit(solution)/shard_map/ppermute | solution.py:61
  25.2 0.0 copy-done.3
  25.2 1.4 %shard_map.67 = (s32[2,40]{1,0:T(2,128)S(1)}, s32[32]{0:T(128)S(1)}) custom-call(s32[1]{0:T(128)} %bitcast.here_ref.refs_0_, s32[2,8]{1,0:T(2,128)S(1)} %bitcast.16), custom_call_target="tpu_custom_call" | custom-call | tf_op jit(solution)/shard_map/pallas_call | solution.py:277
  26.6 0.0 copy-done
  26.6 0.0 copy-start.1
  26.6 1.6 %copy-done.1 = f32[32,1,16,1024]{3,2,1,0:T(8,128)S(1)} copy-done((f32[32,1,16,1024]{3,2,1,0:T(8,128)S(1)}, f32[32,1,16,1024]{3,2,1,0:T(8,128)}, u32[]{:S(2)}) %copy-start.1) | copy-done | bytes 2097176
  28.2 0.4 shard_map.68.refs_1_.decayed_ref
  28.6 0.0 collective-permute-done.8.refs_7_
  28.6 0.0 collective-permute-done.9.refs_8_
  28.6 0.0 collective-permute-done.1.refs_2_
  28.6 0.0 collective-permute-done.2.refs_3_
  28.6 0.0 collective-permute-done.3.refs_4_
  28.6 1.0 %shard_map.74 = (f32[2,2,16,1024]{3,2,1,0:T(8,128)S(1)}, f32[2,2,16,1024]{3,2,1,0:T(8,128)S(1)}, f32[2,2,16,1024]{3,2,1,0:T(8,128)S(1)}, f32[2,2,16,1024]{3,2,1,0:T(8,128)S(1)}, f32[2,8,16,1024]{3,2,1,0:T(8,128)S(1)}) custom-call(s32[2,40]{1,0:T(2,128)S(1)} %get-tuple-element.24.refs_0_, f32[32,16,1024]{2,1,0:T(8,128)S(1)} %shard_map.68.refs_1_.decayed_ref, ...), custom_call_target="tpu_custom_call" | custom-call | tf_op jit(solution)/shard_map/pallas_call | solution.py:300
  29.7 1.6 %collective-permute-start.10 = (f32[2,2,16,1024]{3,2,1,0:T(8,128)S(1)}, f32[2,2,16,1024]{3,2,1,0:T(8,128)S(1)}, u32[]{:S(2)}, u32[]{:S(2)}) collective-permute-start(f32[2,2,16,1024]{3,2,1,0:T(8,128)S(1)} %get-tuple-element.36), channel_id=1, source_target_pairs={{0,24},{4,28},{8,16},{12,20},{16,8},{20,12},{24,0},{28,4},{1,25},{... | collective-permute-start | bytes 786440 | tf_op jit(solution)/shard_map/ppermute | solution.py:61
  31.3 0.6 %collective-permute-start.11 = (f32[2,2,16,1024]{3,2,1,0:T(8,128)S(1)}, f32[2,2,16,1024]{3,2,1,0:T(8,128)S(1)}, u32[]{:S(2)}, u32[]{:S(2)}) collective-permute-start(f32[2,2,16,1024]{3,2,1,0:T(8,128)S(1)} %get-tuple-element.37), channel_id=1, source_target_pairs={{0,8},{4,20},{8,0},{12,28},{16,24},{20,4},{24,16},{28,12},{1,9},{5... | collective-permute-start | bytes 786440 | tf_op jit(solution)/shard_map/ppermute | solution.py:61
  31.9 1.3 %collective-permute-start.12 = (f32[2,2,16,1024]{3,2,1,0:T(8,128)S(1)}, f32[2,2,16,1024]{3,2,1,0:T(8,128)S(1)}, u32[]{:S(2)}, u32[]{:S(2)}) collective-permute-start(f32[2,2,16,1024]{3,2,1,0:T(8,128)S(1)} %get-tuple-element.38), channel_id=1, source_target_pairs={{0,16},{4,12},{8,24},{12,4},{16,0},{20,28},{24,8},{28,20},{1,17},{... | collective-permute-start | bytes 786440 | tf_op jit(solution)/shard_map/ppermute | solution.py:61
  33.2 3.1 %shard_map.75 = (f32[32,16,1024]{2,1,0:T(8,128)}, f32[32,16,1024]{2,1,0:T(8,128)}, f32[8,128]{1,0:T(8,128)S(1)}) custom-call(s32[32]{0:T(128)S(1)} %get-tuple-element.40.module_ref, f32[2,8,16,1024]{3,2,1,0:T(8,128)S(1)} %get-tuple-element.41.grad_ref, f32[32,16,1024]{2,1,0:T(8,128)S(1)} %shard_map.68.refs_1_.decayed_ref, f32[32,16,1024]{2,1,0:T(8,128)S(1)} %bitcast.13), custom_call_target="tpu_custom_call" | custom-call | tf_op jit(solution)/shard_map/pallas_call | solution.py:310
  36.3 3.6 %collective-permute-done.10.refs_1_ = f32[2,2,16,1024]{3,2,1,0:T(8,128)S(1)} collective-permute-done((f32[2,2,16,1024]{3,2,1,0:T(8,128)S(1)}, f32[2,2,16,1024]{3,2,1,0:T(8,128)S(1)}, u32[]{:S(2)}, u32[]{:S(2)}) %collective-permute-start.10) | collective-permute-done | bytes 262176 | tf_op jit(solution)/shard_map/ppermute | solution.py:61
  39.9 3.3 %collective-permute-done.11.refs_2_ = f32[2,2,16,1024]{3,2,1,0:T(8,128)S(1)} collective-permute-done((f32[2,2,16,1024]{3,2,1,0:T(8,128)S(1)}, f32[2,2,16,1024]{3,2,1,0:T(8,128)S(1)}, u32[]{:S(2)}, u32[]{:S(2)}) %collective-permute-start.11) | collective-permute-done | bytes 262176 | tf_op jit(solution)/shard_map/ppermute | solution.py:61
  43.2 0.0 collective-permute-done.12.refs_3_
  43.3 0.1 collective-permute-start.13
  43.3 0.9 %shard_map.77.held_ref = f32[2,4,2,16,1024]{4,3,2,1,0:T(8,128)} custom-call(s32[1]{0:T(128)} %bitcast.here_ref.refs_0_, f32[2,2,16,1024]{3,2,1,0:T(8,128)S(1)} %collective-permute-done.10.refs_1_, f32[2,2,16,1024]{3,2,1,0:T(8,128)S(1)} %collective-permute-done.11.refs_2_, f32[2,2,16,1024]{3,2,1,0:T(8,128)S(1)} %collective-permute-done.12.refs_3_, ...), custom_call_target="tpu_custom_call" | custom-call | tf_op jit(solution)/shard_map/pallas_call | solution.py:322
  44.2 1.0 %collective-permute-done.13.back_ref = f32[2,4,16,1024]{3,2,1,0:T(8,128)S(1)} collective-permute-done((f32[2,4,16,1024]{3,2,1,0:T(8,128)S(1)}, f32[2,4,16,1024]{3,2,1,0:T(8,128)S(1)}, u32[]{:S(2)}, u32[]{:S(2)}) %collective-permute-start.13) | collective-permute-done | bytes 524320 | tf_op jit(solution)/shard_map/ppermute | solution.py:320
  45.2 0.8 %shard_map.78 = f32[2,4,2,16,1024]{4,3,2,1,0:T(8,128)} custom-call(s32[1]{0:T(128)} %bitcast.here_ref.refs_0_, f32[2,4,16,1024]{3,2,1,0:T(8,128)S(1)} %collective-permute-done.13.back_ref, f32[2,4,2,16,1024]{4,3,2,1,0:T(8,128)} %shard_map.77.held_ref), custom_call_target="tpu_custom_call", output_to_operand_aliasing={{}: (2, {})} | custom-call | tf_op jit(solution)/shard_map/pallas_call | solution.py:329
  (4 shorter events, 0.1 us)
Async XLA Ops:
  0.6 26.0 %copy-start = (f32[32,1,16,1024]{3,2,1,0:T(8,128)S(1)}, f32[32,1,16,1024]{3,2,1,0:T(8,128)}, u32[]{:S(2)}) copy-start(f32[32,1,16,1024]{3,2,1,0:T(8,128)} %param.7) | copy-start | bytes 6291460
  0.6 1.4 %copy-start.2 = (f32[1,2,128,1024]{3,2,1,0:T(8,128)S(1)}, f32[1,2,128,1024]{3,2,1,0:T(8,128)}, u32[]{:S(2)}) copy-start(f32[1,2,128,1024]{3,2,1,0:T(8,128)} %param.4) | copy-start | bytes 3145732
  2.0 23.2 %copy-start.3 = (s32[8,2]{0,1:T(2,128)S(1)}, s32[8,2]{0,1:T(2,128)}, u32[]{:S(2)}) copy-start(s32[8,2]{0,1:T(2,128)} %param.5) | copy-start | bytes 196
  2.1 2.0 %collective-permute-start = (f32[2,4,16,1024]{3,2,1,0:T(8,128)S(1)}, f32[2,4,16,1024]{3,2,1,0:T(8,128)S(1)}, u32[]{:S(2)}, u32[]{:S(2)}) collective-permute-start(f32[2,4,16,1024]{3,2,1,0:T(8,128)S(1)} %get-tuple-element.26), channel_id=1, source_target_pairs={{0,4},{4,0},{8,12},{12,8},{16,20},{20,16},{24,28},{28,24},{1,5},{5... | collective-permute-start | bytes 1572872 | tf_op jit(solution)/shard_map/ppermute | solution.py:268
  4.2 24.4 %collective-permute-start.1 = (f32[52,8,128]{2,1,0:T(8,128)S(1)}, f32[52,8,128]{2,1,0:T(8,128)S(1)}, u32[]{:S(2)}, u32[]{:S(2)}) collective-permute-start(f32[52,8,128]{2,1,0:T(8,128)S(1)} %get-tuple-element.27), channel_id=1, source_target_pairs={{0,24},{4,28},{8,16},{12,20},{16,8},{20,12},{24,0},{28,4},{1,25},{... | collective-permute-start | bytes 638984 | tf_op jit(solution)/shard_map/ppermute | solution.py:61
  8.1 20.5 %collective-permute-start.2 = (f32[52,8,128]{2,1,0:T(8,128)S(1)}, f32[52,8,128]{2,1,0:T(8,128)S(1)}, u32[]{:S(2)}, u32[]{:S(2)}) collective-permute-start(f32[52,8,128]{2,1,0:T(8,128)S(1)} %get-tuple-element.28), channel_id=1, source_target_pairs={{0,8},{4,20},{8,0},{12,28},{16,24},{20,4},{24,16},{28,12},{1,9},{5... | collective-permute-start | bytes 638984 | tf_op jit(solution)/shard_map/ppermute | solution.py:61
  8.7 19.9 %collective-permute-start.3 = (f32[52,8,128]{2,1,0:T(8,128)S(1)}, f32[52,8,128]{2,1,0:T(8,128)S(1)}, u32[]{:S(2)}, u32[]{:S(2)}) collective-permute-start(f32[52,8,128]{2,1,0:T(8,128)S(1)} %get-tuple-element.29), channel_id=1, source_target_pairs={{0,16},{4,12},{8,24},{12,4},{16,0},{20,28},{24,8},{28,20},{1,17},{... | collective-permute-start | bytes 638984 | tf_op jit(solution)/shard_map/ppermute | solution.py:61
  8.8 4.6 %collective-permute-start.4 = (f32[8,128]{1,0:T(8,128)S(1)}, f32[8,128]{1,0:T(8,128)S(1)}, u32[]{:S(2)}, u32[]{:S(2)}) collective-permute-start(f32[8,128]{1,0:T(8,128)S(1)} %get-tuple-element.31.a_ref), channel_id=1, source_target_pairs={{0,2},{1,3},{2,0},{3,1},{4,6},{5,7},{6,4},{7,5},{8,10},{9,11},{10,... | collective-permute-start | bytes 12296 | tf_op jit(solution)/shard_map/ppermute | solution.py:288
  13.4 3.6 %collective-permute-start.5 = (f32[8,128]{1,0:T(8,128)S(1)}, f32[8,128]{1,0:T(8,128)S(1)}, u32[]{:S(2)}, u32[]{:S(2)}) collective-permute-start(f32[8,128]{1,0:T(8,128)S(1)} %shard_map.71.a_ref), channel_id=1, source_target_pairs={{0,1},{1,0},{2,3},{3,2},{4,5},{5,4},{6,7},{7,6},{8,9},{9,8},{10,11... | collective-permute-start | bytes 12296 | tf_op jit(solution)/shard_map/ppermute | solution.py:288
  17.0 1.2 %collective-permute-start.6 = (f32[8,128]{1,0:T(8,128)S(1)}, f32[8,128]{1,0:T(8,128)S(1)}, u32[]{:S(2)}, u32[]{:S(2)}) collective-permute-start(f32[8,128]{1,0:T(8,128)S(1)} %shard_map.72.refs_1_), channel_id=1, source_target_pairs={{0,4},{4,0},{8,12},{12,8},{16,20},{20,16},{24,28},{28,24},{1,5},{5... | collective-permute-start | bytes 12296 | tf_op jit(solution)/shard_map/ppermute | solution.py:291
  18.2 5.1 %collective-permute-start.7 = (f32[13,8,128]{2,1,0:T(8,128)S(1)}, f32[13,8,128]{2,1,0:T(8,128)S(1)}, u32[]{:S(2)}, u32[]{:S(2)}) collective-permute-start(f32[13,8,128]{2,1,0:T(8,128)S(1)} %get-tuple-element.32), channel_id=1, source_target_pairs={{0,24},{4,28},{8,16},{12,20},{16,8},{20,12},{24,0},{28,4},{1,25},{... | collective-permute-start | bytes 159752 | tf_op jit(solution)/shard_map/ppermute | solution.py:61
  21.0 7.6 %collective-permute-start.8 = (f32[13,8,128]{2,1,0:T(8,128)S(1)}, f32[13,8,128]{2,1,0:T(8,128)S(1)}, u32[]{:S(2)}, u32[]{:S(2)}) collective-permute-start(f32[13,8,128]{2,1,0:T(8,128)S(1)} %get-tuple-element.33), channel_id=1, source_target_pairs={{0,8},{4,20},{8,0},{12,28},{16,24},{20,4},{24,16},{28,12},{1,9},{5... | collective-permute-start | bytes 159752 | tf_op jit(solution)/shard_map/ppermute | solution.py:61
  23.3 5.3 %collective-permute-start.9 = (f32[13,8,128]{2,1,0:T(8,128)S(1)}, f32[13,8,128]{2,1,0:T(8,128)S(1)}, u32[]{:S(2)}, u32[]{:S(2)}) collective-permute-start(f32[13,8,128]{2,1,0:T(8,128)S(1)} %get-tuple-element.34), channel_id=1, source_target_pairs={{0,16},{4,12},{8,24},{12,4},{16,0},{20,28},{24,8},{28,20},{1,17},{... | collective-permute-start | bytes 159752 | tf_op jit(solution)/shard_map/ppermute | solution.py:61
  26.6 1.6 %copy-start.1 = (f32[32,1,16,1024]{3,2,1,0:T(8,128)S(1)}, f32[32,1,16,1024]{3,2,1,0:T(8,128)}, u32[]{:S(2)}) copy-start(f32[32,1,16,1024]{3,2,1,0:T(8,128)} %param.6) | copy-start | bytes 6291460
  29.7 10.2 %collective-permute-start.10 = (f32[2,2,16,1024]{3,2,1,0:T(8,128)S(1)}, f32[2,2,16,1024]{3,2,1,0:T(8,128)S(1)}, u32[]{:S(2)}, u32[]{:S(2)}) collective-permute-start(f32[2,2,16,1024]{3,2,1,0:T(8,128)S(1)} %get-tuple-element.36), channel_id=1, source_target_pairs={{0,24},{4,28},{8,16},{12,20},{16,8},{20,12},{24,0},{28,4},{1,25},{... | collective-permute-start | bytes 786440 | tf_op jit(solution)/shard_map/ppermute | solution.py:61
  31.3 11.9 %collective-permute-start.11 = (f32[2,2,16,1024]{3,2,1,0:T(8,128)S(1)}, f32[2,2,16,1024]{3,2,1,0:T(8,128)S(1)}, u32[]{:S(2)}, u32[]{:S(2)}) collective-permute-start(f32[2,2,16,1024]{3,2,1,0:T(8,128)S(1)} %get-tuple-element.37), channel_id=1, source_target_pairs={{0,8},{4,20},{8,0},{12,28},{16,24},{20,4},{24,16},{28,12},{1,9},{5... | collective-permute-start | bytes 786440 | tf_op jit(solution)/shard_map/ppermute | solution.py:61
  31.9 11.3 %collective-permute-start.12 = (f32[2,2,16,1024]{3,2,1,0:T(8,128)S(1)}, f32[2,2,16,1024]{3,2,1,0:T(8,128)S(1)}, u32[]{:S(2)}, u32[]{:S(2)}) collective-permute-start(f32[2,2,16,1024]{3,2,1,0:T(8,128)S(1)} %get-tuple-element.38), channel_id=1, source_target_pairs={{0,16},{4,12},{8,24},{12,4},{16,0},{20,28},{24,8},{28,20},{1,17},{... | collective-permute-start | bytes 786440 | tf_op jit(solution)/shard_map/ppermute | solution.py:61
  43.3 2.0 %collective-permute-start.13 = (f32[2,4,16,1024]{3,2,1,0:T(8,128)S(1)}, f32[2,4,16,1024]{3,2,1,0:T(8,128)S(1)}, u32[]{:S(2)}, u32[]{:S(2)}) collective-permute-start(f32[2,4,16,1024]{3,2,1,0:T(8,128)S(1)} %shard_map.76), channel_id=1, source_target_pairs={{0,4},{4,0},{8,12},{12,8},{16,20},{20,16},{24,28},{28,24},{1,5},{5... | collective-permute-start | bytes 1572872 | tf_op jit(solution)/shard_map/ppermute | solution.py:320

commit v10 on v8

--- a/solution.py
+++ b/solution.py
@@ -205,14 +205,12 @@
         new_params_ref[place] = decayed_ref[module] - grad_coef * grad
 
 
-def give_back_kernel(size, here_ref, *refs):
-    here = here_ref[0]
-    for j, k in enumerate(order_of(size)):
-        for level in range(LEVELS):
-            refs[-1][level, origin(here, k, size) // 2] = refs[j][1 - (here & 1), level]
-
-
-def own_rows_kernel(size, here_ref, *refs):
+def give_back_kernel(count, here_ref, *refs):
+    for i in range(count):
+        refs[-1][i] = refs[i][1 - (here_ref[0] & 1)]
+
+
+def first_rows_kernel(size, first, here_ref, back_ref, *refs):
     here = here_ref[0]
     core = here & 1
     out_ref, sems = refs[-2:]
@@ -221,7 +219,15 @@
         chip = origin(here, k, size) // 2
         for level in range(LEVELS):
             copies.append(
-                pltpu.make_async_copy(refs[j].at[core, level], out_ref.at[level, chip, core], sems.at[level, j])
+                pltpu.make_async_copy(refs[j].at[core, level], out_ref.at[level, chip, core], sems.at[0, level, j])
+            )
+    for i, k in enumerate(first):
+        chip = origin(here ^ 1, k, size) // 2
+        for level in range(LEVELS):
+            copies.append(
+                pltpu.make_async_copy(
+                    back_ref.at[i, level], out_ref.at[level, chip, 1 - core], sems.at[1, level, i]
+                )
             )
     for copy in copies:
         copy.start()
@@ -229,15 +235,16 @@
         copy.wait()
 
 
-def other_rows_kernel(here_ref, back_ref, held_ref, out_ref, sems):
+def last_rows_kernel(size, last, here_ref, back_ref, held_ref, out_ref, sems):
     del held_ref
-    core = here_ref[0] & 1
+    here = here_ref[0]
     copies = []
-    for level in range(LEVELS):
-        for chip in range(back_ref.shape[1]):
+    for i, k in enumerate(last):
+        chip = origin(here ^ 1, k, size) // 2
+        for level in range(LEVELS):
             copies.append(
                 pltpu.make_async_copy(
-                    back_ref.at[level, chip], out_ref.at[level, chip, 1 - core], sems.at[level, chip]
+                    back_ref.at[i, level], out_ref.at[level, chip, 1 - (here & 1)], sems.at[level, i]
                 )
             )
     for copy in copies:
@@ -319,26 +326,32 @@
         [state_block, state_block, vmem],
         grid=(module_count // block,),
     )(leaders, grad, decayed, moment_in)
-    back = call(
-        lambda *refs: give_back_kernel(size, *refs), by_chip, [smem] + [vmem] * rounds + [anywhere], vmem
-    )(here, *returned, done)
-    back = lax.ppermute(back, "path", swap)
-    sems = [pltpu.SemaphoreType.DMA((LEVELS, rounds))]
+    first, last = [*order[:-2], order[-1]], order[-2:-1]
+    blocks = dict(zip(order, returned))
+    backs = []
+    for part in (first, last):
+        back = call(
+            lambda *refs, count=len(part): give_back_kernel(count, *refs),
+            shape(len(part), LEVELS, own_rows, width),
+            [smem] + [vmem] * len(part) + [anywhere],
+            vmem,
+        )(here, *[blocks[k] for k in part], done)
+        backs.append(lax.ppermute(back, "path", swap))
     path_params = call(
-        lambda *refs: own_rows_kernel(size, *refs),
+        lambda *refs: first_rows_kernel(size, first, *refs),
         shape(*split_slab.shape),
-        [smem] + [anywhere] * rounds,
+        [smem] + [anywhere] * (1 + rounds),
         anywhere,
-        scratch_shapes=sems,
-    )(here, *returned)
+        scratch_shapes=[pltpu.SemaphoreType.DMA((2, LEVELS, rounds))],
+    )(here, backs[0], *returned)
     path_params = call(
-        other_rows_kernel,
+        lambda *refs: last_rows_kernel(size, last, *refs),
         shape(*split_slab.shape),
         [smem, anywhere, anywhere],
         anywhere,
-        scratch_shapes=sems,
+        scratch_shapes=[pltpu.SemaphoreType.DMA((LEVELS, len(last)))],
         input_output_aliases={2: 0},
-    )(here, back, path_params)
+    )(here, backs[1], path_params)
     return (path_params.reshape(path_delta.shape), new_state[:, None], new_moment[:, None])
 
 

time: 41.8 us -> 45.6 us (1.091)
  waiting for transfers between devices: 13.6 us -> 17 us
  starting transfers between devices: 17.8 us -> 18.3 us
    ppermute x9, waiting for transfers between devices: 11.4 us -> 14.1 us  [move(): lax.ppermute(array, 'path', [(i, target(i, k, size)) for i in range(size)])]
    ppermute x3, waiting for transfers between devices: 0.01 us -> 1.47 us  [local(): lax.ppermute(squares, 'shard', [(i, i ^ step) for i in range(shards)])]
    ppermute x1 -> x2, waiting for transfers between devices: 1.03 us -> 0.26 us  [local(): backs.append(lax.ppermute(back, 'path', swap))]
    ppermute x9, starting transfers between devices: 11.9 us -> 12.4 us  [move(): lax.ppermute(array, 'path', [(i, target(i, k, size)) for i in range(size)])]
    pallas_call x3 -> x4, Pallas kernels: 1.75 us -> 1.76 us  [the longest x1 1.06 us: local(): call(lambda *refs: first_rows_kernel(size, first, *refs), shape(*split_sl...]
  transfers between devices with their start and end apart: 15 -> 16, of which waited for: 6 -> 8; matrix products, arithmetic and copies ran while one was open for 1% -> 1% of each run, Pallas kernels for 14% -> 13%
where the time goes in v10:
time: 45.6 us; the launch traced here: 45.4 us
  starting transfers between devices  18.3 us (40%)
  waiting for transfers between devices  17 us (37%)
  Pallas kernels  7.7 us (17%)
  local copies, waits for them, and re-layouts  1.38 us (3%)
  between operations  0.8 us (2%)
    ppermute x9, waiting for transfers between devices, move(): lax.ppermute(array, 'path', [(i, target(i, k, size)) for i in range(size)])  14.1 us
    ppermute x9, starting transfers between devices, move(): lax.ppermute(array, 'path', [(i, target(i, k, size)) for i in range(size)])  12.4 us
    ppermute x3, starting transfers between devices, local(): lax.ppermute(squares, 'shard', [(i, i ^ step) for i in range(shards)])  5.25 us
    pallas_call x1, Pallas kernels, local(): call(state_kernel, [shape(*state_in.shape)] * 2 + [shape(8, 128)], [smem,...  3.06 us
    ppermute x3, waiting for transfers between devices, local(): lax.ppermute(squares, 'shard', [(i, i ^ step) for i in range(shards)])  1.47 us
    pallas_call x1, Pallas kernels, local(): call(plan_kernel, [jax.ShapeDtypeStruct((LEVELS, 5 * size), jnp.int32), j...  1.4 us
    unnamed x8, local copies, waits for them, and re-layouts  1.38 us
    ppermute x1, waiting for transfers between devices, local(): other = lax.ppermute(squares, 'path', swap)  1.16 us
  transfers between devices with their start and end apart: 16, of which 8 were waited for; matrix products, arithmetic and copies ran while one was open for 1% of the time, Pallas kernels for 13%

profile of v10, /device:TPU:0, one launch (start us, length us, event | category | flops | bytes accessed | tf_op | source)
XLA Modules:
  0.0 45.4 jit_solution(2037898960307790541)
XLA Ops:
  0.6 0.0 copy-start
  0.6 0.0 copy-start.2
  0.7 1.4 %copy-done.2 = f32[1,2,128,1024]{3,2,1,0:T(8,128)S(1)} copy-done((f32[1,2,128,1024]{3,2,1,0:T(8,128)S(1)}, f32[1,2,128,1024]{3,2,1,0:T(8,128)}, u32[]{:S(2)}) %copy-start.2) | copy-done | bytes 1048600
  2.0 0.1 shard_map.69
  2.1 0.5 %collective-permute-start = (f32[2,4,16,1024]{3,2,1,0:T(8,128)S(1)}, f32[2,4,16,1024]{3,2,1,0:T(8,128)S(1)}, u32[]{:S(2)}, u32[]{:S(2)}) collective-permute-start(f32[2,4,16,1024]{3,2,1,0:T(8,128)S(1)} %get-tuple-element.26), channel_id=1, source_target_pairs={{0,4},{4,0},{8,12},{12,8},{16,20},{20,16},{24,28},{28,24},{1,5},{5... | collective-permute-start | bytes 1572872 | tf_op jit(solution)/shard_map/ppermute | solution.py:278
  2.6 2.7 %collective-permute-start.6 = (f32[8,128]{1,0:T(8,128)S(1)}, f32[8,128]{1,0:T(8,128)S(1)}, u32[]{:S(2)}, u32[]{:S(2)}) collective-permute-start(f32[8,128]{1,0:T(8,128)S(1)} %get-tuple-element.31.refs_0_), channel_id=1, source_target_pairs={{0,1},{1,0},{2,3},{3,2},{4,5},{5,4},{6,7},{7,6},{8,9},{9,8},{10,11... | collective-permute-start | bytes 12296 | tf_op jit(solution)/shard_map/ppermute | solution.py:280
  5.3 2.6 %collective-permute-start.5 = (f32[8,128]{1,0:T(8,128)S(1)}, f32[8,128]{1,0:T(8,128)S(1)}, u32[]{:S(2)}, u32[]{:S(2)}) collective-permute-start(f32[8,128]{1,0:T(8,128)S(1)} %get-tuple-element.31.refs_0_), channel_id=1, source_target_pairs={{0,2},{1,3},{2,0},{3,1},{4,6},{5,7},{6,4},{7,5},{8,10},{9,11},{10,... | collective-permute-start | bytes 12296 | tf_op jit(solution)/shard_map/ppermute | solution.py:280
  7.9 0.0 collective-permute-start.4
  7.9 0.0 collective-permute-done.refs_2_.refs_4_
  8.0 2.7 %collective-permute-start.1 = (f32[44,8,128]{2,1,0:T(8,128)S(1)}, f32[44,8,128]{2,1,0:T(8,128)S(1)}, u32[]{:S(2)}, u32[]{:S(2)}) collective-permute-start(f32[44,8,128]{2,1,0:T(8,128)S(1)} %get-tuple-element.27), channel_id=1, source_target_pairs={{0,24},{4,28},{8,16},{12,20},{16,8},{20,12},{24,0},{28,4},{1,25},{... | collective-permute-start | bytes 540680 | tf_op jit(solution)/shard_map/ppermute | solution.py:61
  10.7 0.5 %collective-permute-start.2 = (f32[44,8,128]{2,1,0:T(8,128)S(1)}, f32[44,8,128]{2,1,0:T(8,128)S(1)}, u32[]{:S(2)}, u32[]{:S(2)}) collective-permute-start(f32[44,8,128]{2,1,0:T(8,128)S(1)} %get-tuple-element.28), channel_id=1, source_target_pairs={{0,8},{4,20},{8,0},{12,28},{16,24},{20,4},{24,16},{28,12},{1,9},{5... | collective-permute-start | bytes 540680 | tf_op jit(solution)/shard_map/ppermute | solution.py:61
  11.2 0.0 collective-permute-done.6.refs_3_
  11.2 0.3 collective-permute-start.3
  11.5 0.0 copy-done
  11.5 0.3 broadcast_multiply_fusion.decay_ref.refs_4_
  11.8 0.0 copy-start.3
  11.8 0.0 copy-start.1
  11.8 0.0 collective-permute-done.5.refs_2_
  11.8 1.5 %collective-permute-done.4.refs_1_ = f32[8,128]{1,0:T(8,128)S(1)} collective-permute-done((f32[8,128]{1,0:T(8,128)S(1)}, f32[8,128]{1,0:T(8,128)S(1)}, u32[]{:S(2)}, u32[]{:S(2)}) %collective-permute-start.4) | collective-permute-done | bytes 4128 | tf_op jit(solution)/shard_map/ppermute | solution.py:280
  13.3 0.0 collective-permute-start.7
  13.3 1.2 %collective-permute-done.7.refs_2_ = f32[8,128]{1,0:T(8,128)S(1)} collective-permute-done((f32[8,128]{1,0:T(8,128)S(1)}, f32[8,128]{1,0:T(8,128)S(1)}, u32[]{:S(2)}, u32[]{:S(2)}) %collective-permute-start.7) | collective-permute-done | bytes 4128 | tf_op jit(solution)/shard_map/ppermute | solution.py:303
  14.5 2.5 %collective-permute-start.8 = (f32[21,8,128]{2,1,0:T(8,128)S(1)}, f32[21,8,128]{2,1,0:T(8,128)S(1)}, u32[]{:S(2)}, u32[]{:S(2)}) collective-permute-start(f32[21,8,128]{2,1,0:T(8,128)S(1)} %get-tuple-element.32), channel_id=1, source_target_pairs={{0,24},{4,28},{8,16},{12,20},{16,8},{20,12},{24,0},{28,4},{1,25},{... | collective-permute-start | bytes 258056 | tf_op jit(solution)/shard_map/ppermute | solution.py:61
  17.0 0.5 %collective-permute-start.9 = (f32[21,8,128]{2,1,0:T(8,128)S(1)}, f32[21,8,128]{2,1,0:T(8,128)S(1)}, u32[]{:S(2)}, u32[]{:S(2)}) collective-permute-start(f32[21,8,128]{2,1,0:T(8,128)S(1)} %get-tuple-element.33), channel_id=1, source_target_pairs={{0,8},{4,20},{8,0},{12,28},{16,24},{20,4},{24,16},{28,12},{1,9},{5... | collective-permute-start | bytes 258056 | tf_op jit(solution)/shard_map/ppermute | solution.py:61
  17.6 3.5 %collective-permute-done.8.refs_6_ = f32[21,8,128]{2,1,0:T(8,128)S(1)} collective-permute-done((f32[21,8,128]{2,1,0:T(8,128)S(1)}, f32[21,8,128]{2,1,0:T(8,128)S(1)}, u32[]{:S(2)}, u32[]{:S(2)}) %collective-permute-start.8) | collective-permute-done | bytes 86048 | tf_op jit(solution)/shard_map/ppermute | solution.py:61
  21.1 1.6 %collective-permute-start.10 = (f32[21,8,128]{2,1,0:T(8,128)S(1)}, f32[21,8,128]{2,1,0:T(8,128)S(1)}, u32[]{:S(2)}, u32[]{:S(2)}) collective-permute-start(f32[21,8,128]{2,1,0:T(8,128)S(1)} %get-tuple-element.34), channel_id=1, source_target_pairs={{0,16},{4,12},{8,24},{12,4},{16,0},{20,28},{24,8},{28,20},{1,17},{... | collective-permute-start | bytes 258056 | tf_op jit(solution)/shard_map/ppermute | solution.py:61
  22.6 0.0 copy-done.3
  22.6 1.4 %shard_map.67 = (s32[2,40]{1,0:T(2,128)S(1)}, s32[32]{0:T(128)S(1)}) custom-call(s32[1]{0:T(128)} %bitcast.here_ref.refs_0_, s32[2,8]{1,0:T(2,128)S(1)} %bitcast.16), custom_call_target="tpu_custom_call" | custom-call | tf_op jit(solution)/shard_map/pallas_call | solution.py:291
  24.0 0.0 copy-done.1
  24.1 0.3 shard_map.68.refs_1_.decayed_ref
  24.4 0.0 collective-permute-done.9.refs_7_
  24.4 1.2 %collective-permute-done.10.refs_8_ = f32[21,8,128]{2,1,0:T(8,128)S(1)} collective-permute-done((f32[21,8,128]{2,1,0:T(8,128)S(1)}, f32[21,8,128]{2,1,0:T(8,128)S(1)}, u32[]{:S(2)}, u32[]{:S(2)}) %collective-permute-start.10) | collective-permute-done | bytes 86048 | tf_op jit(solution)/shard_map/ppermute | solution.py:61
  25.6 0.0 collective-permute-done.1.refs_2_
  25.6 0.0 collective-permute-done.2.refs_3_
  25.6 0.0 collective-permute-done.3.refs_4_
  25.6 1.0 %shard_map.73 = (f32[2,2,16,1024]{3,2,1,0:T(8,128)S(1)}, f32[2,2,16,1024]{3,2,1,0:T(8,128)S(1)}, f32[2,2,16,1024]{3,2,1,0:T(8,128)S(1)}, f32[2,2,16,1024]{3,2,1,0:T(8,128)S(1)}, f32[2,8,16,1024]{3,2,1,0:T(8,128)S(1)}) custom-call(s32[2,40]{1,0:T(2,128)S(1)} %get-tuple-element.24.refs_0_, f32[32,16,1024]{2,1,0:T(8,128)S(1)} %shard_map.68.refs_1_.decayed_ref, ...), custom_call_target="tpu_custom_call" | custom-call | tf_op jit(solution)/shard_map/pallas_call | solution.py:312
  26.6 2.6 %collective-permute-start.13 = (f32[2,2,16,1024]{3,2,1,0:T(8,128)S(1)}, f32[2,2,16,1024]{3,2,1,0:T(8,128)S(1)}, u32[]{:S(2)}, u32[]{:S(2)}) collective-permute-start(f32[2,2,16,1024]{3,2,1,0:T(8,128)S(1)} %get-tuple-element.40), channel_id=1, source_target_pairs={{0,24},{4,28},{8,16},{12,20},{16,8},{20,12},{24,0},{28,4},{1,25},{... | collective-permute-start | bytes 786440 | tf_op jit(solution)/shard_map/ppermute | solution.py:61
  29.1 0.5 %collective-permute-start.14 = (f32[2,2,16,1024]{3,2,1,0:T(8,128)S(1)}, f32[2,2,16,1024]{3,2,1,0:T(8,128)S(1)}, u32[]{:S(2)}, u32[]{:S(2)}) collective-permute-start(f32[2,2,16,1024]{3,2,1,0:T(8,128)S(1)} %get-tuple-element.41), channel_id=1, source_target_pairs={{0,8},{4,20},{8,0},{12,28},{16,24},{20,4},{24,16},{28,12},{1,9},{5... | collective-permute-start | bytes 786440 | tf_op jit(solution)/shard_map/ppermute | solution.py:61
  29.7 3.1 %shard_map.74 = (f32[32,16,1024]{2,1,0:T(8,128)}, f32[32,16,1024]{2,1,0:T(8,128)}, f32[8,128]{1,0:T(8,128)S(1)}) custom-call(s32[32]{0:T(128)S(1)} %get-tuple-element.37.module_ref, f32[2,8,16,1024]{3,2,1,0:T(8,128)S(1)} %get-tuple-element.38.grad_ref, f32[32,16,1024]{2,1,0:T(8,128)S(1)} %shard_map.68.refs_1_.decayed_ref, f32[32,16,1024]{2,1,0:T(8,128)S(1)} %bitcast.13), custom_call_target="tpu_custom_call" | custom-call | tf_op jit(solution)/shard_map/pallas_call | solution.py:322
  32.7 1.2 %collective-permute-done.13.refs_1_.refs_2_ = f32[2,2,16,1024]{3,2,1,0:T(8,128)S(1)} collective-permute-done((f32[2,2,16,1024]{3,2,1,0:T(8,128)S(1)}, f32[2,2,16,1024]{3,2,1,0:T(8,128)S(1)}, u32[]{:S(2)}, u32[]{:S(2)}) %collective-permute-start.13) | collective-permute-done | bytes 262176 | tf_op jit(solution)/shard_map/ppermute | solution.py:61
  34.0 2.9 %collective-permute-done.14.refs_2_.refs_3_ = f32[2,2,16,1024]{3,2,1,0:T(8,128)S(1)} collective-permute-done((f32[2,2,16,1024]{3,2,1,0:T(8,128)S(1)}, f32[2,2,16,1024]{3,2,1,0:T(8,128)S(1)}, u32[]{:S(2)}, u32[]{:S(2)}) %collective-permute-start.14) | collective-permute-done | bytes 262176 | tf_op jit(solution)/shard_map/ppermute | solution.py:61
  36.8 0.1 collective-permute-start.15
  36.9 1.1 %collective-permute-start.11 = (f32[2,2,16,1024]{3,2,1,0:T(8,128)S(1)}, f32[2,2,16,1024]{3,2,1,0:T(8,128)S(1)}, u32[]{:S(2)}, u32[]{:S(2)}) collective-permute-start(f32[2,2,16,1024]{3,2,1,0:T(8,128)S(1)} %get-tuple-element.36), channel_id=1, source_target_pairs={{0,16},{4,12},{8,24},{12,4},{16,0},{20,28},{24,8},{28,20},{1,17},{... | collective-permute-start | bytes 786440 | tf_op jit(solution)/shard_map/ppermute | solution.py:61
  38.0 5.3 %collective-permute-done.11.refs_1_.refs_4_ = f32[2,2,16,1024]{3,2,1,0:T(8,128)S(1)} collective-permute-done((f32[2,2,16,1024]{3,2,1,0:T(8,128)S(1)}, f32[2,2,16,1024]{3,2,1,0:T(8,128)S(1)}, u32[]{:S(2)}, u32[]{:S(2)}) %collective-permute-start.11) | collective-permute-done | bytes 262176 | tf_op jit(solution)/shard_map/ppermute | solution.py:61
  43.4 0.1 collective-permute-start.12
  43.4 0.0 collective-permute-done.15.refs_1_
  43.5 1.1 %shard_map.77.refs_2_ = f32[2,4,2,16,1024]{4,3,2,1,0:T(8,128)} custom-call(s32[1]{0:T(128)} %bitcast.here_ref.refs_0_, f32[3,2,16,1024]{3,2,1,0:T(8,128)S(1)} %collective-permute-done.15.refs_1_, f32[2,2,16,1024]{3,2,1,0:T(8,128)S(1)} %collective-permute-done.13.refs_1_.refs_2_, f32[2,2,16,1024]{3,2,1,0:T(8,128)S(1)} %collective-permute-done.14.refs_2_.refs_3_, ...), custom_call_target="tpu_custom_call" | custom-call | tf_op jit(solution)/shard_map/pallas_call | solution.py:340
  44.5 0.3 collective-permute-done.12.refs_1_
  44.8 0.7 %shard_map.78 = f32[2,4,2,16,1024]{4,3,2,1,0:T(8,128)} custom-call(s32[1]{0:T(128)} %bitcast.here_ref.refs_0_, f32[1,2,16,1024]{3,2,1,0:T(8,128)S(1)} %collective-permute-done.12.refs_1_, f32[2,4,2,16,1024]{4,3,2,1,0:T(8,128)} %shard_map.77.refs_2_), custom_call_target="tpu_custom_call", output_to_operand_aliasing={{}: (2, {})} | custom-call | tf_op jit(solution)/shard_map/pallas_call | solution.py:347
  (5 shorter events, 0.1 us)
Async XLA Ops:
  0.6 10.9 %copy-start = (f32[32,1,16,1024]{3,2,1,0:T(8,128)S(1)}, f32[32,1,16,1024]{3,2,1,0:T(8,128)}, u32[]{:S(2)}) copy-start(f32[32,1,16,1024]{3,2,1,0:T(8,128)} %param.7) | copy-start | bytes 6291460
  0.6 1.4 %copy-start.2 = (f32[1,2,128,1024]{3,2,1,0:T(8,128)S(1)}, f32[1,2,128,1024]{3,2,1,0:T(8,128)}, u32[]{:S(2)}) copy-start(f32[1,2,128,1024]{3,2,1,0:T(8,128)} %param.4) | copy-start | bytes 3145732
  2.1 5.8 %collective-permute-start = (f32[2,4,16,1024]{3,2,1,0:T(8,128)S(1)}, f32[2,4,16,1024]{3,2,1,0:T(8,128)S(1)}, u32[]{:S(2)}, u32[]{:S(2)}) collective-permute-start(f32[2,4,16,1024]{3,2,1,0:T(8,128)S(1)} %get-tuple-element.26), channel_id=1, source_target_pairs={{0,4},{4,0},{8,12},{12,8},{16,20},{20,16},{24,28},{28,24},{1,5},{5... | collective-permute-start | bytes 1572872 | tf_op jit(solution)/shard_map/ppermute | solution.py:278
  2.6 8.6 %collective-permute-start.6 = (f32[8,128]{1,0:T(8,128)S(1)}, f32[8,128]{1,0:T(8,128)S(1)}, u32[]{:S(2)}, u32[]{:S(2)}) collective-permute-start(f32[8,128]{1,0:T(8,128)S(1)} %get-tuple-element.31.refs_0_), channel_id=1, source_target_pairs={{0,1},{1,0},{2,3},{3,2},{4,5},{5,4},{6,7},{7,6},{8,9},{9,8},{10,11... | collective-permute-start | bytes 12296 | tf_op jit(solution)/shard_map/ppermute | solution.py:280
  5.3 6.5 %collective-permute-start.5 = (f32[8,128]{1,0:T(8,128)S(1)}, f32[8,128]{1,0:T(8,128)S(1)}, u32[]{:S(2)}, u32[]{:S(2)}) collective-permute-start(f32[8,128]{1,0:T(8,128)S(1)} %get-tuple-element.31.refs_0_), channel_id=1, source_target_pairs={{0,2},{1,3},{2,0},{3,1},{4,6},{5,7},{6,4},{7,5},{8,10},{9,11},{10,... | collective-permute-start | bytes 12296 | tf_op jit(solution)/shard_map/ppermute | solution.py:280
  7.9 5.4 %collective-permute-start.4 = (f32[8,128]{1,0:T(8,128)S(1)}, f32[8,128]{1,0:T(8,128)S(1)}, u32[]{:S(2)}, u32[]{:S(2)}) collective-permute-start(f32[8,128]{1,0:T(8,128)S(1)} %get-tuple-element.31.refs_0_), channel_id=1, source_target_pairs={{0,3},{1,2},{2,1},{3,0},{4,7},{5,6},{6,5},{7,4},{8,11},{9,10},{10,... | collective-permute-start | bytes 12296 | tf_op jit(solution)/shard_map/ppermute | solution.py:280
  8.0 17.6 %collective-permute-start.1 = (f32[44,8,128]{2,1,0:T(8,128)S(1)}, f32[44,8,128]{2,1,0:T(8,128)S(1)}, u32[]{:S(2)}, u32[]{:S(2)}) collective-permute-start(f32[44,8,128]{2,1,0:T(8,128)S(1)} %get-tuple-element.27), channel_id=1, source_target_pairs={{0,24},{4,28},{8,16},{12,20},{16,8},{20,12},{24,0},{28,4},{1,25},{... | collective-permute-start | bytes 540680 | tf_op jit(solution)/shard_map/ppermute | solution.py:61
  10.7 14.9 %collective-permute-start.2 = (f32[44,8,128]{2,1,0:T(8,128)S(1)}, f32[44,8,128]{2,1,0:T(8,128)S(1)}, u32[]{:S(2)}, u32[]{:S(2)}) collective-permute-start(f32[44,8,128]{2,1,0:T(8,128)S(1)} %get-tuple-element.28), channel_id=1, source_target_pairs={{0,8},{4,20},{8,0},{12,28},{16,24},{20,4},{24,16},{28,12},{1,9},{5... | collective-permute-start | bytes 540680 | tf_op jit(solution)/shard_map/ppermute | solution.py:61
  11.2 14.3 %collective-permute-start.3 = (f32[44,8,128]{2,1,0:T(8,128)S(1)}, f32[44,8,128]{2,1,0:T(8,128)S(1)}, u32[]{:S(2)}, u32[]{:S(2)}) collective-permute-start(f32[44,8,128]{2,1,0:T(8,128)S(1)} %get-tuple-element.29), channel_id=1, source_target_pairs={{0,16},{4,12},{8,24},{12,4},{16,0},{20,28},{24,8},{28,20},{1,17},{... | collective-permute-start | bytes 540680 | tf_op jit(solution)/shard_map/ppermute | solution.py:61
  11.8 10.8 %copy-start.3 = (s32[8,2]{0,1:T(2,128)S(1)}, s32[8,2]{0,1:T(2,128)}, u32[]{:S(2)}) copy-start(s32[8,2]{0,1:T(2,128)} %param.5) | copy-start | bytes 196
  11.8 12.2 %copy-start.1 = (f32[32,1,16,1024]{3,2,1,0:T(8,128)S(1)}, f32[32,1,16,1024]{3,2,1,0:T(8,128)}, u32[]{:S(2)}) copy-start(f32[32,1,16,1024]{3,2,1,0:T(8,128)} %param.6) | copy-start | bytes 6291460
  13.3 1.2 %collective-permute-start.7 = (f32[8,128]{1,0:T(8,128)S(1)}, f32[8,128]{1,0:T(8,128)S(1)}, u32[]{:S(2)}, u32[]{:S(2)}) collective-permute-start(f32[8,128]{1,0:T(8,128)S(1)} %shard_map.71.refs_1_), channel_id=1, source_target_pairs={{0,4},{4,0},{8,12},{12,8},{16,20},{20,16},{24,28},{28,24},{1,5},{5... | collective-permute-start | bytes 12296 | tf_op jit(solution)/shard_map/ppermute | solution.py:303
  14.5 6.6 %collective-permute-start.8 = (f32[21,8,128]{2,1,0:T(8,128)S(1)}, f32[21,8,128]{2,1,0:T(8,128)S(1)}, u32[]{:S(2)}, u32[]{:S(2)}) collective-permute-start(f32[21,8,128]{2,1,0:T(8,128)S(1)} %get-tuple-element.32), channel_id=1, source_target_pairs={{0,24},{4,28},{8,16},{12,20},{16,8},{20,12},{24,0},{28,4},{1,25},{... | collective-permute-start | bytes 258056 | tf_op jit(solution)/shard_map/ppermute | solution.py:61
  17.0 7.4 %collective-permute-start.9 = (f32[21,8,128]{2,1,0:T(8,128)S(1)}, f32[21,8,128]{2,1,0:T(8,128)S(1)}, u32[]{:S(2)}, u32[]{:S(2)}) collective-permute-start(f32[21,8,128]{2,1,0:T(8,128)S(1)} %get-tuple-element.33), channel_id=1, source_target_pairs={{0,8},{4,20},{8,0},{12,28},{16,24},{20,4},{24,16},{28,12},{1,9},{5... | collective-permute-start | bytes 258056 | tf_op jit(solution)/shard_map/ppermute | solution.py:61
  21.1 4.5 %collective-permute-start.10 = (f32[21,8,128]{2,1,0:T(8,128)S(1)}, f32[21,8,128]{2,1,0:T(8,128)S(1)}, u32[]{:S(2)}, u32[]{:S(2)}) collective-permute-start(f32[21,8,128]{2,1,0:T(8,128)S(1)} %get-tuple-element.34), channel_id=1, source_target_pairs={{0,16},{4,12},{8,24},{12,4},{16,0},{20,28},{24,8},{28,20},{1,17},{... | collective-permute-start | bytes 258056 | tf_op jit(solution)/shard_map/ppermute | solution.py:61
  26.6 7.4 %collective-permute-start.13 = (f32[2,2,16,1024]{3,2,1,0:T(8,128)S(1)}, f32[2,2,16,1024]{3,2,1,0:T(8,128)S(1)}, u32[]{:S(2)}, u32[]{:S(2)}) collective-permute-start(f32[2,2,16,1024]{3,2,1,0:T(8,128)S(1)} %get-tuple-element.40), channel_id=1, source_target_pairs={{0,24},{4,28},{8,16},{12,20},{16,8},{20,12},{24,0},{28,4},{1,25},{... | collective-permute-start | bytes 786440 | tf_op jit(solution)/shard_map/ppermute | solution.py:61
  29.1 7.7 %collective-permute-start.14 = (f32[2,2,16,1024]{3,2,1,0:T(8,128)S(1)}, f32[2,2,16,1024]{3,2,1,0:T(8,128)S(1)}, u32[]{:S(2)}, u32[]{:S(2)}) collective-permute-start(f32[2,2,16,1024]{3,2,1,0:T(8,128)S(1)} %get-tuple-element.41), channel_id=1, source_target_pairs={{0,8},{4,20},{8,0},{12,28},{16,24},{20,4},{24,16},{28,12},{1,9},{5... | collective-permute-start | bytes 786440 | tf_op jit(solution)/shard_map/ppermute | solution.py:61
  36.8 6.6 %collective-permute-start.15 = (f32[3,2,16,1024]{3,2,1,0:T(8,128)S(1)}, f32[3,2,16,1024]{3,2,1,0:T(8,128)S(1)}, u32[]{:S(2)}, u32[]{:S(2)}) collective-permute-start(f32[3,2,16,1024]{3,2,1,0:T(8,128)S(1)} %shard_map.76), channel_id=1, source_target_pairs={{0,4},{4,0},{8,12},{12,8},{16,20},{20,16},{24,28},{28,24},{1,5},{5... | collective-permute-start | bytes 1179656 | tf_op jit(solution)/shard_map/ppermute | solution.py:339
  36.9 6.4 %collective-permute-start.11 = (f32[2,2,16,1024]{3,2,1,0:T(8,128)S(1)}, f32[2,2,16,1024]{3,2,1,0:T(8,128)S(1)}, u32[]{:S(2)}, u32[]{:S(2)}) collective-permute-start(f32[2,2,16,1024]{3,2,1,0:T(8,128)S(1)} %get-tuple-element.36), channel_id=1, source_target_pairs={{0,16},{4,12},{8,24},{12,4},{16,0},{20,28},{24,8},{28,20},{1,17},{... | collective-permute-start | bytes 786440 | tf_op jit(solution)/shard_map/ppermute | solution.py:61
  43.4 1.4 %collective-permute-start.12 = (f32[1,2,16,1024]{3,2,1,0:T(8,128)S(1)}, f32[1,2,16,1024]{3,2,1,0:T(8,128)S(1)}, u32[]{:S(2)}, u32[]{:S(2)}) collective-permute-start(f32[1,2,16,1024]{3,2,1,0:T(8,128)S(1)} %shard_map.75), channel_id=1, source_target_pairs={{0,4},{4,0},{8,12},{12,8},{16,20},{20,16},{24,28},{28,24},{1,5},{5... | collective-permute-start | bytes 393224 | tf_op jit(solution)/shard_map/ppermute | solution.py:339

commit v11 on v10

--- a/solution.py
+++ b/solution.py
@@ -205,12 +205,13 @@
         new_params_ref[place] = decayed_ref[module] - grad_coef * grad
 
 
-def give_back_kernel(count, here_ref, *refs):
-    for i in range(count):
-        refs[-1][i] = refs[i][1 - (here_ref[0] & 1)]
-
-
-def first_rows_kernel(size, first, here_ref, back_ref, *refs):
+def give_back_kernel(here_ref, block_ref, done_ref, out_ref):
+    del done_ref
+    out_ref[...] = block_ref[1 - (here_ref[0] & 1)]
+
+
+def first_rows_kernel(size, first, here_ref, *refs):
+    backs, refs = refs[: len(first)], refs[len(first) :]
     here = here_ref[0]
     core = here & 1
     out_ref, sems = refs[-2:]
@@ -226,7 +227,7 @@
         for level in range(LEVELS):
             copies.append(
                 pltpu.make_async_copy(
-                    back_ref.at[i, level], out_ref.at[level, chip, 1 - core], sems.at[1, level, i]
+                    backs[i].at[level], out_ref.at[level, chip, 1 - core], sems.at[1, level, i]
                 )
             )
     for copy in copies:
@@ -238,15 +239,11 @@
 def last_rows_kernel(size, last, here_ref, back_ref, held_ref, out_ref, sems):
     del held_ref
     here = here_ref[0]
-    copies = []
-    for i, k in enumerate(last):
-        chip = origin(here ^ 1, k, size) // 2
-        for level in range(LEVELS):
-            copies.append(
-                pltpu.make_async_copy(
-                    back_ref.at[i, level], out_ref.at[level, chip, 1 - (here & 1)], sems.at[level, i]
-                )
-            )
+    chip = origin(here ^ 1, last, size) // 2
+    copies = [
+        pltpu.make_async_copy(back_ref.at[level], out_ref.at[level, chip, 1 - (here & 1)], sems.at[level])
+        for level in range(LEVELS)
+    ]
     for copy in copies:
         copy.start()
     for copy in copies:
@@ -326,32 +323,29 @@
         [state_block, state_block, vmem],
         grid=(module_count // block,),
     )(leaders, grad, decayed, moment_in)
-    first, last = [*order[:-2], order[-1]], order[-2:-1]
     blocks = dict(zip(order, returned))
-    backs = []
-    for part in (first, last):
+    backs = {}
+    for k in (0, *order[:-1]):
         back = call(
-            lambda *refs, count=len(part): give_back_kernel(count, *refs),
-            shape(len(part), LEVELS, own_rows, width),
-            [smem] + [vmem] * len(part) + [anywhere],
-            vmem,
-        )(here, *[blocks[k] for k in part], done)
-        backs.append(lax.ppermute(back, "path", swap))
+            give_back_kernel, shape(LEVELS, own_rows, width), [smem, vmem, anywhere], vmem
+        )(here, blocks[k], done)
+        backs[k] = lax.ppermute(back, "path", swap)
+    first, last = (0, *order[:-2]), order[-2]
     path_params = call(
         lambda *refs: first_rows_kernel(size, first, *refs),
         shape(*split_slab.shape),
-        [smem] + [anywhere] * (1 + rounds),
+        [smem] + [anywhere] * (len(first) + rounds),
         anywhere,
         scratch_shapes=[pltpu.SemaphoreType.DMA((2, LEVELS, rounds))],
-    )(here, backs[0], *returned)
+    )(here, *[backs[k] for k in first], *returned)
     path_params = call(
         lambda *refs: last_rows_kernel(size, last, *refs),
         shape(*split_slab.shape),
         [smem, anywhere, anywhere],
         anywhere,
-        scratch_shapes=[pltpu.SemaphoreType.DMA((LEVELS, len(last)))],
+        scratch_shapes=[pltpu.SemaphoreType.DMA((LEVELS,))],
         input_output_aliases={2: 0},
-    )(here, backs[1], path_params)
+    )(here, backs[last], path_params)
     return (path_params.reshape(path_delta.shape), new_state[:, None], new_moment[:, None])
 
 

time: 45.6 us -> 42.8 us (0.939)
  waiting for transfers between devices: 17 us -> 14.2 us
    ppermute x9, waiting for transfers between devices: 14.1 us -> 10.8 us  [move(): lax.ppermute(array, 'path', [(i, target(i, k, size)) for i in range(size)])]
    ppermute x9, starting transfers between devices: 12.4 us -> 11.7 us  [move(): lax.ppermute(array, 'path', [(i, target(i, k, size)) for i in range(size)])]
    ppermute x2 -> x4, starting transfers between devices: 0.14 us -> 0.76 us  [local(): backs[k] = lax.ppermute(back, 'path', swap)]
    ppermute x2 -> x4, waiting for transfers between devices: 0.26 us -> 0.76 us  [local(): backs[k] = lax.ppermute(back, 'path', swap)]
  transfers between devices with their start and end apart: 16 -> 18, of which waited for: 8 -> 7; matrix products, arithmetic and copies ran while one was open for 1% -> 1% of each run, Pallas kernels for 13% -> 14%
where the time goes in v11:
time: 42.8 us; the launch traced here: 42.7 us
  starting transfers between devices  18.2 us (43%)
  waiting for transfers between devices  14.2 us (33%)
  Pallas kernels  7.71 us (18%)
  local copies, waits for them, and re-layouts  1.38 us (3%)
  between operations  0.83 us (2%)
    ppermute x9, starting transfers between devices, move(): lax.ppermute(array, 'path', [(i, target(i, k, size)) for i in range(size)])  11.7 us
    ppermute x9, waiting for transfers between devices, move(): lax.ppermute(array, 'path', [(i, target(i, k, size)) for i in range(size)])  10.8 us
    ppermute x3, starting transfers between devices, local(): lax.ppermute(squares, 'shard', [(i, i ^ step) for i in range(shards)])  5.25 us
    pallas_call x1, Pallas kernels, local(): call(state_kernel, [shape(*state_in.shape)] * 2 + [shape(8, 128)], [smem,...  3.06 us
    ppermute x3, waiting for transfers between devices, local(): lax.ppermute(squares, 'shard', [(i, i ^ step) for i in range(shards)])  1.47 us
    pallas_call x1, Pallas kernels, local(): call(plan_kernel, [jax.ShapeDtypeStruct((LEVELS, 5 * size), jnp.int32), j...  1.4 us
    unnamed x8, local copies, waits for them, and re-layouts  1.38 us
    ppermute x1, waiting for transfers between devices, local(): other = lax.ppermute(squares, 'path', swap)  1.16 us
  transfers between devices with their start and end apart: 18, of which 7 were waited for; matrix products, arithmetic and copies ran while one was open for 1% of the time, Pallas kernels for 14%

profile of v11, /device:TPU:0, one launch (start us, length us, event | category | flops | bytes accessed | tf_op | source)
XLA Modules:
  0.0 42.7 jit_solution(17899816478714060738)
XLA Ops:
  0.6 0.0 copy-start
  0.7 1.4 %copy-done.2 = f32[1,2,128,1024]{3,2,1,0:T(8,128)S(1)} copy-done((f32[1,2,128,1024]{3,2,1,0:T(8,128)S(1)}, f32[1,2,128,1024]{3,2,1,0:T(8,128)}, u32[]{:S(2)}) %copy-start.2) | copy-done | bytes 1048600
  2.0 0.1 shard_map.69
  2.1 0.5 %collective-permute-start = (f32[2,4,16,1024]{3,2,1,0:T(8,128)S(1)}, f32[2,4,16,1024]{3,2,1,0:T(8,128)S(1)}, u32[]{:S(2)}, u32[]{:S(2)}) collective-permute-start(f32[2,4,16,1024]{3,2,1,0:T(8,128)S(1)} %get-tuple-element.26), channel_id=1, source_target_pairs={{0,4},{4,0},{8,12},{12,8},{16,20},{20,16},{24,28},{28,24},{1,5},{5... | collective-permute-start | bytes 1572872 | tf_op jit(solution)/shard_map/ppermute | solution.py:275
  2.6 2.7 %collective-permute-start.6 = (f32[8,128]{1,0:T(8,128)S(1)}, f32[8,128]{1,0:T(8,128)S(1)}, u32[]{:S(2)}, u32[]{:S(2)}) collective-permute-start(f32[8,128]{1,0:T(8,128)S(1)} %get-tuple-element.31.refs_0_), channel_id=1, source_target_pairs={{0,1},{1,0},{2,3},{3,2},{4,5},{5,4},{6,7},{7,6},{8,9},{9,8},{10,11... | collective-permute-start | bytes 12296 | tf_op jit(solution)/shard_map/ppermute | solution.py:277
  5.3 2.6 %collective-permute-start.5 = (f32[8,128]{1,0:T(8,128)S(1)}, f32[8,128]{1,0:T(8,128)S(1)}, u32[]{:S(2)}, u32[]{:S(2)}) collective-permute-start(f32[8,128]{1,0:T(8,128)S(1)} %get-tuple-element.31.refs_0_), channel_id=1, source_target_pairs={{0,2},{1,3},{2,0},{3,1},{4,6},{5,7},{6,4},{7,5},{8,10},{9,11},{10,... | collective-permute-start | bytes 12296 | tf_op jit(solution)/shard_map/ppermute | solution.py:277
  7.9 0.0 collective-permute-start.4
  7.9 0.0 collective-permute-done.refs_2_.refs_4_
  8.0 2.7 %collective-permute-start.1 = (f32[44,8,128]{2,1,0:T(8,128)S(1)}, f32[44,8,128]{2,1,0:T(8,128)S(1)}, u32[]{:S(2)}, u32[]{:S(2)}) collective-permute-start(f32[44,8,128]{2,1,0:T(8,128)S(1)} %get-tuple-element.27), channel_id=1, source_target_pairs={{0,24},{4,28},{8,16},{12,20},{16,8},{20,12},{24,0},{28,4},{1,25},{... | collective-permute-start | bytes 540680 | tf_op jit(solution)/shard_map/ppermute | solution.py:61
  10.7 0.5 %collective-permute-start.2 = (f32[44,8,128]{2,1,0:T(8,128)S(1)}, f32[44,8,128]{2,1,0:T(8,128)S(1)}, u32[]{:S(2)}, u32[]{:S(2)}) collective-permute-start(f32[44,8,128]{2,1,0:T(8,128)S(1)} %get-tuple-element.28), channel_id=1, source_target_pairs={{0,8},{4,20},{8,0},{12,28},{16,24},{20,4},{24,16},{28,12},{1,9},{5... | collective-permute-start | bytes 540680 | tf_op jit(solution)/shard_map/ppermute | solution.py:61
  11.2 0.0 collective-permute-done.6.refs_3_
  11.2 0.3 collective-permute-start.3
  11.5 0.3 broadcast_multiply_fusion.decay_ref.refs_4_
  11.8 0.0 copy-start.3
  11.8 0.0 copy-start.1
  11.8 0.0 collective-permute-done.5.refs_2_
  11.8 1.5 %collective-permute-done.4.refs_1_ = f32[8,128]{1,0:T(8,128)S(1)} collective-permute-done((f32[8,128]{1,0:T(8,128)S(1)}, f32[8,128]{1,0:T(8,128)S(1)}, u32[]{:S(2)}, u32[]{:S(2)}) %collective-permute-start.4) | collective-permute-done | bytes 4128 | tf_op jit(solution)/shard_map/ppermute | solution.py:277
  13.3 0.0 collective-permute-start.7
  13.3 1.2 %collective-permute-done.7.refs_2_ = f32[8,128]{1,0:T(8,128)S(1)} collective-permute-done((f32[8,128]{1,0:T(8,128)S(1)}, f32[8,128]{1,0:T(8,128)S(1)}, u32[]{:S(2)}, u32[]{:S(2)}) %collective-permute-start.7) | collective-permute-done | bytes 4128 | tf_op jit(solution)/shard_map/ppermute | solution.py:300
  14.5 2.5 %collective-permute-start.8 = (f32[21,8,128]{2,1,0:T(8,128)S(1)}, f32[21,8,128]{2,1,0:T(8,128)S(1)}, u32[]{:S(2)}, u32[]{:S(2)}) collective-permute-start(f32[21,8,128]{2,1,0:T(8,128)S(1)} %get-tuple-element.32), channel_id=1, source_target_pairs={{0,24},{4,28},{8,16},{12,20},{16,8},{20,12},{24,0},{28,4},{1,25},{... | collective-permute-start | bytes 258056 | tf_op jit(solution)/shard_map/ppermute | solution.py:61
  17.0 0.5 %collective-permute-start.9 = (f32[21,8,128]{2,1,0:T(8,128)S(1)}, f32[21,8,128]{2,1,0:T(8,128)S(1)}, u32[]{:S(2)}, u32[]{:S(2)}) collective-permute-start(f32[21,8,128]{2,1,0:T(8,128)S(1)} %get-tuple-element.33), channel_id=1, source_target_pairs={{0,8},{4,20},{8,0},{12,28},{16,24},{20,4},{24,16},{28,12},{1,9},{5... | collective-permute-start | bytes 258056 | tf_op jit(solution)/shard_map/ppermute | solution.py:61
  17.6 3.5 %collective-permute-done.8.refs_6_ = f32[21,8,128]{2,1,0:T(8,128)S(1)} collective-permute-done((f32[21,8,128]{2,1,0:T(8,128)S(1)}, f32[21,8,128]{2,1,0:T(8,128)S(1)}, u32[]{:S(2)}, u32[]{:S(2)}) %collective-permute-start.8) | collective-permute-done | bytes 86048 | tf_op jit(solution)/shard_map/ppermute | solution.py:61
  21.1 1.6 %collective-permute-start.10 = (f32[21,8,128]{2,1,0:T(8,128)S(1)}, f32[21,8,128]{2,1,0:T(8,128)S(1)}, u32[]{:S(2)}, u32[]{:S(2)}) collective-permute-start(f32[21,8,128]{2,1,0:T(8,128)S(1)} %get-tuple-element.34), channel_id=1, source_target_pairs={{0,16},{4,12},{8,24},{12,4},{16,0},{20,28},{24,8},{28,20},{1,17},{... | collective-permute-start | bytes 258056 | tf_op jit(solution)/shard_map/ppermute | solution.py:61
  22.6 1.4 %shard_map.67 = (s32[2,40]{1,0:T(2,128)S(1)}, s32[32]{0:T(128)S(1)}) custom-call(s32[1]{0:T(128)} %bitcast.here_ref.refs_0_, s32[2,8]{1,0:T(2,128)S(1)} %bitcast.16), custom_call_target="tpu_custom_call" | custom-call | tf_op jit(solution)/shard_map/pallas_call | solution.py:288
  24.1 0.3 shard_map.68.refs_1_.decayed_ref
  24.4 0.0 collective-permute-done.9.refs_7_
  24.4 1.2 %collective-permute-done.10.refs_8_ = f32[21,8,128]{2,1,0:T(8,128)S(1)} collective-permute-done((f32[21,8,128]{2,1,0:T(8,128)S(1)}, f32[21,8,128]{2,1,0:T(8,128)S(1)}, u32[]{:S(2)}, u32[]{:S(2)}) %collective-permute-start.10) | collective-permute-done | bytes 86048 | tf_op jit(solution)/shard_map/ppermute | solution.py:61
  25.6 0.0 collective-permute-done.1.refs_2_
  25.6 0.0 collective-permute-done.2.refs_3_
  25.6 0.0 collective-permute-done.3.refs_4_
  25.6 1.0 %shard_map.73 = (f32[2,2,16,1024]{3,2,1,0:T(8,128)S(1)}, f32[2,2,16,1024]{3,2,1,0:T(8,128)S(1)}, f32[2,2,16,1024]{3,2,1,0:T(8,128)S(1)}, f32[2,2,16,1024]{3,2,1,0:T(8,128)S(1)}, f32[2,8,16,1024]{3,2,1,0:T(8,128)S(1)}) custom-call(s32[2,40]{1,0:T(2,128)S(1)} %get-tuple-element.24.refs_0_, f32[32,16,1024]{2,1,0:T(8,128)S(1)} %shard_map.68.refs_1_.decayed_ref, ...), custom_call_target="tpu_custom_call" | custom-call | tf_op jit(solution)/shard_map/pallas_call | solution.py:309
  26.6 2.6 %collective-permute-start.14 = (f32[2,2,16,1024]{3,2,1,0:T(8,128)S(1)}, f32[2,2,16,1024]{3,2,1,0:T(8,128)S(1)}, u32[]{:S(2)}, u32[]{:S(2)}) collective-permute-start(f32[2,2,16,1024]{3,2,1,0:T(8,128)S(1)} %get-tuple-element.41), channel_id=1, source_target_pairs={{0,24},{4,28},{8,16},{12,20},{16,8},{20,12},{24,0},{28,4},{1,25},{... | collective-permute-start | bytes 786440 | tf_op jit(solution)/shard_map/ppermute | solution.py:61
  29.1 0.5 %collective-permute-start.16 = (f32[2,2,16,1024]{3,2,1,0:T(8,128)S(1)}, f32[2,2,16,1024]{3,2,1,0:T(8,128)S(1)}, u32[]{:S(2)}, u32[]{:S(2)}) collective-permute-start(f32[2,2,16,1024]{3,2,1,0:T(8,128)S(1)} %get-tuple-element.42), channel_id=1, source_target_pairs={{0,8},{4,20},{8,0},{12,28},{16,24},{20,4},{24,16},{28,12},{1,9},{5... | collective-permute-start | bytes 786440 | tf_op jit(solution)/shard_map/ppermute | solution.py:61
  29.7 0.5 %collective-permute-start.11 = (f32[2,2,16,1024]{3,2,1,0:T(8,128)S(1)}, f32[2,2,16,1024]{3,2,1,0:T(8,128)S(1)}, u32[]{:S(2)}, u32[]{:S(2)}) collective-permute-start(f32[2,2,16,1024]{3,2,1,0:T(8,128)S(1)} %get-tuple-element.36), channel_id=1, source_target_pairs={{0,16},{4,12},{8,24},{12,4},{16,0},{20,28},{24,8},{28,20},{1,17},{... | collective-permute-start | bytes 786440 | tf_op jit(solution)/shard_map/ppermute | solution.py:61
  30.1 3.1 %shard_map.74 = (f32[32,16,1024]{2,1,0:T(8,128)}, f32[32,16,1024]{2,1,0:T(8,128)}, f32[8,128]{1,0:T(8,128)S(1)}) custom-call(s32[32]{0:T(128)S(1)} %get-tuple-element.37.module_ref, f32[2,8,16,1024]{3,2,1,0:T(8,128)S(1)} %get-tuple-element.38.grad_ref, f32[32,16,1024]{2,1,0:T(8,128)S(1)} %shard_map.68.refs_1_.decayed_ref, f32[32,16,1024]{2,1,0:T(8,128)S(1)} %bitcast.13), custom_call_target="tpu_custom_call" | custom-call | tf_op jit(solution)/shard_map/pallas_call | solution.py:319
  33.2 0.1 collective-permute-start.13
  33.3 3.3 %collective-permute-done.14.block_ref.refs_4_ = f32[2,2,16,1024]{3,2,1,0:T(8,128)S(1)} collective-permute-done((f32[2,2,16,1024]{3,2,1,0:T(8,128)S(1)}, f32[2,2,16,1024]{3,2,1,0:T(8,128)S(1)}, u32[]{:S(2)}, u32[]{:S(2)}) %collective-permute-start.14) | collective-permute-done | bytes 262176 | tf_op jit(solution)/shard_map/ppermute | solution.py:61
  36.6 0.1 collective-permute-start.15
  36.7 2.8 %collective-permute-done.16.block_ref.refs_5_ = f32[2,2,16,1024]{3,2,1,0:T(8,128)S(1)} collective-permute-done((f32[2,2,16,1024]{3,2,1,0:T(8,128)S(1)}, f32[2,2,16,1024]{3,2,1,0:T(8,128)S(1)}, u32[]{:S(2)}, u32[]{:S(2)}) %collective-permute-start.16) | collective-permute-done | bytes 262176 | tf_op jit(solution)/shard_map/ppermute | solution.py:61
  39.5 0.1 collective-permute-start.17
  39.6 0.0 collective-permute-done.11.block_ref.refs_6_
  39.6 0.5 %collective-permute-start.12 = (f32[2,16,1024]{2,1,0:T(8,128)S(1)}, f32[2,16,1024]{2,1,0:T(8,128)S(1)}, u32[]{:S(2)}, u32[]{:S(2)}) collective-permute-start(f32[2,16,1024]{2,1,0:T(8,128)S(1)} %shard_map.75), channel_id=1, source_target_pairs={{0,4},{4,0},{8,12},{12,8},{16,20},{20,16},{24,28},{28,24},{1,5},{5... | collective-permute-start | bytes 393224 | tf_op jit(solution)/shard_map/ppermute | solution.py:332
  40.2 0.0 collective-permute-done.13.refs_1_
  40.2 0.0 collective-permute-done.15.refs_2_
  40.2 0.7 %collective-permute-done.17.refs_3_ = f32[2,16,1024]{2,1,0:T(8,128)S(1)} collective-permute-done((f32[2,16,1024]{2,1,0:T(8,128)S(1)}, f32[2,16,1024]{2,1,0:T(8,128)S(1)}, u32[]{:S(2)}, u32[]{:S(2)}) %collective-permute-start.17) | collective-permute-done | bytes 131104 | tf_op jit(solution)/shard_map/ppermute | solution.py:332
  40.9 1.0 %shard_map.79.refs_2_ = f32[2,4,2,16,1024]{4,3,2,1,0:T(8,128)} custom-call(s32[1]{0:T(128)} %bitcast.here_ref.refs_0_, f32[2,16,1024]{2,1,0:T(8,128)S(1)} %collective-permute-done.13.refs_1_, f32[2,16,1024]{2,1,0:T(8,128)S(1)} %collective-permute-done.15.refs_2_, f32[2,16,1024]{2,1,0:T(8,128)S(1)} %collective-permute-done.17.refs_3_, ...), custom_call_target="tpu_custom_call" | custom-call | tf_op jit(solution)/shard_map/pallas_call | solution.py:334
  42.0 0.0 collective-permute-done.12.refs_1_
  42.0 0.7 %shard_map.80 = f32[2,4,2,16,1024]{4,3,2,1,0:T(8,128)} custom-call(s32[1]{0:T(128)} %bitcast.here_ref.refs_0_, f32[2,16,1024]{2,1,0:T(8,128)S(1)} %collective-permute-done.12.refs_1_, f32[2,4,2,16,1024]{4,3,2,1,0:T(8,128)} %shard_map.79.refs_2_), custom_call_target="tpu_custom_call", output_to_operand_aliasing={{}: (2, {})} | custom-call | tf_op jit(solution)/shard_map/pallas_call | solution.py:341
  (11 shorter events, 0.1 us)
Async XLA Ops:
  0.6 10.9 %copy-start = (f32[32,1,16,1024]{3,2,1,0:T(8,128)S(1)}, f32[32,1,16,1024]{3,2,1,0:T(8,128)}, u32[]{:S(2)}) copy-start(f32[32,1,16,1024]{3,2,1,0:T(8,128)} %param.7) | copy-start | bytes 6291460
  0.6 1.4 %copy-start.2 = (f32[1,2,128,1024]{3,2,1,0:T(8,128)S(1)}, f32[1,2,128,1024]{3,2,1,0:T(8,128)}, u32[]{:S(2)}) copy-start(f32[1,2,128,1024]{3,2,1,0:T(8,128)} %param.4) | copy-start | bytes 3145732
  2.1 5.8 %collective-permute-start = (f32[2,4,16,1024]{3,2,1,0:T(8,128)S(1)}, f32[2,4,16,1024]{3,2,1,0:T(8,128)S(1)}, u32[]{:S(2)}, u32[]{:S(2)}) collective-permute-start(f32[2,4,16,1024]{3,2,1,0:T(8,128)S(1)} %get-tuple-element.26), channel_id=1, source_target_pairs={{0,4},{4,0},{8,12},{12,8},{16,20},{20,16},{24,28},{28,24},{1,5},{5... | collective-permute-start | bytes 1572872 | tf_op jit(solution)/shard_map/ppermute | solution.py:275
  2.6 8.6 %collective-permute-start.6 = (f32[8,128]{1,0:T(8,128)S(1)}, f32[8,128]{1,0:T(8,128)S(1)}, u32[]{:S(2)}, u32[]{:S(2)}) collective-permute-start(f32[8,128]{1,0:T(8,128)S(1)} %get-tuple-element.31.refs_0_), channel_id=1, source_target_pairs={{0,1},{1,0},{2,3},{3,2},{4,5},{5,4},{6,7},{7,6},{8,9},{9,8},{10,11... | collective-permute-start | bytes 12296 | tf_op jit(solution)/shard_map/ppermute | solution.py:277
  5.3 6.5 %collective-permute-start.5 = (f32[8,128]{1,0:T(8,128)S(1)}, f32[8,128]{1,0:T(8,128)S(1)}, u32[]{:S(2)}, u32[]{:S(2)}) collective-permute-start(f32[8,128]{1,0:T(8,128)S(1)} %get-tuple-element.31.refs_0_), channel_id=1, source_target_pairs={{0,2},{1,3},{2,0},{3,1},{4,6},{5,7},{6,4},{7,5},{8,10},{9,11},{10,... | collective-permute-start | bytes 12296 | tf_op jit(solution)/shard_map/ppermute | solution.py:277
  7.9 5.4 %collective-permute-start.4 = (f32[8,128]{1,0:T(8,128)S(1)}, f32[8,128]{1,0:T(8,128)S(1)}, u32[]{:S(2)}, u32[]{:S(2)}) collective-permute-start(f32[8,128]{1,0:T(8,128)S(1)} %get-tuple-element.31.refs_0_), channel_id=1, source_target_pairs={{0,3},{1,2},{2,1},{3,0},{4,7},{5,6},{6,5},{7,4},{8,11},{9,10},{10,... | collective-permute-start | bytes 12296 | tf_op jit(solution)/shard_map/ppermute | solution.py:277
  8.0 17.6 %collective-permute-start.1 = (f32[44,8,128]{2,1,0:T(8,128)S(1)}, f32[44,8,128]{2,1,0:T(8,128)S(1)}, u32[]{:S(2)}, u32[]{:S(2)}) collective-permute-start(f32[44,8,128]{2,1,0:T(8,128)S(1)} %get-tuple-element.27), channel_id=1, source_target_pairs={{0,24},{4,28},{8,16},{12,20},{16,8},{20,12},{24,0},{28,4},{1,25},{... | collective-permute-start | bytes 540680 | tf_op jit(solution)/shard_map/ppermute | solution.py:61
  10.7 14.9 %collective-permute-start.2 = (f32[44,8,128]{2,1,0:T(8,128)S(1)}, f32[44,8,128]{2,1,0:T(8,128)S(1)}, u32[]{:S(2)}, u32[]{:S(2)}) collective-permute-start(f32[44,8,128]{2,1,0:T(8,128)S(1)} %get-tuple-element.28), channel_id=1, source_target_pairs={{0,8},{4,20},{8,0},{12,28},{16,24},{20,4},{24,16},{28,12},{1,9},{5... | collective-permute-start | bytes 540680 | tf_op jit(solution)/shard_map/ppermute | solution.py:61
  11.2 14.3 %collective-permute-start.3 = (f32[44,8,128]{2,1,0:T(8,128)S(1)}, f32[44,8,128]{2,1,0:T(8,128)S(1)}, u32[]{:S(2)}, u32[]{:S(2)}) collective-permute-start(f32[44,8,128]{2,1,0:T(8,128)S(1)} %get-tuple-element.29), channel_id=1, source_target_pairs={{0,16},{4,12},{8,24},{12,4},{16,0},{20,28},{24,8},{28,20},{1,17},{... | collective-permute-start | bytes 540680 | tf_op jit(solution)/shard_map/ppermute | solution.py:61
  11.8 10.8 %copy-start.3 = (s32[8,2]{0,1:T(2,128)S(1)}, s32[8,2]{0,1:T(2,128)}, u32[]{:S(2)}) copy-start(s32[8,2]{0,1:T(2,128)} %param.5) | copy-start | bytes 196
  11.8 12.2 %copy-start.1 = (f32[32,1,16,1024]{3,2,1,0:T(8,128)S(1)}, f32[32,1,16,1024]{3,2,1,0:T(8,128)}, u32[]{:S(2)}) copy-start(f32[32,1,16,1024]{3,2,1,0:T(8,128)} %param.6) | copy-start | bytes 6291460
  13.3 1.2 %collective-permute-start.7 = (f32[8,128]{1,0:T(8,128)S(1)}, f32[8,128]{1,0:T(8,128)S(1)}, u32[]{:S(2)}, u32[]{:S(2)}) collective-permute-start(f32[8,128]{1,0:T(8,128)S(1)} %shard_map.71.refs_1_), channel_id=1, source_target_pairs={{0,4},{4,0},{8,12},{12,8},{16,20},{20,16},{24,28},{28,24},{1,5},{5... | collective-permute-start | bytes 12296 | tf_op jit(solution)/shard_map/ppermute | solution.py:300
  14.5 6.6 %collective-permute-start.8 = (f32[21,8,128]{2,1,0:T(8,128)S(1)}, f32[21,8,128]{2,1,0:T(8,128)S(1)}, u32[]{:S(2)}, u32[]{:S(2)}) collective-permute-start(f32[21,8,128]{2,1,0:T(8,128)S(1)} %get-tuple-element.32), channel_id=1, source_target_pairs={{0,24},{4,28},{8,16},{12,20},{16,8},{20,12},{24,0},{28,4},{1,25},{... | collective-permute-start | bytes 258056 | tf_op jit(solution)/shard_map/ppermute | solution.py:61
  17.0 7.4 %collective-permute-start.9 = (f32[21,8,128]{2,1,0:T(8,128)S(1)}, f32[21,8,128]{2,1,0:T(8,128)S(1)}, u32[]{:S(2)}, u32[]{:S(2)}) collective-permute-start(f32[21,8,128]{2,1,0:T(8,128)S(1)} %get-tuple-element.33), channel_id=1, source_target_pairs={{0,8},{4,20},{8,0},{12,28},{16,24},{20,4},{24,16},{28,12},{1,9},{5... | collective-permute-start | bytes 258056 | tf_op jit(solution)/shard_map/ppermute | solution.py:61
  21.1 4.5 %collective-permute-start.10 = (f32[21,8,128]{2,1,0:T(8,128)S(1)}, f32[21,8,128]{2,1,0:T(8,128)S(1)}, u32[]{:S(2)}, u32[]{:S(2)}) collective-permute-start(f32[21,8,128]{2,1,0:T(8,128)S(1)} %get-tuple-element.34), channel_id=1, source_target_pairs={{0,16},{4,12},{8,24},{12,4},{16,0},{20,28},{24,8},{28,20},{1,17},{... | collective-permute-start | bytes 258056 | tf_op jit(solution)/shard_map/ppermute | solution.py:61
  26.6 10.0 %collective-permute-start.14 = (f32[2,2,16,1024]{3,2,1,0:T(8,128)S(1)}, f32[2,2,16,1024]{3,2,1,0:T(8,128)S(1)}, u32[]{:S(2)}, u32[]{:S(2)}) collective-permute-start(f32[2,2,16,1024]{3,2,1,0:T(8,128)S(1)} %get-tuple-element.41), channel_id=1, source_target_pairs={{0,24},{4,28},{8,16},{12,20},{16,8},{20,12},{24,0},{28,4},{1,25},{... | collective-permute-start | bytes 786440 | tf_op jit(solution)/shard_map/ppermute | solution.py:61
  29.1 10.4 %collective-permute-start.16 = (f32[2,2,16,1024]{3,2,1,0:T(8,128)S(1)}, f32[2,2,16,1024]{3,2,1,0:T(8,128)S(1)}, u32[]{:S(2)}, u32[]{:S(2)}) collective-permute-start(f32[2,2,16,1024]{3,2,1,0:T(8,128)S(1)} %get-tuple-element.42), channel_id=1, source_target_pairs={{0,8},{4,20},{8,0},{12,28},{16,24},{20,4},{24,16},{28,12},{1,9},{5... | collective-permute-start | bytes 786440 | tf_op jit(solution)/shard_map/ppermute | solution.py:61
  29.7 9.9 %collective-permute-start.11 = (f32[2,2,16,1024]{3,2,1,0:T(8,128)S(1)}, f32[2,2,16,1024]{3,2,1,0:T(8,128)S(1)}, u32[]{:S(2)}, u32[]{:S(2)}) collective-permute-start(f32[2,2,16,1024]{3,2,1,0:T(8,128)S(1)} %get-tuple-element.36), channel_id=1, source_target_pairs={{0,16},{4,12},{8,24},{12,4},{16,0},{20,28},{24,8},{28,20},{1,17},{... | collective-permute-start | bytes 786440 | tf_op jit(solution)/shard_map/ppermute | solution.py:61
  33.2 7.0 %collective-permute-start.13 = (f32[2,16,1024]{2,1,0:T(8,128)S(1)}, f32[2,16,1024]{2,1,0:T(8,128)S(1)}, u32[]{:S(2)}, u32[]{:S(2)}) collective-permute-start(f32[2,16,1024]{2,1,0:T(8,128)S(1)} %shard_map.76), channel_id=1, source_target_pairs={{0,4},{4,0},{8,12},{12,8},{16,20},{20,16},{24,28},{28,24},{1,5},{5... | collective-permute-start | bytes 393224 | tf_op jit(solution)/shard_map/ppermute | solution.py:332
  36.6 3.6 %collective-permute-start.15 = (f32[2,16,1024]{2,1,0:T(8,128)S(1)}, f32[2,16,1024]{2,1,0:T(8,128)S(1)}, u32[]{:S(2)}, u32[]{:S(2)}) collective-permute-start(f32[2,16,1024]{2,1,0:T(8,128)S(1)} %shard_map.77), channel_id=1, source_target_pairs={{0,4},{4,0},{8,12},{12,8},{16,20},{20,16},{24,28},{28,24},{1,5},{5... | collective-permute-start | bytes 393224 | tf_op jit(solution)/shard_map/ppermute | solution.py:332
  39.5 1.4 %collective-permute-start.17 = (f32[2,16,1024]{2,1,0:T(8,128)S(1)}, f32[2,16,1024]{2,1,0:T(8,128)S(1)}, u32[]{:S(2)}, u32[]{:S(2)}) collective-permute-start(f32[2,16,1024]{2,1,0:T(8,128)S(1)} %shard_map.78), channel_id=1, source_target_pairs={{0,4},{4,0},{8,12},{12,8},{16,20},{20,16},{24,28},{28,24},{1,5},{5... | collective-permute-start | bytes 393224 | tf_op jit(solution)/shard_map/ppermute | solution.py:332
  39.6 2.4 %collective-permute-start.12 = (f32[2,16,1024]{2,1,0:T(8,128)S(1)}, f32[2,16,1024]{2,1,0:T(8,128)S(1)}, u32[]{:S(2)}, u32[]{:S(2)}) collective-permute-start(f32[2,16,1024]{2,1,0:T(8,128)S(1)} %shard_map.75), channel_id=1, source_target_pairs={{0,4},{4,0},{8,12},{12,8},{16,20},{20,16},{24,28},{28,24},{1,5},{5... | collective-permute-start | bytes 393224 | tf_op jit(solution)/shard_map/ppermute | solution.py:332

commit v12 on v11

--- a/solution.py
+++ b/solution.py
@@ -236,14 +236,18 @@
         copy.wait()
 
 
-def last_rows_kernel(size, last, here_ref, back_ref, held_ref, out_ref, sems):
-    del held_ref
-    here = here_ref[0]
-    chip = origin(here ^ 1, last, size) // 2
-    copies = [
-        pltpu.make_async_copy(back_ref.at[level], out_ref.at[level, chip, 1 - (here & 1)], sems.at[level])
-        for level in range(LEVELS)
-    ]
+def last_rows_kernel(size, last, here_ref, *refs):
+    here = here_ref[0]
+    out_ref, sems = refs[-2:]
+    copies = []
+    for i, k in enumerate(last):
+        chip = origin(here ^ 1, k, size) // 2
+        for level in range(LEVELS):
+            copies.append(
+                pltpu.make_async_copy(
+                    refs[i].at[level], out_ref.at[level, chip, 1 - (here & 1)], sems.at[level, i]
+                )
+            )
     for copy in copies:
         copy.start()
     for copy in copies:
@@ -330,7 +334,7 @@
             give_back_kernel, shape(LEVELS, own_rows, width), [smem, vmem, anywhere], vmem
         )(here, blocks[k], done)
         backs[k] = lax.ppermute(back, "path", swap)
-    first, last = (0, *order[:-2]), order[-2]
+    first, last = (0, *order[:-3]), order[-3:-1]
     path_params = call(
         lambda *refs: first_rows_kernel(size, first, *refs),
         shape(*split_slab.shape),
@@ -341,11 +345,11 @@
     path_params = call(
         lambda *refs: last_rows_kernel(size, last, *refs),
         shape(*split_slab.shape),
-        [smem, anywhere, anywhere],
+        [smem] + [anywhere] * (len(last) + 1),
         anywhere,
-        scratch_shapes=[pltpu.SemaphoreType.DMA((LEVELS,))],
-        input_output_aliases={2: 0},
-    )(here, backs[last], path_params)
+        scratch_shapes=[pltpu.SemaphoreType.DMA((LEVELS, len(last)))],
+        input_output_aliases={1 + len(last): 0},
+    )(here, *[backs[k] for k in last], path_params)
     return (path_params.reshape(path_delta.shape), new_state[:, None], new_moment[:, None])
 
 

time: 42.8 us -> 44 us (1.028)
  waiting for transfers between devices: 14.2 us -> 15.4 us
    ppermute x9, waiting for transfers between devices: 10.8 us -> 12 us  [move(): lax.ppermute(array, 'path', [(i, target(i, k, size)) for i in range(size)])]
  transfers between devices with their start and end apart: 18 -> 18, of which waited for: 7 -> 7; matrix products, arithmetic and copies ran while one was open for 1% -> 1% of each run, Pallas kernels for 14% -> 13%
where the time goes in v12:
time: 44 us; the launch traced here: 43.9 us
  starting transfers between devices  18.2 us (41%)
  waiting for transfers between devices  15.4 us (35%)
  Pallas kernels  7.73 us (18%)
  local copies, waits for them, and re-layouts  1.38 us (3%)
  between operations  0.84 us (2%)
    ppermute x9, waiting for transfers between devices, move(): lax.ppermute(array, 'path', [(i, target(i, k, size)) for i in range(size)])  12 us
    ppermute x9, starting transfers between devices, move(): lax.ppermute(array, 'path', [(i, target(i, k, size)) for i in range(size)])  11.7 us
    ppermute x3, starting transfers between devices, local(): lax.ppermute(squares, 'shard', [(i, i ^ step) for i in range(shards)])  5.25 us
    pallas_call x1, Pallas kernels, local(): call(state_kernel, [shape(*state_in.shape)] * 2 + [shape(8, 128)], [smem,...  3.06 us
    ppermute x3, waiting for transfers between devices, local(): lax.ppermute(squares, 'shard', [(i, i ^ step) for i in range(shards)])  1.47 us
    pallas_call x1, Pallas kernels, local(): call(plan_kernel, [jax.ShapeDtypeStruct((LEVELS, 5 * size), jnp.int32), j...  1.4 us
    unnamed x8, local copies, waits for them, and re-layouts  1.38 us
    ppermute x1, waiting for transfers between devices, local(): other = lax.ppermute(squares, 'path', swap)  1.16 us
  transfers between devices with their start and end apart: 18, of which 7 were waited for; matrix products, arithmetic and copies ran while one was open for 1% of the time, Pallas kernels for 13%

profile of v12, /device:TPU:0, one launch (start us, length us, event | category | flops | bytes accessed | tf_op | source)
XLA Modules:
  0.0 43.9 jit_solution(3127619572360598504)
XLA Ops:
  0.6 0.0 copy-start
  0.7 1.4 %copy-done.2 = f32[1,2,128,1024]{3,2,1,0:T(8,128)S(1)} copy-done((f32[1,2,128,1024]{3,2,1,0:T(8,128)S(1)}, f32[1,2,128,1024]{3,2,1,0:T(8,128)}, u32[]{:S(2)}) %copy-start.2) | copy-done | bytes 1048600
  2.0 0.1 shard_map.69
  2.1 0.5 %collective-permute-start = (f32[2,4,16,1024]{3,2,1,0:T(8,128)S(1)}, f32[2,4,16,1024]{3,2,1,0:T(8,128)S(1)}, u32[]{:S(2)}, u32[]{:S(2)}) collective-permute-start(f32[2,4,16,1024]{3,2,1,0:T(8,128)S(1)} %get-tuple-element.26), channel_id=1, source_target_pairs={{0,4},{4,0},{8,12},{12,8},{16,20},{20,16},{24,28},{28,24},{1,5},{5... | collective-permute-start | bytes 1572872 | tf_op jit(solution)/shard_map/ppermute | solution.py:279
  2.6 2.7 %collective-permute-start.6 = (f32[8,128]{1,0:T(8,128)S(1)}, f32[8,128]{1,0:T(8,128)S(1)}, u32[]{:S(2)}, u32[]{:S(2)}) collective-permute-start(f32[8,128]{1,0:T(8,128)S(1)} %get-tuple-element.31.refs_0_), channel_id=1, source_target_pairs={{0,1},{1,0},{2,3},{3,2},{4,5},{5,4},{6,7},{7,6},{8,9},{9,8},{10,11... | collective-permute-start | bytes 12296 | tf_op jit(solution)/shard_map/ppermute | solution.py:281
  5.3 2.6 %collective-permute-start.5 = (f32[8,128]{1,0:T(8,128)S(1)}, f32[8,128]{1,0:T(8,128)S(1)}, u32[]{:S(2)}, u32[]{:S(2)}) collective-permute-start(f32[8,128]{1,0:T(8,128)S(1)} %get-tuple-element.31.refs_0_), channel_id=1, source_target_pairs={{0,2},{1,3},{2,0},{3,1},{4,6},{5,7},{6,4},{7,5},{8,10},{9,11},{10,... | collective-permute-start | bytes 12296 | tf_op jit(solution)/shard_map/ppermute | solution.py:281
  7.9 0.0 collective-permute-start.4
  7.9 0.0 collective-permute-done.refs_2_.refs_4_
  8.0 2.7 %collective-permute-start.1 = (f32[44,8,128]{2,1,0:T(8,128)S(1)}, f32[44,8,128]{2,1,0:T(8,128)S(1)}, u32[]{:S(2)}, u32[]{:S(2)}) collective-permute-start(f32[44,8,128]{2,1,0:T(8,128)S(1)} %get-tuple-element.27), channel_id=1, source_target_pairs={{0,24},{4,28},{8,16},{12,20},{16,8},{20,12},{24,0},{28,4},{1,25},{... | collective-permute-start | bytes 540680 | tf_op jit(solution)/shard_map/ppermute | solution.py:61
  10.7 0.5 %collective-permute-start.2 = (f32[44,8,128]{2,1,0:T(8,128)S(1)}, f32[44,8,128]{2,1,0:T(8,128)S(1)}, u32[]{:S(2)}, u32[]{:S(2)}) collective-permute-start(f32[44,8,128]{2,1,0:T(8,128)S(1)} %get-tuple-element.28), channel_id=1, source_target_pairs={{0,8},{4,20},{8,0},{12,28},{16,24},{20,4},{24,16},{28,12},{1,9},{5... | collective-permute-start | bytes 540680 | tf_op jit(solution)/shard_map/ppermute | solution.py:61
  11.2 0.0 collective-permute-done.6.refs_3_
  11.2 0.3 collective-permute-start.3
  11.5 0.3 broadcast_multiply_fusion.decay_ref.refs_4_
  11.8 0.0 copy-start.3
  11.8 0.0 copy-start.1
  11.8 0.0 collective-permute-done.5.refs_2_
  11.8 1.5 %collective-permute-done.4.refs_1_ = f32[8,128]{1,0:T(8,128)S(1)} collective-permute-done((f32[8,128]{1,0:T(8,128)S(1)}, f32[8,128]{1,0:T(8,128)S(1)}, u32[]{:S(2)}, u32[]{:S(2)}) %collective-permute-start.4) | collective-permute-done | bytes 4128 | tf_op jit(solution)/shard_map/ppermute | solution.py:281
  13.3 0.0 collective-permute-start.7
  13.3 1.2 %collective-permute-done.7.refs_2_ = f32[8,128]{1,0:T(8,128)S(1)} collective-permute-done((f32[8,128]{1,0:T(8,128)S(1)}, f32[8,128]{1,0:T(8,128)S(1)}, u32[]{:S(2)}, u32[]{:S(2)}) %collective-permute-start.7) | collective-permute-done | bytes 4128 | tf_op jit(solution)/shard_map/ppermute | solution.py:304
  14.5 2.5 %collective-permute-start.8 = (f32[21,8,128]{2,1,0:T(8,128)S(1)}, f32[21,8,128]{2,1,0:T(8,128)S(1)}, u32[]{:S(2)}, u32[]{:S(2)}) collective-permute-start(f32[21,8,128]{2,1,0:T(8,128)S(1)} %get-tuple-element.32), channel_id=1, source_target_pairs={{0,24},{4,28},{8,16},{12,20},{16,8},{20,12},{24,0},{28,4},{1,25},{... | collective-permute-start | bytes 258056 | tf_op jit(solution)/shard_map/ppermute | solution.py:61
  17.0 0.5 %collective-permute-start.9 = (f32[21,8,128]{2,1,0:T(8,128)S(1)}, f32[21,8,128]{2,1,0:T(8,128)S(1)}, u32[]{:S(2)}, u32[]{:S(2)}) collective-permute-start(f32[21,8,128]{2,1,0:T(8,128)S(1)} %get-tuple-element.33), channel_id=1, source_target_pairs={{0,8},{4,20},{8,0},{12,28},{16,24},{20,4},{24,16},{28,12},{1,9},{5... | collective-permute-start | bytes 258056 | tf_op jit(solution)/shard_map/ppermute | solution.py:61
  17.6 3.5 %collective-permute-done.8.refs_6_ = f32[21,8,128]{2,1,0:T(8,128)S(1)} collective-permute-done((f32[21,8,128]{2,1,0:T(8,128)S(1)}, f32[21,8,128]{2,1,0:T(8,128)S(1)}, u32[]{:S(2)}, u32[]{:S(2)}) %collective-permute-start.8) | collective-permute-done | bytes 86048 | tf_op jit(solution)/shard_map/ppermute | solution.py:61
  21.1 1.6 %collective-permute-start.10 = (f32[21,8,128]{2,1,0:T(8,128)S(1)}, f32[21,8,128]{2,1,0:T(8,128)S(1)}, u32[]{:S(2)}, u32[]{:S(2)}) collective-permute-start(f32[21,8,128]{2,1,0:T(8,128)S(1)} %get-tuple-element.34), channel_id=1, source_target_pairs={{0,16},{4,12},{8,24},{12,4},{16,0},{20,28},{24,8},{28,20},{1,17},{... | collective-permute-start | bytes 258056 | tf_op jit(solution)/shard_map/ppermute | solution.py:61
  22.6 1.4 %shard_map.67 = (s32[2,40]{1,0:T(2,128)S(1)}, s32[32]{0:T(128)S(1)}) custom-call(s32[1]{0:T(128)} %bitcast.here_ref.refs_0_, s32[2,8]{1,0:T(2,128)S(1)} %bitcast.16), custom_call_target="tpu_custom_call" | custom-call | tf_op jit(solution)/shard_map/pallas_call | solution.py:292
  24.1 0.3 shard_map.68.refs_1_.decayed_ref
  24.4 0.0 collective-permute-done.9.refs_7_
  24.4 1.2 %collective-permute-done.10.refs_8_ = f32[21,8,128]{2,1,0:T(8,128)S(1)} collective-permute-done((f32[21,8,128]{2,1,0:T(8,128)S(1)}, f32[21,8,128]{2,1,0:T(8,128)S(1)}, u32[]{:S(2)}, u32[]{:S(2)}) %collective-permute-start.10) | collective-permute-done | bytes 86048 | tf_op jit(solution)/shard_map/ppermute | solution.py:61
  25.6 0.0 collective-permute-done.1.refs_2_
  25.6 0.0 collective-permute-done.2.refs_3_
  25.6 0.0 collective-permute-done.3.refs_4_
  25.6 1.0 %shard_map.73 = (f32[2,2,16,1024]{3,2,1,0:T(8,128)S(1)}, f32[2,2,16,1024]{3,2,1,0:T(8,128)S(1)}, f32[2,2,16,1024]{3,2,1,0:T(8,128)S(1)}, f32[2,2,16,1024]{3,2,1,0:T(8,128)S(1)}, f32[2,8,16,1024]{3,2,1,0:T(8,128)S(1)}) custom-call(s32[2,40]{1,0:T(2,128)S(1)} %get-tuple-element.24.refs_0_, f32[32,16,1024]{2,1,0:T(8,128)S(1)} %shard_map.68.refs_1_.decayed_ref, ...), custom_call_target="tpu_custom_call" | custom-call | tf_op jit(solution)/shard_map/pallas_call | solution.py:313
  26.6 1.6 %collective-permute-start.11 = (f32[2,2,16,1024]{3,2,1,0:T(8,128)S(1)}, f32[2,2,16,1024]{3,2,1,0:T(8,128)S(1)}, u32[]{:S(2)}, u32[]{:S(2)}) collective-permute-start(f32[2,2,16,1024]{3,2,1,0:T(8,128)S(1)} %get-tuple-element.36), channel_id=1, source_target_pairs={{0,8},{4,20},{8,0},{12,28},{16,24},{20,4},{24,16},{28,12},{1,9},{5... | collective-permute-start | bytes 786440 | tf_op jit(solution)/shard_map/ppermute | solution.py:61
  28.2 1.5 %collective-permute-start.16 = (f32[2,2,16,1024]{3,2,1,0:T(8,128)S(1)}, f32[2,2,16,1024]{3,2,1,0:T(8,128)S(1)}, u32[]{:S(2)}, u32[]{:S(2)}) collective-permute-start(f32[2,2,16,1024]{3,2,1,0:T(8,128)S(1)} %get-tuple-element.42), channel_id=1, source_target_pairs={{0,24},{4,28},{8,16},{12,20},{16,8},{20,12},{24,0},{28,4},{1,25},{... | collective-permute-start | bytes 786440 | tf_op jit(solution)/shard_map/ppermute | solution.py:61
  29.7 0.4 %collective-permute-start.13 = (f32[2,2,16,1024]{3,2,1,0:T(8,128)S(1)}, f32[2,2,16,1024]{3,2,1,0:T(8,128)S(1)}, u32[]{:S(2)}, u32[]{:S(2)}) collective-permute-start(f32[2,2,16,1024]{3,2,1,0:T(8,128)S(1)} %get-tuple-element.40), channel_id=1, source_target_pairs={{0,16},{4,12},{8,24},{12,4},{16,0},{20,28},{24,8},{28,20},{1,17},{... | collective-permute-start | bytes 786440 | tf_op jit(solution)/shard_map/ppermute | solution.py:61
  30.1 3.1 %shard_map.74 = (f32[32,16,1024]{2,1,0:T(8,128)}, f32[32,16,1024]{2,1,0:T(8,128)}, f32[8,128]{1,0:T(8,128)S(1)}) custom-call(s32[32]{0:T(128)S(1)} %get-tuple-element.37.module_ref, f32[2,8,16,1024]{3,2,1,0:T(8,128)S(1)} %get-tuple-element.38.grad_ref, f32[32,16,1024]{2,1,0:T(8,128)S(1)} %shard_map.68.refs_1_.decayed_ref, f32[32,16,1024]{2,1,0:T(8,128)S(1)} %bitcast.13), custom_call_target="tpu_custom_call" | custom-call | tf_op jit(solution)/shard_map/pallas_call | solution.py:323
  33.2 0.1 collective-permute-start.15
  33.3 2.6 %collective-permute-done.11.block_ref.refs_4_ = f32[2,2,16,1024]{3,2,1,0:T(8,128)S(1)} collective-permute-done((f32[2,2,16,1024]{3,2,1,0:T(8,128)S(1)}, f32[2,2,16,1024]{3,2,1,0:T(8,128)S(1)}, u32[]{:S(2)}, u32[]{:S(2)}) %collective-permute-start.11) | collective-permute-done | bytes 262176 | tf_op jit(solution)/shard_map/ppermute | solution.py:61
  35.9 0.1 collective-permute-start.12
  36.0 4.7 %collective-permute-done.16.block_ref.refs_3_ = f32[2,2,16,1024]{3,2,1,0:T(8,128)S(1)} collective-permute-done((f32[2,2,16,1024]{3,2,1,0:T(8,128)S(1)}, f32[2,2,16,1024]{3,2,1,0:T(8,128)S(1)}, u32[]{:S(2)}, u32[]{:S(2)}) %collective-permute-start.16) | collective-permute-done | bytes 262176 | tf_op jit(solution)/shard_map/ppermute | solution.py:61
  40.7 0.1 collective-permute-start.17
  40.8 0.0 collective-permute-done.13.block_ref.refs_5_
  40.8 0.5 %collective-permute-start.14 = (f32[2,16,1024]{2,1,0:T(8,128)S(1)}, f32[2,16,1024]{2,1,0:T(8,128)S(1)}, u32[]{:S(2)}, u32[]{:S(2)}) collective-permute-start(f32[2,16,1024]{2,1,0:T(8,128)S(1)} %shard_map.76), channel_id=1, source_target_pairs={{0,4},{4,0},{8,12},{12,8},{16,20},{20,16},{24,28},{28,24},{1,5},{5... | collective-permute-start | bytes 393224 | tf_op jit(solution)/shard_map/ppermute | solution.py:336
  41.3 0.0 collective-permute-done.15.refs_1_
  41.3 0.8 %collective-permute-done.17.refs_2_ = f32[2,16,1024]{2,1,0:T(8,128)S(1)} collective-permute-done((f32[2,16,1024]{2,1,0:T(8,128)S(1)}, f32[2,16,1024]{2,1,0:T(8,128)S(1)}, u32[]{:S(2)}, u32[]{:S(2)}) %collective-permute-start.17) | collective-permute-done | bytes 131104 | tf_op jit(solution)/shard_map/ppermute | solution.py:336
  42.1 1.0 %shard_map.79.refs_3_ = f32[2,4,2,16,1024]{4,3,2,1,0:T(8,128)} custom-call(s32[1]{0:T(128)} %bitcast.here_ref.refs_0_, f32[2,16,1024]{2,1,0:T(8,128)S(1)} %collective-permute-done.15.refs_1_, f32[2,16,1024]{2,1,0:T(8,128)S(1)} %collective-permute-done.17.refs_2_, f32[2,2,16,1024]{3,2,1,0:T(8,128)S(1)} %collective-permute-done.16.block_ref.refs_3_, ...), custom_call_target="tpu_custom_call" | custom-call | tf_op jit(solution)/shard_map/pallas_call | solution.py:338
  43.1 0.0 collective-permute-done.12.refs_1_
  43.1 0.0 collective-permute-done.14.refs_2_
  43.1 0.7 %shard_map.80 = f32[2,4,2,16,1024]{4,3,2,1,0:T(8,128)} custom-call(s32[1]{0:T(128)} %bitcast.here_ref.refs_0_, f32[2,16,1024]{2,1,0:T(8,128)S(1)} %collective-permute-done.12.refs_1_, f32[2,16,1024]{2,1,0:T(8,128)S(1)} %collective-permute-done.14.refs_2_, f32[2,4,2,16,1024]{4,3,2,1,0:T(8,128)} %shard_map.79.refs_3_), custom_call_target="tpu_custom_call", output_to_operand_aliasing={{}: (3, {})} | custom-call | tf_op jit(solution)/shard_map/pallas_call | solution.py:345
  (11 shorter events, 0.1 us)
Async XLA Ops:
  0.6 10.9 %copy-start = (f32[32,1,16,1024]{3,2,1,0:T(8,128)S(1)}, f32[32,1,16,1024]{3,2,1,0:T(8,128)}, u32[]{:S(2)}) copy-start(f32[32,1,16,1024]{3,2,1,0:T(8,128)} %param.7) | copy-start | bytes 6291460
  0.6 1.4 %copy-start.2 = (f32[1,2,128,1024]{3,2,1,0:T(8,128)S(1)}, f32[1,2,128,1024]{3,2,1,0:T(8,128)}, u32[]{:S(2)}) copy-start(f32[1,2,128,1024]{3,2,1,0:T(8,128)} %param.4) | copy-start | bytes 3145732
  2.1 5.8 %collective-permute-start = (f32[2,4,16,1024]{3,2,1,0:T(8,128)S(1)}, f32[2,4,16,1024]{3,2,1,0:T(8,128)S(1)}, u32[]{:S(2)}, u32[]{:S(2)}) collective-permute-start(f32[2,4,16,1024]{3,2,1,0:T(8,128)S(1)} %get-tuple-element.26), channel_id=1, source_target_pairs={{0,4},{4,0},{8,12},{12,8},{16,20},{20,16},{24,28},{28,24},{1,5},{5... | collective-permute-start | bytes 1572872 | tf_op jit(solution)/shard_map/ppermute | solution.py:279
  2.6 8.6 %collective-permute-start.6 = (f32[8,128]{1,0:T(8,128)S(1)}, f32[8,128]{1,0:T(8,128)S(1)}, u32[]{:S(2)}, u32[]{:S(2)}) collective-permute-start(f32[8,128]{1,0:T(8,128)S(1)} %get-tuple-element.31.refs_0_), channel_id=1, source_target_pairs={{0,1},{1,0},{2,3},{3,2},{4,5},{5,4},{6,7},{7,6},{8,9},{9,8},{10,11... | collective-permute-start | bytes 12296 | tf_op jit(solution)/shard_map/ppermute | solution.py:281
  5.3 6.5 %collective-permute-start.5 = (f32[8,128]{1,0:T(8,128)S(1)}, f32[8,128]{1,0:T(8,128)S(1)}, u32[]{:S(2)}, u32[]{:S(2)}) collective-permute-start(f32[8,128]{1,0:T(8,128)S(1)} %get-tuple-element.31.refs_0_), channel_id=1, source_target_pairs={{0,2},{1,3},{2,0},{3,1},{4,6},{5,7},{6,4},{7,5},{8,10},{9,11},{10,... | collective-permute-start | bytes 12296 | tf_op jit(solution)/shard_map/ppermute | solution.py:281
  7.9 5.4 %collective-permute-start.4 = (f32[8,128]{1,0:T(8,128)S(1)}, f32[8,128]{1,0:T(8,128)S(1)}, u32[]{:S(2)}, u32[]{:S(2)}) collective-permute-start(f32[8,128]{1,0:T(8,128)S(1)} %get-tuple-element.31.refs_0_), channel_id=1, source_target_pairs={{0,3},{1,2},{2,1},{3,0},{4,7},{5,6},{6,5},{7,4},{8,11},{9,10},{10,... | collective-permute-start | bytes 12296 | tf_op jit(solution)/shard_map/ppermute | solution.py:281
  8.0 17.6 %collective-permute-start.1 = (f32[44,8,128]{2,1,0:T(8,128)S(1)}, f32[44,8,128]{2,1,0:T(8,128)S(1)}, u32[]{:S(2)}, u32[]{:S(2)}) collective-permute-start(f32[44,8,128]{2,1,0:T(8,128)S(1)} %get-tuple-element.27), channel_id=1, source_target_pairs={{0,24},{4,28},{8,16},{12,20},{16,8},{20,12},{24,0},{28,4},{1,25},{... | collective-permute-start | bytes 540680 | tf_op jit(solution)/shard_map/ppermute | solution.py:61
  10.7 14.9 %collective-permute-start.2 = (f32[44,8,128]{2,1,0:T(8,128)S(1)}, f32[44,8,128]{2,1,0:T(8,128)S(1)}, u32[]{:S(2)}, u32[]{:S(2)}) collective-permute-start(f32[44,8,128]{2,1,0:T(8,128)S(1)} %get-tuple-element.28), channel_id=1, source_target_pairs={{0,8},{4,20},{8,0},{12,28},{16,24},{20,4},{24,16},{28,12},{1,9},{5... | collective-permute-start | bytes 540680 | tf_op jit(solution)/shard_map/ppermute | solution.py:61
  11.2 14.3 %collective-permute-start.3 = (f32[44,8,128]{2,1,0:T(8,128)S(1)}, f32[44,8,128]{2,1,0:T(8,128)S(1)}, u32[]{:S(2)}, u32[]{:S(2)}) collective-permute-start(f32[44,8,128]{2,1,0:T(8,128)S(1)} %get-tuple-element.29), channel_id=1, source_target_pairs={{0,16},{4,12},{8,24},{12,4},{16,0},{20,28},{24,8},{28,20},{1,17},{... | collective-permute-start | bytes 540680 | tf_op jit(solution)/shard_map/ppermute | solution.py:61
  11.8 10.8 %copy-start.3 = (s32[8,2]{0,1:T(2,128)S(1)}, s32[8,2]{0,1:T(2,128)}, u32[]{:S(2)}) copy-start(s32[8,2]{0,1:T(2,128)} %param.5) | copy-start | bytes 196
  11.8 12.2 %copy-start.1 = (f32[32,1,16,1024]{3,2,1,0:T(8,128)S(1)}, f32[32,1,16,1024]{3,2,1,0:T(8,128)}, u32[]{:S(2)}) copy-start(f32[32,1,16,1024]{3,2,1,0:T(8,128)} %param.6) | copy-start | bytes 6291460
  13.3 1.2 %collective-permute-start.7 = (f32[8,128]{1,0:T(8,128)S(1)}, f32[8,128]{1,0:T(8,128)S(1)}, u32[]{:S(2)}, u32[]{:S(2)}) collective-permute-start(f32[8,128]{1,0:T(8,128)S(1)} %shard_map.71.refs_1_), channel_id=1, source_target_pairs={{0,4},{4,0},{8,12},{12,8},{16,20},{20,16},{24,28},{28,24},{1,5},{5... | collective-permute-start | bytes 12296 | tf_op jit(solution)/shard_map/ppermute | solution.py:304
  14.5 6.6 %collective-permute-start.8 = (f32[21,8,128]{2,1,0:T(8,128)S(1)}, f32[21,8,128]{2,1,0:T(8,128)S(1)}, u32[]{:S(2)}, u32[]{:S(2)}) collective-permute-start(f32[21,8,128]{2,1,0:T(8,128)S(1)} %get-tuple-element.32), channel_id=1, source_target_pairs={{0,24},{4,28},{8,16},{12,20},{16,8},{20,12},{24,0},{28,4},{1,25},{... | collective-permute-start | bytes 258056 | tf_op jit(solution)/shard_map/ppermute | solution.py:61
  17.0 7.4 %collective-permute-start.9 = (f32[21,8,128]{2,1,0:T(8,128)S(1)}, f32[21,8,128]{2,1,0:T(8,128)S(1)}, u32[]{:S(2)}, u32[]{:S(2)}) collective-permute-start(f32[21,8,128]{2,1,0:T(8,128)S(1)} %get-tuple-element.33), channel_id=1, source_target_pairs={{0,8},{4,20},{8,0},{12,28},{16,24},{20,4},{24,16},{28,12},{1,9},{5... | collective-permute-start | bytes 258056 | tf_op jit(solution)/shard_map/ppermute | solution.py:61
  21.1 4.5 %collective-permute-start.10 = (f32[21,8,128]{2,1,0:T(8,128)S(1)}, f32[21,8,128]{2,1,0:T(8,128)S(1)}, u32[]{:S(2)}, u32[]{:S(2)}) collective-permute-start(f32[21,8,128]{2,1,0:T(8,128)S(1)} %get-tuple-element.34), channel_id=1, source_target_pairs={{0,16},{4,12},{8,24},{12,4},{16,0},{20,28},{24,8},{28,20},{1,17},{... | collective-permute-start | bytes 258056 | tf_op jit(solution)/shard_map/ppermute | solution.py:61
  26.6 9.3 %collective-permute-start.11 = (f32[2,2,16,1024]{3,2,1,0:T(8,128)S(1)}, f32[2,2,16,1024]{3,2,1,0:T(8,128)S(1)}, u32[]{:S(2)}, u32[]{:S(2)}) collective-permute-start(f32[2,2,16,1024]{3,2,1,0:T(8,128)S(1)} %get-tuple-element.36), channel_id=1, source_target_pairs={{0,8},{4,20},{8,0},{12,28},{16,24},{20,4},{24,16},{28,12},{1,9},{5... | collective-permute-start | bytes 786440 | tf_op jit(solution)/shard_map/ppermute | solution.py:61
  28.2 12.5 %collective-permute-start.16 = (f32[2,2,16,1024]{3,2,1,0:T(8,128)S(1)}, f32[2,2,16,1024]{3,2,1,0:T(8,128)S(1)}, u32[]{:S(2)}, u32[]{:S(2)}) collective-permute-start(f32[2,2,16,1024]{3,2,1,0:T(8,128)S(1)} %get-tuple-element.42), channel_id=1, source_target_pairs={{0,24},{4,28},{8,16},{12,20},{16,8},{20,12},{24,0},{28,4},{1,25},{... | collective-permute-start | bytes 786440 | tf_op jit(solution)/shard_map/ppermute | solution.py:61
  29.7 11.1 %collective-permute-start.13 = (f32[2,2,16,1024]{3,2,1,0:T(8,128)S(1)}, f32[2,2,16,1024]{3,2,1,0:T(8,128)S(1)}, u32[]{:S(2)}, u32[]{:S(2)}) collective-permute-start(f32[2,2,16,1024]{3,2,1,0:T(8,128)S(1)} %get-tuple-element.40), channel_id=1, source_target_pairs={{0,16},{4,12},{8,24},{12,4},{16,0},{20,28},{24,8},{28,20},{1,17},{... | collective-permute-start | bytes 786440 | tf_op jit(solution)/shard_map/ppermute | solution.py:61
  33.2 8.2 %collective-permute-start.15 = (f32[2,16,1024]{2,1,0:T(8,128)S(1)}, f32[2,16,1024]{2,1,0:T(8,128)S(1)}, u32[]{:S(2)}, u32[]{:S(2)}) collective-permute-start(f32[2,16,1024]{2,1,0:T(8,128)S(1)} %shard_map.77), channel_id=1, source_target_pairs={{0,4},{4,0},{8,12},{12,8},{16,20},{20,16},{24,28},{28,24},{1,5},{5... | collective-permute-start | bytes 393224 | tf_op jit(solution)/shard_map/ppermute | solution.py:336
  35.9 7.2 %collective-permute-start.12 = (f32[2,16,1024]{2,1,0:T(8,128)S(1)}, f32[2,16,1024]{2,1,0:T(8,128)S(1)}, u32[]{:S(2)}, u32[]{:S(2)}) collective-permute-start(f32[2,16,1024]{2,1,0:T(8,128)S(1)} %shard_map.75), channel_id=1, source_target_pairs={{0,4},{4,0},{8,12},{12,8},{16,20},{20,16},{24,28},{28,24},{1,5},{5... | collective-permute-start | bytes 393224 | tf_op jit(solution)/shard_map/ppermute | solution.py:336
  40.7 1.4 %collective-permute-start.17 = (f32[2,16,1024]{2,1,0:T(8,128)S(1)}, f32[2,16,1024]{2,1,0:T(8,128)S(1)}, u32[]{:S(2)}, u32[]{:S(2)}) collective-permute-start(f32[2,16,1024]{2,1,0:T(8,128)S(1)} %shard_map.78), channel_id=1, source_target_pairs={{0,4},{4,0},{8,12},{12,8},{16,20},{20,16},{24,28},{28,24},{1,5},{5... | collective-permute-start | bytes 393224 | tf_op jit(solution)/shard_map/ppermute | solution.py:336
  40.8 2.3 %collective-permute-start.14 = (f32[2,16,1024]{2,1,0:T(8,128)S(1)}, f32[2,16,1024]{2,1,0:T(8,128)S(1)}, u32[]{:S(2)}, u32[]{:S(2)}) collective-permute-start(f32[2,16,1024]{2,1,0:T(8,128)S(1)} %shard_map.76), channel_id=1, source_target_pairs={{0,4},{4,0},{8,12},{12,8},{16,20},{20,16},{24,28},{28,24},{1,5},{5... | collective-permute-start | bytes 393224 | tf_op jit(solution)/shard_map/ppermute | solution.py:336

commit v13 on v8

--- a/solution.py
+++ b/solution.py
@@ -270,7 +270,7 @@
     )
     gift = lax.ppermute(give, "path", swap)
     tiles = [squares] + [
-        lax.ppermute(squares, "shard", [(i, i ^ step) for i in range(shards)]) for step in range(shards - 1, 0, -1)
+        lax.ppermute(squares, "shard", [(i, i ^ step) for i in range(shards)]) for step in range(1, shards)
     ]
     firsts = call(
         lambda *refs: first_merge_kernel(size, *refs),

time: 41.8 us -> 42.6 us (1.019)
  waiting for transfers between devices: 13.6 us -> 14.7 us
    ppermute x3, waiting for transfers between devices: 0.01 us -> 1.47 us  [local(): lax.ppermute(squares, 'shard', [(i, i ^ step) for i in range(shards)])]
  transfers between devices with their start and end apart: 15 -> 15, of which waited for: 6 -> 7; matrix products, arithmetic and copies ran while one was open for 1% -> 1% of each run, Pallas kernels for 14% -> 14%
where the time goes in v13:
time: 42.6 us; the launch traced here: 42.4 us
  starting transfers between devices  17.6 us (41%)
  waiting for transfers between devices  14.7 us (35%)
  Pallas kernels  7.78 us (18%)
  local copies, waits for them, and re-layouts  1.38 us (3%)
  between operations  0.77 us (2%)
    ppermute x9, starting transfers between devices, move(): lax.ppermute(array, 'path', [(i, target(i, k, size)) for i in range(size)])  11.7 us
    ppermute x9, waiting for transfers between devices, move(): lax.ppermute(array, 'path', [(i, target(i, k, size)) for i in range(size)])  11 us
    ppermute x3, starting transfers between devices, local(): lax.ppermute(squares, 'shard', [(i, i ^ step) for i in range(shards)])  5.25 us
    pallas_call x1, Pallas kernels, local(): call(state_kernel, [shape(*state_in.shape)] * 2 + [shape(8, 128)], [smem,...  3.08 us
    ppermute x3, waiting for transfers between devices, local(): lax.ppermute(squares, 'shard', [(i, i ^ step) for i in range(shards)])  1.47 us
    pallas_call x1, Pallas kernels, local(): call(plan_kernel, [jax.ShapeDtypeStruct((LEVELS, 5 * size), jnp.int32), j...  1.4 us
    unnamed x8, local copies, waits for them, and re-layouts  1.38 us
    ppermute x1, waiting for transfers between devices, local(): other = lax.ppermute(squares, 'path', swap)  1.16 us
  transfers between devices with their start and end apart: 15, of which 7 were waited for; matrix products, arithmetic and copies ran while one was open for 1% of the time, Pallas kernels for 14%

profile of v13, /device:TPU:0, one launch (start us, length us, event | category | flops | bytes accessed | tf_op | source)
XLA Modules:
  0.0 42.4 jit_solution(8957482034175519562)
XLA Ops:
  0.6 0.0 copy-start
  0.6 0.0 copy-start.2
  0.7 1.4 %copy-done.2 = f32[1,2,128,1024]{3,2,1,0:T(8,128)S(1)} copy-done((f32[1,2,128,1024]{3,2,1,0:T(8,128)S(1)}, f32[1,2,128,1024]{3,2,1,0:T(8,128)}, u32[]{:S(2)}) %copy-start.2) | copy-done | bytes 1048600
  2.0 0.1 shard_map.69
  2.1 0.5 %collective-permute-start = (f32[2,4,16,1024]{3,2,1,0:T(8,128)S(1)}, f32[2,4,16,1024]{3,2,1,0:T(8,128)S(1)}, u32[]{:S(2)}, u32[]{:S(2)}) collective-permute-start(f32[2,4,16,1024]{3,2,1,0:T(8,128)S(1)} %get-tuple-element.26), channel_id=1, source_target_pairs={{0,4},{4,0},{8,12},{12,8},{16,20},{20,16},{24,28},{28,24},{1,5},{5... | collective-permute-start | bytes 1572872 | tf_op jit(solution)/shard_map/ppermute | solution.py:271
  2.6 2.7 %collective-permute-start.4 = (f32[8,128]{1,0:T(8,128)S(1)}, f32[8,128]{1,0:T(8,128)S(1)}, u32[]{:S(2)}, u32[]{:S(2)}) collective-permute-start(f32[8,128]{1,0:T(8,128)S(1)} %get-tuple-element.31.refs_0_), channel_id=1, source_target_pairs={{0,1},{1,0},{2,3},{3,2},{4,5},{5,4},{6,7},{7,6},{8,9},{9,8},{10,11... | collective-permute-start | bytes 12296 | tf_op jit(solution)/shard_map/ppermute | solution.py:273
  5.3 2.6 %collective-permute-start.5 = (f32[8,128]{1,0:T(8,128)S(1)}, f32[8,128]{1,0:T(8,128)S(1)}, u32[]{:S(2)}, u32[]{:S(2)}) collective-permute-start(f32[8,128]{1,0:T(8,128)S(1)} %get-tuple-element.31.refs_0_), channel_id=1, source_target_pairs={{0,2},{1,3},{2,0},{3,1},{4,6},{5,7},{6,4},{7,5},{8,10},{9,11},{10,... | collective-permute-start | bytes 12296 | tf_op jit(solution)/shard_map/ppermute | solution.py:273
  7.9 0.0 collective-permute-start.6
  7.9 0.0 collective-permute-done.refs_2_.refs_4_
  8.0 2.7 %collective-permute-start.1 = (f32[44,8,128]{2,1,0:T(8,128)S(1)}, f32[44,8,128]{2,1,0:T(8,128)S(1)}, u32[]{:S(2)}, u32[]{:S(2)}) collective-permute-start(f32[44,8,128]{2,1,0:T(8,128)S(1)} %get-tuple-element.27), channel_id=1, source_target_pairs={{0,24},{4,28},{8,16},{12,20},{16,8},{20,12},{24,0},{28,4},{1,25},{... | collective-permute-start | bytes 540680 | tf_op jit(solution)/shard_map/ppermute | solution.py:61
  10.7 0.5 %collective-permute-start.2 = (f32[44,8,128]{2,1,0:T(8,128)S(1)}, f32[44,8,128]{2,1,0:T(8,128)S(1)}, u32[]{:S(2)}, u32[]{:S(2)}) collective-permute-start(f32[44,8,128]{2,1,0:T(8,128)S(1)} %get-tuple-element.28), channel_id=1, source_target_pairs={{0,8},{4,20},{8,0},{12,28},{16,24},{20,4},{24,16},{28,12},{1,9},{5... | collective-permute-start | bytes 540680 | tf_op jit(solution)/shard_map/ppermute | solution.py:61
  11.2 0.0 collective-permute-done.4.refs_1_
  11.2 0.3 collective-permute-start.3
  11.5 0.0 copy-done
  11.5 0.3 broadcast_multiply_fusion.decay_ref.refs_4_
  11.8 0.0 copy-start.3
  11.8 0.0 copy-start.1
  11.8 0.0 collective-permute-done.5.refs_2_
  11.8 1.5 %collective-permute-done.6.refs_3_ = f32[8,128]{1,0:T(8,128)S(1)} collective-permute-done((f32[8,128]{1,0:T(8,128)S(1)}, f32[8,128]{1,0:T(8,128)S(1)}, u32[]{:S(2)}, u32[]{:S(2)}) %collective-permute-start.6) | collective-permute-done | bytes 4128 | tf_op jit(solution)/shard_map/ppermute | solution.py:273
  13.3 0.0 collective-permute-start.7
  13.3 1.2 %collective-permute-done.7.refs_2_ = f32[8,128]{1,0:T(8,128)S(1)} collective-permute-done((f32[8,128]{1,0:T(8,128)S(1)}, f32[8,128]{1,0:T(8,128)S(1)}, u32[]{:S(2)}, u32[]{:S(2)}) %collective-permute-start.7) | collective-permute-done | bytes 4128 | tf_op jit(solution)/shard_map/ppermute | solution.py:296
  14.5 2.5 %collective-permute-start.8 = (f32[21,8,128]{2,1,0:T(8,128)S(1)}, f32[21,8,128]{2,1,0:T(8,128)S(1)}, u32[]{:S(2)}, u32[]{:S(2)}) collective-permute-start(f32[21,8,128]{2,1,0:T(8,128)S(1)} %get-tuple-element.32), channel_id=1, source_target_pairs={{0,24},{4,28},{8,16},{12,20},{16,8},{20,12},{24,0},{28,4},{1,25},{... | collective-permute-start | bytes 258056 | tf_op jit(solution)/shard_map/ppermute | solution.py:61
  17.0 0.5 %collective-permute-start.9 = (f32[21,8,128]{2,1,0:T(8,128)S(1)}, f32[21,8,128]{2,1,0:T(8,128)S(1)}, u32[]{:S(2)}, u32[]{:S(2)}) collective-permute-start(f32[21,8,128]{2,1,0:T(8,128)S(1)} %get-tuple-element.33), channel_id=1, source_target_pairs={{0,8},{4,20},{8,0},{12,28},{16,24},{20,4},{24,16},{28,12},{1,9},{5... | collective-permute-start | bytes 258056 | tf_op jit(solution)/shard_map/ppermute | solution.py:61
  17.6 3.5 %collective-permute-done.8.refs_6_ = f32[21,8,128]{2,1,0:T(8,128)S(1)} collective-permute-done((f32[21,8,128]{2,1,0:T(8,128)S(1)}, f32[21,8,128]{2,1,0:T(8,128)S(1)}, u32[]{:S(2)}, u32[]{:S(2)}) %collective-permute-start.8) | collective-permute-done | bytes 86048 | tf_op jit(solution)/shard_map/ppermute | solution.py:61
  21.1 1.6 %collective-permute-start.10 = (f32[21,8,128]{2,1,0:T(8,128)S(1)}, f32[21,8,128]{2,1,0:T(8,128)S(1)}, u32[]{:S(2)}, u32[]{:S(2)}) collective-permute-start(f32[21,8,128]{2,1,0:T(8,128)S(1)} %get-tuple-element.34), channel_id=1, source_target_pairs={{0,16},{4,12},{8,24},{12,4},{16,0},{20,28},{24,8},{28,20},{1,17},{... | collective-permute-start | bytes 258056 | tf_op jit(solution)/shard_map/ppermute | solution.py:61
  22.6 0.0 copy-done.3
  22.6 1.4 %shard_map.67 = (s32[2,40]{1,0:T(2,128)S(1)}, s32[32]{0:T(128)S(1)}) custom-call(s32[1]{0:T(128)} %bitcast.here_ref.refs_0_, s32[2,8]{1,0:T(2,128)S(1)} %bitcast.16), custom_call_target="tpu_custom_call" | custom-call | tf_op jit(solution)/shard_map/pallas_call | solution.py:284
  24.0 0.0 copy-done.1
  24.1 0.3 shard_map.68.refs_1_.decayed_ref
  24.4 0.0 collective-permute-done.9.refs_7_
  24.4 1.2 %collective-permute-done.10.refs_8_ = f32[21,8,128]{2,1,0:T(8,128)S(1)} collective-permute-done((f32[21,8,128]{2,1,0:T(8,128)S(1)}, f32[21,8,128]{2,1,0:T(8,128)S(1)}, u32[]{:S(2)}, u32[]{:S(2)}) %collective-permute-start.10) | collective-permute-done | bytes 86048 | tf_op jit(solution)/shard_map/ppermute | solution.py:61
  25.6 0.0 collective-permute-done.1.refs_2_
  25.6 0.0 collective-permute-done.2.refs_3_
  25.6 0.0 collective-permute-done.3.refs_4_
  25.6 1.0 %shard_map.73 = (f32[2,2,16,1024]{3,2,1,0:T(8,128)S(1)}, f32[2,2,16,1024]{3,2,1,0:T(8,128)S(1)}, f32[2,2,16,1024]{3,2,1,0:T(8,128)S(1)}, f32[2,2,16,1024]{3,2,1,0:T(8,128)S(1)}, f32[2,8,16,1024]{3,2,1,0:T(8,128)S(1)}) custom-call(s32[2,40]{1,0:T(2,128)S(1)} %get-tuple-element.24.refs_0_, f32[32,16,1024]{2,1,0:T(8,128)S(1)} %shard_map.68.refs_1_.decayed_ref, ...), custom_call_target="tpu_custom_call" | custom-call | tf_op jit(solution)/shard_map/pallas_call | solution.py:305
  26.6 2.6 %collective-permute-start.11 = (f32[2,2,16,1024]{3,2,1,0:T(8,128)S(1)}, f32[2,2,16,1024]{3,2,1,0:T(8,128)S(1)}, u32[]{:S(2)}, u32[]{:S(2)}) collective-permute-start(f32[2,2,16,1024]{3,2,1,0:T(8,128)S(1)} %get-tuple-element.36), channel_id=1, source_target_pairs={{0,24},{4,28},{8,16},{12,20},{16,8},{20,12},{24,0},{28,4},{1,25},{... | collective-permute-start | bytes 786440 | tf_op jit(solution)/shard_map/ppermute | solution.py:61
  29.2 0.5 %collective-permute-start.12 = (f32[2,2,16,1024]{3,2,1,0:T(8,128)S(1)}, f32[2,2,16,1024]{3,2,1,0:T(8,128)S(1)}, u32[]{:S(2)}, u32[]{:S(2)}) collective-permute-start(f32[2,2,16,1024]{3,2,1,0:T(8,128)S(1)} %get-tuple-element.37), channel_id=1, source_target_pairs={{0,8},{4,20},{8,0},{12,28},{16,24},{20,4},{24,16},{28,12},{1,9},{5... | collective-permute-start | bytes 786440 | tf_op jit(solution)/shard_map/ppermute | solution.py:61
  29.7 0.5 %collective-permute-start.13 = (f32[2,2,16,1024]{3,2,1,0:T(8,128)S(1)}, f32[2,2,16,1024]{3,2,1,0:T(8,128)S(1)}, u32[]{:S(2)}, u32[]{:S(2)}) collective-permute-start(f32[2,2,16,1024]{3,2,1,0:T(8,128)S(1)} %get-tuple-element.38), channel_id=1, source_target_pairs={{0,16},{4,12},{8,24},{12,4},{16,0},{20,28},{24,8},{28,20},{1,17},{... | collective-permute-start | bytes 786440 | tf_op jit(solution)/shard_map/ppermute | solution.py:61
  30.2 3.1 %shard_map.74 = (f32[32,16,1024]{2,1,0:T(8,128)}, f32[32,16,1024]{2,1,0:T(8,128)}, f32[8,128]{1,0:T(8,128)S(1)}) custom-call(s32[32]{0:T(128)S(1)} %get-tuple-element.40.module_ref, f32[2,8,16,1024]{3,2,1,0:T(8,128)S(1)} %get-tuple-element.41.grad_ref, f32[32,16,1024]{2,1,0:T(8,128)S(1)} %shard_map.68.refs_1_.decayed_ref, f32[32,16,1024]{2,1,0:T(8,128)S(1)} %bitcast.13), custom_call_target="tpu_custom_call" | custom-call | tf_op jit(solution)/shard_map/pallas_call | solution.py:315
  33.3 3.4 %collective-permute-done.11.refs_1_ = f32[2,2,16,1024]{3,2,1,0:T(8,128)S(1)} collective-permute-done((f32[2,2,16,1024]{3,2,1,0:T(8,128)S(1)}, f32[2,2,16,1024]{3,2,1,0:T(8,128)S(1)}, u32[]{:S(2)}, u32[]{:S(2)}) %collective-permute-start.11) | collective-permute-done | bytes 262176 | tf_op jit(solution)/shard_map/ppermute | solution.py:61
  36.7 2.9 %collective-permute-done.12.refs_2_ = f32[2,2,16,1024]{3,2,1,0:T(8,128)S(1)} collective-permute-done((f32[2,2,16,1024]{3,2,1,0:T(8,128)S(1)}, f32[2,2,16,1024]{3,2,1,0:T(8,128)S(1)}, u32[]{:S(2)}, u32[]{:S(2)}) %collective-permute-start.12) | collective-permute-done | bytes 262176 | tf_op jit(solution)/shard_map/ppermute | solution.py:61
  39.5 0.0 collective-permute-done.13.refs_3_
  39.6 0.1 collective-permute-start.14
  39.7 0.9 %shard_map.76.held_ref = f32[2,4,2,16,1024]{4,3,2,1,0:T(8,128)} custom-call(s32[1]{0:T(128)} %bitcast.here_ref.refs_0_, f32[2,2,16,1024]{3,2,1,0:T(8,128)S(1)} %collective-permute-done.11.refs_1_, f32[2,2,16,1024]{3,2,1,0:T(8,128)S(1)} %collective-permute-done.12.refs_2_, f32[2,2,16,1024]{3,2,1,0:T(8,128)S(1)} %collective-permute-done.13.refs_3_, ...), custom_call_target="tpu_custom_call" | custom-call | tf_op jit(solution)/shard_map/pallas_call | solution.py:327
  40.5 1.0 %collective-permute-done.14.back_ref = f32[2,4,16,1024]{3,2,1,0:T(8,128)S(1)} collective-permute-done((f32[2,4,16,1024]{3,2,1,0:T(8,128)S(1)}, f32[2,4,16,1024]{3,2,1,0:T(8,128)S(1)}, u32[]{:S(2)}, u32[]{:S(2)}) %collective-permute-start.14) | collective-permute-done | bytes 524320 | tf_op jit(solution)/shard_map/ppermute | solution.py:325
  41.6 0.8 %shard_map.77 = f32[2,4,2,16,1024]{4,3,2,1,0:T(8,128)} custom-call(s32[1]{0:T(128)} %bitcast.here_ref.refs_0_, f32[2,4,16,1024]{3,2,1,0:T(8,128)S(1)} %collective-permute-done.14.back_ref, f32[2,4,2,16,1024]{4,3,2,1,0:T(8,128)} %shard_map.76.held_ref), custom_call_target="tpu_custom_call", output_to_operand_aliasing={{}: (2, {})} | custom-call | tf_op jit(solution)/shard_map/pallas_call | solution.py:334
  (4 shorter events, 0.1 us)
Async XLA Ops:
  0.6 10.9 %copy-start = (f32[32,1,16,1024]{3,2,1,0:T(8,128)S(1)}, f32[32,1,16,1024]{3,2,1,0:T(8,128)}, u32[]{:S(2)}) copy-start(f32[32,1,16,1024]{3,2,1,0:T(8,128)} %param.7) | copy-start | bytes 6291460
  0.6 1.4 %copy-start.2 = (f32[1,2,128,1024]{3,2,1,0:T(8,128)S(1)}, f32[1,2,128,1024]{3,2,1,0:T(8,128)}, u32[]{:S(2)}) copy-start(f32[1,2,128,1024]{3,2,1,0:T(8,128)} %param.4) | copy-start | bytes 3145732
  2.1 5.8 %collective-permute-start = (f32[2,4,16,1024]{3,2,1,0:T(8,128)S(1)}, f32[2,4,16,1024]{3,2,1,0:T(8,128)S(1)}, u32[]{:S(2)}, u32[]{:S(2)}) collective-permute-start(f32[2,4,16,1024]{3,2,1,0:T(8,128)S(1)} %get-tuple-element.26), channel_id=1, source_target_pairs={{0,4},{4,0},{8,12},{12,8},{16,20},{20,16},{24,28},{28,24},{1,5},{5... | collective-permute-start | bytes 1572872 | tf_op jit(solution)/shard_map/ppermute | solution.py:271
  2.6 8.6 %collective-permute-start.4 = (f32[8,128]{1,0:T(8,128)S(1)}, f32[8,128]{1,0:T(8,128)S(1)}, u32[]{:S(2)}, u32[]{:S(2)}) collective-permute-start(f32[8,128]{1,0:T(8,128)S(1)} %get-tuple-element.31.refs_0_), channel_id=1, source_target_pairs={{0,1},{1,0},{2,3},{3,2},{4,5},{5,4},{6,7},{7,6},{8,9},{9,8},{10,11... | collective-permute-start | bytes 12296 | tf_op jit(solution)/shard_map/ppermute | solution.py:273
  5.3 6.5 %collective-permute-start.5 = (f32[8,128]{1,0:T(8,128)S(1)}, f32[8,128]{1,0:T(8,128)S(1)}, u32[]{:S(2)}, u32[]{:S(2)}) collective-permute-start(f32[8,128]{1,0:T(8,128)S(1)} %get-tuple-element.31.refs_0_), channel_id=1, source_target_pairs={{0,2},{1,3},{2,0},{3,1},{4,6},{5,7},{6,4},{7,5},{8,10},{9,11},{10,... | collective-permute-start | bytes 12296 | tf_op jit(solution)/shard_map/ppermute | solution.py:273
  7.9 5.4 %collective-permute-start.6 = (f32[8,128]{1,0:T(8,128)S(1)}, f32[8,128]{1,0:T(8,128)S(1)}, u32[]{:S(2)}, u32[]{:S(2)}) collective-permute-start(f32[8,128]{1,0:T(8,128)S(1)} %get-tuple-element.31.refs_0_), channel_id=1, source_target_pairs={{0,3},{1,2},{2,1},{3,0},{4,7},{5,6},{6,5},{7,4},{8,11},{9,10},{10,... | collective-permute-start | bytes 12296 | tf_op jit(solution)/shard_map/ppermute | solution.py:273
  8.0 17.6 %collective-permute-start.1 = (f32[44,8,128]{2,1,0:T(8,128)S(1)}, f32[44,8,128]{2,1,0:T(8,128)S(1)}, u32[]{:S(2)}, u32[]{:S(2)}) collective-permute-start(f32[44,8,128]{2,1,0:T(8,128)S(1)} %get-tuple-element.27), channel_id=1, source_target_pairs={{0,24},{4,28},{8,16},{12,20},{16,8},{20,12},{24,0},{28,4},{1,25},{... | collective-permute-start | bytes 540680 | tf_op jit(solution)/shard_map/ppermute | solution.py:61
  10.7 14.9 %collective-permute-start.2 = (f32[44,8,128]{2,1,0:T(8,128)S(1)}, f32[44,8,128]{2,1,0:T(8,128)S(1)}, u32[]{:S(2)}, u32[]{:S(2)}) collective-permute-start(f32[44,8,128]{2,1,0:T(8,128)S(1)} %get-tuple-element.28), channel_id=1, source_target_pairs={{0,8},{4,20},{8,0},{12,28},{16,24},{20,4},{24,16},{28,12},{1,9},{5... | collective-permute-start | bytes 540680 | tf_op jit(solution)/shard_map/ppermute | solution.py:61
  11.2 14.3 %collective-permute-start.3 = (f32[44,8,128]{2,1,0:T(8,128)S(1)}, f32[44,8,128]{2,1,0:T(8,128)S(1)}, u32[]{:S(2)}, u32[]{:S(2)}) collective-permute-start(f32[44,8,128]{2,1,0:T(8,128)S(1)} %get-tuple-element.29), channel_id=1, source_target_pairs={{0,16},{4,12},{8,24},{12,4},{16,0},{20,28},{24,8},{28,20},{1,17},{... | collective-permute-start | bytes 540680 | tf_op jit(solution)/shard_map/ppermute | solution.py:61
  11.8 10.8 %copy-start.3 = (s32[8,2]{0,1:T(2,128)S(1)}, s32[8,2]{0,1:T(2,128)}, u32[]{:S(2)}) copy-start(s32[8,2]{0,1:T(2,128)} %param.5) | copy-start | bytes 196
  11.8 12.2 %copy-start.1 = (f32[32,1,16,1024]{3,2,1,0:T(8,128)S(1)}, f32[32,1,16,1024]{3,2,1,0:T(8,128)}, u32[]{:S(2)}) copy-start(f32[32,1,16,1024]{3,2,1,0:T(8,128)} %param.6) | copy-start | bytes 6291460
  13.3 1.2 %collective-permute-start.7 = (f32[8,128]{1,0:T(8,128)S(1)}, f32[8,128]{1,0:T(8,128)S(1)}, u32[]{:S(2)}, u32[]{:S(2)}) collective-permute-start(f32[8,128]{1,0:T(8,128)S(1)} %shard_map.71.refs_1_), channel_id=1, source_target_pairs={{0,4},{4,0},{8,12},{12,8},{16,20},{20,16},{24,28},{28,24},{1,5},{5... | collective-permute-start | bytes 12296 | tf_op jit(solution)/shard_map/ppermute | solution.py:296
  14.5 6.6 %collective-permute-start.8 = (f32[21,8,128]{2,1,0:T(8,128)S(1)}, f32[21,8,128]{2,1,0:T(8,128)S(1)}, u32[]{:S(2)}, u32[]{:S(2)}) collective-permute-start(f32[21,8,128]{2,1,0:T(8,128)S(1)} %get-tuple-element.32), channel_id=1, source_target_pairs={{0,24},{4,28},{8,16},{12,20},{16,8},{20,12},{24,0},{28,4},{1,25},{... | collective-permute-start | bytes 258056 | tf_op jit(solution)/shard_map/ppermute | solution.py:61
  17.0 7.4 %collective-permute-start.9 = (f32[21,8,128]{2,1,0:T(8,128)S(1)}, f32[21,8,128]{2,1,0:T(8,128)S(1)}, u32[]{:S(2)}, u32[]{:S(2)}) collective-permute-start(f32[21,8,128]{2,1,0:T(8,128)S(1)} %get-tuple-element.33), channel_id=1, source_target_pairs={{0,8},{4,20},{8,0},{12,28},{16,24},{20,4},{24,16},{28,12},{1,9},{5... | collective-permute-start | bytes 258056 | tf_op jit(solution)/shard_map/ppermute | solution.py:61
  21.1 4.5 %collective-permute-start.10 = (f32[21,8,128]{2,1,0:T(8,128)S(1)}, f32[21,8,128]{2,1,0:T(8,128)S(1)}, u32[]{:S(2)}, u32[]{:S(2)}) collective-permute-start(f32[21,8,128]{2,1,0:T(8,128)S(1)} %get-tuple-element.34), channel_id=1, source_target_pairs={{0,16},{4,12},{8,24},{12,4},{16,0},{20,28},{24,8},{28,20},{1,17},{... | collective-permute-start | bytes 258056 | tf_op jit(solution)/shard_map/ppermute | solution.py:61
  26.6 10.0 %collective-permute-start.11 = (f32[2,2,16,1024]{3,2,1,0:T(8,128)S(1)}, f32[2,2,16,1024]{3,2,1,0:T(8,128)S(1)}, u32[]{:S(2)}, u32[]{:S(2)}) collective-permute-start(f32[2,2,16,1024]{3,2,1,0:T(8,128)S(1)} %get-tuple-element.36), channel_id=1, source_target_pairs={{0,24},{4,28},{8,16},{12,20},{16,8},{20,12},{24,0},{28,4},{1,25},{... | collective-permute-start | bytes 786440 | tf_op jit(solution)/shard_map/ppermute | solution.py:61
  29.2 10.4 %collective-permute-start.12 = (f32[2,2,16,1024]{3,2,1,0:T(8,128)S(1)}, f32[2,2,16,1024]{3,2,1,0:T(8,128)S(1)}, u32[]{:S(2)}, u32[]{:S(2)}) collective-permute-start(f32[2,2,16,1024]{3,2,1,0:T(8,128)S(1)} %get-tuple-element.37), channel_id=1, source_target_pairs={{0,8},{4,20},{8,0},{12,28},{16,24},{20,4},{24,16},{28,12},{1,9},{5... | collective-permute-start | bytes 786440 | tf_op jit(solution)/shard_map/ppermute | solution.py:61
  29.7 9.8 %collective-permute-start.13 = (f32[2,2,16,1024]{3,2,1,0:T(8,128)S(1)}, f32[2,2,16,1024]{3,2,1,0:T(8,128)S(1)}, u32[]{:S(2)}, u32[]{:S(2)}) collective-permute-start(f32[2,2,16,1024]{3,2,1,0:T(8,128)S(1)} %get-tuple-element.38), channel_id=1, source_target_pairs={{0,16},{4,12},{8,24},{12,4},{16,0},{20,28},{24,8},{28,20},{1,17},{... | collective-permute-start | bytes 786440 | tf_op jit(solution)/shard_map/ppermute | solution.py:61
  39.6 2.0 %collective-permute-start.14 = (f32[2,4,16,1024]{3,2,1,0:T(8,128)S(1)}, f32[2,4,16,1024]{3,2,1,0:T(8,128)S(1)}, u32[]{:S(2)}, u32[]{:S(2)}) collective-permute-start(f32[2,4,16,1024]{3,2,1,0:T(8,128)S(1)} %shard_map.75), channel_id=1, source_target_pairs={{0,4},{4,0},{8,12},{12,8},{16,20},{20,16},{24,28},{28,24},{1,5},{5... | collective-permute-start | bytes 1572872 | tf_op jit(solution)/shard_map/ppermute | solution.py:325

commit v14 on v8

--- a/solution.py
+++ b/solution.py
@@ -232,14 +232,10 @@
 def other_rows_kernel(here_ref, back_ref, held_ref, out_ref, sems):
     del held_ref
     core = here_ref[0] & 1
-    copies = []
-    for level in range(LEVELS):
-        for chip in range(back_ref.shape[1]):
-            copies.append(
-                pltpu.make_async_copy(
-                    back_ref.at[level, chip], out_ref.at[level, chip, 1 - core], sems.at[level, chip]
-                )
-            )
+    copies = [
+        pltpu.make_async_copy(back_ref.at[level], out_ref.at[level, :, 1 - core], sems.at[level, 0])
+        for level in range(LEVELS)
+    ]
     for copy in copies:
         copy.start()
     for copy in copies:

time: 41.8 us -> 41.8 us (level)
  no operation moved by 1% of the time
where the time goes in v14:
time: 41.8 us; the launch traced here: 41.7 us
  starting transfers between devices  17.8 us (43%)
  waiting for transfers between devices  13.6 us (33%)
  Pallas kernels  7.79 us (19%)
  local copies, waits for them, and re-layouts  1.38 us (3%)
  between operations  0.79 us (2%)
    ppermute x9, starting transfers between devices, move(): lax.ppermute(array, 'path', [(i, target(i, k, size)) for i in range(size)])  11.9 us
    ppermute x9, waiting for transfers between devices, move(): lax.ppermute(array, 'path', [(i, target(i, k, size)) for i in range(size)])  11.4 us
    ppermute x3, starting transfers between devices, local(): lax.ppermute(squares, 'shard', [(i, i ^ step) for i in range(shards)])  5.33 us
    pallas_call x1, Pallas kernels, local(): call(state_kernel, [shape(*state_in.shape)] * 2 + [shape(8, 128)], [smem,...  3.08 us
    pallas_call x1, Pallas kernels, local(): call(plan_kernel, [jax.ShapeDtypeStruct((LEVELS, 5 * size), jnp.int32), j...  1.4 us
    unnamed x8, local copies, waits for them, and re-layouts  1.38 us
    ppermute x1, waiting for transfers between devices, local(): other = lax.ppermute(squares, 'path', swap)  1.15 us
    pallas_call x1, Pallas kernels, local(): call(lambda *refs: outgoing_kernel(rounds, entries, *refs), [message] * r...  1.04 us
  transfers between devices with their start and end apart: 15, of which 6 were waited for; matrix products, arithmetic and copies ran while one was open for 1% of the time, Pallas kernels for 14%

profile of v14, /device:TPU:0, one launch (start us, length us, event | category | flops | bytes accessed | tf_op | source)
XLA Modules:
  0.0 41.7 jit_solution(13971040201091695665)
XLA Ops:
  0.6 0.0 copy-start
  0.6 0.0 copy-start.2
  0.7 1.4 %copy-done.2 = f32[1,2,128,1024]{3,2,1,0:T(8,128)S(1)} copy-done((f32[1,2,128,1024]{3,2,1,0:T(8,128)S(1)}, f32[1,2,128,1024]{3,2,1,0:T(8,128)}, u32[]{:S(2)}) %copy-start.2) | copy-done | bytes 1048600
  2.0 0.1 shard_map.69
  2.1 0.5 %collective-permute-start = (f32[2,4,16,1024]{3,2,1,0:T(8,128)S(1)}, f32[2,4,16,1024]{3,2,1,0:T(8,128)S(1)}, u32[]{:S(2)}, u32[]{:S(2)}) collective-permute-start(f32[2,4,16,1024]{3,2,1,0:T(8,128)S(1)} %get-tuple-element.26), channel_id=1, source_target_pairs={{0,4},{4,0},{8,12},{12,8},{16,20},{20,16},{24,28},{28,24},{1,5},{5... | collective-permute-start | bytes 1572872 | tf_op jit(solution)/shard_map/ppermute | solution.py:267
  2.6 4.7 %collective-permute-start.4 = (f32[8,128]{1,0:T(8,128)S(1)}, f32[8,128]{1,0:T(8,128)S(1)}, u32[]{:S(2)}, u32[]{:S(2)}) collective-permute-start(f32[8,128]{1,0:T(8,128)S(1)} %get-tuple-element.31.refs_0_), channel_id=1, source_target_pairs={{0,3},{1,2},{2,1},{3,0},{4,7},{5,6},{6,5},{7,4},{8,11},{9,10},{10,... | collective-permute-start | bytes 12296 | tf_op jit(solution)/shard_map/ppermute | solution.py:269
  7.3 0.0 collective-permute-start.5
  7.3 0.6 %collective-permute-start.6 = (f32[8,128]{1,0:T(8,128)S(1)}, f32[8,128]{1,0:T(8,128)S(1)}, u32[]{:S(2)}, u32[]{:S(2)}) collective-permute-start(f32[8,128]{1,0:T(8,128)S(1)} %get-tuple-element.31.refs_0_), channel_id=1, source_target_pairs={{0,1},{1,0},{2,3},{3,2},{4,5},{5,4},{6,7},{7,6},{8,9},{9,8},{10,11... | collective-permute-start | bytes 12296 | tf_op jit(solution)/shard_map/ppermute | solution.py:269
  8.0 0.0 collective-permute-done.refs_2_.refs_4_
  8.0 2.7 %collective-permute-start.1 = (f32[44,8,128]{2,1,0:T(8,128)S(1)}, f32[44,8,128]{2,1,0:T(8,128)S(1)}, u32[]{:S(2)}, u32[]{:S(2)}) collective-permute-start(f32[44,8,128]{2,1,0:T(8,128)S(1)} %get-tuple-element.27), channel_id=1, source_target_pairs={{0,24},{4,28},{8,16},{12,20},{16,8},{20,12},{24,0},{28,4},{1,25},{... | collective-permute-start | bytes 540680 | tf_op jit(solution)/shard_map/ppermute | solution.py:61
  10.7 0.5 %collective-permute-start.2 = (f32[44,8,128]{2,1,0:T(8,128)S(1)}, f32[44,8,128]{2,1,0:T(8,128)S(1)}, u32[]{:S(2)}, u32[]{:S(2)}) collective-permute-start(f32[44,8,128]{2,1,0:T(8,128)S(1)} %get-tuple-element.28), channel_id=1, source_target_pairs={{0,8},{4,20},{8,0},{12,28},{16,24},{20,4},{24,16},{28,12},{1,9},{5... | collective-permute-start | bytes 540680 | tf_op jit(solution)/shard_map/ppermute | solution.py:61
  11.2 0.0 collective-permute-done.4.refs_1_
  11.2 0.4 collective-permute-start.3
  11.6 0.0 copy-done
  11.6 0.3 broadcast_multiply_fusion.decay_ref.refs_4_
  11.9 0.0 copy-start.3
  11.9 0.0 copy-start.1
  11.9 0.0 collective-permute-done.5.refs_2_
  11.9 0.0 collective-permute-done.6.refs_3_
  11.9 0.1 collective-permute-start.7
  12.0 1.2 %collective-permute-done.7.refs_2_ = f32[8,128]{1,0:T(8,128)S(1)} collective-permute-done((f32[8,128]{1,0:T(8,128)S(1)}, f32[8,128]{1,0:T(8,128)S(1)}, u32[]{:S(2)}, u32[]{:S(2)}) %collective-permute-start.7) | collective-permute-done | bytes 4128 | tf_op jit(solution)/shard_map/ppermute | solution.py:292
  13.2 2.7 %collective-permute-start.8 = (f32[21,8,128]{2,1,0:T(8,128)S(1)}, f32[21,8,128]{2,1,0:T(8,128)S(1)}, u32[]{:S(2)}, u32[]{:S(2)}) collective-permute-start(f32[21,8,128]{2,1,0:T(8,128)S(1)} %get-tuple-element.32), channel_id=1, source_target_pairs={{0,24},{4,28},{8,16},{12,20},{16,8},{20,12},{24,0},{28,4},{1,25},{... | collective-permute-start | bytes 258056 | tf_op jit(solution)/shard_map/ppermute | solution.py:61
  15.9 0.5 %collective-permute-start.9 = (f32[21,8,128]{2,1,0:T(8,128)S(1)}, f32[21,8,128]{2,1,0:T(8,128)S(1)}, u32[]{:S(2)}, u32[]{:S(2)}) collective-permute-start(f32[21,8,128]{2,1,0:T(8,128)S(1)} %get-tuple-element.33), channel_id=1, source_target_pairs={{0,8},{4,20},{8,0},{12,28},{16,24},{20,4},{24,16},{28,12},{1,9},{5... | collective-permute-start | bytes 258056 | tf_op jit(solution)/shard_map/ppermute | solution.py:61
  16.4 4.7 %collective-permute-done.8.refs_6_ = f32[21,8,128]{2,1,0:T(8,128)S(1)} collective-permute-done((f32[21,8,128]{2,1,0:T(8,128)S(1)}, f32[21,8,128]{2,1,0:T(8,128)S(1)}, u32[]{:S(2)}, u32[]{:S(2)}) %collective-permute-start.8) | collective-permute-done | bytes 86048 | tf_op jit(solution)/shard_map/ppermute | solution.py:61
  21.1 1.6 %collective-permute-start.10 = (f32[21,8,128]{2,1,0:T(8,128)S(1)}, f32[21,8,128]{2,1,0:T(8,128)S(1)}, u32[]{:S(2)}, u32[]{:S(2)}) collective-permute-start(f32[21,8,128]{2,1,0:T(8,128)S(1)} %get-tuple-element.34), channel_id=1, source_target_pairs={{0,16},{4,12},{8,24},{12,4},{16,0},{20,28},{24,8},{28,20},{1,17},{... | collective-permute-start | bytes 258056 | tf_op jit(solution)/shard_map/ppermute | solution.py:61
  22.6 0.0 copy-done.3
  22.6 1.4 %shard_map.67 = (s32[2,40]{1,0:T(2,128)S(1)}, s32[32]{0:T(128)S(1)}) custom-call(s32[1]{0:T(128)} %bitcast.here_ref.refs_0_, s32[2,8]{1,0:T(2,128)S(1)} %bitcast.16), custom_call_target="tpu_custom_call" | custom-call | tf_op jit(solution)/shard_map/pallas_call | solution.py:280
  24.0 0.0 copy-done.1
  24.0 0.3 shard_map.68.refs_1_.decayed_ref
  24.4 0.0 collective-permute-done.9.refs_7_
  24.4 1.2 %collective-permute-done.10.refs_8_ = f32[21,8,128]{2,1,0:T(8,128)S(1)} collective-permute-done((f32[21,8,128]{2,1,0:T(8,128)S(1)}, f32[21,8,128]{2,1,0:T(8,128)S(1)}, u32[]{:S(2)}, u32[]{:S(2)}) %collective-permute-start.10) | collective-permute-done | bytes 86048 | tf_op jit(solution)/shard_map/ppermute | solution.py:61
  25.5 0.0 collective-permute-done.1.refs_2_
  25.5 0.0 collective-permute-done.2.refs_3_
  25.5 0.0 collective-permute-done.3.refs_4_
  25.6 1.0 %shard_map.73 = (f32[2,2,16,1024]{3,2,1,0:T(8,128)S(1)}, f32[2,2,16,1024]{3,2,1,0:T(8,128)S(1)}, f32[2,2,16,1024]{3,2,1,0:T(8,128)S(1)}, f32[2,2,16,1024]{3,2,1,0:T(8,128)S(1)}, f32[2,8,16,1024]{3,2,1,0:T(8,128)S(1)}) custom-call(s32[2,40]{1,0:T(2,128)S(1)} %get-tuple-element.24.refs_0_, f32[32,16,1024]{2,1,0:T(8,128)S(1)} %shard_map.68.refs_1_.decayed_ref, ...), custom_call_target="tpu_custom_call" | custom-call | tf_op jit(solution)/shard_map/pallas_call | solution.py:301
  26.6 2.6 %collective-permute-start.11 = (f32[2,2,16,1024]{3,2,1,0:T(8,128)S(1)}, f32[2,2,16,1024]{3,2,1,0:T(8,128)S(1)}, u32[]{:S(2)}, u32[]{:S(2)}) collective-permute-start(f32[2,2,16,1024]{3,2,1,0:T(8,128)S(1)} %get-tuple-element.36), channel_id=1, source_target_pairs={{0,24},{4,28},{8,16},{12,20},{16,8},{20,12},{24,0},{28,4},{1,25},{... | collective-permute-start | bytes 786440 | tf_op jit(solution)/shard_map/ppermute | solution.py:61
  29.2 0.5 %collective-permute-start.12 = (f32[2,2,16,1024]{3,2,1,0:T(8,128)S(1)}, f32[2,2,16,1024]{3,2,1,0:T(8,128)S(1)}, u32[]{:S(2)}, u32[]{:S(2)}) collective-permute-start(f32[2,2,16,1024]{3,2,1,0:T(8,128)S(1)} %get-tuple-element.37), channel_id=1, source_target_pairs={{0,8},{4,20},{8,0},{12,28},{16,24},{20,4},{24,16},{28,12},{1,9},{5... | collective-permute-start | bytes 786440 | tf_op jit(solution)/shard_map/ppermute | solution.py:61
  29.7 0.5 %collective-permute-start.13 = (f32[2,2,16,1024]{3,2,1,0:T(8,128)S(1)}, f32[2,2,16,1024]{3,2,1,0:T(8,128)S(1)}, u32[]{:S(2)}, u32[]{:S(2)}) collective-permute-start(f32[2,2,16,1024]{3,2,1,0:T(8,128)S(1)} %get-tuple-element.38), channel_id=1, source_target_pairs={{0,16},{4,12},{8,24},{12,4},{16,0},{20,28},{24,8},{28,20},{1,17},{... | collective-permute-start | bytes 786440 | tf_op jit(solution)/shard_map/ppermute | solution.py:61
  30.2 3.1 %shard_map.74 = (f32[32,16,1024]{2,1,0:T(8,128)}, f32[32,16,1024]{2,1,0:T(8,128)}, f32[8,128]{1,0:T(8,128)S(1)}) custom-call(s32[32]{0:T(128)S(1)} %get-tuple-element.40.module_ref, f32[2,8,16,1024]{3,2,1,0:T(8,128)S(1)} %get-tuple-element.41.grad_ref, f32[32,16,1024]{2,1,0:T(8,128)S(1)} %shard_map.68.refs_1_.decayed_ref, f32[32,16,1024]{2,1,0:T(8,128)S(1)} %bitcast.13), custom_call_target="tpu_custom_call" | custom-call | tf_op jit(solution)/shard_map/pallas_call | solution.py:311
  33.2 2.8 %collective-permute-done.11.refs_1_ = f32[2,2,16,1024]{3,2,1,0:T(8,128)S(1)} collective-permute-done((f32[2,2,16,1024]{3,2,1,0:T(8,128)S(1)}, f32[2,2,16,1024]{3,2,1,0:T(8,128)S(1)}, u32[]{:S(2)}, u32[]{:S(2)}) %collective-permute-start.11) | collective-permute-done | bytes 262176 | tf_op jit(solution)/shard_map/ppermute | solution.py:61
  36.1 2.7 %collective-permute-done.12.refs_2_ = f32[2,2,16,1024]{3,2,1,0:T(8,128)S(1)} collective-permute-done((f32[2,2,16,1024]{3,2,1,0:T(8,128)S(1)}, f32[2,2,16,1024]{3,2,1,0:T(8,128)S(1)}, u32[]{:S(2)}, u32[]{:S(2)}) %collective-permute-start.12) | collective-permute-done | bytes 262176 | tf_op jit(solution)/shard_map/ppermute | solution.py:61
  38.8 0.0 collective-permute-done.13.refs_3_
  38.8 0.1 collective-permute-start.14
  38.9 0.9 %shard_map.76.held_ref = f32[2,4,2,16,1024]{4,3,2,1,0:T(8,128)} custom-call(s32[1]{0:T(128)} %bitcast.here_ref.refs_0_, f32[2,2,16,1024]{3,2,1,0:T(8,128)S(1)} %collective-permute-done.11.refs_1_, f32[2,2,16,1024]{3,2,1,0:T(8,128)S(1)} %collective-permute-done.12.refs_2_, f32[2,2,16,1024]{3,2,1,0:T(8,128)S(1)} %collective-permute-done.13.refs_3_, ...), custom_call_target="tpu_custom_call" | custom-call | tf_op jit(solution)/shard_map/pallas_call | solution.py:323
  39.8 1.0 %collective-permute-done.14.back_ref = f32[2,4,16,1024]{3,2,1,0:T(8,128)S(1)} collective-permute-done((f32[2,4,16,1024]{3,2,1,0:T(8,128)S(1)}, f32[2,4,16,1024]{3,2,1,0:T(8,128)S(1)}, u32[]{:S(2)}, u32[]{:S(2)}) %collective-permute-start.14) | collective-permute-done | bytes 524320 | tf_op jit(solution)/shard_map/ppermute | solution.py:321
  40.8 0.9 %shard_map.77 = f32[2,4,2,16,1024]{4,3,2,1,0:T(8,128)} custom-call(s32[1]{0:T(128)} %bitcast.here_ref.refs_0_, f32[2,4,16,1024]{3,2,1,0:T(8,128)S(1)} %collective-permute-done.14.back_ref, f32[2,4,2,16,1024]{4,3,2,1,0:T(8,128)} %shard_map.76.held_ref), custom_call_target="tpu_custom_call", output_to_operand_aliasing={{}: (2, {})} | custom-call | tf_op jit(solution)/shard_map/pallas_call | solution.py:330
  (4 shorter events, 0.1 us)
Async XLA Ops:
  0.6 11.0 %copy-start = (f32[32,1,16,1024]{3,2,1,0:T(8,128)S(1)}, f32[32,1,16,1024]{3,2,1,0:T(8,128)}, u32[]{:S(2)}) copy-start(f32[32,1,16,1024]{3,2,1,0:T(8,128)} %param.7) | copy-start | bytes 6291460
  0.6 1.4 %copy-start.2 = (f32[1,2,128,1024]{3,2,1,0:T(8,128)S(1)}, f32[1,2,128,1024]{3,2,1,0:T(8,128)}, u32[]{:S(2)}) copy-start(f32[1,2,128,1024]{3,2,1,0:T(8,128)} %param.4) | copy-start | bytes 3145732
  2.1 5.8 %collective-permute-start = (f32[2,4,16,1024]{3,2,1,0:T(8,128)S(1)}, f32[2,4,16,1024]{3,2,1,0:T(8,128)S(1)}, u32[]{:S(2)}, u32[]{:S(2)}) collective-permute-start(f32[2,4,16,1024]{3,2,1,0:T(8,128)S(1)} %get-tuple-element.26), channel_id=1, source_target_pairs={{0,4},{4,0},{8,12},{12,8},{16,20},{20,16},{24,28},{28,24},{1,5},{5... | collective-permute-start | bytes 1572872 | tf_op jit(solution)/shard_map/ppermute | solution.py:267
  2.6 8.6 %collective-permute-start.4 = (f32[8,128]{1,0:T(8,128)S(1)}, f32[8,128]{1,0:T(8,128)S(1)}, u32[]{:S(2)}, u32[]{:S(2)}) collective-permute-start(f32[8,128]{1,0:T(8,128)S(1)} %get-tuple-element.31.refs_0_), channel_id=1, source_target_pairs={{0,3},{1,2},{2,1},{3,0},{4,7},{5,6},{6,5},{7,4},{8,11},{9,10},{10,... | collective-permute-start | bytes 12296 | tf_op jit(solution)/shard_map/ppermute | solution.py:269
  7.3 4.6 %collective-permute-start.5 = (f32[8,128]{1,0:T(8,128)S(1)}, f32[8,128]{1,0:T(8,128)S(1)}, u32[]{:S(2)}, u32[]{:S(2)}) collective-permute-start(f32[8,128]{1,0:T(8,128)S(1)} %get-tuple-element.31.refs_0_), channel_id=1, source_target_pairs={{0,2},{1,3},{2,0},{3,1},{4,6},{5,7},{6,4},{7,5},{8,10},{9,11},{10,... | collective-permute-start | bytes 12296 | tf_op jit(solution)/shard_map/ppermute | solution.py:269
  7.3 4.6 %collective-permute-start.6 = (f32[8,128]{1,0:T(8,128)S(1)}, f32[8,128]{1,0:T(8,128)S(1)}, u32[]{:S(2)}, u32[]{:S(2)}) collective-permute-start(f32[8,128]{1,0:T(8,128)S(1)} %get-tuple-element.31.refs_0_), channel_id=1, source_target_pairs={{0,1},{1,0},{2,3},{3,2},{4,5},{5,4},{6,7},{7,6},{8,9},{9,8},{10,11... | collective-permute-start | bytes 12296 | tf_op jit(solution)/shard_map/ppermute | solution.py:269
  8.0 17.5 %collective-permute-start.1 = (f32[44,8,128]{2,1,0:T(8,128)S(1)}, f32[44,8,128]{2,1,0:T(8,128)S(1)}, u32[]{:S(2)}, u32[]{:S(2)}) collective-permute-start(f32[44,8,128]{2,1,0:T(8,128)S(1)} %get-tuple-element.27), channel_id=1, source_target_pairs={{0,24},{4,28},{8,16},{12,20},{16,8},{20,12},{24,0},{28,4},{1,25},{... | collective-permute-start | bytes 540680 | tf_op jit(solution)/shard_map/ppermute | solution.py:61
  10.7 14.9 %collective-permute-start.2 = (f32[44,8,128]{2,1,0:T(8,128)S(1)}, f32[44,8,128]{2,1,0:T(8,128)S(1)}, u32[]{:S(2)}, u32[]{:S(2)}) collective-permute-start(f32[44,8,128]{2,1,0:T(8,128)S(1)} %get-tuple-element.28), channel_id=1, source_target_pairs={{0,8},{4,20},{8,0},{12,28},{16,24},{20,4},{24,16},{28,12},{1,9},{5... | collective-permute-start | bytes 540680 | tf_op jit(solution)/shard_map/ppermute | solution.py:61
  11.2 14.3 %collective-permute-start.3 = (f32[44,8,128]{2,1,0:T(8,128)S(1)}, f32[44,8,128]{2,1,0:T(8,128)S(1)}, u32[]{:S(2)}, u32[]{:S(2)}) collective-permute-start(f32[44,8,128]{2,1,0:T(8,128)S(1)} %get-tuple-element.29), channel_id=1, source_target_pairs={{0,16},{4,12},{8,24},{12,4},{16,0},{20,28},{24,8},{28,20},{1,17},{... | collective-permute-start | bytes 540680 | tf_op jit(solution)/shard_map/ppermute | solution.py:61
  11.9 10.7 %copy-start.3 = (s32[8,2]{0,1:T(2,128)S(1)}, s32[8,2]{0,1:T(2,128)}, u32[]{:S(2)}) copy-start(s32[8,2]{0,1:T(2,128)} %param.5) | copy-start | bytes 196
  11.9 12.1 %copy-start.1 = (f32[32,1,16,1024]{3,2,1,0:T(8,128)S(1)}, f32[32,1,16,1024]{3,2,1,0:T(8,128)}, u32[]{:S(2)}) copy-start(f32[32,1,16,1024]{3,2,1,0:T(8,128)} %param.6) | copy-start | bytes 6291460
  11.9 1.2 %collective-permute-start.7 = (f32[8,128]{1,0:T(8,128)S(1)}, f32[8,128]{1,0:T(8,128)S(1)}, u32[]{:S(2)}, u32[]{:S(2)}) collective-permute-start(f32[8,128]{1,0:T(8,128)S(1)} %shard_map.71.refs_1_), channel_id=1, source_target_pairs={{0,4},{4,0},{8,12},{12,8},{16,20},{20,16},{24,28},{28,24},{1,5},{5... | collective-permute-start | bytes 12296 | tf_op jit(solution)/shard_map/ppermute | solution.py:292
  13.2 7.9 %collective-permute-start.8 = (f32[21,8,128]{2,1,0:T(8,128)S(1)}, f32[21,8,128]{2,1,0:T(8,128)S(1)}, u32[]{:S(2)}, u32[]{:S(2)}) collective-permute-start(f32[21,8,128]{2,1,0:T(8,128)S(1)} %get-tuple-element.32), channel_id=1, source_target_pairs={{0,24},{4,28},{8,16},{12,20},{16,8},{20,12},{24,0},{28,4},{1,25},{... | collective-permute-start | bytes 258056 | tf_op jit(solution)/shard_map/ppermute | solution.py:61
  15.9 8.5 %collective-permute-start.9 = (f32[21,8,128]{2,1,0:T(8,128)S(1)}, f32[21,8,128]{2,1,0:T(8,128)S(1)}, u32[]{:S(2)}, u32[]{:S(2)}) collective-permute-start(f32[21,8,128]{2,1,0:T(8,128)S(1)} %get-tuple-element.33), channel_id=1, source_target_pairs={{0,8},{4,20},{8,0},{12,28},{16,24},{20,4},{24,16},{28,12},{1,9},{5... | collective-permute-start | bytes 258056 | tf_op jit(solution)/shard_map/ppermute | solution.py:61
  21.1 4.5 %collective-permute-start.10 = (f32[21,8,128]{2,1,0:T(8,128)S(1)}, f32[21,8,128]{2,1,0:T(8,128)S(1)}, u32[]{:S(2)}, u32[]{:S(2)}) collective-permute-start(f32[21,8,128]{2,1,0:T(8,128)S(1)} %get-tuple-element.34), channel_id=1, source_target_pairs={{0,16},{4,12},{8,24},{12,4},{16,0},{20,28},{24,8},{28,20},{1,17},{... | collective-permute-start | bytes 258056 | tf_op jit(solution)/shard_map/ppermute | solution.py:61
  26.6 9.5 %collective-permute-start.11 = (f32[2,2,16,1024]{3,2,1,0:T(8,128)S(1)}, f32[2,2,16,1024]{3,2,1,0:T(8,128)S(1)}, u32[]{:S(2)}, u32[]{:S(2)}) collective-permute-start(f32[2,2,16,1024]{3,2,1,0:T(8,128)S(1)} %get-tuple-element.36), channel_id=1, source_target_pairs={{0,24},{4,28},{8,16},{12,20},{16,8},{20,12},{24,0},{28,4},{1,25},{... | collective-permute-start | bytes 786440 | tf_op jit(solution)/shard_map/ppermute | solution.py:61
  29.2 9.6 %collective-permute-start.12 = (f32[2,2,16,1024]{3,2,1,0:T(8,128)S(1)}, f32[2,2,16,1024]{3,2,1,0:T(8,128)S(1)}, u32[]{:S(2)}, u32[]{:S(2)}) collective-permute-start(f32[2,2,16,1024]{3,2,1,0:T(8,128)S(1)} %get-tuple-element.37), channel_id=1, source_target_pairs={{0,8},{4,20},{8,0},{12,28},{16,24},{20,4},{24,16},{28,12},{1,9},{5... | collective-permute-start | bytes 786440 | tf_op jit(solution)/shard_map/ppermute | solution.py:61
  29.7 9.1 %collective-permute-start.13 = (f32[2,2,16,1024]{3,2,1,0:T(8,128)S(1)}, f32[2,2,16,1024]{3,2,1,0:T(8,128)S(1)}, u32[]{:S(2)}, u32[]{:S(2)}) collective-permute-start(f32[2,2,16,1024]{3,2,1,0:T(8,128)S(1)} %get-tuple-element.38), channel_id=1, source_target_pairs={{0,16},{4,12},{8,24},{12,4},{16,0},{20,28},{24,8},{28,20},{1,17},{... | collective-permute-start | bytes 786440 | tf_op jit(solution)/shard_map/ppermute | solution.py:61
  38.8 2.0 %collective-permute-start.14 = (f32[2,4,16,1024]{3,2,1,0:T(8,128)S(1)}, f32[2,4,16,1024]{3,2,1,0:T(8,128)S(1)}, u32[]{:S(2)}, u32[]{:S(2)}) collective-permute-start(f32[2,4,16,1024]{3,2,1,0:T(8,128)S(1)} %shard_map.75), channel_id=1, source_target_pairs={{0,4},{4,0},{8,12},{12,8},{16,20},{20,16},{24,28},{28,24},{1,5},{5... | collective-permute-start | bytes 1572872 | tf_op jit(solution)/shard_map/ppermute | solution.py:321

commit v15 on v14

--- a/solution.py
+++ b/solution.py
@@ -209,7 +209,7 @@
     here = here_ref[0]
     for j, k in enumerate(order_of(size)):
         for level in range(LEVELS):
-            refs[-1][level, origin(here, k, size) // 2] = refs[j][1 - (here & 1), level]
+            refs[level - LEVELS][origin(here, k, size) // 2] = refs[j][1 - (here & 1), level]
 
 
 def own_rows_kernel(size, here_ref, *refs):
@@ -229,12 +229,12 @@
         copy.wait()
 
 
-def other_rows_kernel(here_ref, back_ref, held_ref, out_ref, sems):
+def other_rows_kernel(level, here_ref, back_ref, held_ref, out_ref, sems):
     del held_ref
     core = here_ref[0] & 1
     copies = [
-        pltpu.make_async_copy(back_ref.at[level], out_ref.at[level, :, 1 - core], sems.at[level, 0])
-        for level in range(LEVELS)
+        pltpu.make_async_copy(back_ref.at[chip], out_ref.at[level, chip, 1 - core], sems.at[level, chip])
+        for chip in range(back_ref.shape[0])
     ]
     for copy in copies:
         copy.start()
@@ -315,10 +315,13 @@
         [state_block, state_block, vmem],
         grid=(module_count // block,),
     )(leaders, grad, decayed, moment_in)
-    back = call(
-        lambda *refs: give_back_kernel(size, *refs), by_chip, [smem] + [vmem] * rounds + [anywhere], vmem
+    backs = call(
+        lambda *refs: give_back_kernel(size, *refs),
+        [shape(rounds, own_rows, width)] * LEVELS,
+        [smem] + [vmem] * rounds + [anywhere],
+        [vmem] * LEVELS,
     )(here, *returned, done)
-    back = lax.ppermute(back, "path", swap)
+    backs = [lax.ppermute(back, "path", swap) for back in backs]
     sems = [pltpu.SemaphoreType.DMA((LEVELS, rounds))]
     path_params = call(
         lambda *refs: own_rows_kernel(size, *refs),
@@ -327,14 +330,15 @@
         anywhere,
         scratch_shapes=sems,
     )(here, *returned)
-    path_params = call(
-        other_rows_kernel,
-        shape(*split_slab.shape),
-        [smem, anywhere, anywhere],
-        anywhere,
-        scratch_shapes=sems,
-        input_output_aliases={2: 0},
-    )(here, back, path_params)
+    for level in range(LEVELS):
+        path_params = call(
+            lambda *refs, level=level: other_rows_kernel(level, *refs),
+            shape(*split_slab.shape),
+            [smem, anywhere, anywhere],
+            anywhere,
+            scratch_shapes=sems,
+            input_output_aliases={2: 0},
+        )(here, backs[level], path_params)
     return (path_params.reshape(path_delta.shape), new_state[:, None], new_moment[:, None])
 
 

time: 41.8 us -> 42.1 us (level)
  waiting for transfers between devices: 13.6 us -> 12.7 us
  Pallas kernels: 7.79 us -> 8.46 us
  starting transfers between devices: 17.8 us -> 18.3 us
    ppermute x1 -> x2, waiting for transfers between devices: 1.03 us -> 0.17 us  [local(): backs = [lax.ppermute(back, 'path', swap) for back in backs]]
    pallas_call x2 -> x3, Pallas kernels: 0.9 us -> 1.58 us  [the longest x2 1.53 us: local(): call(lambda *refs, level=level: other_rows_kernel(level, *refs), shape(*s...]
    ppermute x1 -> x2, starting transfers between devices: 0.07 us -> 0.57 us  [local(): backs = [lax.ppermute(back, 'path', swap) for back in backs]]
  transfers between devices with their start and end apart: 15 -> 16, of which waited for: 6 -> 6; matrix products, arithmetic and copies ran while one was open for 1% -> 1% of each run, Pallas kernels for 14% -> 15%
where the time goes in v15:
time: 42.1 us; the launch traced here: 42 us
  starting transfers between devices  18.3 us (43%)
  waiting for transfers between devices  12.7 us (30%)
  Pallas kernels  8.46 us (20%)
  local copies, waits for them, and re-layouts  1.38 us (3%)
  between operations  0.81 us (2%)
    ppermute x9, starting transfers between devices, move(): lax.ppermute(array, 'path', [(i, target(i, k, size)) for i in range(size)])  11.9 us
    ppermute x9, waiting for transfers between devices, move(): lax.ppermute(array, 'path', [(i, target(i, k, size)) for i in range(size)])  11.4 us
    ppermute x3, starting transfers between devices, local(): lax.ppermute(squares, 'shard', [(i, i ^ step) for i in range(shards)])  5.33 us
    pallas_call x1, Pallas kernels, local(): call(state_kernel, [shape(*state_in.shape)] * 2 + [shape(8, 128)], [smem,...  3.08 us
    pallas_call x2, Pallas kernels, local(): call(lambda *refs, level=level: other_rows_kernel(level, *refs), shape(*s...  1.53 us
    pallas_call x1, Pallas kernels, local(): call(plan_kernel, [jax.ShapeDtypeStruct((LEVELS, 5 * size), jnp.int32), j...  1.4 us
    unnamed x8, local copies, waits for them, and re-layouts  1.38 us
    ppermute x1, waiting for transfers between devices, local(): other = lax.ppermute(squares, 'path', swap)  1.15 us
  transfers between devices with their start and end apart: 16, of which 6 were waited for; matrix products, arithmetic and copies ran while one was open for 1% of the time, Pallas kernels for 15%

profile of v15, /device:TPU:0, one launch (start us, length us, event | category | flops | bytes accessed | tf_op | source)
XLA Modules:
  0.0 42.0 jit_solution(18356754519599114685)
XLA Ops:
  0.6 0.0 copy-start
  0.6 0.0 copy-start.2
  0.7 1.4 %copy-done.2 = f32[1,2,128,1024]{3,2,1,0:T(8,128)S(1)} copy-done((f32[1,2,128,1024]{3,2,1,0:T(8,128)S(1)}, f32[1,2,128,1024]{3,2,1,0:T(8,128)}, u32[]{:S(2)}) %copy-start.2) | copy-done | bytes 1048600
  2.0 0.1 shard_map.69
  2.1 0.5 %collective-permute-start = (f32[2,4,16,1024]{3,2,1,0:T(8,128)S(1)}, f32[2,4,16,1024]{3,2,1,0:T(8,128)S(1)}, u32[]{:S(2)}, u32[]{:S(2)}) collective-permute-start(f32[2,4,16,1024]{3,2,1,0:T(8,128)S(1)} %get-tuple-element.28), channel_id=1, source_target_pairs={{0,4},{4,0},{8,12},{12,8},{16,20},{20,16},{24,28},{28,24},{1,5},{5... | collective-permute-start | bytes 1572872 | tf_op jit(solution)/shard_map/ppermute | solution.py:267
  2.6 4.7 %collective-permute-start.4 = (f32[8,128]{1,0:T(8,128)S(1)}, f32[8,128]{1,0:T(8,128)S(1)}, u32[]{:S(2)}, u32[]{:S(2)}) collective-permute-start(f32[8,128]{1,0:T(8,128)S(1)} %get-tuple-element.33.refs_0_), channel_id=1, source_target_pairs={{0,3},{1,2},{2,1},{3,0},{4,7},{5,6},{6,5},{7,4},{8,11},{9,10},{10,... | collective-permute-start | bytes 12296 | tf_op jit(solution)/shard_map/ppermute | solution.py:269
  7.3 0.0 collective-permute-start.5
  7.3 0.6 %collective-permute-start.6 = (f32[8,128]{1,0:T(8,128)S(1)}, f32[8,128]{1,0:T(8,128)S(1)}, u32[]{:S(2)}, u32[]{:S(2)}) collective-permute-start(f32[8,128]{1,0:T(8,128)S(1)} %get-tuple-element.33.refs_0_), channel_id=1, source_target_pairs={{0,1},{1,0},{2,3},{3,2},{4,5},{5,4},{6,7},{7,6},{8,9},{9,8},{10,11... | collective-permute-start | bytes 12296 | tf_op jit(solution)/shard_map/ppermute | solution.py:269
  8.0 0.0 collective-permute-done.refs_2_.refs_4_
  8.0 2.7 %collective-permute-start.1 = (f32[44,8,128]{2,1,0:T(8,128)S(1)}, f32[44,8,128]{2,1,0:T(8,128)S(1)}, u32[]{:S(2)}, u32[]{:S(2)}) collective-permute-start(f32[44,8,128]{2,1,0:T(8,128)S(1)} %get-tuple-element.29), channel_id=1, source_target_pairs={{0,24},{4,28},{8,16},{12,20},{16,8},{20,12},{24,0},{28,4},{1,25},{... | collective-permute-start | bytes 540680 | tf_op jit(solution)/shard_map/ppermute | solution.py:61
  10.7 0.5 %collective-permute-start.2 = (f32[44,8,128]{2,1,0:T(8,128)S(1)}, f32[44,8,128]{2,1,0:T(8,128)S(1)}, u32[]{:S(2)}, u32[]{:S(2)}) collective-permute-start(f32[44,8,128]{2,1,0:T(8,128)S(1)} %get-tuple-element.30), channel_id=1, source_target_pairs={{0,8},{4,20},{8,0},{12,28},{16,24},{20,4},{24,16},{28,12},{1,9},{5... | collective-permute-start | bytes 540680 | tf_op jit(solution)/shard_map/ppermute | solution.py:61
  11.2 0.0 collective-permute-done.4.refs_1_
  11.2 0.4 collective-permute-start.3
  11.6 0.0 copy-done
  11.6 0.3 broadcast_multiply_fusion.decay_ref.refs_4_
  11.9 0.0 copy-start.3
  11.9 0.0 copy-start.1
  11.9 0.0 collective-permute-done.5.refs_2_
  11.9 0.0 collective-permute-done.6.refs_3_
  11.9 0.1 collective-permute-start.7
  12.0 1.2 %collective-permute-done.7.refs_2_ = f32[8,128]{1,0:T(8,128)S(1)} collective-permute-done((f32[8,128]{1,0:T(8,128)S(1)}, f32[8,128]{1,0:T(8,128)S(1)}, u32[]{:S(2)}, u32[]{:S(2)}) %collective-permute-start.7) | collective-permute-done | bytes 4128 | tf_op jit(solution)/shard_map/ppermute | solution.py:292
  13.2 2.7 %collective-permute-start.8 = (f32[21,8,128]{2,1,0:T(8,128)S(1)}, f32[21,8,128]{2,1,0:T(8,128)S(1)}, u32[]{:S(2)}, u32[]{:S(2)}) collective-permute-start(f32[21,8,128]{2,1,0:T(8,128)S(1)} %get-tuple-element.34), channel_id=1, source_target_pairs={{0,24},{4,28},{8,16},{12,20},{16,8},{20,12},{24,0},{28,4},{1,25},{... | collective-permute-start | bytes 258056 | tf_op jit(solution)/shard_map/ppermute | solution.py:61
  15.9 0.5 %collective-permute-start.9 = (f32[21,8,128]{2,1,0:T(8,128)S(1)}, f32[21,8,128]{2,1,0:T(8,128)S(1)}, u32[]{:S(2)}, u32[]{:S(2)}) collective-permute-start(f32[21,8,128]{2,1,0:T(8,128)S(1)} %get-tuple-element.35), channel_id=1, source_target_pairs={{0,8},{4,20},{8,0},{12,28},{16,24},{20,4},{24,16},{28,12},{1,9},{5... | collective-permute-start | bytes 258056 | tf_op jit(solution)/shard_map/ppermute | solution.py:61
  16.4 4.7 %collective-permute-done.8.refs_6_ = f32[21,8,128]{2,1,0:T(8,128)S(1)} collective-permute-done((f32[21,8,128]{2,1,0:T(8,128)S(1)}, f32[21,8,128]{2,1,0:T(8,128)S(1)}, u32[]{:S(2)}, u32[]{:S(2)}) %collective-permute-start.8) | collective-permute-done | bytes 86048 | tf_op jit(solution)/shard_map/ppermute | solution.py:61
  21.1 1.6 %collective-permute-start.10 = (f32[21,8,128]{2,1,0:T(8,128)S(1)}, f32[21,8,128]{2,1,0:T(8,128)S(1)}, u32[]{:S(2)}, u32[]{:S(2)}) collective-permute-start(f32[21,8,128]{2,1,0:T(8,128)S(1)} %get-tuple-element.36), channel_id=1, source_target_pairs={{0,16},{4,12},{8,24},{12,4},{16,0},{20,28},{24,8},{28,20},{1,17},{... | collective-permute-start | bytes 258056 | tf_op jit(solution)/shard_map/ppermute | solution.py:61
  22.6 0.0 copy-done.3
  22.6 1.4 %shard_map.67 = (s32[2,40]{1,0:T(2,128)S(1)}, s32[32]{0:T(128)S(1)}) custom-call(s32[1]{0:T(128)} %bitcast.here_ref.refs_0_, s32[2,8]{1,0:T(2,128)S(1)} %bitcast.16), custom_call_target="tpu_custom_call" | custom-call | tf_op jit(solution)/shard_map/pallas_call | solution.py:280
  24.0 0.3 shard_map.68.refs_1_.decayed_ref
  24.4 0.0 collective-permute-done.9.refs_7_
  24.4 1.2 %collective-permute-done.10.refs_8_ = f32[21,8,128]{2,1,0:T(8,128)S(1)} collective-permute-done((f32[21,8,128]{2,1,0:T(8,128)S(1)}, f32[21,8,128]{2,1,0:T(8,128)S(1)}, u32[]{:S(2)}, u32[]{:S(2)}) %collective-permute-start.10) | collective-permute-done | bytes 86048 | tf_op jit(solution)/shard_map/ppermute | solution.py:61
  25.5 0.0 collective-permute-done.1.refs_2_
  25.5 0.0 collective-permute-done.2.refs_3_
  25.5 0.0 collective-permute-done.3.refs_4_
  25.6 1.0 %shard_map.73 = (f32[2,2,16,1024]{3,2,1,0:T(8,128)S(1)}, f32[2,2,16,1024]{3,2,1,0:T(8,128)S(1)}, f32[2,2,16,1024]{3,2,1,0:T(8,128)S(1)}, f32[2,2,16,1024]{3,2,1,0:T(8,128)S(1)}, f32[2,8,16,1024]{3,2,1,0:T(8,128)S(1)}) custom-call(s32[2,40]{1,0:T(2,128)S(1)} %get-tuple-element.26.refs_0_, f32[32,16,1024]{2,1,0:T(8,128)S(1)} %shard_map.68.refs_1_.decayed_ref, ...), custom_call_target="tpu_custom_call" | custom-call | tf_op jit(solution)/shard_map/pallas_call | solution.py:301
  26.6 2.6 %collective-permute-start.11 = (f32[2,2,16,1024]{3,2,1,0:T(8,128)S(1)}, f32[2,2,16,1024]{3,2,1,0:T(8,128)S(1)}, u32[]{:S(2)}, u32[]{:S(2)}) collective-permute-start(f32[2,2,16,1024]{3,2,1,0:T(8,128)S(1)} %get-tuple-element.38), channel_id=1, source_target_pairs={{0,24},{4,28},{8,16},{12,20},{16,8},{20,12},{24,0},{28,4},{1,25},{... | collective-permute-start | bytes 786440 | tf_op jit(solution)/shard_map/ppermute | solution.py:61
  29.2 0.5 %collective-permute-start.12 = (f32[2,2,16,1024]{3,2,1,0:T(8,128)S(1)}, f32[2,2,16,1024]{3,2,1,0:T(8,128)S(1)}, u32[]{:S(2)}, u32[]{:S(2)}) collective-permute-start(f32[2,2,16,1024]{3,2,1,0:T(8,128)S(1)} %get-tuple-element.39), channel_id=1, source_target_pairs={{0,8},{4,20},{8,0},{12,28},{16,24},{20,4},{24,16},{28,12},{1,9},{5... | collective-permute-start | bytes 786440 | tf_op jit(solution)/shard_map/ppermute | solution.py:61
  29.7 0.5 %collective-permute-start.13 = (f32[2,2,16,1024]{3,2,1,0:T(8,128)S(1)}, f32[2,2,16,1024]{3,2,1,0:T(8,128)S(1)}, u32[]{:S(2)}, u32[]{:S(2)}) collective-permute-start(f32[2,2,16,1024]{3,2,1,0:T(8,128)S(1)} %get-tuple-element.40), channel_id=1, source_target_pairs={{0,16},{4,12},{8,24},{12,4},{16,0},{20,28},{24,8},{28,20},{1,17},{... | collective-permute-start | bytes 786440 | tf_op jit(solution)/shard_map/ppermute | solution.py:61
  30.2 3.1 %shard_map.74 = (f32[32,16,1024]{2,1,0:T(8,128)}, f32[32,16,1024]{2,1,0:T(8,128)}, f32[8,128]{1,0:T(8,128)S(1)}) custom-call(s32[32]{0:T(128)S(1)} %get-tuple-element.42.module_ref, f32[2,8,16,1024]{3,2,1,0:T(8,128)S(1)} %get-tuple-element.43.grad_ref, f32[32,16,1024]{2,1,0:T(8,128)S(1)} %shard_map.68.refs_1_.decayed_ref, f32[32,16,1024]{2,1,0:T(8,128)S(1)} %bitcast.13), custom_call_target="tpu_custom_call" | custom-call | tf_op jit(solution)/shard_map/pallas_call | solution.py:311
  33.2 2.8 %collective-permute-done.11.refs_1_ = f32[2,2,16,1024]{3,2,1,0:T(8,128)S(1)} collective-permute-done((f32[2,2,16,1024]{3,2,1,0:T(8,128)S(1)}, f32[2,2,16,1024]{3,2,1,0:T(8,128)S(1)}, u32[]{:S(2)}, u32[]{:S(2)}) %collective-permute-start.11) | collective-permute-done | bytes 262176 | tf_op jit(solution)/shard_map/ppermute | solution.py:61
  36.1 2.7 %collective-permute-done.12.refs_2_ = f32[2,2,16,1024]{3,2,1,0:T(8,128)S(1)} collective-permute-done((f32[2,2,16,1024]{3,2,1,0:T(8,128)S(1)}, f32[2,2,16,1024]{3,2,1,0:T(8,128)S(1)}, u32[]{:S(2)}, u32[]{:S(2)}) %collective-permute-start.12) | collective-permute-done | bytes 262176 | tf_op jit(solution)/shard_map/ppermute | solution.py:61
  38.8 0.0 collective-permute-done.13.refs_3_
  38.8 0.1 collective-permute-start.15
  38.9 0.5 %collective-permute-start.14 = (f32[4,16,1024]{2,1,0:T(8,128)S(1)}, f32[4,16,1024]{2,1,0:T(8,128)S(1)}, u32[]{:S(2)}, u32[]{:S(2)}) collective-permute-start(f32[4,16,1024]{2,1,0:T(8,128)S(1)} %get-tuple-element.45), channel_id=1, source_target_pairs={{0,4},{4,0},{8,12},{12,8},{16,20},{20,16},{24,28},{28,24},{1,5},{5... | collective-permute-start | bytes 786440 | tf_op jit(solution)/shard_map/ppermute | solution.py:324
  39.4 0.8 %shard_map.76.refs_2_ = f32[2,4,2,16,1024]{4,3,2,1,0:T(8,128)} custom-call(s32[1]{0:T(128)} %bitcast.here_ref.refs_0_, f32[2,2,16,1024]{3,2,1,0:T(8,128)S(1)} %collective-permute-done.11.refs_1_, f32[2,2,16,1024]{3,2,1,0:T(8,128)S(1)} %collective-permute-done.12.refs_2_, f32[2,2,16,1024]{3,2,1,0:T(8,128)S(1)} %collective-permute-done.13.refs_3_, ...), custom_call_target="tpu_custom_call" | custom-call | tf_op jit(solution)/shard_map/pallas_call | solution.py:326
  40.3 0.2 collective-permute-done.15.refs_1_
  40.4 0.8 %shard_map.77.refs_2_ = f32[2,4,2,16,1024]{4,3,2,1,0:T(8,128)} custom-call(s32[1]{0:T(128)} %bitcast.here_ref.refs_0_, f32[4,16,1024]{2,1,0:T(8,128)S(1)} %collective-permute-done.15.refs_1_, f32[2,4,2,16,1024]{4,3,2,1,0:T(8,128)} %shard_map.76.refs_2_), custom_call_target="tpu_custom_call", output_to_operand_aliasing={{}: (2, {})} | custom-call | tf_op jit(solution)/shard_map/pallas_call | solution.py:334
  41.2 0.0 collective-permute-done.14.refs_1_
  41.2 0.8 %shard_map.78 = f32[2,4,2,16,1024]{4,3,2,1,0:T(8,128)} custom-call(s32[1]{0:T(128)} %bitcast.here_ref.refs_0_, f32[4,16,1024]{2,1,0:T(8,128)S(1)} %collective-permute-done.14.refs_1_, f32[2,4,2,16,1024]{4,3,2,1,0:T(8,128)} %shard_map.77.refs_2_), custom_call_target="tpu_custom_call", output_to_operand_aliasing={{}: (2, {})} | custom-call | tf_op jit(solution)/shard_map/pallas_call | solution.py:334
  (5 shorter events, 0.1 us)
Async XLA Ops:
  0.6 11.0 %copy-start = (f32[32,1,16,1024]{3,2,1,0:T(8,128)S(1)}, f32[32,1,16,1024]{3,2,1,0:T(8,128)}, u32[]{:S(2)}) copy-start(f32[32,1,16,1024]{3,2,1,0:T(8,128)} %param.7) | copy-start | bytes 6291460
  0.6 1.4 %copy-start.2 = (f32[1,2,128,1024]{3,2,1,0:T(8,128)S(1)}, f32[1,2,128,1024]{3,2,1,0:T(8,128)}, u32[]{:S(2)}) copy-start(f32[1,2,128,1024]{3,2,1,0:T(8,128)} %param.4) | copy-start | bytes 3145732
  2.1 5.8 %collective-permute-start = (f32[2,4,16,1024]{3,2,1,0:T(8,128)S(1)}, f32[2,4,16,1024]{3,2,1,0:T(8,128)S(1)}, u32[]{:S(2)}, u32[]{:S(2)}) collective-permute-start(f32[2,4,16,1024]{3,2,1,0:T(8,128)S(1)} %get-tuple-element.28), channel_id=1, source_target_pairs={{0,4},{4,0},{8,12},{12,8},{16,20},{20,16},{24,28},{28,24},{1,5},{5... | collective-permute-start | bytes 1572872 | tf_op jit(solution)/shard_map/ppermute | solution.py:267
  2.6 8.6 %collective-permute-start.4 = (f32[8,128]{1,0:T(8,128)S(1)}, f32[8,128]{1,0:T(8,128)S(1)}, u32[]{:S(2)}, u32[]{:S(2)}) collective-permute-start(f32[8,128]{1,0:T(8,128)S(1)} %get-tuple-element.33.refs_0_), channel_id=1, source_target_pairs={{0,3},{1,2},{2,1},{3,0},{4,7},{5,6},{6,5},{7,4},{8,11},{9,10},{10,... | collective-permute-start | bytes 12296 | tf_op jit(solution)/shard_map/ppermute | solution.py:269
  7.3 4.6 %collective-permute-start.5 = (f32[8,128]{1,0:T(8,128)S(1)}, f32[8,128]{1,0:T(8,128)S(1)}, u32[]{:S(2)}, u32[]{:S(2)}) collective-permute-start(f32[8,128]{1,0:T(8,128)S(1)} %get-tuple-element.33.refs_0_), channel_id=1, source_target_pairs={{0,2},{1,3},{2,0},{3,1},{4,6},{5,7},{6,4},{7,5},{8,10},{9,11},{10,... | collective-permute-start | bytes 12296 | tf_op jit(solution)/shard_map/ppermute | solution.py:269
  7.3 4.6 %collective-permute-start.6 = (f32[8,128]{1,0:T(8,128)S(1)}, f32[8,128]{1,0:T(8,128)S(1)}, u32[]{:S(2)}, u32[]{:S(2)}) collective-permute-start(f32[8,128]{1,0:T(8,128)S(1)} %get-tuple-element.33.refs_0_), channel_id=1, source_target_pairs={{0,1},{1,0},{2,3},{3,2},{4,5},{5,4},{6,7},{7,6},{8,9},{9,8},{10,11... | collective-permute-start | bytes 12296 | tf_op jit(solution)/shard_map/ppermute | solution.py:269
  8.0 17.5 %collective-permute-start.1 = (f32[44,8,128]{2,1,0:T(8,128)S(1)}, f32[44,8,128]{2,1,0:T(8,128)S(1)}, u32[]{:S(2)}, u32[]{:S(2)}) collective-permute-start(f32[44,8,128]{2,1,0:T(8,128)S(1)} %get-tuple-element.29), channel_id=1, source_target_pairs={{0,24},{4,28},{8,16},{12,20},{16,8},{20,12},{24,0},{28,4},{1,25},{... | collective-permute-start | bytes 540680 | tf_op jit(solution)/shard_map/ppermute | solution.py:61
  10.7 14.9 %collective-permute-start.2 = (f32[44,8,128]{2,1,0:T(8,128)S(1)}, f32[44,8,128]{2,1,0:T(8,128)S(1)}, u32[]{:S(2)}, u32[]{:S(2)}) collective-permute-start(f32[44,8,128]{2,1,0:T(8,128)S(1)} %get-tuple-element.30), channel_id=1, source_target_pairs={{0,8},{4,20},{8,0},{12,28},{16,24},{20,4},{24,16},{28,12},{1,9},{5... | collective-permute-start | bytes 540680 | tf_op jit(solution)/shard_map/ppermute | solution.py:61
  11.2 14.3 %collective-permute-start.3 = (f32[44,8,128]{2,1,0:T(8,128)S(1)}, f32[44,8,128]{2,1,0:T(8,128)S(1)}, u32[]{:S(2)}, u32[]{:S(2)}) collective-permute-start(f32[44,8,128]{2,1,0:T(8,128)S(1)} %get-tuple-element.31), channel_id=1, source_target_pairs={{0,16},{4,12},{8,24},{12,4},{16,0},{20,28},{24,8},{28,20},{1,17},{... | collective-permute-start | bytes 540680 | tf_op jit(solution)/shard_map/ppermute | solution.py:61
  11.9 10.7 %copy-start.3 = (s32[8,2]{0,1:T(2,128)S(1)}, s32[8,2]{0,1:T(2,128)}, u32[]{:S(2)}) copy-start(s32[8,2]{0,1:T(2,128)} %param.5) | copy-start | bytes 196
  11.9 12.1 %copy-start.1 = (f32[32,1,16,1024]{3,2,1,0:T(8,128)S(1)}, f32[32,1,16,1024]{3,2,1,0:T(8,128)}, u32[]{:S(2)}) copy-start(f32[32,1,16,1024]{3,2,1,0:T(8,128)} %param.6) | copy-start | bytes 6291460
  11.9 1.2 %collective-permute-start.7 = (f32[8,128]{1,0:T(8,128)S(1)}, f32[8,128]{1,0:T(8,128)S(1)}, u32[]{:S(2)}, u32[]{:S(2)}) collective-permute-start(f32[8,128]{1,0:T(8,128)S(1)} %shard_map.71.refs_1_), channel_id=1, source_target_pairs={{0,4},{4,0},{8,12},{12,8},{16,20},{20,16},{24,28},{28,24},{1,5},{5... | collective-permute-start | bytes 12296 | tf_op jit(solution)/shard_map/ppermute | solution.py:292
  13.2 7.9 %collective-permute-start.8 = (f32[21,8,128]{2,1,0:T(8,128)S(1)}, f32[21,8,128]{2,1,0:T(8,128)S(1)}, u32[]{:S(2)}, u32[]{:S(2)}) collective-permute-start(f32[21,8,128]{2,1,0:T(8,128)S(1)} %get-tuple-element.34), channel_id=1, source_target_pairs={{0,24},{4,28},{8,16},{12,20},{16,8},{20,12},{24,0},{28,4},{1,25},{... | collective-permute-start | bytes 258056 | tf_op jit(solution)/shard_map/ppermute | solution.py:61
  15.9 8.5 %collective-permute-start.9 = (f32[21,8,128]{2,1,0:T(8,128)S(1)}, f32[21,8,128]{2,1,0:T(8,128)S(1)}, u32[]{:S(2)}, u32[]{:S(2)}) collective-permute-start(f32[21,8,128]{2,1,0:T(8,128)S(1)} %get-tuple-element.35), channel_id=1, source_target_pairs={{0,8},{4,20},{8,0},{12,28},{16,24},{20,4},{24,16},{28,12},{1,9},{5... | collective-permute-start | bytes 258056 | tf_op jit(solution)/shard_map/ppermute | solution.py:61
  21.1 4.5 %collective-permute-start.10 = (f32[21,8,128]{2,1,0:T(8,128)S(1)}, f32[21,8,128]{2,1,0:T(8,128)S(1)}, u32[]{:S(2)}, u32[]{:S(2)}) collective-permute-start(f32[21,8,128]{2,1,0:T(8,128)S(1)} %get-tuple-element.36), channel_id=1, source_target_pairs={{0,16},{4,12},{8,24},{12,4},{16,0},{20,28},{24,8},{28,20},{1,17},{... | collective-permute-start | bytes 258056 | tf_op jit(solution)/shard_map/ppermute | solution.py:61
  26.6 9.5 %collective-permute-start.11 = (f32[2,2,16,1024]{3,2,1,0:T(8,128)S(1)}, f32[2,2,16,1024]{3,2,1,0:T(8,128)S(1)}, u32[]{:S(2)}, u32[]{:S(2)}) collective-permute-start(f32[2,2,16,1024]{3,2,1,0:T(8,128)S(1)} %get-tuple-element.38), channel_id=1, source_target_pairs={{0,24},{4,28},{8,16},{12,20},{16,8},{20,12},{24,0},{28,4},{1,25},{... | collective-permute-start | bytes 786440 | tf_op jit(solution)/shard_map/ppermute | solution.py:61
  29.2 9.6 %collective-permute-start.12 = (f32[2,2,16,1024]{3,2,1,0:T(8,128)S(1)}, f32[2,2,16,1024]{3,2,1,0:T(8,128)S(1)}, u32[]{:S(2)}, u32[]{:S(2)}) collective-permute-start(f32[2,2,16,1024]{3,2,1,0:T(8,128)S(1)} %get-tuple-element.39), channel_id=1, source_target_pairs={{0,8},{4,20},{8,0},{12,28},{16,24},{20,4},{24,16},{28,12},{1,9},{5... | collective-permute-start | bytes 786440 | tf_op jit(solution)/shard_map/ppermute | solution.py:61
  29.7 9.1 %collective-permute-start.13 = (f32[2,2,16,1024]{3,2,1,0:T(8,128)S(1)}, f32[2,2,16,1024]{3,2,1,0:T(8,128)S(1)}, u32[]{:S(2)}, u32[]{:S(2)}) collective-permute-start(f32[2,2,16,1024]{3,2,1,0:T(8,128)S(1)} %get-tuple-element.40), channel_id=1, source_target_pairs={{0,16},{4,12},{8,24},{12,4},{16,0},{20,28},{24,8},{28,20},{1,17},{... | collective-permute-start | bytes 786440 | tf_op jit(solution)/shard_map/ppermute | solution.py:61
  38.8 1.6 %collective-permute-start.15 = (f32[4,16,1024]{2,1,0:T(8,128)S(1)}, f32[4,16,1024]{2,1,0:T(8,128)S(1)}, u32[]{:S(2)}, u32[]{:S(2)}) collective-permute-start(f32[4,16,1024]{2,1,0:T(8,128)S(1)} %get-tuple-element.46), channel_id=1, source_target_pairs={{0,4},{4,0},{8,12},{12,8},{16,20},{20,16},{24,28},{28,24},{1,5},{5... | collective-permute-start | bytes 786440 | tf_op jit(solution)/shard_map/ppermute | solution.py:324
  38.9 2.3 %collective-permute-start.14 = (f32[4,16,1024]{2,1,0:T(8,128)S(1)}, f32[4,16,1024]{2,1,0:T(8,128)S(1)}, u32[]{:S(2)}, u32[]{:S(2)}) collective-permute-start(f32[4,16,1024]{2,1,0:T(8,128)S(1)} %get-tuple-element.45), channel_id=1, source_target_pairs={{0,4},{4,0},{8,12},{12,8},{16,20},{20,16},{24,28},{28,24},{1,5},{5... | collective-permute-start | bytes 786440 | tf_op jit(solution)/shard_map/ppermute | solution.py:324
